TPU v7x, 32 devices: a whole 2x2x4 slice. The times are simulated.
32 devices in a mesh: seq: 4 (over y, x), fsdp: 8 (over z, core).
Axes of the slice: x: 2, y: 2, z: 4, core: 2. Of those that a mesh axis runs over, the one named last changes fastest.
Arguments:
- clip_tokens: float32 [16, 1024, 1024], P('fsdp', 'seq'), may hold values from -6 to 6
- patch_coords: int32 [3, 16, 1024], P(None, 'fsdp', 'seq'), may hold values from 0 to 15, as said below
- out_cotangent: float32 [16, 1024, 1024], P('fsdp', 'seq'), may hold values from -6 to 6
- vector_params: float32 [2, 13312], P(None, 'fsdp'), may hold values from -0.6 to 1.4, as said below
- qkv_weight: float32 [2, 1024, 3072], P(None, 'fsdp'), may hold values from -0.1875 to 0.1875
- proj_weight: float32 [2, 1024, 1024], P(None, 'fsdp'), may hold values from -0.75 to 0.75
- up_weight: float32 [2, 1024, 4096], P(None, 'fsdp'), may hold values from -0.1875 to 0.1875
- down_weight: float32 [2, 4096, 1024], P(None, 'fsdp'), may hold values from -0.09375 to 0.09375
- first_vector: float32 [2, 13312], P(None, 'fsdp'), may hold values from -1 to 1
- first_qkv: float32 [2, 1024, 3072], P(None, 'fsdp'), may hold values from -1 to 1
- first_proj: float32 [2, 1024, 1024], P(None, 'fsdp'), may hold values from -1 to 1
- first_up: float32 [2, 1024, 4096], P(None, 'fsdp'), may hold values from -1 to 1
- first_down: float32 [2, 4096, 1024], P(None, 'fsdp'), may hold values from -1 to 1
- second_vector: float32 [2, 13312], P(None, 'fsdp'), may hold values from 0.005 to 0.1
- second_qkv: float32 [2, 1024, 3072], P(None, 'fsdp'), may hold values from 0.005 to 0.1
- second_proj: float32 [2, 1024, 1024], P(None, 'fsdp'), may hold values from 0.005 to 0.1
- second_up: float32 [2, 1024, 4096], P(None, 'fsdp'), may hold values from 0.005 to 0.1
- second_down: float32 [2, 4096, 1024], P(None, 'fsdp'), may hold values from 0.005 to 0.1
Outputs:
- block_output: float32 [16, 1024, 1024], P('fsdp', 'seq')
- input_grad: float32 [16, 1024, 1024], P('fsdp', 'seq')
- grad_vector: float32 [2, 13312], P(None, 'fsdp')
- grad_qkv: float32 [2, 1024, 3072], P(None, 'fsdp')
- grad_proj: float32 [2, 1024, 1024], P(None, 'fsdp')
- grad_up: float32 [2, 1024, 4096], P(None, 'fsdp')
- grad_down: float32 [2, 4096, 1024], P(None, 'fsdp')
- grad_norm: float32 [1], replicated
- new_first_vector: float32 [2, 13312], P(None, 'fsdp')
- new_first_qkv: float32 [2, 1024, 3072], P(None, 'fsdp')
- new_first_proj: float32 [2, 1024, 1024], P(None, 'fsdp')
- new_first_up: float32 [2, 1024, 4096], P(None, 'fsdp')
- new_first_down: float32 [2, 4096, 1024], P(None, 'fsdp')
- new_second_vector: float32 [2, 13312], P(None, 'fsdp')
- new_second_qkv: float32 [2, 1024, 3072], P(None, 'fsdp')
- new_second_proj: float32 [2, 1024, 1024], P(None, 'fsdp')
- new_second_up: float32 [2, 1024, 4096], P(None, 'fsdp')
- new_second_down: float32 [2, 4096, 1024], P(None, 'fsdp')
- new_vector: float32 [2, 13312], P(None, 'fsdp')
- new_qkv: float32 [2, 1024, 3072], P(None, 'fsdp')
- new_proj: float32 [2, 1024, 1024], P(None, 'fsdp')
- new_up: float32 [2, 1024, 4096], P(None, 'fsdp')
- new_down: float32 [2, 4096, 1024], P(None, 'fsdp')
- copy_vector: bfloat16 [2, 13312], P(None, 'fsdp')
- copy_qkv: bfloat16 [2, 1024, 3072], P(None, 'fsdp')
- copy_proj: bfloat16 [2, 1024, 1024], P(None, 'fsdp')
- copy_up: bfloat16 [2, 1024, 4096], P(None, 'fsdp')
- copy_down: bfloat16 [2, 4096, 1024], P(None, 'fsdp')
Inputs may be any that keep to these rules, and one draw needn't show every extreme that they name: patch_coords[0] is a token's frame among 8, patch_coords[1] and [2] its row and column among 16; the 1024 patches of a clip are distinct and in raster order. `vector_params`: gains lie within 0.6 to 1.4, biases within -0.6 to 0.6.
All inputs are finite; a program needn't handle non-finite values.
Results may differ from a plain program's by a relative error of at most 0.01.
The roundings to bfloat16 on the way count: a program that leaves them out, or rounds other values in their place, can miss the bound.
Values may be sent and summed in bfloat16 or wider, within the bound.
A program may use at most 576 MiB of HBM per device.

v0:
```python
from functools import partial
import math

import jax
import jax.numpy as jnp
from jax import lax
from jax.sharding import PartitionSpec as P

D = 1024
HEADS = 16
HEAD_DIM = 64


BETA_ONE = 0.5
BETA_TWO = 0.75
LEARN_RATE = 0.1
DECAY_RATE = 0.1
CLIP_RATIO = 0.2
ADAM_EPS = 1e-08
ROPE_BASE = 10000.0


def pieces(vector):
    return (
        vector[0:D],
        vector[D : 2 * D],
        vector[2 * D : 3 * D],
        vector[3 * D : 4 * D],
        vector[4 * D : 5 * D],
        vector[5 * D : 6 * D],
        vector[6 * D : 9 * D],
        vector[9 * D :],
    )


def layer_norm(hidden, ln_gain, ln_shift):
    center = hidden - jnp.mean(hidden, axis=-1, keepdims=True)
    spread = jnp.mean(center * center, axis=-1, keepdims=True)
    return center * lax.rsqrt(spread + 1e-06) * ln_gain + ln_shift


def gelu_exact(upward):
    return 0.5 * upward * (1.0 + jax.scipy.special.erf(upward * (1.0 / math.sqrt(2.0))))


def rotary_tables(coords_clip, pair_count):
    pair_index = jnp.arange(pair_count, dtype=jnp.int32)
    side_pairs = pair_count // 3
    time_pairs = pair_count - 2 * side_pairs
    in_time = pair_index < time_pairs
    in_height = jnp.logical_and(pair_index >= time_pairs, pair_index < time_pairs + side_pairs)
    offset = jnp.where(in_time, 0, jnp.where(in_height, time_pairs, time_pairs + side_pairs))
    seg_span = jnp.where(in_time, time_pairs, side_pairs)
    local_rank = (pair_index - offset).astype(jnp.float32)
    frequency = jnp.exp(-math.log(ROPE_BASE) * local_rank / seg_span.astype(jnp.float32))
    positions = coords_clip.astype(jnp.float32)
    chosen = jnp.where(
        in_time[None, :],
        positions[0][:, None],
        jnp.where(in_height[None, :], positions[1][:, None], positions[2][:, None]),
    )
    angles = chosen * frequency[None, :]
    return (jnp.cos(angles), jnp.sin(angles))


def rotate(values_in, cosine, sine_table):
    half_width = values_in.shape[-1] // 2
    first_half = values_in[..., :half_width]
    second_half = values_in[..., half_width:]
    cos_wide = cosine[:, None, :]
    sin_wide = sine_table[:, None, :]
    return jnp.concatenate(
        [
            first_half * cos_wide - second_half * sin_wide,
            first_half * sin_wide + second_half * cos_wide,
        ],
        axis=-1,
    )


def attend_forward(queries, key_rows, value_rows):
    full_len = queries.shape[0]
    block_rows = min(512, full_len)
    score_scale = HEAD_DIM ** (-0.5)
    query_blocks = queries.reshape(
        full_len // block_rows, block_rows, queries.shape[1], queries.shape[2]
    )

    def one_block(query_block):
        scores = (
            jnp.einsum("qhd,khd->hqk", query_block, key_rows, preferred_element_type=jnp.float32)
            * score_scale
        )
        row_max = jnp.max(scores, axis=-1, keepdims=True)
        exponent = jnp.exp(scores - row_max)
        row_total = jnp.sum(exponent, axis=-1, keepdims=True)
        prob_low = (exponent / row_total).astype(jnp.bfloat16)
        mixed_rows = jnp.einsum(
            "hqk,khd->qhd", prob_low, value_rows, preferred_element_type=jnp.float32
        )
        return (mixed_rows, row_max[..., 0] + jnp.log(row_total[..., 0]))

    mixed_rows, log_sums = lax.map(one_block, query_blocks)
    return (mixed_rows.reshape(queries.shape), log_sums)


def attend_backward(queries, key_rows, value_rows, log_sums, head_grad):
    full_len = queries.shape[0]
    block_rows = min(512, full_len)
    score_scale = HEAD_DIM ** (-0.5)
    block_shape = (full_len // block_rows, block_rows, queries.shape[1], queries.shape[2])

    def one_block(carry, block_in):
        key_grad, value_grad = carry
        query_block, grad_block, lse_block = block_in
        scores = (
            jnp.einsum("qhd,khd->hqk", query_block, key_rows, preferred_element_type=jnp.float32)
            * score_scale
        )
        prob_rows = jnp.exp(scores - lse_block[..., None])
        prob_low = prob_rows.astype(jnp.bfloat16)
        value_grad = value_grad + jnp.einsum(
            "hqk,qhd->khd", prob_low, grad_block, preferred_element_type=jnp.float32
        )
        prob_grad = jnp.einsum(
            "qhd,khd->hqk", grad_block, value_rows, preferred_element_type=jnp.float32
        )
        score_grad = prob_rows * (
            prob_grad - jnp.sum(prob_rows * prob_grad, axis=-1, keepdims=True)
        )
        score_low = (score_grad * score_scale).astype(jnp.bfloat16)
        query_grad = jnp.einsum(
            "hqk,khd->qhd", score_low, key_rows, preferred_element_type=jnp.float32
        )
        key_grad = key_grad + jnp.einsum(
            "hqk,qhd->khd", score_low, query_block, preferred_element_type=jnp.float32
        )
        return ((key_grad, value_grad), query_grad)

    zero_heads = jnp.zeros(queries.shape, jnp.float32)
    (key_grad, value_grad), query_grad = lax.scan(
        one_block,
        (zero_heads, zero_heads),
        (queries.reshape(block_shape), head_grad.reshape(block_shape), log_sums),
    )
    return (query_grad.reshape(queries.shape), key_grad, value_grad)


def layer_forward(hidden, cosine, sine_table, weights, seq_parts):
    vector_low, qkv_w, proj_w, up_w, down_w = weights
    gain_one, shift_one, gain_two, shift_two, proj_bias, down_bias, qkv_bias, up_bias = pieces(
        vector_low.astype(jnp.float32)
    )
    row_count = hidden.shape[0]
    local_heads = HEADS // seq_parts
    normed = layer_norm(hidden, gain_one, shift_one).astype(jnp.bfloat16)
    qkv_all = jnp.dot(normed, qkv_w, preferred_element_type=jnp.float32) + qkv_bias
    split_qkv = qkv_all.reshape(row_count, 3, HEADS, HEAD_DIM)
    stacked = jnp.stack(
        [
            rotate(split_qkv[:, 0], cosine, sine_table),
            rotate(split_qkv[:, 1], cosine, sine_table),
            split_qkv[:, 2],
        ],
        axis=1,
    ).astype(jnp.bfloat16)
    packed = stacked.reshape(row_count, 3, seq_parts, local_heads * HEAD_DIM)
    by_heads = lax.all_to_all(packed, "seq", split_axis=2, concat_axis=0, tiled=True)
    full_len = by_heads.shape[0]
    by_heads = by_heads.reshape(full_len, 3, local_heads, HEAD_DIM)
    mixed_rows, log_sums = attend_forward(by_heads[:, 0], by_heads[:, 1], by_heads[:, 2])
    mixed_low = mixed_rows.astype(jnp.bfloat16).reshape(full_len, 1, local_heads * HEAD_DIM)
    by_tokens = lax.all_to_all(mixed_low, "seq", split_axis=0, concat_axis=1, tiled=True).reshape(
        row_count, D
    )
    after_attn = hidden + jnp.dot(by_tokens, proj_w, preferred_element_type=jnp.float32) + proj_bias
    normed_two = layer_norm(after_attn, gain_two, shift_two).astype(jnp.bfloat16)
    upward = jnp.dot(normed_two, up_w, preferred_element_type=jnp.float32) + up_bias
    active = gelu_exact(upward).astype(jnp.bfloat16)
    result = after_attn + jnp.dot(active, down_w, preferred_element_type=jnp.float32) + down_bias
    saved_state = (
        hidden,
        normed,
        by_heads,
        log_sums,
        by_tokens,
        after_attn,
        normed_two,
        upward,
        active,
    )
    return (result, saved_state)


def layer_backward(grad_out, saved_state, weights, cosine, sine_table, seq_parts):
    vector_low, qkv_w, proj_w, up_w, down_w = weights
    gain_one, shift_one, gain_two, shift_two, proj_bias, down_bias, qkv_bias, up_bias = pieces(
        vector_low.astype(jnp.float32)
    )
    hidden, normed, by_heads, log_sums, by_tokens, after_attn, normed_two, upward, active = (
        saved_state
    )
    row_count = hidden.shape[0]
    local_heads = HEADS // seq_parts
    down_bias_grad = jnp.sum(grad_out, axis=0)
    grad_low = grad_out.astype(jnp.bfloat16)
    down_grad = jnp.dot(active.T, grad_low, preferred_element_type=jnp.float32)
    active_grad = jnp.dot(grad_low, down_w.T, preferred_element_type=jnp.float32)
    gelu_value, gelu_pull = jax.vjp(gelu_exact, upward)
    upward_grad = gelu_pull(active_grad)[0]
    up_bias_grad = jnp.sum(upward_grad, axis=0)
    upward_low = upward_grad.astype(jnp.bfloat16)
    up_grad = jnp.dot(normed_two.T, upward_low, preferred_element_type=jnp.float32)
    normed_two_grad = jnp.dot(upward_low, up_w.T, preferred_element_type=jnp.float32)
    norm_value_two, norm_pull_two = jax.vjp(layer_norm, after_attn, gain_two, shift_two)
    attn_in_grad, gain_two_grad, shift_two_grad = norm_pull_two(normed_two_grad)
    after_grad = grad_out + attn_in_grad
    proj_bias_grad = jnp.sum(after_grad, axis=0)
    after_low = after_grad.astype(jnp.bfloat16)
    proj_grad = jnp.dot(by_tokens.T, after_low, preferred_element_type=jnp.float32)
    mixed_grad = jnp.dot(after_low, proj_w.T, preferred_element_type=jnp.float32).astype(
        jnp.bfloat16
    )
    head_grad = lax.all_to_all(
        mixed_grad.reshape(row_count, seq_parts, local_heads * HEAD_DIM),
        "seq",
        split_axis=1,
        concat_axis=0,
        tiled=True,
    )
    full_len = head_grad.shape[0]
    head_grad = head_grad.reshape(full_len, local_heads, HEAD_DIM)
    query_grad, key_grad, value_grad = attend_backward(
        by_heads[:, 0], by_heads[:, 1], by_heads[:, 2], log_sums, head_grad
    )
    stacked_grad = (
        jnp.stack([query_grad, key_grad, value_grad], axis=1)
        .astype(jnp.bfloat16)
        .reshape(full_len, 3, 1, local_heads * HEAD_DIM)
    )
    token_grad = (
        lax.all_to_all(stacked_grad, "seq", split_axis=0, concat_axis=2, tiled=True)
        .reshape(row_count, 3, HEADS, HEAD_DIM)
        .astype(jnp.float32)
    )
    pair_grad_in = token_grad[:, :2].reshape(row_count, 2 * HEADS, HEAD_DIM)
    rotated_value, rotate_pull = jax.vjp(
        partial(rotate, cosine=cosine, sine_table=sine_table), pair_grad_in
    )
    pair_grad = rotate_pull(pair_grad_in)[0].reshape(row_count, 2, HEADS, HEAD_DIM)
    qkv_grad = jnp.concatenate([pair_grad, token_grad[:, 2:]], axis=1).reshape(row_count, 3 * D)
    qkv_bias_grad = jnp.sum(qkv_grad, axis=0)
    qkv_low = qkv_grad.astype(jnp.bfloat16)
    qkv_w_grad = jnp.dot(normed.T, qkv_low, preferred_element_type=jnp.float32)
    normed_grad = jnp.dot(qkv_low, qkv_w.T, preferred_element_type=jnp.float32)
    norm_value_one, norm_pull_one = jax.vjp(layer_norm, hidden, gain_one, shift_one)
    in_grad, gain_one_grad, shift_one_grad = norm_pull_one(normed_grad)
    input_grad = after_grad + in_grad
    vector_grad = jnp.concatenate(
        [
            gain_one_grad,
            shift_one_grad,
            gain_two_grad,
            shift_two_grad,
            proj_bias_grad,
            down_bias_grad,
            qkv_bias_grad,
            up_bias_grad,
        ]
    )
    return (input_grad, (vector_grad, qkv_w_grad, proj_grad, up_grad, down_grad))


def adam_update(master, grad_item, first_old, second_old, factor):
    clipped = grad_item * factor
    first_new = BETA_ONE * first_old + (1.0 - BETA_ONE) * clipped
    second_new = BETA_TWO * second_old + (1.0 - BETA_TWO) * clipped * clipped
    updated = master - LEARN_RATE * (
        first_new / (jnp.sqrt(second_new) + ADAM_EPS) + DECAY_RATE * master
    )
    return (first_new, second_new, updated)


def per_device(
    clip_tokens,
    patch_coords,
    out_cotangent,
    vector_params,
    qkv_weight,
    proj_weight,
    up_weight,
    down_weight,
    first_vector,
    first_qkv,
    first_proj,
    first_up,
    first_down,
    second_vector,
    second_qkv,
    second_proj,
    second_up,
    second_down,
):
    masters = (vector_params, qkv_weight, proj_weight, up_weight, down_weight)
    firsts = (first_vector, first_qkv, first_proj, first_up, first_down)
    seconds = (second_vector, second_qkv, second_proj, second_up, second_down)
    lowered = tuple((master.astype(jnp.bfloat16) for master in masters))
    layer_count = vector_params.shape[0]
    batch_local = clip_tokens.shape[0]
    seq_parts = lax.axis_size("seq")
    fsdp_parts = lax.axis_size("fsdp")
    grad_accum = tuple(
        (
            jnp.zeros((layer_count, master.shape[1] * fsdp_parts) + master.shape[2:], jnp.float32)
            for master in masters
        )
    )
    output_rows = []
    input_rows = []
    for batch_idx in range(batch_local):
        cosine, sine_table = rotary_tables(patch_coords[:, batch_idx], HEAD_DIM // 2)
        hidden = clip_tokens[batch_idx]
        saved_layers = []
        for layer_idx in range(layer_count):
            weights = (
                lax.all_gather(lowered[0][layer_idx], "fsdp", axis=0, tiled=True),
                lax.all_gather(lowered[1][layer_idx], "fsdp", axis=0, tiled=True),
                lax.all_gather(lowered[2][layer_idx], "fsdp", axis=0, tiled=True),
                lax.all_gather(lowered[3][layer_idx], "fsdp", axis=0, tiled=True),
                lax.all_gather(lowered[4][layer_idx], "fsdp", axis=0, tiled=True),
            )
            hidden, saved_state = layer_forward(hidden, cosine, sine_table, weights, seq_parts)
            saved_layers.append(saved_state)
        output_rows.append(hidden)
        grad_rows = out_cotangent[batch_idx]
        for layer_idx in reversed(range(layer_count)):
            weights = (
                lax.all_gather(lowered[0][layer_idx], "fsdp", axis=0, tiled=True),
                lax.all_gather(lowered[1][layer_idx], "fsdp", axis=0, tiled=True),
                lax.all_gather(lowered[2][layer_idx], "fsdp", axis=0, tiled=True),
                lax.all_gather(lowered[3][layer_idx], "fsdp", axis=0, tiled=True),
                lax.all_gather(lowered[4][layer_idx], "fsdp", axis=0, tiled=True),
            )
            grad_rows, layer_grads = layer_backward(
                grad_rows, saved_layers[layer_idx], weights, cosine, sine_table, seq_parts
            )
            grad_accum = tuple(
                (
                    accum_item.at[layer_idx].add(grad_item)
                    for accum_item, grad_item in zip(grad_accum, layer_grads)
                )
            )
        input_rows.append(grad_rows)
    shard_sums = (
        lax.psum_scatter(grad_accum[0], "fsdp", scatter_dimension=1, tiled=True),
        lax.psum_scatter(grad_accum[1], "fsdp", scatter_dimension=1, tiled=True),
        lax.psum_scatter(grad_accum[2], "fsdp", scatter_dimension=1, tiled=True),
        lax.psum_scatter(grad_accum[3], "fsdp", scatter_dimension=1, tiled=True),
        lax.psum_scatter(grad_accum[4], "fsdp", scatter_dimension=1, tiled=True),
    )
    seq_sums = lax.psum(
        (shard_sums[0], shard_sums[1], shard_sums[2], shard_sums[3], shard_sums[4]), "seq"
    )
    clip_count = batch_local * fsdp_parts
    grad_shards = tuple((sum_item / clip_count for sum_item in seq_sums))
    local_squares = sum((jnp.sum(grad_item * grad_item) for grad_item in grad_shards))
    squares_total = lax.psum(local_squares, "fsdp")
    norm_value = jnp.sqrt(squares_total)
    param_count = sum((master.size for master in masters)) * fsdp_parts
    factor = jnp.minimum(1.0, CLIP_RATIO * math.sqrt(float(param_count)) / (norm_value + 1e-06))
    updates = [
        adam_update(master, grad_item, first_old, second_old, factor)
        for master, grad_item, first_old, second_old in zip(masters, grad_shards, firsts, seconds)
    ]
    return (
        jnp.stack(output_rows),
        jnp.stack(input_rows),
        grad_shards[0],
        grad_shards[1],
        grad_shards[2],
        grad_shards[3],
        grad_shards[4],
        norm_value.reshape(1),
        updates[0][0],
        updates[1][0],
        updates[2][0],
        updates[3][0],
        updates[4][0],
        updates[0][1],
        updates[1][1],
        updates[2][1],
        updates[3][1],
        updates[4][1],
        updates[0][2],
        updates[1][2],
        updates[2][2],
        updates[3][2],
        updates[4][2],
        updates[0][2].astype(jnp.bfloat16),
        updates[1][2].astype(jnp.bfloat16),
        updates[2][2].astype(jnp.bfloat16),
        updates[3][2].astype(jnp.bfloat16),
        updates[4][2].astype(jnp.bfloat16),
    )


def solution(mesh):
    in_specs = (
        P("fsdp", "seq", None),
        P(None, "fsdp", "seq"),
        P("fsdp", "seq", None),
        P(None, "fsdp"),
        P(None, "fsdp", None),
        P(None, "fsdp", None),
        P(None, "fsdp", None),
        P(None, "fsdp", None),
        P(None, "fsdp"),
        P(None, "fsdp", None),
        P(None, "fsdp", None),
        P(None, "fsdp", None),
        P(None, "fsdp", None),
        P(None, "fsdp"),
        P(None, "fsdp", None),
        P(None, "fsdp", None),
        P(None, "fsdp", None),
        P(None, "fsdp", None),
    )
    out_specs = (
        P("fsdp", "seq", None),
        P("fsdp", "seq", None),
        P(None, "fsdp"),
        P(None, "fsdp", None),
        P(None, "fsdp", None),
        P(None, "fsdp", None),
        P(None, "fsdp", None),
        P(),
        P(None, "fsdp"),
        P(None, "fsdp", None),
        P(None, "fsdp", None),
        P(None, "fsdp", None),
        P(None, "fsdp", None),
        P(None, "fsdp"),
        P(None, "fsdp", None),
        P(None, "fsdp", None),
        P(None, "fsdp", None),
        P(None, "fsdp", None),
        P(None, "fsdp"),
        P(None, "fsdp", None),
        P(None, "fsdp", None),
        P(None, "fsdp", None),
        P(None, "fsdp", None),
        P(None, "fsdp"),
        P(None, "fsdp", None),
        P(None, "fsdp", None),
        P(None, "fsdp", None),
        P(None, "fsdp", None),
    )
    return jax.shard_map(
        per_device, mesh=mesh, in_specs=in_specs, out_specs=out_specs, check_vma=False
    )
```

profile of v0, /device:TPU:0, one launch (start us, length us, event | category | flops | bytes accessed | tf_op | source)
XLA Modules:
  0.0 2585.2 jit_solution(7772518018821503351)
XLA Ops:
  56.8 22.2 all-gather.19.cloned.1.call-done
  222.8 52.6 %all-gather.25.cloned.1.call-done = bf16[1,4096,1024]{2,1,0:T(8,128)(2,1)} async-done(((bf16[1,512,1024]{2,1,0:T(8,128)(2,1)}), bf16[1,4096,1024]{2,1,0:T(8,128)(2,1)}) %all-gather.25.cloned.1.call-update) | async-done | bytes 8388624 | tf_op jit(solution)/shard_map/all_gather | solution.py:330
  282.9 58.0 %all-gather.27.cloned.1.call-done = bf16[1,1024,3072]{2,1,0:T(8,128)(2,1)} async-done(((bf16[1,128,3072]{2,1,0:T(8,128)(2,1)}), bf16[1,1024,3072]{2,1,0:T(8,128)(2,1)}) %all-gather.27.cloned.1.call-update) | async-done | bytes 6291472 | tf_op jit(solution)/shard_map/all_gather | solution.py:327
  497.7 39.5 %all-gather.33.cloned.1.call-done = bf16[1,4096,1024]{2,1,0:T(8,128)(2,1)} async-done(((bf16[1,512,1024]{2,1,0:T(8,128)(2,1)}), bf16[1,4096,1024]{2,1,0:T(8,128)(2,1)}) %all-gather.33.cloned.1.call-update) | async-done | bytes 8388624 | tf_op jit(solution)/shard_map/all_gather | solution.py:330
  598.7 113.2 %while.134 = (s32[]{:T(128)}, f32[1024,4,64]{0,2,1:T(8,128)}, f32[1024,4,64]{0,2,1:T(8,128)S(1)}, bf16[2,512,4,64]{1,3,2,0:T(8,128)(2,1)}, bf16[2,512,4,64]{1,3,...) while((s32[]{:T(128)}, f32[1024,4,64]{0,2,1:T(8,128)}, ...), condition=%wide.region_50.51_spmd.clone, body=%wide.region_48.50_spmd.clone.sunk | while | flops 1387272192 | bytes 101769392 | solution.py:141
  609.1 18.7 fusion.741
  633.1 22.1 fusion.743
  665.6 18.9 fusion.741
  689.8 22.1 fusion.743
  732.1 109.0 %while.132 = (s32[]{:T(128)}, f32[1024,4,64]{0,2,1:T(8,128)}, f32[1024,4,64]{0,2,1:T(8,128)S(1)}, bf16[2,512,4,64]{1,3,2,0:T(8,128)(2,1)}, bf16[2,512,4,64]{1,3,...) while((s32[]{:T(128)}, f32[1024,4,64]{0,2,1:T(8,128)}, ...), condition=%wide.region_36.37_spmd.clone, body=%wide.region_34.36_spmd.clone.sunk | while | flops 1387272192 | bytes 99672208 | solution.py:141
  741.3 18.6 fusion.711
  764.3 22.1 fusion.713
  795.6 18.9 fusion.711
  818.9 22.1 fusion.713
  969.5 113.4 %while.135 = (s32[]{:T(128)}, f32[1024,4,64]{0,2,1:T(8,128)}, f32[1024,4,64]{0,2,1:T(8,128)S(1)}, bf16[2,512,4,64]{1,3,2,0:T(8,128)(2,1)}, bf16[2,512,4,64]{1,3,...) while((s32[]{:T(128)}, f32[1024,4,64]{0,2,1:T(8,128)}, ...), condition=%wide.region_57.58_spmd.clone, body=%wide.region_55.57_spmd.clone.sunk | while | flops 1387272192 | bytes 99672208 | solution.py:141
  979.9 18.8 fusion.756
  1004.0 22.1 fusion.758
  1036.5 18.9 fusion.756
  1060.6 22.1 fusion.758
  1100.9 109.1 %while.133 = (s32[]{:T(128)}, f32[1024,4,64]{0,2,1:T(8,128)}, f32[1024,4,64]{0,2,1:T(8,128)S(1)}, bf16[2,512,4,64]{1,3,2,0:T(8,128)(2,1)}, bf16[2,512,4,64]{1,3,...) while((s32[]{:T(128)}, f32[1024,4,64]{0,2,1:T(8,128)}, ...), condition=%wide.region_43.44_spmd.clone, body=%wide.region_41.43_spmd.clone.sunk | while | flops 1387272192 | bytes 99672208 | solution.py:141
  1110.1 18.6 fusion.726
  1133.2 22.1 fusion.728
  1164.6 18.9 fusion.726
  1187.9 22.1 fusion.728
  1302.0 18.5 pad_maximum_fusion
  1359.1 19.0 pad_maximum_fusion.1
  1430.4 102.8 %reduce-scatter.8.cloned.1.call-done = f32[2,128,3072]{2,1,0:T(8,128)} async-done(((f32[2,1024,3072]{2,1,0:T(8,128)}), f32[2,128,3072]{2,1,0:T(8,128)}) %reduce-scatter.8.cloned.1.call-update) | async-done | bytes 3145744 | tf_op jit(solution)/shard_map/reduce_scatter | solution.py:356
  1533.2 326.3 %reduce-scatter.12.cloned.1.call-done = f32[2,128,4096]{2,1,0:T(8,128)} async-done(((f32[2,1024,4096]{2,1,0:T(8,128)}), f32[2,128,4096]{2,1,0:T(8,128)}) %reduce-scatter.12.cloned.1.call-update) | async-done | bytes 4194320 | tf_op jit(solution)/shard_map/reduce_scatter | solution.py:358
  1859.5 326.3 %reduce-scatter.14.cloned.1.call-done = f32[2,512,1024]{2,1,0:T(8,128)} async-done(((f32[2,4096,1024]{2,1,0:T(8,128)}), f32[2,512,1024]{2,1,0:T(8,128)}) %reduce-scatter.14.cloned.1.call-update) | async-done | bytes 4194320 | tf_op jit(solution)/shard_map/reduce_scatter | solution.py:359
  2204.7 56.6 %reduce-scatter.16.cloned.1.call-done = f32[1664,2]{1,0:T(8,128)} async-done(((f32[13312,2]{1,0:T(8,128)}), f32[1664,2]{1,0:T(8,128)}) %reduce-scatter.16.cloned.1.call-update) | async-done | bytes 13328
  2280.2 224.9 %all-reduce.11.cloned.1.call-done = (f32[2,128,3072]{2,1,0:T(8,128)}, f32[2,128,1024]{2,1,0:T(8,128)}, f32[2,128,4096]{2,1,0:T(8,128)}, f32[2,512,1024]{2,1,0:T(8,128)}) async-done(((f32[2,128,3072]{2,1,0:T(8,128)}, f32[2,128,1024]{2,1,0:T(8,128)}, f32[2,128,4096]{2,1,0:T(8,128)}, f32[2,512,1024]{2,1,0:T(8,128)}), (f32[2,128,3072]{2,1,0:T(8,128)}, f32[2,128,1024]{2,1,0:T(8,128)}, f32[2,128,4096]{2,1,0:T(8,128)}, ...) | async-done | bytes 12582928 | tf_op jit(solution)/shard_map/psum | solution.py:361
  2525.9 17.1 psum.47
  (1040 shorter events, 1016.1 us)
Async XLA Ops:
  7.2 71.8 %all-gather.19.cloned.1.call-start = ((), (), s32[]{:S(2)}) async-start(), calls=%async_computation.25 | async-start | bytes 7077888 | tf_op jit(solution)/shard_map/all_gather | solution.py:327
  10.7 188.9 %all-gather.21.cloned.1.call-start = ((), (), s32[]{:S(2)}) async-start(), calls=%async_computation.26 | async-start | bytes 2359296 | tf_op jit(solution)/shard_map/all_gather | solution.py:328
  11.7 203.2 %all-gather.23.cloned.1.call-start = ((), (), s32[]{:S(2)}) async-start(), calls=%async_computation.27 | async-start | bytes 9437184 | tf_op jit(solution)/shard_map/all_gather | solution.py:329
  15.7 259.7 %all-gather.25.cloned.1.call-start = ((), (), s32[]{:S(2)}) async-start(), calls=%async_computation.28 | async-start | bytes 9437184 | tf_op jit(solution)/shard_map/all_gather | solution.py:330
  19.8 321.0 %all-gather.27.cloned.1.call-start = ((), (), s32[]{:S(2)}) async-start(), calls=%async_computation.29 | async-start | bytes 7077888 | tf_op jit(solution)/shard_map/all_gather | solution.py:327
  20.4 456.7 %all-gather.29.cloned.1.call-start = ((), (), s32[]{:S(2)}) async-start(), calls=%async_computation.30 | async-start | bytes 2359296 | tf_op jit(solution)/shard_map/all_gather | solution.py:328
  21.0 463.8 %all-gather.31.cloned.1.call-start = ((), (), s32[]{:S(2)}) async-start(), calls=%async_computation.31 | async-start | bytes 9437184 | tf_op jit(solution)/shard_map/all_gather | solution.py:329
  21.7 515.5 %all-gather.33.cloned.1.call-start = ((), (), s32[]{:S(2)}) async-start(), calls=%async_computation.32 | async-start | bytes 9437184 | tf_op jit(solution)/shard_map/all_gather | solution.py:330
  93.8 24.4 all-to-all-start.4
  118.2 41.2 %all-to-all-start = ((bf16[256,3,4,256]{0,3,1,2:T(8,128)(2,1)}), bf16[256,3,4,256]{0,3,1,2:T(8,128)(2,1)S(1)}, u32[]{:S(2)}, u32[]{:S(2)}) async-start(bf16[256,3,4,256]{0,3,1,2:T(8,128)(2,1)} %copy.261), calls=%async_computation | async-start | bytes 3145728 | tf_op jit(solution)/shard_map/all_to_all | solution.py:168
  159.4 30.6 %all-to-all-start.5 = ((bf16[4,2,32768]{2,1,0:T(2,128)(2,1)}), bf16[4,2,32768]{2,1,0:T(2,128)(2,1)}, u32[]{:S(2)}, u32[]{:S(2)}) async-start(bf16[4,2,32768]{2,1,0:T(2,128)(2,1)} %reshape.1925), calls=%async_computation.5 | async-start | bytes 1048576 | tf_op jit(solution)/shard_map/all_to_all | solution.py:173
  190.0 12.7 all-to-all-start.1
  213.7 146.7 %copy-start.169 = (f32[256]{0:T(256)}, f32[256]{0:T(256)S(1)}, u32[]{:S(2)}) copy-start(f32[256]{0:T(256)S(1)} %broadcast_multiply_fusion.11) | copy-start | bytes 3076
  214.9 145.4 %copy-start.180 = (f32[256]{0:T(256)}, f32[256]{0:T(256)S(1)}, u32[]{:S(2)}) copy-start(f32[256]{0:T(256)S(1)} %fusion.511) | copy-start | bytes 3076
  355.7 28.1 %all-to-all-start.6 = ((bf16[256,3,4,256]{0,3,1,2:T(8,128)(2,1)}), bf16[256,3,4,256]{0,3,1,2:T(8,128)(2,1)}, u32[]{:S(2)}, u32[]{:S(2)}) async-start(bf16[256,3,4,256]{0,3,1,2:T(8,128)(2,1)} %copy.282), calls=%async_computation.6 | async-start | bytes 3145728 | tf_op jit(solution)/shard_map/all_to_all | solution.py:168
  383.8 41.3 %all-to-all-start.2 = ((bf16[256,3,4,256]{0,3,1,2:T(8,128)(2,1)}), bf16[256,3,4,256]{0,3,1,2:T(8,128)(2,1)S(1)}, u32[]{:S(2)}, u32[]{:S(2)}) async-start(bf16[256,3,4,256]{0,3,1,2:T(8,128)(2,1)} %copy.268), calls=%async_computation.2 | async-start | bytes 3145728 | tf_op jit(solution)/shard_map/all_to_all | solution.py:168
  425.1 35.9 %all-to-all-start.7 = ((bf16[4,2,32768]{2,1,0:T(2,128)(2,1)}), bf16[4,2,32768]{2,1,0:T(2,128)(2,1)}, u32[]{:S(2)}, u32[]{:S(2)}) async-start(bf16[4,2,32768]{2,1,0:T(2,128)(2,1)} %reshape.1927), calls=%async_computation.7 | async-start | bytes 1048576 | tf_op jit(solution)/shard_map/all_to_all | solution.py:173
  461.1 12.7 all-to-all-start.3
  574.0 13.0 all-to-all-start.12
  587.0 135.5 %all-to-all-start.8 = ((bf16[256,4,256]{0,2,1:T(8,128)(2,1)}), bf16[256,4,256]{0,2,1:T(8,128)(2,1)}, u32[]{:S(2)}, u32[]{:S(2)}) async-start(bf16[256,4,256]{0,2,1:T(8,128)(2,1)} %bitcast.859), calls=%async_computation.8 | async-start | bytes 1048576 | tf_op jit(solution)/shard_map/all_to_all | solution.py:224
  722.5 124.6 %all-to-all-start.13 = ((bf16[1024,3,1,256]{3,1,2,0:T(4,128)(2,1)}), bf16[1024,3,1,256]{3,1,2,0:T(4,128)(2,1)}, u32[]{:S(2)}, u32[]{:S(2)}) async-start(bf16[1024,3,1,256]{3,1,2,0:T(4,128)(2,1)} %copy.309), calls=%async_computation.13 | async-start | bytes 4194304 | tf_op jit(solution)/shard_map/all_to_all | solution.py:242
  847.1 29.3 %all-to-all-start.9 = ((bf16[1024,3,1,256]{3,1,2,0:T(4,128)(2,1)}), bf16[1024,3,1,256]{3,1,2,0:T(4,128)(2,1)}, u32[]{:S(2)}, u32[]{:S(2)}) async-start(bf16[1024,3,1,256]{3,1,2,0:T(4,128)(2,1)} %copy.293), calls=%async_computation.9 | async-start | bytes 4194304 | tf_op jit(solution)/shard_map/all_to_all | solution.py:242
  851.6 578.8 %reduce-scatter.10.cloned.1.call-start = ((), (), s32[]{:S(2)}) async-start(), calls=%async_computation.22 | async-start | bytes 9437184 | tf_op jit(solution)/shard_map/reduce_scatter | solution.py:357
  945.7 12.0 all-to-all-start.14
  957.7 134.0 %all-to-all-start.10 = ((bf16[256,4,256]{0,2,1:T(8,128)(2,1)}), bf16[256,4,256]{0,2,1:T(8,128)(2,1)}, u32[]{:S(2)}, u32[]{:S(2)}) async-start(bf16[256,4,256]{0,2,1:T(8,128)(2,1)} %bitcast.860), calls=%async_computation.10 | async-start | bytes 1048576 | tf_op jit(solution)/shard_map/all_to_all | solution.py:224
  1091.7 127.2 %all-to-all-start.15 = ((bf16[1024,3,1,256]{3,1,2,0:T(4,128)(2,1)}), bf16[1024,3,1,256]{3,1,2,0:T(4,128)(2,1)}, u32[]{:S(2)}, u32[]{:S(2)}) async-start(bf16[1024,3,1,256]{3,1,2,0:T(4,128)(2,1)} %copy.317), calls=%async_computation.15 | async-start | bytes 4194304 | tf_op jit(solution)/shard_map/all_to_all | solution.py:242
  1219.0 27.9 %all-to-all-start.11 = ((bf16[1024,3,1,256]{3,1,2,0:T(4,128)(2,1)}), bf16[1024,3,1,256]{3,1,2,0:T(4,128)(2,1)}, u32[]{:S(2)}, u32[]{:S(2)}) async-start(bf16[1024,3,1,256]{3,1,2,0:T(4,128)(2,1)} %copy.301), calls=%async_computation.11 | async-start | bytes 4194304 | tf_op jit(solution)/shard_map/all_to_all | solution.py:242
  1223.4 309.8 %reduce-scatter.8.cloned.1.call-start = ((), (), s32[]{:S(2)}) async-start(), calls=%async_computation.21 | async-start | bytes 28311552 | tf_op jit(solution)/shard_map/reduce_scatter | solution.py:356
  1288.1 571.3 %reduce-scatter.12.cloned.1.call-start = ((), (), s32[]{:S(2)}) async-start(), calls=%async_computation.23 | async-start | bytes 37748736 | tf_op jit(solution)/shard_map/reduce_scatter | solution.py:358
  1342.2 843.6 %reduce-scatter.14.cloned.1.call-start = ((), (), s32[]{:S(2)}) async-start(), calls=%async_computation.24 | async-start | bytes 37748736 | tf_op jit(solution)/shard_map/reduce_scatter | solution.py:359
  1401.5 859.8 %reduce-scatter.16.cloned.1.call-start = ((), (), s32[]{:S(2)}) async-start(), calls=%async_computation.33 | async-start | bytes 7667712
  1430.0 1075.0 %all-reduce.11.cloned.1.call-start = ((), (), s32[]{:S(2)}) async-start(), calls=%async_computation.34 | async-start | bytes 25165824 | tf_op jit(solution)/shard_map/psum | solution.py:361
  (266 other events, 3085.2 us)
Sparse Core Ops, SparseCore 0:
  10.8 68.1 all-gather.18
  81.2 27.7 all-gather.20
  111.2 81.5 all-gather.22
  194.8 80.5 all-gather.24
  277.5 63.2 all-gather.26
  342.8 27.7 all-gather.28
  372.8 81.5 all-gather.30
  456.6 80.5 all-gather.32
  940.6 87.1 reduce-scatter.9
  1288.2 244.9 reduce-scatter.7
  1535.6 323.8 reduce-scatter.11
  1861.8 323.8 reduce-scatter.13
  2188.1 73.1 reduce-scatter.15
  2265.0 240.0 all-reduce.10
where the time goes:
time: 2600 us; the launch traced here: 2590 us
  waiting for transfers between devices  1250 us (48%)
  matrix products  741 us (28%)
  local copies, waits for them, and re-layouts  251 us (10%)
  other arithmetic  187 us (7%)
  starting transfers between devices  72.9 us (3%)
  blocking collectives  63.7 us (2%)
    reduce_scatter x1, waiting for transfers between devices, per_device(): lax.psum_scatter(grad_accum[3], 'fsdp', scatter_dimension=1, tiled=True)  326 us
    reduce_scatter x1, waiting for transfers between devices, per_device(): lax.psum_scatter(grad_accum[4], 'fsdp', scatter_dimension=1, tiled=True)  326 us
    psum x1, waiting for transfers between devices, per_device(): lax.psum((shard_sums[0], shard_sums[1], shard_sums[2], shard_sums[3], sha...  225 us
    dot_general x8, matrix products, one_block(): jnp.einsum('hqk,khd->qhd', score_low, key_rows, preferred_element_type=jn...  177 us
    dot_general x8, matrix products, one_block(): jnp.einsum('hqk,qhd->khd', score_low, query_block, preferred_element_type...  150 us
    reduce_scatter x1, waiting for transfers between devices, per_device(): lax.psum_scatter(grad_accum[1], 'fsdp', scatter_dimension=1, tiled=True)  103 us
    all_gather x2, waiting for transfers between devices, per_device(): lax.all_gather(lowered[4][layer_idx], 'fsdp', axis=0, tiled=True)  92.1 us
    all_gather x2, waiting for transfers between devices, per_device(): lax.all_gather(lowered[1][layer_idx], 'fsdp', axis=0, tiled=True)  80.1 us
  transfers between devices with their start and end apart: 30, of which 15 were waited for; matrix products, arithmetic and copies ran while one was open for 39% of the time, Pallas kernels for 0%

commit v1 on v0

--- a/solution.py
+++ b/solution.py
@@ -4,6 +4,8 @@
 import jax
 import jax.numpy as jnp
 from jax import lax
+from jax.experimental import pallas as pl
+from jax.experimental.pallas import tpu as pltpu
 from jax.sharding import PartitionSpec as P
 
 D = 1024
@@ -281,7 +283,7 @@
     return (first_new, second_new, updated)
 
 
-def per_device(
+def general_device(
     clip_tokens,
     patch_coords,
     out_cotangent,
@@ -404,6 +406,604 @@
     )
 
 
+ROWS_Q = 256
+PAIR = 2 * HEAD_DIM
+BF = jnp.bfloat16
+F32 = jnp.float32
+VMEM_LIMIT = 56 * 1024 * 1024
+
+
+def fits_fast(mesh):
+    return dict(mesh.shape) == {"seq": 4, "fsdp": 8}
+
+
+def swap_core(item):
+    parts = lax.axis_size("fsdp")
+    return lax.ppermute(item, "fsdp", [(idx, idx ^ 1) for idx in range(parts)])
+
+
+def send_up(item):
+    parts = lax.axis_size("fsdp")
+    return lax.ppermute(item, "fsdp", [(idx, (idx + 2) % parts) for idx in range(parts)])
+
+
+def swap_seq(item, mask):
+    parts = lax.axis_size("seq")
+    return lax.ppermute(item, "seq", [(idx, idx ^ mask) for idx in range(parts)])
+
+
+def pick(item, index, axis=0):
+    return lax.dynamic_index_in_dim(item, index, axis, keepdims=False)
+
+
+def swap_halves(item):
+    lane = lax.broadcasted_iota(jnp.int32, item.shape, 1)
+    half = HEAD_DIM // 2
+    width = item.shape[1]
+    ahead = pltpu.roll(item, width - half, 1)
+    behind = pltpu.roll(item, half, 1)
+    return jnp.where(lane % HEAD_DIM < half, ahead, behind)
+
+
+NT = (((1,), (1,)), ((), ()))
+
+
+def head_mask(item, head):
+    lane = lax.broadcasted_iota(jnp.int32, item.shape, 1)
+    return jnp.where(lane // HEAD_DIM == head, item, jnp.zeros_like(item))
+
+
+def attn_fwd_kernel(qkv_ref, cos_ref, sin_ref, mixed_ref, low_ref, lse_ref, qs_ref):
+    cosine, sine = cos_ref[...], sin_ref[...]
+    queries = qkv_ref[:, 0:PAIR]
+    key_rows = qkv_ref[:, PAIR : 2 * PAIR]
+    values = qkv_ref[:, 2 * PAIR : 3 * PAIR]
+    queries = (queries * cosine + swap_halves(queries) * sine).astype(BF)
+    key_rows = (key_rows * cosine + swap_halves(key_rows) * sine).astype(BF)
+    low_ref[:, 0:PAIR] = queries
+    low_ref[:, PAIR : 2 * PAIR] = key_rows
+    low_ref[:, 2 * PAIR : 3 * PAIR] = values.astype(BF)
+    qs_ref[...] = queries * jnp.asarray(HEAD_DIM**-0.5, BF)
+    values_t = values.T.astype(BF)
+    keys_by_head = [head_mask(key_rows, head) for head in range(2)]
+    length = qs_ref.shape[0]
+
+    @pl.loop(0, length // ROWS_Q)
+    def _(step):
+        rows = pl.ds(pl.multiple_of(step * ROWS_Q, ROWS_Q), ROWS_Q)
+        block = qs_ref[rows, :]
+        outs = []
+        for head in range(2):
+            scores = lax.dot_general(keys_by_head[head], block, NT, preferred_element_type=F32)
+            top = jnp.max(scores, axis=0, keepdims=True)
+            exponent = jnp.exp(scores - top)
+            total = jnp.sum(exponent, axis=0, keepdims=True)
+            lse_ref[0, head : head + 1, rows] = top + jnp.log(total)
+            probs = (exponent * (1.0 / total)).astype(BF)
+            outs.append(
+                jnp.dot(
+                    values_t[head * HEAD_DIM : (head + 1) * HEAD_DIM],
+                    probs,
+                    preferred_element_type=F32,
+                )
+            )
+        mixed_ref[rows, :] = jnp.concatenate(outs, axis=0).T.astype(BF)
+
+
+def attend(qkv_all, cos_wide, sin_wide):
+    length, width = qkv_all.shape
+    pairs = width // (3 * PAIR)
+    table = pl.BlockSpec((length, PAIR), lambda pair: (0, 0))
+    triple = pl.BlockSpec((length, 3 * PAIR), lambda pair: (0, pair))
+    return pl.pallas_call(
+        attn_fwd_kernel,
+        grid=(pairs,),
+        in_specs=[triple, table, table],
+        out_specs=[
+            pl.BlockSpec((length, PAIR), lambda pair: (0, pair)),
+            triple,
+            pl.BlockSpec((1, 8, length), lambda pair: (pair, 0, 0)),
+        ],
+        out_shape=[
+            jax.ShapeDtypeStruct((length, pairs * PAIR), BF),
+            jax.ShapeDtypeStruct((length, width), BF),
+            jax.ShapeDtypeStruct((pairs, 8, length), F32),
+        ],
+        scratch_shapes=[pltpu.VMEM((length, PAIR), BF)],
+        compiler_params=pltpu.CompilerParams(vmem_limit_bytes=VMEM_LIMIT),
+        cost_estimate=pl.CostEstimate(
+            flops=16 * pairs * length * length * PAIR,
+            bytes_accessed=length * width * 8,
+            transcendentals=2 * pairs * length * length,
+        ),
+        name="attend",
+    )(qkv_all, cos_wide, sin_wide)
+
+
+def attn_bwd_kernel(
+    low_ref, dout_ref, lse_ref, cos_ref, sin_ref, grad_ref, bias_ref, dq_ref, dk_ref, dv_ref
+):
+    length = low_ref.shape[0]
+    key_rows = low_ref[:, PAIR : 2 * PAIR]
+    values = low_ref[:, 2 * PAIR : 3 * PAIR]
+    keys_t = key_rows.astype(F32).T.astype(BF)
+    keys_by_head = [head_mask(key_rows, head) for head in range(2)]
+    values_by_head = [head_mask(values, head) for head in range(2)]
+    scale = HEAD_DIM**-0.5
+    dk_ref[...] = jnp.zeros_like(dk_ref)
+    dv_ref[...] = jnp.zeros_like(dv_ref)
+
+    @pl.loop(0, length // ROWS_Q)
+    def _(step):
+        rows = pl.ds(pl.multiple_of(step * ROWS_Q, ROWS_Q), ROWS_Q)
+        block = low_ref[rows, 0:PAIR]
+        scaled = block * jnp.asarray(scale, BF)
+        dout = dout_ref[rows, :]
+        outs = []
+        for head in range(2):
+            scores = lax.dot_general(keys_by_head[head], scaled, NT, preferred_element_type=F32)
+            probs = jnp.exp(scores - lse_ref[0, head : head + 1, rows])
+            prob_grad = lax.dot_general(values_by_head[head], dout, NT, preferred_element_type=F32)
+            delta = jnp.sum(probs * prob_grad, axis=0, keepdims=True)
+            score_low = (probs * (prob_grad - delta) * scale).astype(BF)
+            dv_ref[head] += jnp.dot(probs.astype(BF), dout, preferred_element_type=F32)
+            dk_ref[head] += jnp.dot(score_low, block, preferred_element_type=F32)
+            outs.append(
+                jnp.dot(
+                    keys_t[head * HEAD_DIM : (head + 1) * HEAD_DIM],
+                    score_low,
+                    preferred_element_type=F32,
+                )
+            )
+        dq_ref[rows, :] = jnp.concatenate(outs, axis=0).T
+
+    lane = lax.broadcasted_iota(jnp.int32, (length, PAIR), 1)
+    first = lane // HEAD_DIM == 0
+    cosine, sine = cos_ref[...], sin_ref[...]
+
+    def rounded(item):
+        return item.astype(BF).astype(F32)
+
+    def back(item):
+        return item * cosine - swap_halves(item) * sine
+
+    parts = [
+        back(rounded(dq_ref[...])),
+        back(rounded(jnp.where(first, dk_ref[0], dk_ref[1]))),
+        rounded(jnp.where(first, dv_ref[0], dv_ref[1])),
+    ]
+    for idx, part in enumerate(parts):
+        cols = slice(idx * PAIR, (idx + 1) * PAIR)
+        grad_ref[:, cols] = part.astype(BF)
+        bias_ref[:, cols] = jnp.broadcast_to(jnp.sum(part, axis=0, keepdims=True), (8, PAIR))
+
+
+def attend_grad(low_all, mixed_grad, lse, cos_wide, sin_wide):
+    length, width = low_all.shape
+    pairs = width // (3 * PAIR)
+    table = pl.BlockSpec((length, PAIR), lambda pair: (0, 0))
+    triple = pl.BlockSpec((length, 3 * PAIR), lambda pair: (0, pair))
+    return pl.pallas_call(
+        attn_bwd_kernel,
+        grid=(pairs,),
+        in_specs=[
+            triple,
+            pl.BlockSpec((length, PAIR), lambda pair: (0, pair)),
+            pl.BlockSpec((1, 8, length), lambda pair: (pair, 0, 0)),
+            table,
+            table,
+        ],
+        out_specs=[triple, pl.BlockSpec((8, 3 * PAIR), lambda pair: (0, pair))],
+        out_shape=[
+            jax.ShapeDtypeStruct((length, width), BF),
+            jax.ShapeDtypeStruct((8, width), F32),
+        ],
+        scratch_shapes=[
+            pltpu.VMEM((length, PAIR), F32),
+            pltpu.VMEM((2, length, PAIR), F32),
+            pltpu.VMEM((2, length, PAIR), F32),
+        ],
+        compiler_params=pltpu.CompilerParams(vmem_limit_bytes=VMEM_LIMIT),
+        cost_estimate=pl.CostEstimate(
+            flops=40 * pairs * length * length * PAIR,
+            bytes_accessed=length * width * 6,
+            transcendentals=2 * pairs * length * length,
+        ),
+        name="attend_grad",
+    )(low_all, mixed_grad, lse, cos_wide, sin_wide)
+
+
+def place_kernel(plans, n_pieces, *refs):
+    n_out = len(plans)
+    owns = refs[:n_out]
+    pieces = refs[n_out : n_out + n_pieces]
+    outs = refs[n_out + n_pieces : 2 * n_out + n_pieces]
+    sem = refs[-1]
+    chip = lax.axis_index("fsdp") // 2
+    ring = lax.axis_size("fsdp") // 2
+    seq = lax.axis_index("seq")
+    copies = []
+    for (quarter, first, blocks), own, out in zip(plans, owns, outs):
+        slab = 4 * quarter
+        copies.append((own, out.at[pl.ds(pl.multiple_of(chip * slab, slab), slab), :]))
+        for idx, piece in enumerate(pieces):
+            hop, mask = idx // 4 + 1, idx % 4
+            place = lax.rem(chip - hop + ring, ring) * slab + (seq ^ mask) * quarter
+            rows = pl.ds(pl.multiple_of(place, quarter), quarter)
+            for block in range(blocks):
+                copies.append(
+                    (
+                        piece.at[pl.ds(first + block * quarter, quarter), :],
+                        out.at[rows, pl.ds(block * 512, 512)],
+                    )
+                )
+    made = [pltpu.make_async_copy(src, dst, sem.at[idx]) for idx, (src, dst) in enumerate(copies)]
+    for item in made:
+        item.start()
+    for item in made:
+        item.wait()
+
+
+def gather_group(slabs):
+    seq = lax.axis_index("seq")
+    packed = []
+    plans = []
+    first = 0
+    for slab in slabs:
+        quarter = slab.shape[0] // 4
+        mine = lax.dynamic_slice_in_dim(slab, seq * quarter, quarter, 0)
+        blocks = slab.shape[1] // 512
+        packed += [mine[:, block * 512 : (block + 1) * 512] for block in range(blocks)]
+        plans.append((quarter, first, blocks))
+        first += quarter * blocks
+    current = jnp.concatenate(packed, axis=0)
+    ring = lax.axis_size("fsdp") // 2
+    half = first // 2
+    pieces = []
+    for hop in range(1, ring):
+        current = send_up(current)
+        over_x = swap_seq(current, 1)
+        over_y = swap_seq(current, 2)
+        if hop % 3 == 0:
+            far = swap_seq(over_x, 2)
+        elif hop % 3 == 1:
+            far = swap_seq(over_y, 1)
+        else:
+            far = jnp.concatenate(
+                [swap_seq(over_x[:half], 2), swap_seq(over_y[half:], 1)], axis=0
+            )
+        pieces += [current, over_x, over_y, far]
+    n_copies = sum(1 + len(pieces) * plan[2] for plan in plans)
+    anywhere = pl.BlockSpec(memory_space=pl.ANY)
+    return pl.pallas_call(
+        partial(place_kernel, plans, len(pieces)),
+        in_specs=[anywhere] * (len(slabs) + len(pieces)),
+        out_specs=[pl.BlockSpec(memory_space=pltpu.VMEM)] * len(slabs),
+        out_shape=[jax.ShapeDtypeStruct((ring * slab.shape[0], slab.shape[1]), BF) for slab in slabs],
+        scratch_shapes=[pltpu.SemaphoreType.DMA((n_copies,))],
+        compiler_params=pltpu.CompilerParams(vmem_limit_bytes=VMEM_LIMIT),
+        cost_estimate=pl.CostEstimate(
+            flops=0,
+            bytes_accessed=sum(ring * slab.size * 4 for slab in slabs),
+            transcendentals=0,
+        ),
+        name="place",
+    )(*slabs, *pieces)
+
+
+def ring_sum(item):
+    ring = item.shape[0]
+    chip = lax.axis_index("fsdp") // 2
+
+    def own(back):
+        return pick(item, lax.rem(chip - back + ring, ring))
+
+    moving = own(1)
+    for hop in range(2, ring + 1):
+        moving = (send_up(moving).astype(F32) + own(hop).astype(F32)).astype(BF)
+    return moving
+
+
+def plane_sum(item, axis, x_first):
+    seq = lax.axis_index("seq")
+    at_x, at_y = lax.rem(seq, 2), seq // 2
+
+    def one(data, dim, place, mask):
+        other = swap_seq(pick(data, 1 - place, dim), mask)
+        return (pick(data, place, dim).astype(F32) + other.astype(F32)).astype(BF)
+
+    if x_first:
+        return one(one(item, axis + 1, at_x, 1), axis, at_y, 2)
+    return one(one(item, axis, at_y, 2), axis, at_x, 1)
+
+
+def norm_parts(hidden):
+    center = hidden - jnp.mean(hidden, axis=-1, keepdims=True)
+    spread = jnp.mean(center * center, axis=-1, keepdims=True)
+    inverse = lax.rsqrt(spread + 1e-06)
+    return center * inverse, inverse
+
+
+def norm_forward(hidden, gain, shift):
+    scaled, _ = norm_parts(hidden)
+    return (scaled * gain + shift).astype(BF)
+
+
+def norm_backward(hidden, gain, grad):
+    scaled, inverse = norm_parts(hidden)
+    entry = grad * gain
+    mean_one = jnp.mean(entry, axis=-1, keepdims=True)
+    mean_two = jnp.mean(entry * scaled, axis=-1, keepdims=True)
+    result = inverse * (entry - mean_one - scaled * mean_two)
+    return result, jnp.sum(grad * scaled, axis=0), jnp.sum(grad, axis=0)
+
+
+def gelu_and_slope(upward):
+    erf_part = 0.5 * (1.0 + lax.erf(upward * (1.0 / math.sqrt(2.0))))
+    density = jnp.exp(-0.5 * upward * upward) * (1.0 / math.sqrt(2.0 * math.pi))
+    return upward * erf_part, erf_part + upward * density
+
+
+def dot(left, right):
+    return jnp.dot(left, right, preferred_element_type=F32)
+
+
+def dot_nt(left, right):
+    return lax.dot_general(left, right, NT, preferred_element_type=F32)
+
+
+def dot_tn(left, right):
+    return lax.dot_general(left, right, (((0,), (0,)), ((), ())), preferred_element_type=F32)
+
+
+def own_bias(bias, core, fsdp_parts, kinds):
+    width = bias.shape[0] // (kinds * fsdp_parts)
+    view = bias.reshape(kinds, fsdp_parts // 2, 2, width)
+    mine = pick(view, core, 2)
+    return mine.transpose(1, 0, 2).reshape(-1)
+
+
+def spread_bias(grad, core, fsdp_parts, kinds):
+    width = grad.shape[0] // (kinds * (fsdp_parts // 2))
+    view = grad.reshape(fsdp_parts // 2, kinds, width).transpose(1, 0, 2)
+    zero = jnp.zeros_like(view)
+    first = jnp.where(core == 0, view, zero)
+    second = jnp.where(core == 0, zero, view)
+    return jnp.stack([first, second], axis=2).reshape(-1)
+
+
+def fast_device(
+    clip_tokens,
+    patch_coords,
+    out_cotangent,
+    vector_params,
+    qkv_weight,
+    proj_weight,
+    up_weight,
+    down_weight,
+    first_vector,
+    first_qkv,
+    first_proj,
+    first_up,
+    first_down,
+    second_vector,
+    second_qkv,
+    second_proj,
+    second_up,
+    second_down,
+):
+    masters = (vector_params, qkv_weight, proj_weight, up_weight, down_weight)
+    firsts = (first_vector, first_qkv, first_proj, first_up, first_down)
+    seconds = (second_vector, second_qkv, second_proj, second_up, second_down)
+    layer_count = vector_params.shape[0]
+    batch_local, chunk_len = clip_tokens.shape[:2]
+    seq_parts = lax.axis_size("seq")
+    parts = lax.axis_size("fsdp")
+    ring = parts // 2
+    seq = lax.axis_index("seq")
+    shard = lax.axis_index("fsdp")
+    core = lax.rem(shard, 2)
+    even = lax.rem(seq, 2) == 0
+
+    def to_clips(item, extra=None):
+        halves = []
+        for turn in range(2):
+            piece = jnp.where(even, item[turn], item[1 - turn])
+            pairs = []
+            for src_seq in range(seq_parts):
+                for src in range(parts):
+                    dst_seq = 2 * (src % 2) + (src_seq + turn) % 2
+                    dst = src - src % 2 + src_seq // 2
+                    pairs.append((src_seq * parts + src, dst_seq * parts + dst))
+            halves.append(lax.ppermute(piece, ("seq", "fsdp"), pairs))
+        mine = jnp.where(
+            even, jnp.stack([halves[0], halves[1]]), jnp.stack([halves[1], halves[0]])
+        )
+        other = swap_core(mine)
+        both = jnp.where(core == 0, jnp.stack([mine, other]), jnp.stack([other, mine]))
+        return both.reshape((4,) + item.shape[1:])
+
+    def from_clips(item):
+        mine = pick(item.reshape((2, 2, chunk_len) + item.shape[1:]), core)
+        pieces = [None, None]
+        for turn in range(2):
+            piece = jnp.where(even, mine[turn], mine[1 - turn])
+            pairs = []
+            for src_seq in range(seq_parts):
+                for src in range(parts):
+                    dst_seq = 2 * (src % 2) + (src_seq + turn) % 2
+                    dst = src - src % 2 + src_seq // 2
+                    pairs.append((dst_seq * parts + dst, src_seq * parts + src))
+            pieces[turn] = lax.ppermute(piece, ("seq", "fsdp"), pairs)
+        return jnp.where(
+            even, jnp.stack([pieces[0], pieces[1]]), jnp.stack([pieces[1], pieces[0]])
+        )
+
+    coord_rows = jnp.zeros((batch_local, 8, D), F32)
+    coord_rows = lax.dynamic_update_slice(
+        coord_rows, jnp.swapaxes(patch_coords, 0, 1).astype(F32), (0, 0, 0)
+    )
+    arrived = to_clips(jnp.concatenate([clip_tokens, coord_rows], axis=1))
+    hidden = arrived[:, :chunk_len].reshape(4 * chunk_len, D)
+    coords = arrived[:, chunk_len : chunk_len + 3, :chunk_len]
+    coords = jnp.swapaxes(coords, 0, 1).reshape(3, 4 * chunk_len)
+    cosine, sine = rotary_tables(coords, HEAD_DIM // 2)
+    cos_wide = jnp.concatenate([cosine] * 4, axis=1)
+    sin_wide = jnp.concatenate([-sine, sine, -sine, sine], axis=1)
+
+    vector_all = lax.all_gather(vector_params.astype(BF), "fsdp", axis=1, tiled=True).astype(F32)
+
+    def by_core(low, kinds):
+        rows = low.shape[0]
+        width = low.shape[1] // (kinds * parts)
+        view = low.reshape(rows, kinds, ring, 2, width)
+        mine = pick(view, core, 3).transpose(0, 2, 1, 3).reshape(rows, -1)
+        away = pick(view, 1 - core, 3).transpose(0, 2, 1, 3).reshape(rows, -1)
+        other = swap_core(away)
+        return jnp.where(
+            core == 0, jnp.stack([mine, other]), jnp.stack([other, mine])
+        ).reshape(2 * rows, -1)
+
+    layers = []
+    for idx in range(layer_count):
+        qkv_slab = by_core(qkv_weight[idx].astype(BF), 3)
+        up_slab = by_core(up_weight[idx].astype(BF), 1)
+        qkv_w, proj_w = gather_group([qkv_slab, proj_weight[idx].astype(BF)])
+        up_w, down_w = gather_group([up_slab, down_weight[idx].astype(BF)])
+        proj_other = swap_core(proj_w)
+        layers.append((qkv_w, proj_w, proj_other, up_w, down_w))
+
+    saved = []
+    for idx in range(layer_count):
+        qkv_w, proj_w, proj_other, up_w, down_w = layers[idx]
+        gain_one, shift_one, gain_two, shift_two, proj_bias, down_bias, qkv_bias, up_bias = pieces(
+            vector_all[idx]
+        )
+        qkv_bias = own_bias(qkv_bias, core, parts, 3)
+        up_bias = own_bias(up_bias, core, parts, 1)
+        normed = norm_forward(hidden, gain_one, shift_one)
+        qkv_all = dot(normed, qkv_w) + qkv_bias
+        mixed, low_all, lse = attend(qkv_all, cos_wide, sin_wide)
+        mixed_other = swap_core(mixed)
+        after_attn = hidden + (dot(mixed, proj_w) + dot(mixed_other, proj_other)) + proj_bias
+        normed_two = norm_forward(after_attn, gain_two, shift_two)
+        upward = dot(normed_two, up_w) + up_bias
+        active, slope = gelu_and_slope(upward)
+        active, slope = active.astype(BF), slope.astype(BF)
+        part = dot(active, down_w)
+        other = swap_core(part.astype(BF))
+        result = after_attn + (part + other.astype(F32)) + down_bias
+        saved.append((hidden, normed, low_all, lse, mixed, after_attn, normed_two, active, slope))
+        hidden = result
+    block_output = from_clips(hidden)
+
+    grad = to_clips(out_cotangent).reshape(4 * chunk_len, D)
+    sums = [None] * layer_count
+    vector_sums = [None] * layer_count
+    for idx in reversed(range(layer_count)):
+        qkv_w, proj_w, proj_other, up_w, down_w = layers[idx]
+        entry, normed, low_all, lse, mixed, after_attn, normed_two, active, slope = saved[idx]
+        gain_one, shift_one, gain_two, shift_two, proj_bias, down_bias, qkv_bias, up_bias = pieces(
+            vector_all[idx]
+        )
+        down_bias_grad = jnp.sum(grad, axis=0)
+        grad_low = grad.astype(BF)
+        upward_grad = dot_nt(grad_low, down_w) * slope.astype(F32)
+        up_bias_grad = jnp.sum(upward_grad, axis=0)
+        upward_low = upward_grad.astype(BF)
+        part = dot_nt(upward_low, up_w)
+        other = swap_core(part.astype(BF))
+        down_grad = dot_tn(active, grad_low).astype(BF)
+        up_grad = dot_tn(normed_two, upward_low).astype(BF)
+        attn_in, gain_two_grad, shift_two_grad = norm_backward(
+            after_attn, gain_two, part + other.astype(F32)
+        )
+        after_grad = grad + attn_in
+        proj_bias_grad = jnp.sum(after_grad, axis=0)
+        after_low = after_grad.astype(BF)
+        mixed_grad = dot_nt(after_low, proj_w).astype(BF)
+        proj_grad = dot_tn(mixed, after_low).astype(BF)
+        qkv_low, bias_rows = attend_grad(low_all, mixed_grad, lse, cos_wide, sin_wide)
+        part = dot_nt(qkv_low, qkv_w)
+        other = swap_core(part.astype(BF))
+        qkv_grad = dot_tn(normed, qkv_low).astype(BF)
+        attn_in, gain_one_grad, shift_one_grad = norm_backward(
+            entry, gain_one, part + other.astype(F32)
+        )
+        grad = after_grad + attn_in
+
+        shared = jnp.concatenate(
+            [
+                gain_one_grad,
+                shift_one_grad,
+                gain_two_grad,
+                shift_two_grad,
+                proj_bias_grad,
+                down_bias_grad,
+            ]
+        )
+        vector_sums[idx] = jnp.concatenate(
+            [
+                jnp.where(core == 0, shared, jnp.zeros_like(shared)),
+                spread_bias(bias_rows[0], core, parts, 3),
+                spread_bias(up_bias_grad, core, parts, 1),
+            ]
+        )
+
+        def owner_view(item, halves):
+            rows = item.shape[0] // (ring * halves * 4)
+            return item.reshape(ring, halves, 2, 2, rows, item.shape[1])
+
+        def to_core(item):
+            other = swap_core(pick(item, 1 - core))
+            mine = pick(item, core)
+            return jnp.where(core == 0, jnp.stack([mine, other]), jnp.stack([other, mine]))
+
+        down_sum = ring_sum(plane_sum(owner_view(down_grad, 1), 2, False))[0]
+        up_sum = to_core(ring_sum(plane_sum(owner_view(up_grad, 2), 2, True)))
+        proj_sum = plane_sum(ring_sum(owner_view(proj_grad, 1)), 1, False)[0]
+        qkv_sum = to_core(plane_sum(ring_sum(owner_view(qkv_grad, 2)), 1, True))
+        rows = up_sum.shape[1]
+        up_sum = up_sum.reshape(2, rows, ring, -1).transpose(1, 2, 0, 3).reshape(rows, -1)
+        rows = qkv_sum.shape[1]
+        qkv_sum = qkv_sum.reshape(2, rows, ring, 3, -1).transpose(1, 3, 2, 0, 4).reshape(rows, -1)
+        sums[idx] = (qkv_sum, proj_sum, up_sum, down_sum)
+    input_grad = from_clips(grad)
+
+    clip_count = batch_local * parts
+    quarter_sums = tuple(
+        jnp.stack([sums[idx][kind] for idx in range(layer_count)]) for kind in range(4)
+    )
+    local_squares = sum(
+        jnp.sum(jnp.square(item.astype(F32) * (1.0 / clip_count))) for item in quarter_sums
+    )
+    vector_total = lax.psum(jnp.stack(vector_sums), ("seq", "fsdp")) / clip_count
+    squares = lax.psum(local_squares, ("seq", "fsdp")) + jnp.sum(vector_total * vector_total)
+    norm_value = jnp.sqrt(squares)
+    param_count = sum(master.size for master in masters) * parts
+    factor = jnp.minimum(1.0, CLIP_RATIO * math.sqrt(float(param_count)) / (norm_value + 1e-06))
+
+    share = vector_params.shape[1]
+    grad_shards = [lax.dynamic_slice_in_dim(vector_total, shard * share, share, 1)]
+    for item in quarter_sums:
+        whole = lax.all_gather(item, "seq", axis=1, tiled=True)
+        grad_shards.append(whole.astype(F32) / clip_count)
+    updates = [
+        adam_update(master, grad_item, first_old, second_old, factor)
+        for master, grad_item, first_old, second_old in zip(masters, grad_shards, firsts, seconds)
+    ]
+    return (
+        block_output,
+        input_grad,
+        *grad_shards,
+        norm_value.reshape(1),
+        *[item[0] for item in updates],
+        *[item[1] for item in updates],
+        *[item[2] for item in updates],
+        *[item[2].astype(BF) for item in updates],
+    )
+
+
 def solution(mesh):
     in_specs = (
         P("fsdp", "seq", None),
@@ -455,6 +1055,7 @@
         P(None, "fsdp", None),
         P(None, "fsdp", None),
     )
+    body = fast_device if fits_fast(mesh) else general_device
     return jax.shard_map(
-        per_device, mesh=mesh, in_specs=in_specs, out_specs=out_specs, check_vma=False
-    )
+        body, mesh=mesh, in_specs=in_specs, out_specs=out_specs, check_vma=False
+    )

time: 2600 us -> 1270 us (0.49)
  waiting for transfers between devices: 1250 us -> 461 us
  matrix products: 741 us -> 169 us
  Pallas kernels: 0 us -> 167 us
  local copies, waits for them, and re-layouts: 251 us -> 102 us
    reduce_scatter x4 -> x0, waiting for transfers between devices: 755 us -> none  [the longest x1 326 us: per_device(): lax.psum_scatter(grad_accum[3], 'fsdp', scatter_dimension=1, tiled=True)]
    dot_general x104 -> x26, matrix products: 741 us -> 169 us  [the longest x8 60.2 us: dot_nt(): return lax.dot_general(left, right, NT, preferred_element_type=F32)]
    ppermute x0 -> x120, waiting for transfers between devices: none -> 398 us  [the longest x56 205 us: swap_seq(): lax.ppermute(item, 'seq', [(idx, idx ^ mask) for idx in range(parts)])]
    all_gather x8 -> x3, waiting for transfers between devices: 172 us -> 0.03 us  [fast_device(): whole = lax.all_gather(item, 'seq', axis=1, tiled=True)]
    pallas_call x0 -> x8, Pallas kernels: none -> 167 us  [the longest x2 74.5 us: attend_grad(): pl.pallas_call(attn_bwd_kernel, grid=(pairs,), in_specs=[triple, pl.Block...]
    psum x1, waiting for transfers between devices: 225 us -> 62.5 us  [fast_device(): lax.psum(jnp.stack(vector_sums), ('seq', 'fsdp')) / clip_count]
    ppermute x0 -> x120, starting transfers between devices: none -> 92.1 us  [the longest x56 57.6 us: swap_seq(): lax.ppermute(item, 'seq', [(idx, idx ^ mask) for idx in range(parts)])]
    all_to_all x16 -> x0, starting transfers between devices: 70.9 us -> none  [the longest x4 18.5 us: layer_backward(): lax.all_to_all(stacked_grad, 'seq', split_axis=0, concat_axis=2, tiled=True)]
  transfers between devices with their start and end apart: 30 -> 124, of which waited for: 15 -> 43; matrix products, arithmetic and copies ran while one was open for 39% -> 29% of each run, Pallas kernels for 0% -> 13%
where the time goes in v1:
time: 1270 us; the launch traced here: 1260 us
  waiting for transfers between devices  461 us (36%)
  other arithmetic  172 us (14%)
  matrix products  169 us (13%)
  Pallas kernels  167 us (13%)
  local copies, waits for them, and re-layouts  102 us (8%)
  starting transfers between devices  92.3 us (7%)
  blocking collectives  71.8 us (6%)
  between operations  24.2 us (2%)
    ppermute x56, waiting for transfers between devices, swap_seq(): lax.ppermute(item, 'seq', [(idx, idx ^ mask) for idx in range(parts)])  205 us
    ppermute x36, waiting for transfers between devices, send_up(): lax.ppermute(item, 'fsdp', [(idx, (idx + 2) % parts) for idx in range(par...  181 us
    pallas_call x2, Pallas kernels, attend_grad(): pl.pallas_call(attn_bwd_kernel, grid=(pairs,), in_specs=[triple, pl.Block...  74.5 us
    pallas_call x2, Pallas kernels, attend(): pl.pallas_call(attn_fwd_kernel, grid=(pairs,), in_specs=[triple, table, t...  68.9 us
    psum x1, waiting for transfers between devices, fast_device(): lax.psum(jnp.stack(vector_sums), ('seq', 'fsdp')) / clip_count  62.5 us
    dot_general x8, matrix products, dot_nt(): return lax.dot_general(left, right, NT, preferred_element_type=F32)  60.2 us
    dot_general x10, matrix products, dot(): return jnp.dot(left, right, preferred_element_type=F32)  59.3 us
    ppermute x56, starting transfers between devices, swap_seq(): lax.ppermute(item, 'seq', [(idx, idx ^ mask) for idx in range(parts)])  57.6 us
  transfers between devices with their start and end apart: 124, of which 43 were waited for; matrix products, arithmetic and copies ran while one was open for 29% of the time, Pallas kernels for 13%

profile of v1, /device:TPU:0, one launch (start us, length us, event | category | flops | bytes accessed | tf_op | source)
XLA Modules:
  0.0 1259.8 jit_solution(7256301004658349003)
XLA Ops:
  24.3 16.9 %all_gather.15 = bf16[2,13312]{1,0:T(2,128)(2,1)S(1)} all-gather(bf16[2,1664]{1,0:T(2,128)(2,1)S(1)} %convert_element_type.865), channel_id=1, replica_groups=mesh['seq'=4,'fsdp'=8] {'fsdp'}, dimensions={1}, use_global_device_ids=true | all-gather | bytes 59904 | tf_op jit(solution)/shard_map/all_gather | solution.py:854
  71.4 10.7 collective-permute-done.1
  89.7 19.1 %collective-permute-done.8.refs_6_ = bf16[256,512]{1,0:T(8,128)(2,1)} collective-permute-done((bf16[256,512]{1,0:T(8,128)(2,1)}, bf16[256,512]{1,0:T(8,128)(2,1)}, u32[]{:S(2)}, u32[]{:S(2)}) %collective-permute-start.8) | collective-permute-done | bytes 262176 | tf_op jit(solution)/shard_map/ppermute | solution.py:427
  194.3 34.5 %attend.2 = (bf16[1024,512]{1,0:T(8,128)(2,1)}, bf16[1024,1536]{1,0:T(8,128)(2,1)}, f32[4,8,1024]{2,1,0:T(8,128)}) custom-call(f32[1024,1536]{1,0:T(8,128)} %convolution_add_fusion.1.qkv_ref, f32[1024,128]{1,0:T(8,128)} %get-tuple-element.234.cos_ref, f32[1024,128]{1,0:T(8,128)} %get-tuple-element.235.sin_ref), custom_call_target="tpu_custom_call" | custom-call | flops 8589934592 | bytes 12582912 | tf_op jit(solution)/shard_map/attend/pallas_call | solution.py:498
  253.4 10.3 collective-permute-done.32.refs_13_
  319.3 17.9 %collective-permute-done.42 = bf16[128,512]{1,0:T(8,128)(2,1)S(1)} collective-permute-done((bf16[128,512]{1,0:T(8,128)(2,1)S(1)}, bf16[128,512]{1,0:T(8,128)(2,1)S(1)}, u32[]{:S(2)}, u32[]{:S(2)}) %collective-permute-start.42) | collective-permute-done | bytes 131104 | tf_op jit(solution)/shard_map/ppermute | solution.py:432
  393.4 34.4 %attend.3 = (bf16[1024,512]{1,0:T(8,128)(2,1)}, bf16[1024,1536]{1,0:T(8,128)(2,1)}, f32[4,8,1024]{2,1,0:T(8,128)}) custom-call(f32[1024,1536]{1,0:T(8,128)} %convolution_add_fusion.qkv_ref, f32[1024,128]{1,0:T(8,128)} %get-tuple-element.234.cos_ref, f32[1024,128]{1,0:T(8,128)} %get-tuple-element.235.sin_ref), custom_call_target="tpu_custom_call" | custom-call | flops 8589934592 | bytes 12582912 | tf_op jit(solution)/shard_map/attend/pallas_call | solution.py:498
  454.2 12.4 fusion.10
  466.6 11.7 fusion.132
  478.3 13.0 %convolution_convert_fusion.4 = bf16[1024,2048]{1,0:T(8,128)(2,1)} fusion(f32[1024,2048]{1,0:T(8,128)} %copy-done.135, bf16[1024,2048]{1,0:T(8,128)(2,1)} %get-tuple-element.118, f32[1024,1024]{1,0:T(8,128)S(1)} %get-tuple-element.216, f32[1024]{0:T(1024)S(1)} %bitcast.542, f32[1024]{0:T(1024)S(1)} %bitcast.511, f32[1024]{0:T(1024)S(1)} %add_rsqrt_fusion, ...), kind=kOutput, calls=%fused_computation.90 | convolution fusion | flops 4308598784 | bytes 20987904 | tf_op jit(solution)/shard_map/dot_general | solution.py:756
  491.7 10.8 fusion.133
  533.1 28.1 %collective-permute-done.104 = bf16[4,2,2,32,2048]{4,3,1,0,2:T(8,128)(2,1)S(1)} collective-permute-done((bf16[4,2,2,32,2048]{4,3,1,0,2:T(8,128)(2,1)}, bf16[4,2,2,32,2048]{4,3,1,0,2:T(8,128)(2,1)S(1)}, u32[]{:S(2)}, u32[]{:S(2)}) %collective-permute-start.104) | collective-permute-done | bytes 2097184 | tf_op jit(solution)/shard_map/ppermute | solution.py:432
  566.4 37.2 %attend_grad.2 = (bf16[1024,1536]{1,0:T(8,128)(2,1)}, f32[8,1536]{1,0:T(8,128)}) custom-call(bf16[1024,1536]{1,0:T(8,128)(2,1)} %get-tuple-element.56.low_ref, bf16[1024,512]{1,0:T(8,128)(2,1)} %convolution_convert_fusion.9.dout_ref, f32[4,8,1024]{2,1,0:T(8,128)} %get-tuple-element.57.lse_ref, f32[1024,128]{1,0:T(8,128)} %get-tuple-element.234.cos_ref, ...), custom_call_target="tpu_custom_call" | custom-call | flops 21474836480 | bytes 9437184 | tf_op jit(solution)/shard_map/attend_grad/pallas_call | solution.py:586
  634.0 9.8 collective-permute-done.95
  659.4 17.5 %collective-permute-done.97 = bf16[1,32,1024]{2,1,0:T(8,128)(2,1)S(1)} collective-permute-done((bf16[1,32,1024]{2,1,0:T(8,128)(2,1)S(1)}, bf16[1,32,1024]{2,1,0:T(8,128)(2,1)S(1)}, u32[]{:S(2)}, u32[]{:S(2)}) %collective-permute-start.97) | collective-permute-done | bytes 65568 | tf_op jit(solution)/shard_map/ppermute | solution.py:432
  680.4 23.9 %collective-permute-done.106 = bf16[2,32,2048]{2,1,0:T(8,128)(2,1)S(1)} collective-permute-done((bf16[2,32,2048]{2,1,0:T(8,128)(2,1)S(1)}, bf16[2,32,2048]{2,1,0:T(8,128)(2,1)S(1)}, u32[]{:S(2)}, u32[]{:S(2)}) %collective-permute-start.106) | collective-permute-done | bytes 262176 | tf_op jit(solution)/shard_map/ppermute | solution.py:427
  706.0 9.4 collective-permute-done.117
  758.0 11.9 fusion.12
  769.9 11.3 fusion.135
  781.2 9.8 convolution_convert_fusion.5
  800.5 48.6 %collective-permute-done.85 = bf16[2,2,32,1536]{3,2,0,1:T(8,128)(2,1)S(1)} collective-permute-done((bf16[2,2,32,1536]{3,2,0,1:T(8,128)(2,1)S(1)}, bf16[2,2,32,1536]{3,2,0,1:T(8,128)(2,1)S(1)}, u32[]{:S(2)}, u32[]{:S(2)}) %collective-permute-start.85) | collective-permute-done | bytes 393248 | tf_op jit(solution)/shard_map/ppermute | solution.py:432
  873.0 37.3 %attend_grad.3 = (bf16[1024,1536]{1,0:T(8,128)(2,1)}, f32[8,1536]{1,0:T(8,128)}) custom-call(bf16[1024,1536]{1,0:T(8,128)(2,1)} %get-tuple-element.59.low_ref, bf16[1024,512]{1,0:T(8,128)(2,1)} %convolution_convert_fusion.8.dout_ref, f32[4,8,1024]{2,1,0:T(8,128)} %get-tuple-element.60.lse_ref, f32[1024,128]{1,0:T(8,128)} %get-tuple-element.234.cos_ref, ...), custom_call_target="tpu_custom_call" | custom-call | flops 21474836480 | bytes 9437184 | tf_op jit(solution)/shard_map/attend_grad/pallas_call | solution.py:586
  944.5 17.4 %collective-permute-done.90 = bf16[1,2,2,32,1024]{4,3,2,1,0:T(8,128)(2,1)S(1)} collective-permute-done((bf16[1,2,2,32,1024]{4,3,2,1,0:T(8,128)(2,1)S(1)}, bf16[1,2,2,32,1024]{4,3,2,1,0:T(8,128)(2,1)S(1)}, u32[]{:S(2)}, u32[]{:S(2)}) %collective-permute-start.90) | collective-permute-done | bytes 262176 | tf_op jit(solution)/shard_map/ppermute | solution.py:427
  969.6 21.1 %collective-permute-done.112 = bf16[1,128,1024]{2,1,0:T(8,128)(2,1)S(1)} collective-permute-done((bf16[1,128,1024]{2,1,0:T(8,128)(2,1)S(1)}, bf16[1,128,1024]{2,1,0:T(8,128)(2,1)S(1)}, u32[]{:S(2)}, u32[]{:S(2)}) %collective-permute-start.112) | collective-permute-done | bytes 262176 | tf_op jit(solution)/shard_map/ppermute | solution.py:427
  1021.0 13.5 %all_gather.17 = bf16[2,128,1024]{2,1,0:T(8,128)(2,1)} all-gather(bf16[2,32,1024]{2,1,0:T(8,128)(2,1)S(1)} %pad_maximum_fusion.7), channel_id=1, replica_groups=mesh['seq'=4,'fsdp'=8] {'seq'}, dimensions={1}, use_global_device_ids=true | all-gather | bytes 655360 | tf_op jit(solution)/shard_map/all_gather | solution.py:989
  1044.3 15.3 %collective-permute-done.78 = bf16[2,2,2,32,1536]{4,3,0,1,2:T(8,128)(2,1)} collective-permute-done((bf16[2,2,2,32,1536]{4,3,0,1,2:T(8,128)(2,1)}, bf16[2,2,2,32,1536]{4,3,0,1,2:T(8,128)(2,1)}, u32[]{:S(2)}, u32[]{:S(2)}) %collective-permute-start.78) | collective-permute-done | bytes 786464 | tf_op jit(solution)/shard_map/ppermute | solution.py:427
  1061.8 16.0 %collective-permute-done.79 = bf16[2,2,32,1536]{3,2,0,1:T(8,128)(2,1)S(1)} collective-permute-done((bf16[2,2,32,1536]{3,2,0,1:T(8,128)(2,1)S(1)}, bf16[2,2,32,1536]{3,2,0,1:T(8,128)(2,1)S(1)}, u32[]{:S(2)}, u32[]{:S(2)}) %collective-permute-start.79) | collective-permute-done | bytes 393248 | tf_op jit(solution)/shard_map/ppermute | solution.py:432
  1084.0 9.6 collective-permute-start.74
  1095.8 62.5 %all-reduce.3.cloned.1.call-done = f32[2,13312]{1,0:T(2,128)} async-done(((f32[2,13312]{1,0:T(2,128)}), f32[2,13312]{1,0:T(2,128)}) %all-reduce.3.cloned.1.call-update) | async-done | bytes 106512 | tf_op jit(solution)/shard_map/psum | solution.py:980
  1166.3 41.5 %psum.15 = f32[]{:T(128)} all-reduce(f32[]{:T(128)S(6)} %add.754), channel_id=1, replica_groups=mesh['seq'=4,'fsdp'=8] {'seq','fsdp'}, use_global_device_ids=true, to_apply=%region_35.36 | all-reduce | flops 1 | bytes 8 | tf_op jit(solution)/shard_map/psum | solution.py:981
  1218.7 11.9 fusion.101
  1230.7 11.5 fusion.104
  (814 shorter events, 578.9 us)
Async XLA Ops:
  8.0 1150.3 %all-reduce.3.cloned.1.call-start = ((), (), s32[]{:S(2)}) async-start(), calls=%async_computation | async-start | bytes 212992 | tf_op jit(solution)/shard_map/psum | solution.py:980
  85.4 84.5 %collective-permute-start.2 = (f32[2,264,1024]{2,1,0:T(8,128)}, f32[2,264,1024]{2,1,0:T(8,128)}, u32[]{:S(2)}, u32[]{:S(2)}) collective-permute-start(f32[2,264,1024]{2,1,0:T(8,128)} %maximum_select_fusion.3), channel_id=1, source_target_pairs={{0,1},{1,0},{2,3},{3,2},{4,5},{5,4},{6,7},{7,6},{8,9},{9,8},{10,11... | collective-permute-start | bytes 6488072 | tf_op jit(solution)/shard_map/ppermute | solution.py:422
  154.3 74.5 %collective-permute-start.68 = (f32[256,1024]{1,0:T(8,128)}, f32[256,1024]{1,0:T(8,128)S(1)}, u32[]{:S(2)}, u32[]{:S(2)}) collective-permute-start(f32[256,1024]{1,0:T(8,128)} %get-tuple-element.150), channel_id=1, source_target_pairs={{0,8},{1,24},{2,10},{3,26},{4,12},{5,28},{6,14},{7,30},{8,0},{9,16... | collective-permute-start | bytes 3145736 | tf_op jit(solution)/shard_map/ppermute | solution.py:818
  290.0 82.4 %collective-permute-start.69 = (f32[2,256,1024]{2,1,0:T(8,128)}, f32[2,256,1024]{2,1,0:T(8,128)}, u32[]{:S(2)}, u32[]{:S(2)}) collective-permute-start(f32[2,256,1024]{2,1,0:T(8,128)} %maximum_select_fusion.6), channel_id=1, source_target_pairs={{0,1},{1,0},{2,3},{3,2},{4,5},{5,4},{6,7},{7,6},{8,9},{9,8},{10,11... | collective-permute-start | bytes 6291464 | tf_op jit(solution)/shard_map/ppermute | solution.py:422
  300.7 80.2 %collective-permute-start.33 = (bf16[1024,1024]{1,0:T(8,128)(2,1)}, bf16[1024,1024]{1,0:T(8,128)(2,1)}, u32[]{:S(2)}, u32[]{:S(2)}) collective-permute-start(bf16[1024,1024]{1,0:T(8,128)(2,1)} %get-tuple-element.213), channel_id=1, source_target_pairs={{0,1},{1,0},{2,3},{3,2},{4,5},{5,4},{6,7},{7,6},{8,9},{9,8},{10,11... | collective-permute-start | bytes 6291464 | tf_op jit(solution)/shard_map/ppermute | solution.py:422
  369.5 58.2 %collective-permute-start.52 = (bf16[512,512]{1,0:T(8,128)(2,1)}, bf16[512,512]{1,0:T(8,128)(2,1)S(1)}, u32[]{:S(2)}, u32[]{:S(2)}) collective-permute-start(bf16[512,512]{1,0:T(8,128)(2,1)} %collective-permute-done.51.refs_2_), channel_id=1, source_target_pairs={{0,8},{8,0},{16,24},{24,16},{1,9},{9,1},{17,25},{25,17},{2,10},{10... | collective-permute-start | bytes 1572872 | tf_op jit(solution)/shard_map/ppermute | solution.py:432
  370.2 60.3 %collective-permute-start.54 = (bf16[512,512]{1,0:T(8,128)(2,1)}, bf16[512,512]{1,0:T(8,128)(2,1)S(1)}, u32[]{:S(2)}, u32[]{:S(2)}) collective-permute-start(bf16[512,512]{1,0:T(8,128)(2,1)} %collective-permute-done.53.refs_4_), channel_id=1, source_target_pairs={{0,8},{8,0},{16,24},{24,16},{1,9},{9,1},{17,25},{25,17},{2,10},{10... | collective-permute-start | bytes 1572872 | tf_op jit(solution)/shard_map/ppermute | solution.py:432
  372.5 72.8 %collective-permute-start.49 = (bf16[512,1024]{1,0:T(8,128)(2,1)}, bf16[512,1024]{1,0:T(8,128)(2,1)}, u32[]{:S(2)}, u32[]{:S(2)}) collective-permute-start(bf16[512,1024]{1,0:T(8,128)(2,1)} %get-tuple-element.53), channel_id=1, source_target_pairs={{0,1},{1,0},{2,3},{3,2},{4,5},{5,4},{6,7},{7,6},{8,9},{9,8},{10,11... | collective-permute-start | bytes 3145736 | tf_op jit(solution)/shard_map/ppermute | solution.py:422
  379.7 50.8 %collective-permute-start.62 = (bf16[512,512]{1,0:T(8,128)(2,1)}, bf16[512,512]{1,0:T(8,128)(2,1)S(1)}, u32[]{:S(2)}, u32[]{:S(2)}) collective-permute-start(bf16[512,512]{1,0:T(8,128)(2,1)} %collective-permute-done.60.refs_10_), channel_id=1, source_target_pairs={{0,16},{8,24},{16,0},{24,8},{1,17},{9,25},{17,1},{25,9},{2,18},{10... | collective-permute-start | bytes 1572872 | tf_op jit(solution)/shard_map/ppermute | solution.py:432
  381.0 49.5 %collective-permute-start.63 = (bf16[512,512]{1,0:T(8,128)(2,1)}, bf16[512,512]{1,0:T(8,128)(2,1)}, u32[]{:S(2)}, u32[]{:S(2)}) collective-permute-start(bf16[512,512]{1,0:T(8,128)(2,1)} %collective-permute-done.61.refs_11_), channel_id=1, source_target_pairs={{0,16},{8,24},{16,0},{24,8},{1,17},{9,25},{17,1},{25,9},{2,18},{10... | collective-permute-start | bytes 1572872 | tf_op jit(solution)/shard_map/ppermute | solution.py:432
  514.6 103.4 %collective-permute-start.115 = (bf16[4,1,2,128,1024]{4,3,0,2,1:T(8,128)(2,1)}, bf16[4,1,2,128,1024]{4,3,0,2,1:T(8,128)(2,1)}, u32[]{:S(2)}, u32[]{:S(2)}) collective-permute-start(bf16[4,1,2,128,1024]{4,3,0,2,1:T(8,128)(2,1)} %bitcast.424), channel_id=1, source_target_pairs={{0,16},{8,24},{16,0},{24,8},{1,17},{9,25},{17,1},{25,9},{2,18},{10... | collective-permute-start | bytes 6291464 | tf_op jit(solution)/shard_map/ppermute | solution.py:432
  564.4 112.5 %collective-permute-start.105 = (bf16[4,2,32,2048]{3,2,1,0:T(8,128)(2,1)}, bf16[4,2,32,2048]{3,2,1,0:T(8,128)(2,1)}, u32[]{:S(2)}, u32[]{:S(2)}) collective-permute-start(bf16[4,2,32,2048]{3,2,1,0:T(8,128)(2,1)} %dynamic-slice_bitcast_fusion.2), channel_id=1, source_target_pairs={{0,16},{8,24},{16,0},{24,8},{1,17},{9,25},{17,1},{25,9},{2,18},{10... | collective-permute-start | bytes 3145736 | tf_op jit(solution)/shard_map/ppermute | solution.py:432
  565.7 54.9 %collective-permute-start.93 = (bf16[1,2,2,32,1024]{4,3,2,1,0:T(8,128)(2,1)S(1)}, bf16[1,2,2,32,1024]{4,3,2,1,0:T(8,128)(2,1)}, u32[]{:S(2)}, u32[]{:S(2)}) collective-permute-start(bf16[1,2,2,32,1024]{4,3,2,1,0:T(8,128)(2,1)S(1)} %dynamic-slice_bitcast_fusion.14), channel_id=1, source_target_pairs={{0,2},{1,3},{2,4},{3,5},{4,6},{5,7},{6,0},{7,1},{8,10},{9,11},{10,... | collective-permute-start | bytes 786440 | tf_op jit(solution)/shard_map/ppermute | solution.py:427
  624.8 53.9 %collective-permute-start.116 = (bf16[4,1,128,1024]{3,2,1,0:T(8,128)(2,1)}, bf16[4,1,128,1024]{3,2,1,0:T(8,128)(2,1)}, u32[]{:S(2)}, u32[]{:S(2)}) collective-permute-start(bf16[4,1,128,1024]{3,2,1,0:T(8,128)(2,1)} %dynamic-slice_bitcast_fusion), channel_id=1, source_target_pairs={{0,8},{8,0},{16,24},{24,16},{1,9},{9,1},{17,25},{25,17},{2,10},{10... | collective-permute-start | bytes 3145736 | tf_op jit(solution)/shard_map/ppermute | solution.py:432
  645.9 58.5 %collective-permute-start.65 = (f32[256,1024]{1,0:T(8,128)S(1)}, f32[256,1024]{1,0:T(8,128)S(1)}, u32[]{:S(2)}, u32[]{:S(2)}) collective-permute-start(f32[256,1024]{1,0:T(8,128)S(1)} %get-tuple-element.135), channel_id=1, source_target_pairs={{0,0},{16,1},{2,2},{18,3},{4,4},{20,5},{6,6},{22,7},{8,8},{24,9},{... | collective-permute-start | bytes 3145736 | tf_op jit(solution)/shard_map/ppermute | solution.py:837
  649.8 54.7 %collective-permute-start.66 = (f32[256,1024]{1,0:T(8,128)S(1)}, f32[256,1024]{1,0:T(8,128)S(1)}, u32[]{:S(2)}, u32[]{:S(2)}) collective-permute-start(f32[256,1024]{1,0:T(8,128)S(1)} %get-tuple-element.136), channel_id=1, source_target_pairs={{8,0},{24,1},{10,2},{26,3},{12,4},{28,5},{14,6},{30,7},{0,8},{16,9... | collective-permute-start | bytes 3145736 | tf_op jit(solution)/shard_map/ppermute | solution.py:837
  676.9 65.9 %collective-permute-start.71 = (bf16[1024,1024]{1,0:T(8,128)(2,1)}, bf16[1024,1024]{1,0:T(8,128)(2,1)S(1)}, u32[]{:S(2)}, u32[]{:S(2)}) collective-permute-start(bf16[1024,1024]{1,0:T(8,128)(2,1)} %get-tuple-element.221), channel_id=1, source_target_pairs={{0,1},{1,0},{2,3},{3,2},{4,5},{5,4},{6,7},{7,6},{8,9},{9,8},{10,11... | collective-permute-start | bytes 6291464 | tf_op jit(solution)/shard_map/ppermute | solution.py:422
  676.9 50.4 %collective-permute-start.83 = (bf16[2,2,2,32,1536]{4,3,0,1,2:T(8,128)(2,1)S(1)}, bf16[2,2,2,32,1536]{4,3,0,1,2:T(8,128)(2,1)S(1)}, u32[]{:S(2)}, u32[]{:S(2)}) collective-permute-start(bf16[2,2,2,32,1536]{4,3,0,1,2:T(8,128)(2,1)S(1)} %fusion.35), channel_id=1, source_target_pairs={{0,2},{1,3},{2,4},{3,5},{4,6},{5,7},{6,0},{7,1},{8,10},{9,11},{10,... | collective-permute-start | bytes 2359304 | tf_op jit(solution)/shard_map/ppermute | solution.py:427
  728.5 69.9 %collective-permute-start.84 = (bf16[2,2,2,32,1536]{4,3,0,1,2:T(8,128)(2,1)}, bf16[2,2,2,32,1536]{4,3,0,1,2:T(8,128)(2,1)}, u32[]{:S(2)}, u32[]{:S(2)}) collective-permute-start(bf16[2,2,2,32,1536]{4,3,0,1,2:T(8,128)(2,1)} %fusion.34), channel_id=1, source_target_pairs={{0,2},{1,3},{2,4},{3,5},{4,6},{5,7},{6,0},{7,1},{8,10},{9,11},{10,... | collective-permute-start | bytes 2359304 | tf_op jit(solution)/shard_map/ppermute | solution.py:427
  796.9 120.3 %collective-permute-start.98 = (bf16[4,2,2,32,2048]{4,3,1,0,2:T(8,128)(2,1)}, bf16[4,2,2,32,2048]{4,3,1,0,2:T(8,128)(2,1)}, u32[]{:S(2)}, u32[]{:S(2)}) collective-permute-start(bf16[4,2,2,32,2048]{4,3,1,0,2:T(8,128)(2,1)} %bitcast.427), channel_id=1, source_target_pairs={{0,8},{8,0},{16,24},{24,16},{1,9},{9,1},{17,25},{25,17},{2,10},{10... | collective-permute-start | bytes 6291464 | tf_op jit(solution)/shard_map/ppermute | solution.py:432
  798.4 59.3 %collective-permute-start.72 = (bf16[1024,1024]{1,0:T(8,128)(2,1)}, bf16[1024,1024]{1,0:T(8,128)(2,1)}, u32[]{:S(2)}, u32[]{:S(2)}) collective-permute-start(bf16[1024,1024]{1,0:T(8,128)(2,1)} %get-tuple-element.224), channel_id=1, source_target_pairs={{0,1},{1,0},{2,3},{3,2},{4,5},{5,4},{6,7},{7,6},{8,9},{9,8},{10,11... | collective-permute-start | bytes 6291464 | tf_op jit(solution)/shard_map/ppermute | solution.py:422
  798.4 141.9 %collective-permute-start.110 = (bf16[4,1,2,128,1024]{4,3,0,2,1:T(8,128)(2,1)}, bf16[4,1,2,128,1024]{4,3,0,2,1:T(8,128)(2,1)}, u32[]{:S(2)}, u32[]{:S(2)}) collective-permute-start(bf16[4,1,2,128,1024]{4,3,0,2,1:T(8,128)(2,1)} %bitcast.425), channel_id=1, source_target_pairs={{0,16},{8,24},{16,0},{24,8},{1,17},{9,25},{17,1},{25,9},{2,18},{10... | collective-permute-start | bytes 6291464 | tf_op jit(solution)/shard_map/ppermute | solution.py:432
  799.8 49.2 %collective-permute-start.85 = (bf16[2,2,32,1536]{3,2,0,1:T(8,128)(2,1)S(1)}, bf16[2,2,32,1536]{3,2,0,1:T(8,128)(2,1)S(1)}, u32[]{:S(2)}, u32[]{:S(2)}) collective-permute-start(bf16[2,2,32,1536]{3,2,0,1:T(8,128)(2,1)S(1)} %dynamic-slice_bitcast_fusion.4), channel_id=1, source_target_pairs={{0,8},{8,0},{16,24},{24,16},{1,9},{9,1},{17,25},{25,17},{2,10},{10... | collective-permute-start | bytes 1179656 | tf_op jit(solution)/shard_map/ppermute | solution.py:432
  872.9 55.0 %collective-permute-start.88 = (bf16[1,2,2,32,1024]{4,3,2,1,0:T(8,128)(2,1)S(1)}, bf16[1,2,2,32,1024]{4,3,2,1,0:T(8,128)(2,1)}, u32[]{:S(2)}, u32[]{:S(2)}) collective-permute-start(bf16[1,2,2,32,1024]{4,3,2,1,0:T(8,128)(2,1)S(1)} %dynamic-slice_bitcast_fusion.15), channel_id=1, source_target_pairs={{0,2},{1,3},{2,4},{3,5},{4,6},{5,7},{6,0},{7,1},{8,10},{9,11},{10,... | collective-permute-start | bytes 786440 | tf_op jit(solution)/shard_map/ppermute | solution.py:427
  933.2 79.5 %collective-permute-start.73 = (bf16[1024,1024]{1,0:T(8,128)(2,1)S(1)}, bf16[1024,1024]{1,0:T(8,128)(2,1)S(1)}, u32[]{:S(2)}, u32[]{:S(2)}) collective-permute-start(bf16[1024,1024]{1,0:T(8,128)(2,1)S(1)} %copy-done.134), channel_id=1, source_target_pairs={{0,1},{1,0},{2,3},{3,2},{4,5},{5,4},{6,7},{7,6},{8,9},{9,8},{10,11... | collective-permute-start | bytes 6291464 | tf_op jit(solution)/shard_map/ppermute | solution.py:422
  964.8 69.8 %collective-permute-start.77 = (bf16[2,2,2,32,1536]{4,3,0,1,2:T(8,128)(2,1)}, bf16[2,2,2,32,1536]{4,3,0,1,2:T(8,128)(2,1)}, u32[]{:S(2)}, u32[]{:S(2)}) collective-permute-start(bf16[2,2,2,32,1536]{4,3,0,1,2:T(8,128)(2,1)} %fusion.38), channel_id=1, source_target_pairs={{0,2},{1,3},{2,4},{3,5},{4,6},{5,7},{6,0},{7,1},{8,10},{9,11},{10,... | collective-permute-start | bytes 2359304 | tf_op jit(solution)/shard_map/ppermute | solution.py:427
  1017.4 201.3 %all-gather.8.cloned.1.call-start = ((), (), s32[]{:S(2)}) async-start(), calls=%async_computation.3 | async-start | bytes 2621440 | tf_op jit(solution)/shard_map/all_gather | solution.py:989
  1018.3 212.3 %all-gather.6.cloned.1.call-start = ((), (), s32[]{:S(2)}) async-start(), calls=%async_computation.2 | async-start | bytes 2621440 | tf_op jit(solution)/shard_map/all_gather | solution.py:989
  1042.2 200.0 %all-gather.4.cloned.1.call-start = ((), (), s32[]{:S(2)}) async-start(), calls=%async_computation.1 | async-start | bytes 1966080 | tf_op jit(solution)/shard_map/all_gather | solution.py:989
  1084.0 130.6 %collective-permute-start.74 = (f32[256,1024]{1,0:T(8,128)}, f32[256,1024]{1,0:T(8,128)}, u32[]{:S(2)}, u32[]{:S(2)}) collective-permute-start(f32[256,1024]{1,0:T(8,128)} %get-tuple-element.132), channel_id=1, source_target_pairs={{0,0},{16,1},{2,2},{18,3},{4,4},{20,5},{6,6},{22,7},{8,8},{24,9},{... | collective-permute-start | bytes 3145736 | tf_op jit(solution)/shard_map/ppermute | solution.py:837
  1093.6 121.0 %collective-permute-start.75 = (f32[256,1024]{1,0:T(8,128)}, f32[256,1024]{1,0:T(8,128)}, u32[]{:S(2)}, u32[]{:S(2)}) collective-permute-start(f32[256,1024]{1,0:T(8,128)} %get-tuple-element.133), channel_id=1, source_target_pairs={{8,0},{24,1},{10,2},{26,3},{12,4},{28,5},{14,6},{30,7},{0,8},{16,9... | collective-permute-start | bytes 3145736 | tf_op jit(solution)/shard_map/ppermute | solution.py:837
  1095.7 64.9 %collective-permute-start.81 = (bf16[32,1536]{1,0:T(8,128)(2,1)S(1)}, bf16[32,1536]{1,0:T(8,128)(2,1)S(1)}, u32[]{:S(2)}, u32[]{:S(2)}) collective-permute-start(bf16[32,1536]{1,0:T(8,128)(2,1)S(1)} %get-tuple-element.180), channel_id=1, source_target_pairs={{0,1},{1,0},{2,3},{3,2},{4,5},{5,4},{6,7},{7,6},{8,9},{9,8},{10,11... | collective-permute-start | bytes 294920 | tf_op jit(solution)/shard_map/ppermute | solution.py:422
  (234 other events, 4974.5 us)
Sparse Core Ops, SparseCore 0:
  1017.5 140.7 all-reduce.2
Sparse Core Ops, SparseCore 1:
  1020.3 34.2 all-gather.7
  1056.8 43.8 all-gather.5
  1166.4 31.8 all-gather.3

commit v2 on v1

--- a/solution.py
+++ b/solution.py
@@ -613,82 +613,244 @@
     )(low_all, mixed_grad, lse, cos_wide, sin_wide)
 
 
-def place_kernel(plans, n_pieces, *refs):
-    n_out = len(plans)
-    owns = refs[:n_out]
-    pieces = refs[n_out : n_out + n_pieces]
-    outs = refs[n_out + n_pieces : 2 * n_out + n_pieces]
-    sem = refs[-1]
-    chip = lax.axis_index("fsdp") // 2
+def gather_kernel(
+    qkv_mine, qkv_away, up_mine, up_away, down_in, proj_in,
+    qkv_out, up_out, down_out, proj_out,
+    qkv_slab, up_slab, down_slab, proj_slab,
+    z_send, z_recv, p_send, p_recv, d_send, d_recv, c_send, c_recv, l_in, l_out,
+):
+    shard, seq = lax.axis_index("fsdp"), lax.axis_index("seq")
+    parts = lax.axis_size("fsdp")
+    ring = parts // 2
+    chip, core = shard // 2, lax.rem(shard, 2)
+    other = {"fsdp": shard + 1 - 2 * core}
+    up_chip = {"fsdp": lax.rem(shard + 2, parts)}
+    down_chip = {"fsdp": lax.rem(shard + parts - 2, parts)}
+    at_x, at_y = lax.rem(seq, 2), seq // 2
+    over_x = {"seq": 2 * at_y + 1 - at_x}
+    over_y = {"seq": 2 * (1 - at_y) + at_x}
+    near_x, near_y = 2 * at_y + 1 - at_x, 2 * (1 - at_y) + at_x
+    layers = qkv_mine.shape[0]
+
+    barrier = pltpu.get_barrier_semaphore()
+    for target in (other, up_chip, down_chip, over_x, over_y):
+        pl.semaphore_signal(barrier, inc=1, device_id=target, device_id_type=pl.DeviceIdType.MESH)
+    pl.semaphore_wait(barrier, 5)
+
+    def remote(src, dst, send, recv, target):
+        return pltpu.make_async_remote_copy(
+            src_ref=src,
+            dst_ref=dst,
+            send_sem=send,
+            recv_sem=recv,
+            device_id=target,
+            device_id_type=pl.DeviceIdType.MESH,
+        )
+
+    outs = {"qkv": qkv_out, "up": up_out, "down": down_out, "proj": proj_out}
+    slabs = {"qkv": qkv_slab, "up": up_slab, "down": down_slab, "proj": proj_slab}
+    items = [(name, layer) for layer in range(layers) for name in ("qkv", "proj", "up", "down")]
+
+    def place(name, layer, chip_at, part):
+        slab = slabs[name].shape[1]
+        if part is None:
+            start, size = chip_at * slab, slab
+        else:
+            size = slab // 4
+            start = chip_at * slab + part * size
+        rows = pl.ds(pl.multiple_of(start, size), size)
+        if name == "proj":
+            return outs[name].at[layer, 0, rows, :]
+        return outs[name].at[layer, rows, :]
+
+    local_in, swaps = [], []
+    for idx, (name, layer) in enumerate(items):
+        slab = slabs[name]
+        if name in ("qkv", "up"):
+            mine, away = (qkv_mine, qkv_away) if name == "qkv" else (up_mine, up_away)
+            half = mine.shape[1]
+            rows = pl.ds(pl.multiple_of(core * half, half), half)
+            swap = remote(
+                away.at[layer], slab.at[layer, rows, :], c_send.at[idx], c_recv.at[idx], other
+            )
+            local = pltpu.make_async_copy(mine.at[layer], slab.at[layer, rows, :], l_in.at[idx])
+        else:
+            swap = None
+            source = down_in if name == "down" else proj_in
+            local = pltpu.make_async_copy(source.at[layer], slab.at[layer], l_in.at[idx])
+        swaps.append(swap)
+        local_in.append(local)
+        if swap is not None:
+            swap.start()
+        local.start()
+
+    hops = ring - 1
+    order = []
+    for first in range(0, len(items), 2):
+        for hop in range(hops):
+            order += [(first, hop), (first + 1, hop)]
+
+    stores = []
+    z_copies = {}
+
+    def begin(idx):
+        name, layer = items[idx]
+        local_in[idx].wait()
+        if swaps[idx] is not None:
+            swaps[idx].wait_recv()
+        store = pltpu.make_async_copy(
+            slabs[name].at[layer], place(name, layer, chip, None), l_out.at[idx]
+        )
+        store.start()
+        stores.append(store)
+
+    def z_copy(idx, hop):
+        name, layer = items[idx]
+        part = None if name == "proj" else seq
+        source = place(name, layer, lax.rem(chip - hop + ring, ring), part)
+        if hop == 0:
+            if part is None:
+                from_ref = slabs[name].at[layer]
+            else:
+                size = slabs[name].shape[1] // 4
+                from_ref = slabs[name].at[layer, pl.ds(pl.multiple_of(seq * size, size), size), :]
+        else:
+            from_ref = source
+        slot = idx * hops + hop
+        copy = remote(from_ref, source, z_send.at[slot], z_recv.at[slot], up_chip)
+        copy.start()
+        z_copies[idx, hop] = copy
+
+    plane, far = {}, {}
+
+    def plane_copies(idx, hop):
+        name, layer = items[idx]
+        ref = place(name, layer, lax.rem(chip - hop - 1 + ring, ring), seq)
+        slot = 2 * (idx * hops + hop)
+        plane[idx, hop] = [
+            remote(ref, ref, p_send.at[slot], p_recv.at[slot], over_x),
+            remote(ref, ref, p_send.at[slot + 1], p_recv.at[slot + 1], over_y),
+        ]
+        for copy in plane[idx, hop]:
+            copy.start()
+
+    def far_copies(idx, hop):
+        name, layer = items[idx]
+        slot = 2 * (idx * hops + hop)
+        size = slabs[name].shape[1] // 4
+        half = size // 2
+        base = lax.rem(chip - hop - 1 + ring, ring) * 4 * size
+        for copy in plane[idx, hop]:
+            copy.wait_recv()
+        made = []
+        for turn, (origin, target) in enumerate(((near_y, over_x), (near_x, over_y))):
+            rows = pl.ds(pl.multiple_of(base + origin * size + turn * half, half), half)
+            ref = outs[name].at[layer, rows, :]
+            made.append(
+                remote(ref, ref, d_send.at[slot + turn], d_recv.at[slot + turn], target)
+            )
+        far[idx, hop] = made
+        for copy in made:
+            copy.start()
+
+    pending = []
+    proj_swaps = []
+    begin(0)
+    z_copy(0, 0)
+    begin(1)
+    z_copy(1, 0)
+    for idx, hop in order:
+        z_copies[idx, hop].wait_recv()
+        if hop + 1 < hops:
+            z_copy(idx, hop + 1)
+        elif idx + 2 < len(items):
+            begin(idx + 2)
+            z_copy(idx + 2, 0)
+        name, layer = items[idx]
+        if name == "proj":
+            if hop + 1 == hops:
+                stores[idx].wait()
+                slot = len(items) + layer
+                swap = remote(
+                    proj_out.at[layer, 0],
+                    proj_out.at[layer, 1],
+                    c_send.at[slot],
+                    c_recv.at[slot],
+                    other,
+                )
+                swap.start()
+                proj_swaps.append(swap)
+        else:
+            plane_copies(idx, hop)
+            pending.append((idx, hop))
+            if len(pending) > 1:
+                far_copies(*pending.pop(0))
+    while pending:
+        far_copies(*pending.pop(0))
+
+    for key, made in far.items():
+        for copy in made:
+            copy.wait()
+    for made in plane.values():
+        for copy in made:
+            copy.wait_send()
+    for copy in z_copies.values():
+        copy.wait_send()
+    for copy in swaps:
+        if copy is not None:
+            copy.wait_send()
+    for copy in proj_swaps:
+        copy.wait()
+    for idx, store in enumerate(stores):
+        if items[idx][0] != "proj":
+            store.wait()
+
+
+def gather_weights(qkv_mine, qkv_away, up_mine, up_away, down_low, proj_low):
+    layers = qkv_mine.shape[0]
     ring = lax.axis_size("fsdp") // 2
-    seq = lax.axis_index("seq")
-    copies = []
-    for (quarter, first, blocks), own, out in zip(plans, owns, outs):
-        slab = 4 * quarter
-        copies.append((own, out.at[pl.ds(pl.multiple_of(chip * slab, slab), slab), :]))
-        for idx, piece in enumerate(pieces):
-            hop, mask = idx // 4 + 1, idx % 4
-            place = lax.rem(chip - hop + ring, ring) * slab + (seq ^ mask) * quarter
-            rows = pl.ds(pl.multiple_of(place, quarter), quarter)
-            for block in range(blocks):
-                copies.append(
-                    (
-                        piece.at[pl.ds(first + block * quarter, quarter), :],
-                        out.at[rows, pl.ds(block * 512, 512)],
-                    )
-                )
-    made = [pltpu.make_async_copy(src, dst, sem.at[idx]) for idx, (src, dst) in enumerate(copies)]
-    for item in made:
-        item.start()
-    for item in made:
-        item.wait()
-
-
-def gather_group(slabs):
-    seq = lax.axis_index("seq")
-    packed = []
-    plans = []
-    first = 0
-    for slab in slabs:
-        quarter = slab.shape[0] // 4
-        mine = lax.dynamic_slice_in_dim(slab, seq * quarter, quarter, 0)
-        blocks = slab.shape[1] // 512
-        packed += [mine[:, block * 512 : (block + 1) * 512] for block in range(blocks)]
-        plans.append((quarter, first, blocks))
-        first += quarter * blocks
-    current = jnp.concatenate(packed, axis=0)
-    ring = lax.axis_size("fsdp") // 2
-    half = first // 2
-    pieces = []
-    for hop in range(1, ring):
-        current = send_up(current)
-        over_x = swap_seq(current, 1)
-        over_y = swap_seq(current, 2)
-        if hop % 3 == 0:
-            far = swap_seq(over_x, 2)
-        elif hop % 3 == 1:
-            far = swap_seq(over_y, 1)
-        else:
-            far = jnp.concatenate(
-                [swap_seq(over_x[:half], 2), swap_seq(over_y[half:], 1)], axis=0
-            )
-        pieces += [current, over_x, over_y, far]
-    n_copies = sum(1 + len(pieces) * plan[2] for plan in plans)
+    count = 4 * layers
+    hops = ring - 1
     anywhere = pl.BlockSpec(memory_space=pl.ANY)
+    dma = pltpu.SemaphoreType.DMA
+    qkv_rows, up_rows = 2 * qkv_mine.shape[1], 2 * up_mine.shape[1]
+    down_rows, proj_rows = down_low.shape[1], proj_low.shape[1]
+    width = down_low.shape[2]
+    shapes = [
+        (layers, ring * qkv_rows, qkv_mine.shape[2]),
+        (layers, ring * up_rows, up_mine.shape[2]),
+        (layers, ring * down_rows, width),
+        (layers, 2, ring * proj_rows, width),
+    ]
     return pl.pallas_call(
-        partial(place_kernel, plans, len(pieces)),
-        in_specs=[anywhere] * (len(slabs) + len(pieces)),
-        out_specs=[pl.BlockSpec(memory_space=pltpu.VMEM)] * len(slabs),
-        out_shape=[jax.ShapeDtypeStruct((ring * slab.shape[0], slab.shape[1]), BF) for slab in slabs],
-        scratch_shapes=[pltpu.SemaphoreType.DMA((n_copies,))],
-        compiler_params=pltpu.CompilerParams(vmem_limit_bytes=VMEM_LIMIT),
+        gather_kernel,
+        in_specs=[anywhere] * 6,
+        out_specs=[anywhere] * 4,
+        out_shape=[jax.ShapeDtypeStruct(shape, BF) for shape in shapes],
+        scratch_shapes=[
+            pltpu.VMEM((layers, qkv_rows, qkv_mine.shape[2]), BF),
+            pltpu.VMEM((layers, up_rows, up_mine.shape[2]), BF),
+            pltpu.VMEM((layers, down_rows, width), BF),
+            pltpu.VMEM((layers, proj_rows, width), BF),
+            dma((count * hops,)),
+            dma((count * hops,)),
+            dma((2 * count * hops,)),
+            dma((2 * count * hops,)),
+            dma((2 * count * hops,)),
+            dma((2 * count * hops,)),
+            dma((count + layers,)),
+            dma((count + layers,)),
+            dma((count,)),
+            dma((count,)),
+        ],
+        compiler_params=pltpu.CompilerParams(
+            collective_id=0, has_side_effects=True, vmem_limit_bytes=VMEM_LIMIT
+        ),
         cost_estimate=pl.CostEstimate(
-            flops=0,
-            bytes_accessed=sum(ring * slab.size * 4 for slab in slabs),
-            transcendentals=0,
+            flops=0, bytes_accessed=600_000_000, transcendentals=0
         ),
-        name="place",
-    )(*slabs, *pieces)
+        name="gather_weights",
+    )(qkv_mine, qkv_away, up_mine, up_away, down_low, proj_low)
 
 
 def ring_sum(item):
@@ -854,24 +1016,25 @@
     vector_all = lax.all_gather(vector_params.astype(BF), "fsdp", axis=1, tiled=True).astype(F32)
 
     def by_core(low, kinds):
-        rows = low.shape[0]
-        width = low.shape[1] // (kinds * parts)
-        view = low.reshape(rows, kinds, ring, 2, width)
-        mine = pick(view, core, 3).transpose(0, 2, 1, 3).reshape(rows, -1)
-        away = pick(view, 1 - core, 3).transpose(0, 2, 1, 3).reshape(rows, -1)
-        other = swap_core(away)
-        return jnp.where(
-            core == 0, jnp.stack([mine, other]), jnp.stack([other, mine])
-        ).reshape(2 * rows, -1)
-
-    layers = []
-    for idx in range(layer_count):
-        qkv_slab = by_core(qkv_weight[idx].astype(BF), 3)
-        up_slab = by_core(up_weight[idx].astype(BF), 1)
-        qkv_w, proj_w = gather_group([qkv_slab, proj_weight[idx].astype(BF)])
-        up_w, down_w = gather_group([up_slab, down_weight[idx].astype(BF)])
-        proj_other = swap_core(proj_w)
-        layers.append((qkv_w, proj_w, proj_other, up_w, down_w))
+        width = low.shape[2] // (kinds * parts)
+        view = low.reshape(layer_count, low.shape[1], kinds, ring, 2, width)
+
+        def half(which):
+            cut = pick(view, which, 4).transpose(0, 1, 3, 2, 4)
+            return cut.reshape(layer_count, low.shape[1], -1)
+
+        return half(core), half(1 - core)
+
+    gathered = gather_weights(
+        *by_core(qkv_weight.astype(BF), 3),
+        *by_core(up_weight.astype(BF), 1),
+        down_weight.astype(BF),
+        proj_weight.astype(BF),
+    )
+    layers = [
+        (gathered[0][idx], gathered[3][idx, 0], gathered[3][idx, 1], gathered[1][idx], gathered[2][idx])
+        for idx in range(layer_count)
+    ]
 
     saved = []
     for idx in range(layer_count):

time: 1270 us -> 1220 us (0.961)
  waiting for transfers between devices: 461 us -> 305 us
  Pallas kernels: 167 us -> 316 us
  local copies, waits for them, and re-layouts: 102 us -> 76.5 us
  starting transfers between devices: 92.3 us -> 71.4 us
    pallas_call x4 -> x1, Pallas kernels: 24 us -> 173 us  [gather_weights(): pl.pallas_call(gather_kernel, in_specs=[anywhere] * 6, out_specs=[anywher...]
    ppermute x56 -> x16, waiting for transfers between devices: 205 us -> 91.7 us  [swap_seq(): lax.ppermute(item, 'seq', [(idx, idx ^ mask) for idx in range(parts)])]
    ppermute x36 -> x24, waiting for transfers between devices: 181 us -> 125 us  [send_up(): lax.ppermute(item, 'fsdp', [(idx, (idx + 2) % parts) for idx in range(par...]
    ppermute x56 -> x16, starting transfers between devices: 57.6 us -> 19.6 us  [swap_seq(): lax.ppermute(item, 'seq', [(idx, idx ^ mask) for idx in range(parts)])]
    ppermute x4, waiting for transfers between devices: 10.7 us -> 42.1 us  [to_clips(): halves.append(lax.ppermute(piece, ('seq', 'fsdp'), pairs))]
    unnamed x321 -> x207, local copies, waits for them, and re-layouts: 44.5 us -> 14.3 us
    psum x1, waiting for transfers between devices: 62.5 us -> 41.4 us  [fast_device(): lax.psum(jnp.stack(vector_sums), ('seq', 'fsdp')) / clip_count]
    dynamic_slice x23 -> x22, local copies, waits for them, and re-layouts: 18.6 us -> 35 us  [pick(): return lax.dynamic_index_in_dim(item, index, axis, keepdims=False)]
  transfers between devices with their start and end apart: 124 -> 66, of which waited for: 43 -> 26; matrix products, arithmetic and copies ran while one was open for 29% -> 25% of each run, Pallas kernels for 13% -> 23%
where the time goes in v2:
time: 1220 us; the launch traced here: 1210 us
  Pallas kernels  316 us (26%)
  waiting for transfers between devices  305 us (25%)
  matrix products  173 us (14%)
  other arithmetic  169 us (14%)
  local copies, waits for them, and re-layouts  76.5 us (6%)
  blocking collectives  72.3 us (6%)
  starting transfers between devices  71.4 us (6%)
  between operations  23.1 us (2%)
    pallas_call x1, Pallas kernels, gather_weights(): pl.pallas_call(gather_kernel, in_specs=[anywhere] * 6, out_specs=[anywher...  173 us
    ppermute x24, waiting for transfers between devices, send_up(): lax.ppermute(item, 'fsdp', [(idx, (idx + 2) % parts) for idx in range(par...  125 us
    ppermute x16, waiting for transfers between devices, swap_seq(): lax.ppermute(item, 'seq', [(idx, idx ^ mask) for idx in range(parts)])  91.7 us
    dot_general x8, matrix products, dot_nt(): return lax.dot_general(left, right, NT, preferred_element_type=F32)  76.1 us
    pallas_call x2, Pallas kernels, attend_grad(): pl.pallas_call(attn_bwd_kernel, grid=(pairs,), in_specs=[triple, pl.Block...  74.1 us
    pallas_call x2, Pallas kernels, attend(): pl.pallas_call(attn_fwd_kernel, grid=(pairs,), in_specs=[triple, table, t...  68.9 us
    dot_general x10, matrix products, dot(): return jnp.dot(left, right, preferred_element_type=F32)  51.3 us
    dot_general x8, matrix products, dot_tn(): lax.dot_general(left, right, (((0,), (0,)), ((), ())), preferred_element_...  45.8 us
  transfers between devices with their start and end apart: 66, of which 26 were waited for; matrix products, arithmetic and copies ran while one was open for 25% of the time, Pallas kernels for 23%

profile of v2, /device:TPU:0, one launch (start us, length us, event | category | flops | bytes accessed | tf_op | source)
XLA Modules:
  0.0 1206.7 jit_solution(16154215952036785187)
XLA Ops:
  12.1 9.9 collective-permute-start
  24.9 18.2 %collective-permute-done.1 = f32[264,1024]{1,0:T(8,128)} collective-permute-done((f32[264,1024]{1,0:T(8,128)}, f32[264,1024]{1,0:T(8,128)}, u32[]{:S(2)}, u32[]{:S(2)}) %collective-permute-start.1) | collective-permute-done | bytes 1081376 | tf_op jit(solution)/shard_map/ppermute | solution.py:980
  47.4 14.3 %all_gather.15 = bf16[2,13312]{1,0:T(2,128)(2,1)S(1)} all-gather(bf16[2,1664]{1,0:T(2,128)(2,1)S(1)} %convert_element_type.849), channel_id=1, replica_groups=mesh['seq'=4,'fsdp'=8] {'fsdp'}, dimensions={1}, use_global_device_ids=true | all-gather | bytes 59904 | tf_op jit(solution)/shard_map/all_gather | solution.py:1016
  87.9 14.2 %dynamic-slice_reduce_fusion = (bf16[2,128,4,512]{3,2,1,0:T(4,128)(2,1)}, bf16[2,128,4,512]{3,2,1,0:T(4,128)(2,1)S(1)}) fusion(bf16[2,128,1,4,2,512]{5,4,3,1,0,2:T(2,128)(2,1)S(1)} %reshape.913, s32[]{:T(128)S(6)} %select_n.488, s32[]{:T(128)S(6)} %select_n.487), kind=kLoop, calls=%fused_computation.159 | loop fusion | bytes 4194312 | tf_op jit(solution)/shard_map/jit(dynamic_index_in_dim)/dynamic_slice | solution.py:436
  110.5 173.1 %gather_weights.1 = (bf16[2,1024,1536]{2,1,0:T(8,128)(2,1)}, bf16[2,1024,2048]{2,1,0:T(8,128)(2,1)}, bf16[2,2048,1024]{2,1,0:T(8,128)(2,1)}, bf16[2,2,512,1024]{3,2,1,0:T(8,128)(2,1)}) custom-call(bf16[2,128,1536]{2,1,0:T(8,128)(2,1)} %copy.99.qkv_mine, bf16[2,128,1536]{2,1,0:T(8,128)(2,1)} %copy.100.qkv_away, ...), custom_call_target="tpu_custom_call" | custom-call | bytes 600000000 | tf_op jit(solution)/shard_map/gather_weights/pallas_call | solution.py:825
  306.1 34.5 %attend.2 = (bf16[1024,512]{1,0:T(8,128)(2,1)}, bf16[1024,1536]{1,0:T(8,128)(2,1)}, f32[4,8,1024]{2,1,0:T(8,128)}) custom-call(f32[1024,1536]{1,0:T(8,128)} %convolution_add_fusion.1.qkv_ref, f32[1024,128]{1,0:T(8,128)} %pad_maximum_fusion.cos_ref, f32[1024,128]{1,0:T(8,128)} %pad_maximum_fusion.1.sin_ref), custom_call_target="tpu_custom_call" | custom-call | flops 8589934592 | bytes 12582912 | tf_op jit(solution)/shard_map/attend/pallas_call | solution.py:498
  367.2 23.9 %collective-permute-done.10 = f32[256,1024]{1,0:T(8,128)S(1)} collective-permute-done((f32[256,1024]{1,0:T(8,128)S(1)}, f32[256,1024]{1,0:T(8,128)S(1)}, u32[]{:S(2)}, u32[]{:S(2)}) %collective-permute-start.10) | collective-permute-done | bytes 1048608 | tf_op jit(solution)/shard_map/ppermute | solution.py:980
  403.7 34.4 %attend.3 = (bf16[1024,512]{1,0:T(8,128)(2,1)}, bf16[1024,1536]{1,0:T(8,128)(2,1)}, f32[4,8,1024]{2,1,0:T(8,128)}) custom-call(f32[1024,1536]{1,0:T(8,128)} %convolution_add_fusion.qkv_ref, f32[1024,128]{1,0:T(8,128)} %pad_maximum_fusion.cos_ref, f32[1024,128]{1,0:T(8,128)} %pad_maximum_fusion.1.sin_ref), custom_call_target="tpu_custom_call" | custom-call | flops 8589934592 | bytes 12582912 | tf_op jit(solution)/shard_map/attend/pallas_call | solution.py:498
  456.3 13.8 %fusion.10 = (f32[2048]{0:T(1024)S(1)}, bf16[1024,2048]{1,0:T(8,128)(2,1)}, bf16[1024,2048]{1,0:T(8,128)(2,1)}, f32[1024,2048]{1,0:T(8,128)}) fusion(f32[1024,2048]{1,0:T(8,128)} %fusion.30, f32[2048]{0:T(1024)S(1)} %bitcast.522, bf16[1024,1024]{1,0:T(8,128)(2,1)S(1)} %bitcast.462, bf16[2,2048,1024]{2,1,0:T(8,128)(2,1)} %get-tuple-element.46), kind=kOutput, calls=%fused_computation.20 | convolution fusion | flops 4326422528 | bytes 31473664 | tf_op jit(solution)/shard_map/dot_general | solution.py:914
  470.0 11.6 convolution_convert_fusion.4
  481.7 13.1 %fusion.172 = (bf16[1024,1024]{1,0:T(8,128)(2,1)}, f32[1024,1024]{1,0:T(8,128)}) fusion(bf16[2,1024,2048]{2,1,0:T(8,128)(2,1)} %get-tuple-element.45, f32[1024,2048]{1,0:T(8,128)} %get-tuple-element.199, bf16[1024,2048]{1,0:T(8,128)(2,1)} %get-tuple-element.112), kind=kOutput, calls=%fused_computation.433 | convolution fusion | flops 4302307328 | bytes 23068672 | tf_op jit(solution)/shard_map/dot_general | solution.py:914
  495.1 10.1 fusion.173
  529.4 37.0 %attend_grad.2 = (bf16[1024,1536]{1,0:T(8,128)(2,1)}, f32[8,1536]{1,0:T(8,128)}) custom-call(bf16[1024,1536]{1,0:T(8,128)(2,1)} %get-tuple-element.48.low_ref, bf16[1024,512]{1,0:T(8,128)(2,1)} %convolution_convert_fusion.9.dout_ref, f32[4,8,1024]{2,1,0:T(8,128)} %get-tuple-element.49.lse_ref, f32[1024,128]{1,0:T(8,128)} %pad_maximum_fusion.cos_ref, ...), custom_call_target="tpu_custom_call" | custom-call | flops 21474836480 | bytes 9437184 | tf_op jit(solution)/shard_map/attend_grad/pallas_call | solution.py:586
  581.6 9.3 collective-permute-done.36
  598.6 13.8 %collective-permute-done.37 = bf16[1,2,2,32,1024]{4,3,2,1,0:T(8,128)(2,1)} collective-permute-done((bf16[1,2,2,32,1024]{4,3,2,1,0:T(8,128)(2,1)}, bf16[1,2,2,32,1024]{4,3,2,1,0:T(8,128)(2,1)}, u32[]{:S(2)}, u32[]{:S(2)}) %collective-permute-start.37) | collective-permute-done | bytes 262176 | tf_op jit(solution)/shard_map/ppermute | solution.py:427
  647.5 12.9 %fusion.12 = (f32[2048]{0:T(1024)S(1)}, bf16[1024,2048]{1,0:T(8,128)(2,1)}, f32[1024,2048]{1,0:T(8,128)}) fusion(f32[1024,2048]{1,0:T(8,128)} %get-tuple-element.194, f32[2048]{0:T(1024)S(1)} %bitcast.521, bf16[2,2048,1024]{2,1,0:T(8,128)(2,1)} %get-tuple-element.46, f32[1024,1024]{1,0:T(8,128)S(1)} %get-tuple-element.102), kind=kOutput, calls=%fused_computation.22 | convolution fusion | flops 4323276800 | bytes 29376512 | tf_op jit(solution)/shard_map/dot_general | solution.py:914
  668.8 10.5 convolution_convert_fusion.5
  679.3 12.0 fusion.175
  704.2 57.1 %collective-permute-done.28 = bf16[2,32,1536]{2,1,0:T(8,128)(2,1)S(1)} collective-permute-done((bf16[2,32,1536]{2,1,0:T(8,128)(2,1)S(1)}, bf16[2,32,1536]{2,1,0:T(8,128)(2,1)S(1)}, u32[]{:S(2)}, u32[]{:S(2)}) %collective-permute-start.28) | collective-permute-done | bytes 196640 | tf_op jit(solution)/shard_map/ppermute | solution.py:432
  790.9 37.1 %attend_grad.3 = (bf16[1024,1536]{1,0:T(8,128)(2,1)}, f32[8,1536]{1,0:T(8,128)}) custom-call(bf16[1024,1536]{1,0:T(8,128)(2,1)} %get-tuple-element.51.low_ref, bf16[1024,512]{1,0:T(8,128)(2,1)} %convolution_convert_fusion.8.dout_ref, f32[4,8,1024]{2,1,0:T(8,128)} %get-tuple-element.52.lse_ref, f32[1024,128]{1,0:T(8,128)} %pad_maximum_fusion.cos_ref, ...), custom_call_target="tpu_custom_call" | custom-call | flops 21474836480 | bytes 9437184 | tf_op jit(solution)/shard_map/attend_grad/pallas_call | solution.py:586
  827.9 9.1 fusion.176
  886.6 9.2 collective-permute-done.47
  931.9 14.8 %collective-permute-done.44 = bf16[2,32,2048]{2,1,0:T(8,128)(2,1)S(1)} collective-permute-done((bf16[2,32,2048]{2,1,0:T(8,128)(2,1)S(1)}, bf16[2,32,2048]{2,1,0:T(8,128)(2,1)S(1)}, u32[]{:S(2)}, u32[]{:S(2)}) %collective-permute-start.44) | collective-permute-done | bytes 262176 | tf_op jit(solution)/shard_map/ppermute | solution.py:427
  963.1 19.6 %collective-permute-done.18 = bf16[2,2,2,32,1536]{4,3,0,1,2:T(8,128)(2,1)} collective-permute-done((bf16[2,2,2,32,1536]{4,3,0,1,2:T(8,128)(2,1)}, bf16[2,2,2,32,1536]{4,3,0,1,2:T(8,128)(2,1)}, u32[]{:S(2)}, u32[]{:S(2)}) %collective-permute-start.18) | collective-permute-done | bytes 786464 | tf_op jit(solution)/shard_map/ppermute | solution.py:427
  987.9 18.9 %collective-permute-done.19 = bf16[2,2,2,32,1536]{4,3,0,1,2:T(8,128)(2,1)} collective-permute-done((bf16[2,2,2,32,1536]{4,3,0,1,2:T(8,128)(2,1)}, bf16[2,2,2,32,1536]{4,3,0,1,2:T(8,128)(2,1)}, u32[]{:S(2)}, u32[]{:S(2)}) %collective-permute-start.19) | collective-permute-done | bytes 786464 | tf_op jit(solution)/shard_map/ppermute | solution.py:427
  1013.8 15.5 %collective-permute-done.20 = bf16[2,2,2,32,1536]{4,3,0,1,2:T(8,128)(2,1)S(1)} collective-permute-done((bf16[2,2,2,32,1536]{4,3,0,1,2:T(8,128)(2,1)}, bf16[2,2,2,32,1536]{4,3,0,1,2:T(8,128)(2,1)S(1)}, u32[]{:S(2)}, u32[]{:S(2)}) %collective-permute-start.20) | collective-permute-done | bytes 786464 | tf_op jit(solution)/shard_map/ppermute | solution.py:427
  1034.8 17.1 %all_gather.17 = bf16[2,128,1024]{2,1,0:T(8,128)(2,1)S(1)} all-gather(bf16[2,32,1024]{2,1,0:T(8,128)(2,1)S(1)} %copy-done.40), channel_id=1, replica_groups=mesh['seq'=4,'fsdp'=8] {'seq'}, dimensions={1}, use_global_device_ids=true | all-gather | bytes 655360 | tf_op jit(solution)/shard_map/all_gather | solution.py:1152
  1064.1 41.4 %all-reduce.3.cloned.1.call-done = f32[2,13312]{1,0:T(2,128)} async-done(((f32[2,13312]{1,0:T(2,128)}), f32[2,13312]{1,0:T(2,128)}) %all-reduce.3.cloned.1.call-update) | async-done | bytes 106512 | tf_op jit(solution)/shard_map/psum | solution.py:1143
  1116.0 40.9 %psum.15 = f32[]{:T(128)} all-reduce(f32[]{:T(128)S(6)} %add.741), channel_id=1, replica_groups=mesh['seq'=4,'fsdp'=8] {'seq','fsdp'}, use_global_device_ids=true, to_apply=%region_35.36 | all-reduce | flops 1 | bytes 8 | tf_op jit(solution)/shard_map/psum | solution.py:1144
  1158.5 12.1 %fusion.145 = (bf16[2,512,1024]{2,1,0:T(8,128)(2,1)}, f32[2,512,1024]{2,1,0:T(8,128)}, f32[2,512,1024]{2,1,0:T(8,128)}, f32[2,512,1024]{2,1,0:T(8,128)}, f32[2,512,1024]{2,1,0:T(8,128)}) fusion(f32[2,512,1024]{2,1,0:T(8,128)} %param.25, f32[]{:T(128)S(6)} %mul.554, bf16[2,512,1024]{2,1,0:T(8,128)(2,1)} %all-gather.8.cloned.1.call-done, ...), kind=kLoop, calls=%fused_computation.417 | loop fusion | flops 16777216 | bytes 33554436 | tf_op jit(solution)/shard_map/convert_element_type | solution.py:1166
  1174.7 11.7 fusion.148
  1189.4 8.4 fusion.154
  (556 shorter events, 404.2 us)
Async XLA Ops:
  8.0 1097.5 %all-reduce.3.cloned.1.call-start = ((), (), s32[]{:S(2)}) async-start(), calls=%async_computation | async-start | bytes 212992 | tf_op jit(solution)/shard_map/psum | solution.py:1143
  47.4 239.7 %collective-permute-start.2 = (f32[2,264,1024]{2,1,0:T(8,128)}, f32[2,264,1024]{2,1,0:T(8,128)}, u32[]{:S(2)}, u32[]{:S(2)}) collective-permute-start(f32[2,264,1024]{2,1,0:T(8,128)} %maximum_select_fusion.3), channel_id=1, source_target_pairs={{0,1},{1,0},{2,3},{3,2},{4,5},{5,4},{6,7},{7,6},{8,9},{9,8},{10,11... | collective-permute-start | bytes 6488072 | tf_op jit(solution)/shard_map/ppermute | solution.py:422
  362.0 30.9 %collective-permute-start.4 = (bf16[1024,1024]{1,0:T(8,128)(2,1)}, bf16[1024,1024]{1,0:T(8,128)(2,1)}, u32[]{:S(2)}, u32[]{:S(2)}) collective-permute-start(bf16[1024,1024]{1,0:T(8,128)(2,1)} %get-tuple-element.195), channel_id=1, source_target_pairs={{0,1},{1,0},{2,3},{3,2},{4,5},{5,4},{6,7},{7,6},{8,9},{9,8},{10,11... | collective-permute-start | bytes 6291464 | tf_op jit(solution)/shard_map/ppermute | solution.py:422
  365.5 25.5 %collective-permute-start.10 = (f32[256,1024]{1,0:T(8,128)S(1)}, f32[256,1024]{1,0:T(8,128)S(1)}, u32[]{:S(2)}, u32[]{:S(2)}) collective-permute-start(f32[256,1024]{1,0:T(8,128)S(1)} %get-tuple-element.148), channel_id=1, source_target_pairs={{0,8},{1,24},{2,10},{3,26},{4,12},{5,28},{6,14},{7,30},{8,0},{9,16... | collective-permute-start | bytes 3145736 | tf_op jit(solution)/shard_map/ppermute | solution.py:980
  392.5 45.8 %collective-permute-start.11 = (f32[2,256,1024]{2,1,0:T(8,128)}, f32[2,256,1024]{2,1,0:T(8,128)}, u32[]{:S(2)}, u32[]{:S(2)}) collective-permute-start(f32[2,256,1024]{2,1,0:T(8,128)} %maximum_select_fusion.6), channel_id=1, source_target_pairs={{0,1},{1,0},{2,3},{3,2},{4,5},{5,4},{6,7},{7,6},{8,9},{9,8},{10,11... | collective-permute-start | bytes 6291464 | tf_op jit(solution)/shard_map/ppermute | solution.py:422
  527.9 51.9 %collective-permute-start.35 = (bf16[1,2,2,32,1024]{4,3,2,1,0:T(8,128)(2,1)S(1)}, bf16[1,2,2,32,1024]{4,3,2,1,0:T(8,128)(2,1)S(1)}, u32[]{:S(2)}, u32[]{:S(2)}) collective-permute-start(bf16[1,2,2,32,1024]{4,3,2,1,0:T(8,128)(2,1)S(1)} %dynamic-slice_bitcast_fusion.10), channel_id=1, source_target_pairs={{0,2},{1,3},{2,4},{3,5},{4,6},{5,7},{6,0},{7,1},{8,10},{9,11},{10,... | collective-permute-start | bytes 786440 | tf_op jit(solution)/shard_map/ppermute | solution.py:427
  581.6 33.7 %collective-permute-start.24 = (bf16[2,2,2,32,1536]{4,3,0,1,2:T(8,128)(2,1)}, bf16[2,2,2,32,1536]{4,3,0,1,2:T(8,128)(2,1)}, u32[]{:S(2)}, u32[]{:S(2)}) collective-permute-start(bf16[2,2,2,32,1536]{4,3,0,1,2:T(8,128)(2,1)} %bitcast.438), channel_id=1, source_target_pairs={{0,2},{1,3},{2,4},{3,5},{4,6},{5,7},{6,0},{7,1},{8,10},{9,11},{10,... | collective-permute-start | bytes 2359304 | tf_op jit(solution)/shard_map/ppermute | solution.py:427
  594.4 35.8 %collective-permute-start.7 = (f32[256,1024]{1,0:T(8,128)S(1)}, f32[256,1024]{1,0:T(8,128)S(1)}, u32[]{:S(2)}, u32[]{:S(2)}) collective-permute-start(f32[256,1024]{1,0:T(8,128)S(1)} %get-tuple-element.133), channel_id=1, source_target_pairs={{0,0},{16,1},{2,2},{18,3},{4,4},{20,5},{6,6},{22,7},{8,8},{24,9},{... | collective-permute-start | bytes 3145736 | tf_op jit(solution)/shard_map/ppermute | solution.py:999
  595.1 35.1 %collective-permute-start.8 = (f32[256,1024]{1,0:T(8,128)S(1)}, f32[256,1024]{1,0:T(8,128)S(1)}, u32[]{:S(2)}, u32[]{:S(2)}) collective-permute-start(f32[256,1024]{1,0:T(8,128)S(1)} %get-tuple-element.134), channel_id=1, source_target_pairs={{8,0},{24,1},{10,2},{26,3},{12,4},{28,5},{14,6},{30,7},{0,8},{16,9... | collective-permute-start | bytes 3145736 | tf_op jit(solution)/shard_map/ppermute | solution.py:999
  595.7 41.3 %collective-permute-start.13 = (bf16[1024,1024]{1,0:T(8,128)(2,1)S(1)}, bf16[1024,1024]{1,0:T(8,128)(2,1)S(1)}, u32[]{:S(2)}, u32[]{:S(2)}) collective-permute-start(bf16[1024,1024]{1,0:T(8,128)(2,1)S(1)} %copy-done.74), channel_id=1, source_target_pairs={{0,1},{1,0},{2,3},{3,2},{4,5},{5,4},{6,7},{7,6},{8,9},{9,8},{10,11... | collective-permute-start | bytes 6291464 | tf_op jit(solution)/shard_map/ppermute | solution.py:422
  636.9 54.4 %collective-permute-start.26 = (bf16[2,2,2,32,1536]{4,3,0,1,2:T(8,128)(2,1)S(1)}, bf16[2,2,2,32,1536]{4,3,0,1,2:T(8,128)(2,1)S(1)}, u32[]{:S(2)}, u32[]{:S(2)}) collective-permute-start(bf16[2,2,2,32,1536]{4,3,0,1,2:T(8,128)(2,1)S(1)} %fusion.68), channel_id=1, source_target_pairs={{0,2},{1,3},{2,4},{3,5},{4,6},{5,7},{6,0},{7,1},{8,10},{9,11},{10,... | collective-permute-start | bytes 2359304 | tf_op jit(solution)/shard_map/ppermute | solution.py:427
  666.7 97.9 %collective-permute-start.52 = (bf16[4,1,2,128,1024]{4,3,0,2,1:T(8,128)(2,1)}, bf16[4,1,2,128,1024]{4,3,0,2,1:T(8,128)(2,1)}, u32[]{:S(2)}, u32[]{:S(2)}) collective-permute-start(bf16[4,1,2,128,1024]{4,3,0,2,1:T(8,128)(2,1)} %bitcast.435), channel_id=1, source_target_pairs={{0,16},{8,24},{16,0},{24,8},{1,17},{9,25},{17,1},{25,9},{2,18},{10... | collective-permute-start | bytes 6291464 | tf_op jit(solution)/shard_map/ppermute | solution.py:432
  667.1 116.9 %collective-permute-start.57 = (bf16[4,1,2,128,1024]{4,3,0,2,1:T(8,128)(2,1)}, bf16[4,1,2,128,1024]{4,3,0,2,1:T(8,128)(2,1)}, u32[]{:S(2)}, u32[]{:S(2)}) collective-permute-start(bf16[4,1,2,128,1024]{4,3,0,2,1:T(8,128)(2,1)} %bitcast.434), channel_id=1, source_target_pairs={{0,16},{8,24},{16,0},{24,8},{1,17},{9,25},{17,1},{25,9},{2,18},{10... | collective-permute-start | bytes 6291464 | tf_op jit(solution)/shard_map/ppermute | solution.py:432
  691.3 78.3 %collective-permute-start.14 = (bf16[1024,1024]{1,0:T(8,128)(2,1)}, bf16[1024,1024]{1,0:T(8,128)(2,1)}, u32[]{:S(2)}, u32[]{:S(2)}) collective-permute-start(bf16[1024,1024]{1,0:T(8,128)(2,1)} %get-tuple-element.207), channel_id=1, source_target_pairs={{0,1},{1,0},{2,3},{3,2},{4,5},{5,4},{6,7},{7,6},{8,9},{9,8},{10,11... | collective-permute-start | bytes 6291464 | tf_op jit(solution)/shard_map/ppermute | solution.py:422
  697.7 139.4 %collective-permute-start.40 = (bf16[4,2,2,32,2048]{4,3,1,0,2:T(8,128)(2,1)}, bf16[4,2,2,32,2048]{4,3,1,0,2:T(8,128)(2,1)}, u32[]{:S(2)}, u32[]{:S(2)}) collective-permute-start(bf16[4,2,2,32,2048]{4,3,1,0,2:T(8,128)(2,1)} %bitcast.437), channel_id=1, source_target_pairs={{0,8},{8,0},{16,24},{24,16},{1,9},{9,1},{17,25},{25,17},{2,10},{10... | collective-permute-start | bytes 6291464 | tf_op jit(solution)/shard_map/ppermute | solution.py:432
  703.7 57.5 %collective-permute-start.28 = (bf16[2,32,1536]{2,1,0:T(8,128)(2,1)S(1)}, bf16[2,32,1536]{2,1,0:T(8,128)(2,1)S(1)}, u32[]{:S(2)}, u32[]{:S(2)}) collective-permute-start(bf16[2,32,1536]{2,1,0:T(8,128)(2,1)S(1)} %dynamic-slice_bitcast_fusion.12), channel_id=1, source_target_pairs={{0,16},{8,24},{16,0},{24,8},{1,17},{9,25},{17,1},{25,9},{2,18},{10... | collective-permute-start | bytes 589832 | tf_op jit(solution)/shard_map/ppermute | solution.py:432
  762.7 89.7 %collective-permute-start.46 = (bf16[4,2,2,32,2048]{4,3,1,0,2:T(8,128)(2,1)}, bf16[4,2,2,32,2048]{4,3,1,0,2:T(8,128)(2,1)}, u32[]{:S(2)}, u32[]{:S(2)}) collective-permute-start(bf16[4,2,2,32,2048]{4,3,1,0,2:T(8,128)(2,1)} %bitcast.461), channel_id=1, source_target_pairs={{0,8},{8,0},{16,24},{24,16},{1,9},{9,1},{17,25},{25,17},{2,10},{10... | collective-permute-start | bytes 6291464 | tf_op jit(solution)/shard_map/ppermute | solution.py:432
  768.1 108.4 %collective-permute-start.53 = (bf16[4,1,128,1024]{3,2,1,0:T(8,128)(2,1)S(1)}, bf16[4,1,128,1024]{3,2,1,0:T(8,128)(2,1)}, u32[]{:S(2)}, u32[]{:S(2)}) collective-permute-start(bf16[4,1,128,1024]{3,2,1,0:T(8,128)(2,1)S(1)} %dynamic-slice_bitcast_fusion.1), channel_id=1, source_target_pairs={{0,8},{8,0},{16,24},{24,16},{1,9},{9,1},{17,25},{25,17},{2,10},{10... | collective-permute-start | bytes 3145736 | tf_op jit(solution)/shard_map/ppermute | solution.py:432
  789.3 92.7 %collective-permute-start.58 = (bf16[4,1,128,1024]{3,2,1,0:T(8,128)(2,1)}, bf16[4,1,128,1024]{3,2,1,0:T(8,128)(2,1)}, u32[]{:S(2)}, u32[]{:S(2)}) collective-permute-start(bf16[4,1,128,1024]{3,2,1,0:T(8,128)(2,1)} %dynamic-slice_bitcast_fusion), channel_id=1, source_target_pairs={{0,8},{8,0},{16,24},{24,16},{1,9},{9,1},{17,25},{25,17},{2,10},{10... | collective-permute-start | bytes 3145736 | tf_op jit(solution)/shard_map/ppermute | solution.py:432
  790.8 50.0 %collective-permute-start.30 = (bf16[1,2,2,32,1024]{4,3,2,1,0:T(8,128)(2,1)S(1)}, bf16[1,2,2,32,1024]{4,3,2,1,0:T(8,128)(2,1)S(1)}, u32[]{:S(2)}, u32[]{:S(2)}) collective-permute-start(bf16[1,2,2,32,1024]{4,3,2,1,0:T(8,128)(2,1)S(1)} %dynamic-slice_bitcast_fusion.11), channel_id=1, source_target_pairs={{0,2},{1,3},{2,4},{3,5},{4,6},{5,7},{6,0},{7,1},{8,10},{9,11},{10,... | collective-permute-start | bytes 786440 | tf_op jit(solution)/shard_map/ppermute | solution.py:427
  844.9 39.7 %collective-permute-start.41 = (bf16[4,2,32,2048]{3,2,1,0:T(8,128)(2,1)}, bf16[4,2,32,2048]{3,2,1,0:T(8,128)(2,1)}, u32[]{:S(2)}, u32[]{:S(2)}) collective-permute-start(bf16[4,2,32,2048]{3,2,1,0:T(8,128)(2,1)} %dynamic-slice_bitcast_fusion.3), channel_id=1, source_target_pairs={{0,16},{8,24},{16,0},{24,8},{1,17},{9,25},{17,1},{25,9},{2,18},{10... | collective-permute-start | bytes 3145736 | tf_op jit(solution)/shard_map/ppermute | solution.py:432
  876.5 71.2 %collective-permute-start.15 = (bf16[1024,1024]{1,0:T(8,128)(2,1)}, bf16[1024,1024]{1,0:T(8,128)(2,1)S(1)}, u32[]{:S(2)}, u32[]{:S(2)}) collective-permute-start(bf16[1024,1024]{1,0:T(8,128)(2,1)} %get-tuple-element.209), channel_id=1, source_target_pairs={{0,1},{1,0},{2,3},{3,2},{4,5},{5,4},{6,7},{7,6},{8,9},{9,8},{10,11... | collective-permute-start | bytes 6291464 | tf_op jit(solution)/shard_map/ppermute | solution.py:422
  913.1 34.4 %collective-permute-start.56 = (bf16[1,128,1024]{2,1,0:T(8,128)(2,1)S(1)}, bf16[1,128,1024]{2,1,0:T(8,128)(2,1)S(1)}, u32[]{:S(2)}, u32[]{:S(2)}) collective-permute-start(bf16[1,128,1024]{2,1,0:T(8,128)(2,1)S(1)} %fusion.102), channel_id=1, source_target_pairs={{0,2},{1,3},{2,4},{3,5},{4,6},{5,7},{6,0},{7,1},{8,10},{9,11},{10,... | collective-permute-start | bytes 786440 | tf_op jit(solution)/shard_map/ppermute | solution.py:427
  918.7 28.9 %collective-permute-start.61 = (bf16[1,128,1024]{2,1,0:T(8,128)(2,1)S(1)}, bf16[1,128,1024]{2,1,0:T(8,128)(2,1)S(1)}, u32[]{:S(2)}, u32[]{:S(2)}) collective-permute-start(bf16[1,128,1024]{2,1,0:T(8,128)(2,1)S(1)} %fusion.99), channel_id=1, source_target_pairs={{0,2},{1,3},{2,4},{3,5},{4,6},{5,7},{6,0},{7,1},{8,10},{9,11},{10,... | collective-permute-start | bytes 786440 | tf_op jit(solution)/shard_map/ppermute | solution.py:427
  929.9 56.2 %collective-permute-start.50 = (bf16[2,32,2048]{2,1,0:T(8,128)(2,1)S(1)}, bf16[2,32,2048]{2,1,0:T(8,128)(2,1)}, u32[]{:S(2)}, u32[]{:S(2)}) collective-permute-start(bf16[2,32,2048]{2,1,0:T(8,128)(2,1)S(1)} %fusion.105), channel_id=1, source_target_pairs={{0,2},{1,3},{2,4},{3,5},{4,6},{5,7},{6,0},{7,1},{8,10},{9,11},{10,... | collective-permute-start | bytes 786440 | tf_op jit(solution)/shard_map/ppermute | solution.py:427
  947.5 63.9 %collective-permute-start.45 = (bf16[32,2048]{1,0:T(8,128)(2,1)}, bf16[32,2048]{1,0:T(8,128)(2,1)}, u32[]{:S(2)}, u32[]{:S(2)}) collective-permute-start(bf16[32,2048]{1,0:T(8,128)(2,1)} %get-tuple-element.156), channel_id=1, source_target_pairs={{0,1},{1,0},{2,3},{3,2},{4,5},{5,4},{6,7},{7,6},{8,9},{9,8},{10,11... | collective-permute-start | bytes 393224 | tf_op jit(solution)/shard_map/ppermute | solution.py:422
  963.1 195.4 %all-gather.8.cloned.1.call-start = ((), (), s32[]{:S(2)}) async-start(), calls=%async_computation.3 | async-start | bytes 2621440 | tf_op jit(solution)/shard_map/all_gather | solution.py:1152
  986.1 188.6 %all-gather.6.cloned.1.call-start = ((), (), s32[]{:S(2)}) async-start(), calls=%async_computation.2 | async-start | bytes 2621440 | tf_op jit(solution)/shard_map/all_gather | solution.py:1152
  1034.8 154.6 %all-gather.4.cloned.1.call-start = ((), (), s32[]{:S(2)}) async-start(), calls=%async_computation.1 | async-start | bytes 1966080 | tf_op jit(solution)/shard_map/all_gather | solution.py:1152
  1060.2 52.6 %collective-permute-start.16 = (f32[256,1024]{1,0:T(8,128)}, f32[256,1024]{1,0:T(8,128)S(1)}, u32[]{:S(2)}, u32[]{:S(2)}) collective-permute-start(f32[256,1024]{1,0:T(8,128)} %get-tuple-element.130), channel_id=1, source_target_pairs={{0,0},{16,1},{2,2},{18,3},{4,4},{20,5},{6,6},{22,7},{8,8},{24,9},{... | collective-permute-start | bytes 3145736 | tf_op jit(solution)/shard_map/ppermute | solution.py:999
  1062.1 50.7 %collective-permute-start.17 = (f32[256,1024]{1,0:T(8,128)S(1)}, f32[256,1024]{1,0:T(8,128)}, u32[]{:S(2)}, u32[]{:S(2)}) collective-permute-start(f32[256,1024]{1,0:T(8,128)S(1)} %get-tuple-element.131), channel_id=1, source_target_pairs={{8,0},{24,1},{10,2},{26,3},{12,4},{28,5},{14,6},{30,7},{0,8},{16,9... | collective-permute-start | bytes 3145736 | tf_op jit(solution)/shard_map/ppermute | solution.py:999
  1062.7 45.1 %collective-permute-start.23 = (bf16[32,1536]{1,0:T(8,128)(2,1)S(1)}, bf16[32,1536]{1,0:T(8,128)(2,1)S(1)}, u32[]{:S(2)}, u32[]{:S(2)}) collective-permute-start(bf16[32,1536]{1,0:T(8,128)(2,1)S(1)} %get-tuple-element.160), channel_id=1, source_target_pairs={{0,1},{1,0},{2,3},{3,2},{4,5},{5,4},{6,7},{7,6},{8,9},{9,8},{10,11... | collective-permute-start | bytes 294920 | tf_op jit(solution)/shard_map/ppermute | solution.py:422
  (128 other events, 1908.6 us)
Sparse Core Ops, SparseCore 0:
  963.2 142.2 all-reduce.2
Sparse Core Ops, SparseCore 1:
  986.2 37.0 all-gather.7
  1034.8 43.0 all-gather.5
  1158.4 30.9 all-gather.3

commit v3 on v2

--- a/solution.py
+++ b/solution.py
@@ -613,39 +613,74 @@
     )(low_all, mixed_grad, lse, cos_wide, sin_wide)
 
 
+class Places:
+    def __init__(self):
+        shard, seq = lax.axis_index("fsdp"), lax.axis_index("seq")
+        parts = lax.axis_size("fsdp")
+        self.ring = parts // 2
+        self.seq = seq
+        self.chip, self.core = shard // 2, lax.rem(shard, 2)
+        self.at_x, self.at_y = lax.rem(seq, 2), seq // 2
+        self.near_x = 2 * self.at_y + 1 - self.at_x
+        self.near_y = 2 * (1 - self.at_y) + self.at_x
+        self.other = {"fsdp": shard + 1 - 2 * self.core}
+        self.up = {"fsdp": lax.rem(shard + 2, parts)}
+        self.down = {"fsdp": lax.rem(shard + parts - 2, parts)}
+        self.over_x = {"seq": self.near_x}
+        self.over_y = {"seq": self.near_y}
+
+    def back(self, hops):
+        return lax.rem(self.chip - hops + self.ring, self.ring)
+
+
+def remote(src, dst, send, recv, target):
+    return pltpu.make_async_remote_copy(
+        src_ref=src,
+        dst_ref=dst,
+        send_sem=send,
+        recv_sem=recv,
+        device_id=target,
+        device_id_type=pl.DeviceIdType.MESH,
+    )
+
+
+def greet(targets, waits):
+    barrier = pltpu.get_barrier_semaphore()
+    for target in targets:
+        pl.semaphore_signal(barrier, inc=1, device_id=target, device_id_type=pl.DeviceIdType.MESH)
+    pl.semaphore_wait(barrier, waits)
+
+
+def aligned(start, size, unit=None):
+    return pl.ds(pl.multiple_of(start, unit or size), size)
+
+
 def gather_kernel(
-    qkv_mine, qkv_away, up_mine, up_away, down_in, proj_in,
-    qkv_out, up_out, down_out, proj_out,
-    qkv_slab, up_slab, down_slab, proj_slab,
+    qkv_in, up_in, down_in, proj_in, clip_in, coord_in, vec_in,
+    qkv_out, up_out, down_out, proj_out, clip_out, coord_out, vec_out,
+    qkv_full, up_full, down_full, proj_full,
+    qkv_away, up_away,
+    qkv_slab, up_slab, down_slab, proj_slab, clip_slab,
     z_send, z_recv, p_send, p_recv, d_send, d_recv, c_send, c_recv, l_in, l_out,
+    m_send, m_recv, m_load,
 ):
-    shard, seq = lax.axis_index("fsdp"), lax.axis_index("seq")
-    parts = lax.axis_size("fsdp")
-    ring = parts // 2
-    chip, core = shard // 2, lax.rem(shard, 2)
-    other = {"fsdp": shard + 1 - 2 * core}
-    up_chip = {"fsdp": lax.rem(shard + 2, parts)}
-    down_chip = {"fsdp": lax.rem(shard + parts - 2, parts)}
-    at_x, at_y = lax.rem(seq, 2), seq // 2
-    over_x = {"seq": 2 * at_y + 1 - at_x}
-    over_y = {"seq": 2 * (1 - at_y) + at_x}
-    near_x, near_y = 2 * at_y + 1 - at_x, 2 * (1 - at_y) + at_x
-    layers = qkv_mine.shape[0]
-
-    barrier = pltpu.get_barrier_semaphore()
-    for target in (other, up_chip, down_chip, over_x, over_y):
-        pl.semaphore_signal(barrier, inc=1, device_id=target, device_id_type=pl.DeviceIdType.MESH)
-    pl.semaphore_wait(barrier, 5)
-
-    def remote(src, dst, send, recv, target):
-        return pltpu.make_async_remote_copy(
-            src_ref=src,
-            dst_ref=dst,
-            send_sem=send,
-            recv_sem=recv,
-            device_id=target,
-            device_id_type=pl.DeviceIdType.MESH,
-        )
+    at = Places()
+    ring, seq, chip, core = at.ring, at.seq, at.chip, at.core
+    other, up_chip = at.other, at.up
+    over_x, over_y, near_x, near_y = at.over_x, at.over_y, at.near_x, at.near_y
+    layers = qkv_in.shape[0]
+    loads = {}
+
+    def start_load(name, layer, slot):
+        source, full = {
+            "qkv": (qkv_in, qkv_full),
+            "up": (up_in, up_full),
+            "down": (down_in, down_full),
+            "proj": (proj_in, proj_full),
+        }[name]
+        copy = pltpu.make_async_copy(source.at[layer], full.at[layer], l_in.at[slot])
+        copy.start()
+        loads[name, layer] = copy
 
     outs = {"qkv": qkv_out, "up": up_out, "down": down_out, "proj": proj_out}
     slabs = {"qkv": qkv_slab, "up": up_slab, "down": down_slab, "proj": proj_slab}
@@ -663,26 +698,135 @@
             return outs[name].at[layer, 0, rows, :]
         return outs[name].at[layer, rows, :]
 
-    local_in, swaps = [], []
     for idx, (name, layer) in enumerate(items):
+        start_load(name, layer, idx)
+    clip_load = pltpu.make_async_copy(clip_in.at[lax.rem(seq, 2)], clip_slab, m_load.at[0])
+    clip_load.start()
+    barrier = pltpu.get_barrier_semaphore()
+    for target in (other, up_chip, at.down):
+        pl.semaphore_signal(barrier, inc=1, device_id=target, device_id_type=pl.DeviceIdType.MESH)
+    for step in range(1, 4):
+        for half in range(2):
+            pl.semaphore_signal(
+                barrier,
+                inc=1,
+                device_id={"fsdp": 2 * chip + half, "seq": seq ^ step},
+                device_id_type=pl.DeviceIdType.MESH,
+            )
+    pl.semaphore_wait(barrier, 9)
+
+    length = clip_in.shape[1]
+    token_core = seq // 2
+    token_rows = aligned(seq * length, length)
+    stays = core == token_core
+    clip_copies = []
+    for turn in range(2):
+        target = {"seq": 2 * core + turn, "fsdp": 2 * chip + token_core}
+        slot = 2 * lax.rem(seq, 2)
+        copies = [
+            remote(
+                clip_in.at[turn], clip_out.at[token_rows, :], m_send.at[2 * turn], m_recv.at[slot], target
+            ),
+            remote(
+                coord_in.at[turn], coord_out.at[seq], m_send.at[2 * turn + 1], m_recv.at[slot + 1], target
+            ),
+        ]
+        away = jnp.logical_not(jnp.logical_and(stays, lax.rem(seq, 2) == turn))
+        clip_copies.append((away, copies))
+
+        @pl.when(away)
+        def _(copies=copies):
+            for copy in copies:
+                copy.start()
+
+    clip_load.wait()
+    clip_store = pltpu.make_async_copy(clip_slab, clip_out.at[token_rows, :], m_load.at[1])
+
+    @pl.when(stays)
+    def _():
+        clip_store.start()
+        coord_out[seq] = coord_in[lax.rem(seq, 2)]
+
+    vec_out[2 * chip + core] = vec_in[...]
+    vec_swap = remote(
+        vec_in, vec_out.at[2 * chip + core], m_send.at[8], m_recv.at[8], other
+    )
+    vec_swap.start()
+
+    def clip_arrived():
+        for part in range(2):
+            came = jnp.logical_not(jnp.logical_and(stays, lax.rem(seq, 2) == part))
+
+            @pl.when(came)
+            def _(part=part):
+                rows = aligned((2 * core + part) * length, length)
+                remote(
+                    clip_in.at[0], clip_out.at[rows, :], m_send.at[0], m_recv.at[2 * part], other
+                ).wait_recv()
+                remote(
+                    coord_in.at[0],
+                    coord_out.at[2 * core + part],
+                    m_send.at[0],
+                    m_recv.at[2 * part + 1],
+                    other,
+                ).wait_recv()
+
+        @pl.when(stays)
+        def _():
+            clip_store.wait()
+
+        rows = clip_out.at[aligned(core * 2 * length, 2 * length), :]
+        swaps = [remote(rows, rows, m_send.at[4], m_recv.at[4], other)]
+        ref = coord_out.at[pl.ds(2 * core, 2)]
+        swaps.append(remote(ref, ref, m_send.at[5], m_recv.at[5], other))
+        for copy in swaps:
+            copy.start()
+        return swaps
+
+    vec_copies = []
+
+    def vec_hop(hop):
+        (vec_copies[-1] if vec_copies else vec_swap).wait_recv()
+        ref = vec_out.at[pl.ds(2 * at.back(hop), 2)]
+        copy = remote(ref, ref, m_send.at[9 + hop], m_recv.at[9 + hop], up_chip)
+        copy.start()
+        vec_copies.append(copy)
+
+    swaps, prepared = {}, []
+
+    def prepare():
+        if len(prepared) == len(items):
+            return
+        idx = len(prepared)
+        name, layer = items[idx]
+        prepared.append(name)
         slab = slabs[name]
-        if name in ("qkv", "up"):
-            mine, away = (qkv_mine, qkv_away) if name == "qkv" else (up_mine, up_away)
-            half = mine.shape[1]
-            rows = pl.ds(pl.multiple_of(core * half, half), half)
-            swap = remote(
-                away.at[layer], slab.at[layer, rows, :], c_send.at[idx], c_recv.at[idx], other
-            )
-            local = pltpu.make_async_copy(mine.at[layer], slab.at[layer, rows, :], l_in.at[idx])
-        else:
-            swap = None
-            source = down_in if name == "down" else proj_in
-            local = pltpu.make_async_copy(source.at[layer], slab.at[layer], l_in.at[idx])
-        swaps.append(swap)
-        local_in.append(local)
-        if swap is not None:
-            swap.start()
-        local.start()
+        loads[name, layer].wait()
+        swaps[idx] = None
+        if name in ("down", "proj"):
+            full = down_full if name == "down" else proj_full
+            slab[layer] = full[layer].astype(BF)
+            return
+        full, away, kinds = (
+            (qkv_full, qkv_away, 3) if name == "qkv" else (up_full, up_away, 1)
+        )
+        half, columns = full.shape[1], full.shape[2]
+        width = columns // (kinds * 2 * ring)
+        rows = aligned(core * half, half)
+        for pair in range(ring):
+            for kind in range(kinds):
+                place = slice((pair * kinds + kind) * width, (pair * kinds + kind + 1) * width)
+                for ref, which in ((None, core), (away, 1 - core)):
+                    start = (kind * 2 * ring + 2 * pair + which) * width
+                    block = full[layer, :, aligned(start, width)].astype(BF)
+                    if ref is None:
+                        slab[layer, rows, place] = block
+                    else:
+                        ref[layer, :, place] = block
+        swaps[idx] = remote(
+            away.at[layer], slab.at[layer, rows, :], c_send.at[idx], c_recv.at[idx], other
+        )
+        swaps[idx].start()
 
     hops = ring - 1
     order = []
@@ -695,7 +839,6 @@
 
     def begin(idx):
         name, layer = items[idx]
-        local_in[idx].wait()
         if swaps[idx] is not None:
             swaps[idx].wait_recv()
         store = pltpu.make_async_copy(
@@ -755,11 +898,22 @@
 
     pending = []
     proj_swaps = []
+    clip_swaps = []
+    prepare()
+    prepare()
     begin(0)
     z_copy(0, 0)
     begin(1)
     z_copy(1, 0)
-    for idx, hop in order:
+    prepare()
+    prepare()
+    for event, (idx, hop) in enumerate(order):
+        if event == 2:
+            clip_swaps = clip_arrived()
+        if 3 <= event < 3 + hops:
+            vec_hop(event - 3)
+        if event % 2 == 1:
+            prepare()
         z_copies[idx, hop].wait_recv()
         if hop + 1 < hops:
             z_copy(idx, hop + 1)
@@ -796,42 +950,63 @@
             copy.wait_send()
     for copy in z_copies.values():
         copy.wait_send()
-    for copy in swaps:
+    for copy in swaps.values():
         if copy is not None:
             copy.wait_send()
-    for copy in proj_swaps:
+    for copy in proj_swaps + clip_swaps:
         copy.wait()
+    vec_copies[-1].wait_recv()
+    for copy in [vec_swap] + vec_copies:
+        copy.wait_send()
+    for away, copies in clip_copies:
+
+        @pl.when(away)
+        def _(copies=copies):
+            for copy in copies:
+                copy.wait_send()
+
     for idx, store in enumerate(stores):
         if items[idx][0] != "proj":
             store.wait()
 
 
-def gather_weights(qkv_mine, qkv_away, up_mine, up_away, down_low, proj_low):
-    layers = qkv_mine.shape[0]
-    ring = lax.axis_size("fsdp") // 2
+def gather_weights(qkv, up, down, proj, clips, coords, vectors):
+    layers, rows, width = proj.shape
+    parts = lax.axis_size("fsdp")
+    ring = parts // 2
     count = 4 * layers
     hops = ring - 1
     anywhere = pl.BlockSpec(memory_space=pl.ANY)
+    vmem = pl.BlockSpec(memory_space=pltpu.VMEM)
     dma = pltpu.SemaphoreType.DMA
-    qkv_rows, up_rows = 2 * qkv_mine.shape[1], 2 * up_mine.shape[1]
-    down_rows, proj_rows = down_low.shape[1], proj_low.shape[1]
-    width = down_low.shape[2]
+    down_rows = down.shape[1]
+    halves = qkv.shape[2] // 2, up.shape[2] // 2
     shapes = [
-        (layers, ring * qkv_rows, qkv_mine.shape[2]),
-        (layers, ring * up_rows, up_mine.shape[2]),
-        (layers, ring * down_rows, width),
-        (layers, 2, ring * proj_rows, width),
+        ((layers, parts * rows, halves[0]), BF),
+        ((layers, parts * rows, halves[1]), BF),
+        ((layers, ring * down_rows, width), BF),
+        ((layers, 2, ring * rows, width), BF),
+        ((4 * clips.shape[1], width), F32),
+        ((4,) + coords.shape[1:], jnp.int32),
+        ((parts,) + vectors.shape, F32),
     ]
     return pl.pallas_call(
         gather_kernel,
-        in_specs=[anywhere] * 6,
-        out_specs=[anywhere] * 4,
-        out_shape=[jax.ShapeDtypeStruct(shape, BF) for shape in shapes],
+        in_specs=[anywhere] * 5 + [vmem] * 2,
+        out_specs=[anywhere] * 5 + [vmem] * 2,
+        out_shape=[jax.ShapeDtypeStruct(*shape) for shape in shapes],
         scratch_shapes=[
-            pltpu.VMEM((layers, qkv_rows, qkv_mine.shape[2]), BF),
-            pltpu.VMEM((layers, up_rows, up_mine.shape[2]), BF),
+            pltpu.VMEM(qkv.shape, F32),
+            pltpu.VMEM(up.shape, F32),
+            pltpu.VMEM(down.shape, F32),
+            pltpu.VMEM(proj.shape, F32),
+            pltpu.VMEM((layers, rows, halves[0]), BF),
+            pltpu.VMEM((layers, rows, halves[1]), BF),
+            pltpu.VMEM((layers, 2 * rows, halves[0]), BF),
+            pltpu.VMEM((layers, 2 * rows, halves[1]), BF),
             pltpu.VMEM((layers, down_rows, width), BF),
-            pltpu.VMEM((layers, proj_rows, width), BF),
+            pltpu.VMEM((layers, rows, width), BF),
+            pltpu.VMEM(clips.shape[1:], F32),
             dma((count * hops,)),
             dma((count * hops,)),
             dma((2 * count * hops,)),
@@ -842,41 +1017,506 @@
             dma((count + layers,)),
             dma((count,)),
             dma((count,)),
+            dma((9 + hops,)),
+            dma((9 + hops,)),
+            dma((2,)),
         ],
         compiler_params=pltpu.CompilerParams(
             collective_id=0, has_side_effects=True, vmem_limit_bytes=VMEM_LIMIT
         ),
+        cost_estimate=pl.CostEstimate(flops=0, bytes_accessed=600_000_000, transcendentals=0),
+        name="gather_weights",
+    )(qkv, up, down, proj, clips, coords, vectors)
+
+
+ADD_ROWS = 32
+
+
+def add_into(target, term):
+    rows = target.shape[0]
+
+    @pl.loop(0, rows // ADD_ROWS)
+    def _(step):
+        at = aligned(step * ADD_ROWS, ADD_ROWS)
+        total = target[at, :].astype(F32) + term[at, :].astype(F32)
+        target[at, :] = total.astype(BF)
+
+
+class Sems:
+    def __init__(self, ref):
+        self.ref, self.used = ref, 0
+
+    def take(self):
+        self.used += 1
+        return self.ref.at[self.used - 1]
+
+
+class Sum:
+    def __init__(self, at, sems, grad, own, one, two, three, z_first, x_first, stage, layer):
+        self.at, self.sems = at, sems
+        self.grad, self.own, self.one, self.two, self.three = grad, own, one, two, three
+        self.z_first, self.x_first = z_first, x_first
+        self.stage, self.layer = stage, layer
+        self.rows = grad.shape[0] // (4 * at.ring)
+        self.sends, self.loads = [], {}
+        self.first, self.second, self.hop = {}, {}, {}
+
+    def make(self, src, dst, target):
+        copy = remote(src, dst, self.sems[0].take(), self.sems[1].take(), target)
+        copy.start()
+        self.sends.append(copy)
+        return copy
+
+    def load(self, src, dst):
+        copy = pltpu.make_async_copy(src, dst, self.sems[2].take())
+        copy.start()
+        return copy
+
+    def kept(self):
+        at = self.at
+        if self.x_first:
+            return [(at.at_x, 1), (2 + at.at_x, 1)]
+        return [(2 * at.at_y, 2)]
+
+    def given(self):
+        at = self.at
+        if self.x_first:
+            return [(1 - at.at_x, 1), (3 - at.at_x, 1)]
+        return [(2 * (1 - at.at_y), 2)]
+
+    def fetch_own(self, tile):
+        base = self.at.back(tile + 1) * 4 * self.rows
+        copies = []
+        if self.z_first:
+            copies.append(
+                self.load(self.grad.at[aligned(base, 4 * self.rows), :], self.own.at[tile])
+            )
+        else:
+            place = 0
+            for first, count in self.kept():
+                size = count * self.rows
+                copies.append(
+                    self.load(
+                        self.grad.at[aligned(base + first * self.rows, size, self.rows), :],
+                        self.own.at[tile, pl.ds(place, size), :],
+                    )
+                )
+                place += size
+        self.loads[tile] = copies
+
+    def own_ready(self, tile):
+        for copy in self.loads[tile]:
+            copy.wait()
+
+    def plane_one(self, tile, source, base):
+        target = self.at.over_x if self.x_first else self.at.over_y
+        place, made = 0, []
+        for first, count in self.given():
+            size = count * self.rows
+            made.append(
+                self.make(
+                    source.at[aligned(base + first * self.rows, size, self.rows), :],
+                    self.one.at[tile, pl.ds(place, size), :],
+                    target,
+                )
+            )
+            place += size
+        self.first[tile] = made
+
+    def plane_two(self, tile, kept_ref):
+        for copy in self.first[tile]:
+            copy.wait_recv()
+        place = 0
+        for ref in kept_ref:
+            size = ref.shape[0]
+            add_into(self.one.at[tile, pl.ds(place, size), :], ref)
+            place += size
+        at = self.at
+        target = at.over_y if self.x_first else at.over_x
+        keep = at.at_y if self.x_first else at.at_x
+        self.keep_ref = lambda: self.one.at[tile, aligned(keep * self.rows, self.rows), :]
+        self.second[tile] = self.make(
+            self.one.at[tile, aligned((1 - keep) * self.rows, self.rows), :],
+            self.two.at[tile],
+            target,
+        )
+
+    def plane_three(self, tile):
+        at = self.at
+        keep = at.at_y if self.x_first else at.at_x
+        self.second[tile].wait_recv()
+        add_into(self.two.at[tile], self.one.at[tile, aligned(keep * self.rows, self.rows), :])
+
+    def start(self, tile):
+        base = self.at.back(tile + 1) * 4 * self.rows
+        if self.z_first:
+            self.own_ready(tile)
+            self.hop[0] = self.make(self.own.at[0], self.three.at[0], self.at.up)
+        else:
+            self.plane_one(tile, self.grad, base)
+
+    def middle(self, tile):
+        self.own_ready(tile)
+        self.plane_two(tile, [self.own.at[tile]])
+
+    def finish(self, tile):
+        self.plane_three(tile)
+        if tile > 0:
+            self.hop[tile - 1].wait_recv()
+            add_into(self.two.at[tile], self.three.at[tile - 1])
+        if tile < self.at.ring - 1:
+            self.hop[tile] = self.make(self.two.at[tile], self.three.at[tile], self.at.up)
+
+    def ring_step(self, tile):
+        last = tile == self.at.ring - 1
+        self.hop[tile - 1].wait_recv()
+        self.own_ready(tile)
+        total = self.three.at[tile - 1]
+        add_into(total, self.own.at[tile])
+        if last:
+            self.plane_one(0, total, 0)
+        else:
+            self.hop[tile] = self.make(total, self.three.at[tile], self.at.up)
+
+    def slab_middle(self):
+        total = self.three.at[self.at.ring - 2]
+        refs = [
+            total.at[aligned(first * self.rows, count * self.rows, self.rows), :]
+            for first, count in self.kept()
+        ]
+        self.plane_two(0, refs)
+
+    def slab_finish(self):
+        self.plane_three(0)
+
+    def total(self):
+        return self.two.at[0 if self.z_first else self.at.ring - 1]
+
+    def place(self, quarter, turn=0, size=None):
+        size = size or self.rows
+        return self.stage.at[aligned(quarter * self.rows + turn * size, size), :]
+
+    def gather(self):
+        at = self.at
+        self.kept_store = self.load(self.total(), self.place(at.seq))
+        self.near = [
+            self.make(self.total(), self.place(at.seq), at.over_x),
+            self.make(self.total(), self.place(at.seq), at.over_y),
+        ]
+
+    def gather_far(self):
+        at = self.at
+        for copy in self.near:
+            copy.wait_recv()
+        half = self.rows // 2
+        self.far = []
+        for turn, (origin, target) in enumerate(((at.near_y, at.over_x), (at.near_x, at.over_y))):
+            ref = self.place(origin, turn, half)
+            self.far.append(self.make(ref, ref, target))
+
+    def gather_end(self, arrive):
+        at = self.at
+        self.kept_store.wait()
+        for copy in self.far:
+            copy.wait_recv()
+        self.swap = None
+        if arrive is not None:
+            half = 2 * self.rows
+            self.swap = self.make(
+                self.stage.at[aligned((1 - at.core) * half, half), :], arrive, at.other
+            )
+
+    def drain(self):
+        if self.swap is not None:
+            self.swap.wait_recv()
+        for copy in self.sends:
+            copy.wait_send()
+
+
+def reduce_kernel(
+    last,
+    qkv_grad, proj_grad, up_grad, down_grad, vec_in, square_in,
+    qkv_stage, qkv_arrive, proj_stage, up_stage, up_arrive, down_stage, vec_out, square_out,
+    qkv_own, qkv_one, qkv_two, qkv_three,
+    proj_own, proj_one, proj_two, proj_three,
+    up_own, up_one, up_two, up_three,
+    down_own, down_one, down_two, down_three,
+    vec_got, vec_hop, vec_sum, square_got, square_sum,
+    send_sem, recv_sem, load_sem,
+):
+    at = Places()
+    ring = at.ring
+    sems = (Sems(send_sem), Sems(recv_sem), Sems(load_sem))
+    greet((at.other, at.over_x, at.over_y, at.down), 4)
+    qkv = Sum(at, sems, qkv_grad, qkv_own, qkv_one, qkv_two, qkv_three, True, True, qkv_stage, 0)
+    proj = Sum(
+        at, sems, proj_grad, proj_own, proj_one, proj_two, proj_three, True, False, proj_stage, 0
+    )
+    up = Sum(at, sems, up_grad, up_own, up_one, up_two, up_three, False, True, up_stage, 0)
+    down = Sum(
+        at, sems, down_grad, down_own, down_one, down_two, down_three, False, False, down_stage, 0
+    )
+    wide, slabs = (up, down), (qkv, proj)
+
+    vec_copies = []
+
+    def vec_copy(src, dst, target):
+        copy = remote(src, dst, sems[0].take(), sems[1].take(), target)
+        copy.start()
+        vec_copies.append(copy)
+        return copy
+
+    partners = (at.other, at.over_x, at.over_y)
+    vec_sum[0] = vec_in[...]
+
+    for item in slabs:
+        item.fetch_own(0)
+    for item in wide:
+        item.start(0)
+    for item in slabs:
+        item.start(0)
+    for item in wide:
+        item.start(1)
+    for tile in range(ring):
+        for item in wide:
+            item.fetch_own(tile)
+        if tile > 0:
+            for item in slabs:
+                item.fetch_own(tile)
+    vec_state = {"copy": vec_copy(vec_sum.at[0], vec_got.at[0], partners[0])}
+
+    def vec_step(idx):
+        vec_state["copy"].wait_recv()
+        if idx <= 3:
+            vec_sum[idx] = vec_sum[idx - 1] + vec_got[idx - 1]
+            if idx < 3:
+                vec_state["copy"] = vec_copy(vec_sum.at[idx], vec_got.at[idx], partners[idx])
+            else:
+                vec_state["copy"] = vec_copy(
+                    vec_sum.at[3, at.back(1)], vec_hop.at[0], at.up
+                )
+        else:
+            hop = idx - 3
+            vec_hop[hop - 1] = vec_hop[hop - 1] + vec_sum[3, at.back(hop + 1)]
+            if hop < ring - 1:
+                vec_state["copy"] = vec_copy(vec_hop.at[hop - 1], vec_hop.at[hop], at.up)
+
+    for tile in range(ring):
+        for item in wide:
+            item.middle(tile)
+        if tile + 2 < ring:
+            for item in wide:
+                item.start(tile + 2)
+        if tile > 0:
+            for item in wide:
+                item.finish(tile - 1)
+        if tile + 1 < ring:
+            for item in slabs:
+                item.ring_step(tile + 1)
+        vec_step(tile + 1)
+    for item in slabs:
+        item.slab_middle()
+    vec_step(5)
+    for item in wide:
+        item.finish(ring - 1)
+        item.gather()
+    vec_step(6)
+    vec_total = vec_hop[ring - 2]
+    vec_out[...] = vec_total
+    for item in slabs:
+        item.slab_finish()
+        item.gather()
+
+    def squares(ref):
+        rows, columns = ref.shape
+        total = jnp.zeros((8, 128), F32)
+
+        def body(step, total):
+            part = ref[aligned(step * 16, 16), :].astype(F32)
+            part = part * part
+            part = part[0:8] + part[8:16]
+            for column in range(0, columns, 128):
+                total = total + part[:, column : column + 128]
+            return total
+
+        return lax.fori_loop(0, rows // 16, body, total)
+
+    total = square_in[...]
+    for item in (*wide, *slabs):
+        total = total + squares(item.total())
+    vec_square = vec_total * vec_total * 0.125
+    for column in range(0, vec_square.shape[1], 128):
+        total = total + vec_square[:, column : column + 128]
+    square_sum[0] = total
+    if last:
+        for idx, target in enumerate(partners):
+            copy = vec_copy(square_sum.at[idx], square_got.at[idx], target)
+            if idx == 0:
+                for item in wide:
+                    item.gather_far()
+            if idx == 1:
+                for item in slabs:
+                    item.gather_far()
+            copy.wait_recv()
+            square_sum[idx + 1] = square_sum[idx] + square_got[idx]
+        total = square_sum[3]
+        for hop in range(ring - 1):
+            source = square_sum.at[3] if hop == 0 else square_got.at[2 + hop]
+            copy = vec_copy(source, square_got.at[3 + hop], at.up)
+            if hop == 0:
+                for item in wide:
+                    item.gather_end(up_arrive if item is up else None)
+            copy.wait_recv()
+            total = total + square_got[3 + hop]
+        square_out[...] = total
+    else:
+        square_out[...] = total
+        for item in (*wide, *slabs):
+            item.gather_far()
+        for item in wide:
+            item.gather_end(up_arrive if item is up else None)
+    for item in slabs:
+        item.gather_end(qkv_arrive if item is qkv else None)
+    for item in (*wide, *slabs):
+        item.drain()
+    for copy in vec_copies:
+        copy.wait_send()
+
+
+def reduce_grads(grads, vec, squares, last, call_id):
+    ring = lax.axis_size("fsdp") // 2
+    anywhere = pl.BlockSpec(memory_space=pl.ANY)
+    vmem = pl.BlockSpec(memory_space=pltpu.VMEM)
+    dma = pltpu.SemaphoreType.DMA
+    scratch, slab_shapes = [], []
+    for idx, grad in enumerate(grads):
+        slab, width = grad.shape[0] // ring, grad.shape[1]
+        quarter = slab // 4
+        slab_shapes.append(jax.ShapeDtypeStruct((slab, width), BF))
+        z_first = idx < 2
+        tiles = 1 if z_first else ring
+        scratch += [
+            pltpu.VMEM((ring, slab if z_first else 2 * quarter, width), BF),
+            pltpu.VMEM((tiles, 2 * quarter, width), BF),
+            pltpu.VMEM((tiles, quarter, width), BF),
+            pltpu.VMEM((ring - 1, slab if z_first else quarter, width), BF),
+        ]
+    half = [
+        jax.ShapeDtypeStruct((shape.shape[0] // 2, shape.shape[1]), BF) for shape in slab_shapes
+    ]
+    return pl.pallas_call(
+        partial(reduce_kernel, last),
+        in_specs=[anywhere] * 4 + [vmem] * 2,
+        out_specs=[anywhere] * 6 + [vmem] * 2,
+        out_shape=[
+            slab_shapes[0],
+            half[0],
+            slab_shapes[1],
+            slab_shapes[2],
+            half[2],
+            slab_shapes[3],
+            jax.ShapeDtypeStruct(vec.shape[1:], F32),
+            jax.ShapeDtypeStruct((8, 128), F32),
+        ],
+        scratch_shapes=[
+            *scratch,
+            pltpu.VMEM((3,) + vec.shape, F32),
+            pltpu.VMEM((ring - 1,) + vec.shape[1:], F32),
+            pltpu.VMEM((4,) + vec.shape, F32),
+            pltpu.VMEM((3 + ring - 1, 8, 128), F32),
+            pltpu.VMEM((4, 8, 128), F32),
+            dma((120,)),
+            dma((120,)),
+            dma((120,)),
+        ],
+        compiler_params=pltpu.CompilerParams(
+            collective_id=call_id, has_side_effects=True, vmem_limit_bytes=VMEM_LIMIT
+        ),
+        cost_estimate=pl.CostEstimate(flops=0, bytes_accessed=300_000_000, transcendentals=0),
+        name="reduce_grads",
+    )(*grads, vec, squares)
+
+
+def adam_kernel(
+    kinds, ring, count, core_ref, factor_ref, *refs
+):
+    n_grads = len(refs) - 8
+    grads = refs[:n_grads]
+    master, first, second, grad_out, first_out, second_out, new_out, copy_out = refs[n_grads:]
+    layer = pl.program_id(0)
+    factor = factor_ref[0]
+    scale = 1.0 / count
+    columns = master.shape[2]
+    per_layer = n_grads // 2
+    width = columns // (kinds * ring * 2) if per_layer == 2 else 512
+
+    def update(at, total):
+        grad = total.astype(F32) * scale
+        first_new, second_new, new = [], [], []
+        first_new, second_new, new = adam_update(
+            master[0, :, at], grad, first[0, :, at], second[0, :, at], factor
+        )
+        grad_out[0, :, at] = grad
+        first_out[0, :, at] = first_new
+        second_out[0, :, at] = second_new
+        new_out[0, :, at] = new
+        copy_out[0, :, at] = new.astype(BF)
+
+    def choose(which, at):
+        values = [grads[idx * per_layer + which][:, at] for idx in range(2)]
+        return jnp.where(layer == 0, values[0], values[1])
+
+    if per_layer == 1:
+        for start in range(0, columns, width):
+            update(slice(start, start + width), choose(0, slice(start, start + width)))
+        return
+    core = core_ref[0]
+    for pair in range(ring):
+        for kind in range(kinds):
+            source = (pair * kinds + kind) * width
+            mine, arrive = [choose(which, slice(source, source + width)) for which in range(2)]
+            for which in range(2):
+                start = (kind * ring * 2 + 2 * pair + which) * width
+                update(slice(start, start + width), jnp.where(core == which, mine, arrive))
+
+
+def adam_matrix(grads, master, first, second, factor, core, kinds, count):
+    layers, rows, columns = master.shape
+    ring = lax.axis_size("fsdp") // 2
+    block = 32 if columns > 1024 else 64
+    steps = rows // block
+    per_layer = len(grads) // layers
+
+    def grad_spec(idx):
+        layer, which = divmod(idx, per_layer)
+        lift = steps if per_layer == 2 and which == 0 else 0
+
+        def where(at_layer, step, core_ref, layer=layer, lift=lift):
+            held = 0 if layer > 0 else steps - 1
+            row = jnp.where(at_layer == layer, step, held)
+            return (row + lift * core_ref[0], 0)
+
+        return pl.BlockSpec((block, grads[idx].shape[1]), where)
+
+    whole = pl.BlockSpec((1, block, columns), lambda layer, step, core_ref: (layer, step, 0))
+    shape = jax.ShapeDtypeStruct(master.shape, F32)
+    return pl.pallas_call(
+        partial(adam_kernel, kinds, ring, count),
+        grid_spec=pltpu.PrefetchScalarGridSpec(
+            num_scalar_prefetch=1,
+            grid=(layers, steps),
+            in_specs=[pl.BlockSpec(memory_space=pltpu.SMEM)]
+            + [grad_spec(idx) for idx in range(len(grads))]
+            + [whole] * 3,
+            out_specs=[whole] * 5,
+        ),
+        out_shape=[shape] * 4 + [jax.ShapeDtypeStruct(master.shape, BF)],
+        compiler_params=pltpu.CompilerParams(vmem_limit_bytes=VMEM_LIMIT),
         cost_estimate=pl.CostEstimate(
-            flops=0, bytes_accessed=600_000_000, transcendentals=0
+            flops=20 * master.size, bytes_accessed=32 * master.size, transcendentals=master.size
         ),
-        name="gather_weights",
-    )(qkv_mine, qkv_away, up_mine, up_away, down_low, proj_low)
-
-
-def ring_sum(item):
-    ring = item.shape[0]
-    chip = lax.axis_index("fsdp") // 2
-
-    def own(back):
-        return pick(item, lax.rem(chip - back + ring, ring))
-
-    moving = own(1)
-    for hop in range(2, ring + 1):
-        moving = (send_up(moving).astype(F32) + own(hop).astype(F32)).astype(BF)
-    return moving
-
-
-def plane_sum(item, axis, x_first):
-    seq = lax.axis_index("seq")
-    at_x, at_y = lax.rem(seq, 2), seq // 2
-
-    def one(data, dim, place, mask):
-        other = swap_seq(pick(data, 1 - place, dim), mask)
-        return (pick(data, place, dim).astype(F32) + other.astype(F32)).astype(BF)
-
-    if x_first:
-        return one(one(item, axis + 1, at_x, 1), axis, at_y, 2)
-    return one(one(item, axis, at_y, 2), axis, at_x, 1)
+        name="update",
+    )(core.reshape(1).astype(jnp.int32), factor.reshape(1), *grads, master, first, second)
 
 
 def norm_parts(hidden):
@@ -967,7 +1607,7 @@
     core = lax.rem(shard, 2)
     even = lax.rem(seq, 2) == 0
 
-    def to_clips(item, extra=None):
+    def to_clips(item):
         halves = []
         for turn in range(2):
             piece = jnp.where(even, item[turn], item[1 - turn])
@@ -1001,40 +1641,23 @@
             even, jnp.stack([pieces[0], pieces[1]]), jnp.stack([pieces[1], pieces[0]])
         )
 
-    coord_rows = jnp.zeros((batch_local, 8, D), F32)
-    coord_rows = lax.dynamic_update_slice(
-        coord_rows, jnp.swapaxes(patch_coords, 0, 1).astype(F32), (0, 0, 0)
-    )
-    arrived = to_clips(jnp.concatenate([clip_tokens, coord_rows], axis=1))
-    hidden = arrived[:, :chunk_len].reshape(4 * chunk_len, D)
-    coords = arrived[:, chunk_len : chunk_len + 3, :chunk_len]
-    coords = jnp.swapaxes(coords, 0, 1).reshape(3, 4 * chunk_len)
+    coord_rows = jnp.pad(jnp.swapaxes(patch_coords, 0, 1), ((0, 0), (0, 5), (0, 0)))
+    vector_rows = vector_params.astype(BF).astype(F32).reshape(-1)
+    vector_rows = jnp.pad(vector_rows, (0, -vector_rows.shape[0] % 1024)).reshape(8, -1)
+    qkv_all_w, up_all_w, down_all_w, proj_all_w, hidden, coords, vector_got = gather_weights(
+        qkv_weight, up_weight, down_weight, proj_weight, clip_tokens, coord_rows, vector_rows
+    )
+    layers = [
+        (qkv_all_w[idx], proj_all_w[idx, 0], proj_all_w[idx, 1], up_all_w[idx], down_all_w[idx])
+        for idx in range(layer_count)
+    ]
+    coords = jnp.swapaxes(coords[:, :3], 0, 1).reshape(3, 4 * chunk_len)
     cosine, sine = rotary_tables(coords, HEAD_DIM // 2)
     cos_wide = jnp.concatenate([cosine] * 4, axis=1)
     sin_wide = jnp.concatenate([-sine, sine, -sine, sine], axis=1)
-
-    vector_all = lax.all_gather(vector_params.astype(BF), "fsdp", axis=1, tiled=True).astype(F32)
-
-    def by_core(low, kinds):
-        width = low.shape[2] // (kinds * parts)
-        view = low.reshape(layer_count, low.shape[1], kinds, ring, 2, width)
-
-        def half(which):
-            cut = pick(view, which, 4).transpose(0, 1, 3, 2, 4)
-            return cut.reshape(layer_count, low.shape[1], -1)
-
-        return half(core), half(1 - core)
-
-    gathered = gather_weights(
-        *by_core(qkv_weight.astype(BF), 3),
-        *by_core(up_weight.astype(BF), 1),
-        down_weight.astype(BF),
-        proj_weight.astype(BF),
-    )
-    layers = [
-        (gathered[0][idx], gathered[3][idx, 0], gathered[3][idx, 1], gathered[1][idx], gathered[2][idx])
-        for idx in range(layer_count)
-    ]
+    vector_all = vector_got.reshape(parts, -1)[:, : vector_params.size]
+    vector_all = vector_all.reshape(parts, layer_count, -1).transpose(1, 0, 2)
+    vector_all = vector_all.reshape(layer_count, -1)
 
     saved = []
     for idx in range(layer_count):
@@ -1063,6 +1686,7 @@
     grad = to_clips(out_cotangent).reshape(4 * chunk_len, D)
     sums = [None] * layer_count
     vector_sums = [None] * layer_count
+    squares = jnp.zeros((8, 128), F32)
     for idx in reversed(range(layer_count)):
         qkv_w, proj_w, proj_other, up_w, down_w = layers[idx]
         entry, normed, low_all, lse, mixed, after_attn, normed_two, active, slope = saved[idx]
@@ -1113,57 +1737,51 @@
             ]
         )
 
-        def owner_view(item, halves):
-            rows = item.shape[0] // (ring * halves * 4)
-            return item.reshape(ring, halves, 2, 2, rows, item.shape[1])
-
-        def to_core(item):
-            other = swap_core(pick(item, 1 - core))
-            mine = pick(item, core)
-            return jnp.where(core == 0, jnp.stack([mine, other]), jnp.stack([other, mine]))
-
-        down_sum = ring_sum(plane_sum(owner_view(down_grad, 1), 2, False))[0]
-        up_sum = to_core(ring_sum(plane_sum(owner_view(up_grad, 2), 2, True)))
-        proj_sum = plane_sum(ring_sum(owner_view(proj_grad, 1)), 1, False)[0]
-        qkv_sum = to_core(plane_sum(ring_sum(owner_view(qkv_grad, 2)), 1, True))
-        rows = up_sum.shape[1]
-        up_sum = up_sum.reshape(2, rows, ring, -1).transpose(1, 2, 0, 3).reshape(rows, -1)
-        rows = qkv_sum.shape[1]
-        qkv_sum = qkv_sum.reshape(2, rows, ring, 3, -1).transpose(1, 3, 2, 0, 4).reshape(rows, -1)
-        sums[idx] = (qkv_sum, proj_sum, up_sum, down_sum)
+        total_vec = vector_sums[idx].reshape(ring, -1)
+        pad = -total_vec.shape[1] % 1024
+        total_vec = jnp.pad(total_vec, ((0, 0), (0, pad))).reshape(ring, 8, -1)
+        sums[idx] = reduce_grads(
+            (qkv_grad, proj_grad, up_grad, down_grad),
+            total_vec,
+            squares,
+            idx == 0,
+            1 + idx,
+        )
+        squares = sums[idx][7]
     input_grad = from_clips(grad)
 
     clip_count = batch_local * parts
-    quarter_sums = tuple(
-        jnp.stack([sums[idx][kind] for idx in range(layer_count)]) for kind in range(4)
-    )
-    local_squares = sum(
-        jnp.sum(jnp.square(item.astype(F32) * (1.0 / clip_count))) for item in quarter_sums
-    )
-    vector_total = lax.psum(jnp.stack(vector_sums), ("seq", "fsdp")) / clip_count
-    squares = lax.psum(local_squares, ("seq", "fsdp")) + jnp.sum(vector_total * vector_total)
-    norm_value = jnp.sqrt(squares)
+    norm_value = jnp.sqrt(jnp.sum(squares)) / clip_count
     param_count = sum(master.size for master in masters) * parts
     factor = jnp.minimum(1.0, CLIP_RATIO * math.sqrt(float(param_count)) / (norm_value + 1e-06))
 
     share = vector_params.shape[1]
-    grad_shards = [lax.dynamic_slice_in_dim(vector_total, shard * share, share, 1)]
-    for item in quarter_sums:
-        whole = lax.all_gather(item, "seq", axis=1, tiled=True)
-        grad_shards.append(whole.astype(F32) / clip_count)
-    updates = [
-        adam_update(master, grad_item, first_old, second_old, factor)
-        for master, grad_item, first_old, second_old in zip(masters, grad_shards, firsts, seconds)
-    ]
+    vector_total = jnp.stack([item[6].reshape(-1)[: 2 * share] for item in sums])
+    vector_grad = lax.dynamic_slice_in_dim(vector_total, core * share, share, 1) / clip_count
+    vector_new = adam_update(vector_params, vector_grad, first_vector, second_vector, factor)
+    updates = [(vector_grad, *vector_new, vector_new[2].astype(BF))]
+    for kind, keys in enumerate(((0, 1), (2,), (3, 4), (5,))):
+        updates.append(
+            adam_matrix(
+                [item[key] for item in sums for key in keys],
+                masters[kind + 1],
+                firsts[kind + 1],
+                seconds[kind + 1],
+                factor,
+                core,
+                3 if kind == 0 else 1,
+                clip_count,
+            )
+        )
     return (
         block_output,
         input_grad,
-        *grad_shards,
+        *[item[0] for item in updates],
         norm_value.reshape(1),
-        *[item[0] for item in updates],
         *[item[1] for item in updates],
         *[item[2] for item in updates],
-        *[item[2].astype(BF) for item in updates],
+        *[item[3] for item in updates],
+        *[item[4] for item in updates],
     )
 
 

time: 1220 us -> 996 us (0.82)
  Pallas kernels: 316 us -> 671 us
  waiting for transfers between devices: 305 us -> 32.4 us
  other arithmetic: 169 us -> 61.2 us
  blocking collectives: 72.3 us -> 0 us
  local copies, waits for them, and re-layouts: 76.5 us -> 9.65 us
  starting transfers between devices: 71.4 us -> 16.3 us
  matrix products: 173 us -> 192 us
  between operations: 23.1 us -> 4.46 us
    pallas_call x1 -> x7, Pallas kernels: 173 us -> 528 us  [the longest x2 296 us: reduce_grads(): pl.pallas_call(partial(reduce_kernel, last), in_specs=[anywhere] * 4 + [v...]
    ppermute x40 -> x0, waiting for transfers between devices: 217 us -> none  [the longest x24 125 us: send_up(): lax.ppermute(item, 'fsdp', [(idx, (idx + 2) % parts) for idx in range(par...]
    convert_element_type x54 -> x3, other arithmetic: 88.4 us -> 1.46 us  [the longest x1 0.74 us: fast_device(): updates = [(vector_grad, *vector_new, vector_new[2].astype(BF))]]
    ppermute x40 -> x0, starting transfers between devices: 45.5 us -> none  [the longest x24 25.9 us: send_up(): lax.ppermute(item, 'fsdp', [(idx, (idx + 2) % parts) for idx in range(par...]
    psum x1 -> x0, waiting for transfers between devices: 41.4 us -> none  [fast_device(): lax.psum(jnp.stack(vector_sums), ('seq', 'fsdp')) / clip_count]
    psum x1 -> x0, blocking collectives: 40.9 us -> none  [fast_device(): lax.psum(local_squares, ('seq', 'fsdp'))]
    dynamic_slice x22 -> x3, local copies, waits for them, and re-layouts: 35 us -> 0.04 us  [pick(): return lax.dynamic_index_in_dim(item, index, axis, keepdims=False)]
    all_gather x2 -> x0, blocking collectives: 31.3 us -> none  [the longest x1 17.1 us: fast_device(): whole = lax.all_gather(item, 'seq', axis=1, tiled=True)]
  transfers between devices with their start and end apart: 66 -> 15, of which waited for: 26 -> 2; matrix products, arithmetic and copies ran while one was open for 25% -> 11% of each run, Pallas kernels for 23% -> 38%
where the time goes in v3:
time: 996 us; the launch traced here: 987 us
  Pallas kernels  671 us (67%)
  matrix products  192 us (19%)
  other arithmetic  61.2 us (6%)
  waiting for transfers between devices  32.4 us (3%)
  starting transfers between devices  16.3 us (2%)
    pallas_call x2, Pallas kernels, reduce_grads(): pl.pallas_call(partial(reduce_kernel, last), in_specs=[anywhere] * 4 + [v...  296 us
    pallas_call x1, Pallas kernels, gather_weights(): pl.pallas_call(gather_kernel, in_specs=[anywhere] * 5 + [vmem] * 2, out_s...  183 us
    pallas_call x2, Pallas kernels, attend_grad(): pl.pallas_call(attn_bwd_kernel, grid=(pairs,), in_specs=[triple, pl.Block...  74.6 us
    dot_general x8, matrix products, dot_nt(): return lax.dot_general(left, right, NT, preferred_element_type=F32)  73.2 us
    pallas_call x2, Pallas kernels, attend(): pl.pallas_call(attn_fwd_kernel, grid=(pairs,), in_specs=[triple, table, t...  68.7 us
    dot_general x8, matrix products, dot_tn(): lax.dot_general(left, right, (((0,), (0,)), ((), ())), preferred_element_...  60.4 us
    dot_general x10, matrix products, dot(): return jnp.dot(left, right, preferred_element_type=F32)  57.9 us
    pallas_call x4, Pallas kernels, adam_matrix(): pl.pallas_call(partial(adam_kernel, kinds, ring, count), grid_spec=pltpu....  48.8 us
  transfers between devices with their start and end apart: 15, of which 2 were waited for; matrix products, arithmetic and copies ran while one was open for 11% of the time, Pallas kernels for 38%

profile of v3, /device:TPU:0, one launch (start us, length us, event | category | flops | bytes accessed | tf_op | source)
XLA Modules:
  0.0 987.1 jit_solution(16993870182805472191)
XLA Ops:
  3.4 183.0 %gather_weights.1 = (bf16[2,1024,1536]{2,1,0:T(8,128)(2,1)}, bf16[2,1024,2048]{2,1,0:T(8,128)(2,1)}, bf16[2,2048,1024]{2,1,0:T(8,128)(2,1)}, bf16[2,2,512,1024]{...) custom-call(f32[2,128,3072]{2,1,0:T(8,128)} %refs_4_.4, ...), custom_call_target="tpu_custom_call" | custom-call | bytes 600000000 | tf_op jit(solution)/shard_map/gather_weights/pallas_call | solution.py:993
  199.3 7.8 convolution_add_fusion.1.qkv_ref
  207.1 34.4 %attend.2 = (bf16[1024,512]{1,0:T(8,128)(2,1)}, bf16[1024,1536]{1,0:T(8,128)(2,1)}, f32[4,8,1024]{2,1,0:T(8,128)}) custom-call(f32[1024,1536]{1,0:T(8,128)} %convolution_add_fusion.1.qkv_ref, f32[1024,128]{1,0:T(8,128)} %get-tuple-element.230.cos_ref, f32[1024,128]{1,0:T(8,128)} %get-tuple-element.231.sin_ref), custom_call_target="tpu_custom_call" | custom-call | flops 8589934592 | bytes 12582912 | tf_op jit(solution)/shard_map/attend/pallas_call | solution.py:498
  248.3 8.0 multiply_convert_fusion.1
  256.4 6.4 fusion.101
  266.9 25.4 %collective-permute-done.7 = f32[256,1024]{1,0:T(8,128)S(1)} collective-permute-done((f32[256,1024]{1,0:T(8,128)S(1)}, f32[256,1024]{1,0:T(8,128)S(1)}, u32[]{:S(2)}, u32[]{:S(2)}) %collective-permute-start.7) | collective-permute-done | bytes 1048608 | tf_op jit(solution)/shard_map/ppermute | solution.py:1620
  298.5 5.7 convolution_add_fusion.qkv_ref
  304.2 34.4 %attend.3 = (bf16[1024,512]{1,0:T(8,128)(2,1)}, bf16[1024,1536]{1,0:T(8,128)(2,1)}, f32[4,8,1024]{2,1,0:T(8,128)}) custom-call(f32[1024,1536]{1,0:T(8,128)} %convolution_add_fusion.qkv_ref, f32[1024,128]{1,0:T(8,128)} %get-tuple-element.230.cos_ref, f32[1024,128]{1,0:T(8,128)} %get-tuple-element.231.sin_ref), custom_call_target="tpu_custom_call" | custom-call | flops 8589934592 | bytes 12582912 | tf_op jit(solution)/shard_map/attend/pallas_call | solution.py:498
  348.5 9.3 fusion.20
  357.8 13.3 %fusion.10 = (f32[2048]{0:T(1024)S(1)}, bf16[1024,2048]{1,0:T(8,128)(2,1)S(1)}, bf16[1024,2048]{1,0:T(8,128)(2,1)}, f32[1024,2048]{1,0:T(8,128)}) fusion(f32[1024,2048]{1,0:T(8,128)} %fusion.20, f32[2048]{0:T(1024)S(1)} %bitcast.213, bf16[1024,1024]{1,0:T(8,128)(2,1)S(1)} %bitcast.180, bf16[2,2048,1024]{2,1,0:T(8,128)(2,1)} %get-tuple-element.88), kind=kOutput, calls=%fused_computation.18 | convolution fusion | flops 4326422528 | bytes 31473664 | tf_op jit(solution)/shard_map/dot_general | solution.py:1554
  371.1 12.1 %fusion.104 = (bf16[1024,1024]{1,0:T(8,128)(2,1)}, f32[1024,1024]{1,0:T(8,128)}) fusion(bf16[1024,2048]{1,0:T(8,128)(2,1)} %get-tuple-element.173, bf16[2,2048,1024]{2,1,0:T(8,128)(2,1)} %get-tuple-element.88), kind=kOutput, calls=%fused_computation.229 | convolution fusion | flops 4296015872 | bytes 14680064 | tf_op jit(solution)/shard_map/dot_general | solution.py:1550
  383.3 10.5 %fusion.103 = (bf16[1024,1024]{1,0:T(8,128)(2,1)}, f32[1024,1024]{1,0:T(8,128)S(1)}) fusion(bf16[2,1024,2048]{2,1,0:T(8,128)(2,1)} %get-tuple-element.87, f32[1024,2048]{1,0:T(8,128)} %get-tuple-element.215, bf16[1024,2048]{1,0:T(8,128)(2,1)S(1)} %get-tuple-element.164), kind=kOutput, calls=%fused_computation.228 | convolution fusion | flops 4302307328 | bytes 23068672 | tf_op jit(solution)/shard_map/dot_general | solution.py:1554
  394.3 13.1 %convolution_convert_fusion.3.up_grad = bf16[1024,2048]{1,0:T(8,128)(2,1)} fusion(f32[1024,2048]{1,0:T(8,128)} %get-tuple-element.215, bf16[1024,2048]{1,0:T(8,128)(2,1)} %copy-done.52, f32[1024,1024]{1,0:T(8,128)S(1)} %get-tuple-element.214, f32[1024]{0:T(1024)S(1)} %get-tuple-element.186, f32[1024]{0:T(1024)S(1)} %get-tuple-element.187, ...), kind=kOutput, calls=%fused_computation.77 | convolution fusion | flops 4308598784 | bytes 20987904 | tf_op jit(solution)/shard_map/dot_general | solution.py:1558
  407.4 8.3 convolution_convert_fusion.2.down_grad
  418.3 5.6 fusion.90
  428.2 37.4 %attend_grad.2 = (bf16[1024,1536]{1,0:T(8,128)(2,1)}, f32[8,1536]{1,0:T(8,128)}) custom-call(bf16[1024,1536]{1,0:T(8,128)(2,1)} %get-tuple-element.90.low_ref, bf16[1024,512]{1,0:T(8,128)(2,1)} %convolution_convert_fusion.9.dout_ref, f32[4,8,1024]{2,1,0:T(8,128)} %get-tuple-element.91.lse_ref, f32[1024,128]{1,0:T(8,128)} %get-tuple-element.230.cos_ref, ...), custom_call_target="tpu_custom_call" | custom-call | flops 21474836480 | bytes 9437184 | tf_op jit(solution)/shard_map/attend_grad/pallas_call | solution.py:586
  465.6 9.1 fusion.105
  476.2 9.5 collective-permute-start.4
  489.4 8.8 convolution_convert_fusion.qkv_grad
  498.2 7.0 collective-permute-done.5
  514.3 13.7 %fusion.12 = (f32[2048]{0:T(1024)S(1)}, bf16[1024,2048]{1,0:T(8,128)(2,1)S(1)}, f32[1024,2048]{1,0:T(8,128)}) fusion(f32[1024,2048]{1,0:T(8,128)} %get-tuple-element.210, f32[2048]{0:T(1024)S(1)} %bitcast.212, bf16[2,2048,1024]{2,1,0:T(8,128)(2,1)} %get-tuple-element.88, f32[1024,1024]{1,0:T(8,128)S(1)} %get-tuple-element.166), kind=kOutput, calls=%fused_computation.20 | convolution fusion | flops 4323276800 | bytes 29376512 | tf_op jit(solution)/shard_map/dot_general | solution.py:1554
  528.2 11.3 %fusion.106 = (bf16[1024,1024]{1,0:T(8,128)(2,1)}, f32[1024,1024]{1,0:T(8,128)}) fusion(bf16[2,1024,2048]{2,1,0:T(8,128)(2,1)S(1)} %bitcast.217, f32[1024,2048]{1,0:T(8,128)} %get-tuple-element.222, bf16[1024,2048]{1,0:T(8,128)(2,1)S(1)} %get-tuple-element.170), kind=kOutput, calls=%fused_computation.231 | convolution fusion | flops 4302307328 | bytes 23068672 | tf_op jit(solution)/shard_map/dot_general | solution.py:1554
  540.8 141.2 %reduce_grads.2 = (bf16[256,1536]{1,0:T(8,128)(2,1)}, bf16[128,1536]{1,0:T(8,128)(2,1)}, bf16[128,1024]{1,0:T(8,128)(2,1)}, bf16[256,2048]{1,0:T(8,128)(2,1)}, b...) custom-call(bf16[1024,1536]{1,0:T(8,128)(2,1)} %convolution_convert_fusion.qkv_grad, ...), custom_call_target="tpu_custom_call" | custom-call | bytes 300000000 | tf_op jit(solution)/shard_map/reduce_grads/pallas_call | solution.py:1407
  682.9 11.7 %convolution_convert_fusion.5.up_grad = bf16[1024,2048]{1,0:T(8,128)(2,1)} fusion(f32[1024,2048]{1,0:T(8,128)} %get-tuple-element.222, bf16[1024,2048]{1,0:T(8,128)(2,1)} %copy-done.51, f32[1024,1024]{1,0:T(8,128)S(1)} %copy-done.2, f32[1024]{0:T(1024)S(1)} %copy-done.46, f32[1024]{0:T(1024)S(1)} %copy-done.34, f32[1024]{0:T(1024)S(1)} %copy-done.36, ...), kind=kOutput, calls=%fused_computation.79 | convolution fusion | flops 4308598784 | bytes 20987904 | tf_op jit(solution)/shard_map/dot_general | solution.py:1558
  704.8 37.2 %attend_grad.3 = (bf16[1024,1536]{1,0:T(8,128)(2,1)}, f32[8,1536]{1,0:T(8,128)}) custom-call(bf16[1024,1536]{1,0:T(8,128)(2,1)} %get-tuple-element.93.low_ref, bf16[1024,512]{1,0:T(8,128)(2,1)} %convolution_convert_fusion.8.dout_ref, f32[4,8,1024]{2,1,0:T(8,128)} %get-tuple-element.94.lse_ref, f32[1024,128]{1,0:T(8,128)} %get-tuple-element.230.cos_ref, ...), custom_call_target="tpu_custom_call" | custom-call | flops 21474836480 | bytes 9437184 | tf_op jit(solution)/shard_map/attend_grad/pallas_call | solution.py:586
  742.0 7.4 fusion.107
  749.8 6.5 convolution_convert_fusion.4.down_grad
  761.9 5.2 convolution_convert_fusion.1.qkv_grad
  774.2 155.2 %reduce_grads.3 = (bf16[256,1536]{1,0:T(8,128)(2,1)}, bf16[128,1536]{1,0:T(8,128)(2,1)}, bf16[128,1024]{1,0:T(8,128)(2,1)}, bf16[256,2048]{1,0:T(8,128)(2,1)}, b...) custom-call(bf16[1024,1536]{1,0:T(8,128)(2,1)} %convolution_convert_fusion.1.qkv_grad, ...), custom_call_target="tpu_custom_call" | custom-call | bytes 300000000 | tf_op jit(solution)/shard_map/reduce_grads/pallas_call | solution.py:1407
  937.1 11.9 %update.4 = (f32[2,128,3072]{2,1,0:T(8,128)}, f32[2,128,3072]{2,1,0:T(8,128)}, f32[2,128,3072]{2,1,0:T(8,128)}, f32[2,128,3072]{2,1,0:T(8,128)}, bf16[2,128,3072]{2,1,0:T(8,128)(2,1)}) custom-call(s32[1]{0:T(128)} %bitcast.57.core_ref, f32[1]{0:T(128)} %bitcast.58.factor_ref, bf16[256,1536]{1,0:T(8,128)(2,1)} %get-tuple-element.102.refs_0_, ...), custom_call_target="tpu_custom_call" | custom-call | flops 15728640 | bytes 25165824 | tf_op jit(solution)/shard_map/update/pallas_call | solution.py:1503
  949.1 17.6 %update.7 = (f32[2,512,1024]{2,1,0:T(8,128)}, f32[2,512,1024]{2,1,0:T(8,128)}, f32[2,512,1024]{2,1,0:T(8,128)}, f32[2,512,1024]{2,1,0:T(8,128)}, bf16[2,512,1024]{2,1,0:T(8,128)(2,1)}) custom-call(s32[1]{0:T(128)} %bitcast.57.core_ref, f32[1]{0:T(128)} %bitcast.58.factor_ref, bf16[512,1024]{1,0:T(8,128)(2,1)} %get-tuple-element.115.refs_0_, ...), custom_call_target="tpu_custom_call" | custom-call | flops 20971520 | bytes 33554432 | tf_op jit(solution)/shard_map/update/pallas_call | solution.py:1503
  966.7 14.2 %update.6 = (f32[2,128,4096]{2,1,0:T(8,128)}, f32[2,128,4096]{2,1,0:T(8,128)}, f32[2,128,4096]{2,1,0:T(8,128)}, f32[2,128,4096]{2,1,0:T(8,128)}, bf16[2,128,4096]{2,1,0:T(8,128)(2,1)}) custom-call(s32[1]{0:T(128)} %bitcast.57.core_ref, f32[1]{0:T(128)} %bitcast.58.factor_ref, bf16[256,2048]{1,0:T(8,128)(2,1)} %get-tuple-element.110.refs_0_, ...), custom_call_target="tpu_custom_call" | custom-call | flops 20971520 | bytes 33554432 | tf_op jit(solution)/shard_map/update/pallas_call | solution.py:1503
  (289 shorter events, 100.4 us)
Async XLA Ops:
  192.9 55.1 %copy-start.33 = (f32[1024]{0:T(1024)}, f32[1024]{0:T(1024)S(1)}, u32[]{:S(2)}) copy-start(f32[1024]{0:T(1024)S(1)} %get-tuple-element.191) | copy-start | bytes 12292
  192.9 55.1 %copy-start.45 = (f32[1024]{0:T(1024)}, f32[1024]{0:T(1024)S(1)}, u32[]{:S(2)}) copy-start(f32[1024]{0:T(1024)S(1)} %get-tuple-element.193) | copy-start | bytes 12292
  241.5 3.0 collective-permute-start
  262.7 31.1 %collective-permute-start.1 = (bf16[1024,1024]{1,0:T(8,128)(2,1)}, bf16[1024,1024]{1,0:T(8,128)(2,1)}, u32[]{:S(2)}, u32[]{:S(2)}) collective-permute-start(bf16[1024,1024]{1,0:T(8,128)(2,1)} %get-tuple-element.211), channel_id=1, source_target_pairs={{0,1},{1,0},{2,3},{3,2},{4,5},{5,4},{6,7},{7,6},{8,9},{9,8},{10,11... | collective-permute-start | bytes 6291464 | tf_op jit(solution)/shard_map/ppermute | solution.py:422
  264.4 2.5 collective-permute-start.6
  266.7 25.6 %collective-permute-start.7 = (f32[256,1024]{1,0:T(8,128)S(1)}, f32[256,1024]{1,0:T(8,128)S(1)}, u32[]{:S(2)}, u32[]{:S(2)}) collective-permute-start(f32[256,1024]{1,0:T(8,128)S(1)} %get-tuple-element.182), channel_id=1, source_target_pairs={{0,8},{1,24},{2,10},{3,26},{4,12},{5,28},{6,14},{7,30},{8,0},{9,16... | collective-permute-start | bytes 3145736 | tf_op jit(solution)/shard_map/ppermute | solution.py:1620
  266.8 26.9 %copy-start.1 = (f32[1024,1024]{1,0:T(8,128)S(1)}, f32[1024,1024]{1,0:T(8,128)}, u32[]{:S(2)}) copy-start(f32[1024,1024]{1,0:T(8,128)} %copy-done) | copy-start | bytes 12582916
  293.8 45.5 %collective-permute-start.8 = (f32[2,256,1024]{2,1,0:T(8,128)}, f32[2,256,1024]{2,1,0:T(8,128)}, u32[]{:S(2)}, u32[]{:S(2)}) collective-permute-start(f32[2,256,1024]{2,1,0:T(8,128)} %maximum_select_fusion.3), channel_id=1, source_target_pairs={{0,1},{1,0},{2,3},{3,2},{4,5},{5,4},{6,7},{7,6},{8,9},{9,8},{10,11... | collective-permute-start | bytes 6291464 | tf_op jit(solution)/shard_map/ppermute | solution.py:422
  297.6 48.7 %copy-start.3 = (f32[1024,1024]{1,0:T(8,128)}, f32[1024,1024]{1,0:T(8,128)S(1)}, u32[]{:S(2)}) copy-start(f32[1024,1024]{1,0:T(8,128)S(1)} %get-tuple-element.172) | copy-start | bytes 12582916
  338.6 7.7 collective-permute-start.2
  383.2 35.0 %collective-permute-start.3 = (bf16[1024,1024]{1,0:T(8,128)(2,1)}, bf16[1024,1024]{1,0:T(8,128)(2,1)}, u32[]{:S(2)}, u32[]{:S(2)}) collective-permute-start(bf16[1024,1024]{1,0:T(8,128)(2,1)} %get-tuple-element.218), channel_id=1, source_target_pairs={{0,1},{1,0},{2,3},{3,2},{4,5},{5,4},{6,7},{7,6},{8,9},{9,8},{10,11... | collective-permute-start | bytes 6291464 | tf_op jit(solution)/shard_map/ppermute | solution.py:422
  393.8 21.9 %copy-start.18 = (f32[1024,1024]{1,0:T(8,128)}, f32[1024,1024]{1,0:T(8,128)S(1)}, u32[]{:S(2)}) copy-start(f32[1024,1024]{1,0:T(8,128)S(1)} %get-tuple-element.217) | copy-start | bytes 12582916
  393.8 21.9 %collective-permute-start.9 = (bf16[1024,1024]{1,0:T(8,128)(2,1)}, bf16[1024,1024]{1,0:T(8,128)(2,1)S(1)}, u32[]{:S(2)}, u32[]{:S(2)}) collective-permute-start(bf16[1024,1024]{1,0:T(8,128)(2,1)} %get-tuple-element.216), channel_id=1, source_target_pairs={{0,1},{1,0},{2,3},{3,2},{4,5},{5,4},{6,7},{7,6},{8,9},{9,8},{10,11... | collective-permute-start | bytes 6291464 | tf_op jit(solution)/shard_map/ppermute | solution.py:422
  423.9 62.4 %copy-start.13 = (f32[1024,1024]{1,0:T(8,128)}, f32[1024,1024]{1,0:T(8,128)S(1)}, u32[]{:S(2)}) copy-start(f32[1024,1024]{1,0:T(8,128)S(1)} %get-tuple-element.162) | copy-start | bytes 12582916
  474.7 34.8 %collective-permute-start.10 = (bf16[1024,1024]{1,0:T(8,128)(2,1)}, bf16[1024,1024]{1,0:T(8,128)(2,1)S(1)}, u32[]{:S(2)}, u32[]{:S(2)}) collective-permute-start(bf16[1024,1024]{1,0:T(8,128)(2,1)} %get-tuple-element.220), channel_id=1, source_target_pairs={{0,1},{1,0},{2,3},{3,2},{4,5},{5,4},{6,7},{7,6},{8,9},{9,8},{10,11... | collective-permute-start | bytes 6291464 | tf_op jit(solution)/shard_map/ppermute | solution.py:422
  476.2 22.0 %collective-permute-start.4 = (f32[256,1024]{1,0:T(8,128)}, f32[256,1024]{1,0:T(8,128)}, u32[]{:S(2)}, u32[]{:S(2)}) collective-permute-start(f32[256,1024]{1,0:T(8,128)} %get-tuple-element.179), channel_id=1, source_target_pairs={{0,0},{16,1},{2,2},{18,3},{4,4},{20,5},{6,6},{22,7},{8,8},{24,9},{... | collective-permute-start | bytes 3145736 | tf_op jit(solution)/shard_map/ppermute | solution.py:1639
  485.7 19.5 %collective-permute-start.5 = (f32[256,1024]{1,0:T(8,128)S(1)}, f32[256,1024]{1,0:T(8,128)}, u32[]{:S(2)}, u32[]{:S(2)}) collective-permute-start(f32[256,1024]{1,0:T(8,128)S(1)} %get-tuple-element.180), channel_id=1, source_target_pairs={{8,0},{24,1},{10,2},{26,3},{12,4},{28,5},{14,6},{30,7},{0,8},{16,9... | collective-permute-start | bytes 3145736 | tf_op jit(solution)/shard_map/ppermute | solution.py:1639
  489.4 20.1 %copy-start.11 = (f32[1024,1024]{1,0:T(8,128)S(1)}, f32[1024,1024]{1,0:T(8,128)}, u32[]{:S(2)}) copy-start(f32[1024,1024]{1,0:T(8,128)} %get-tuple-element.221) | copy-start | bytes 12582916
  512.3 15.8 %slice-start.2 = ((s8[8388608]{0:T(1024)(128)(4,1)}), s8[4194304]{0:T(1024)(128)(4,1)S(1)}, s32[]{:S(2)}) async-start(s8[8388608]{0:T(1024)(128)(4,1)} %bitcast.216), calls=%async_computation.2 | async-start | bytes 8388608
  539.5 155.1 %collective-permute-start.11 = (bf16[1024,1024]{1,0:T(8,128)(2,1)}, bf16[1024,1024]{1,0:T(8,128)(2,1)S(1)}, u32[]{:S(2)}, u32[]{:S(2)}) collective-permute-start(bf16[1024,1024]{1,0:T(8,128)(2,1)} %get-tuple-element.223), channel_id=1, source_target_pairs={{0,1},{1,0},{2,3},{3,2},{4,5},{5,4},{6,7},{7,6},{8,9},{9,8},{10,11... | collective-permute-start | bytes 6291464 | tf_op jit(solution)/shard_map/ppermute | solution.py:422
  540.8 142.0 %copy-start.2 = (f32[1024,1024]{1,0:T(8,128)S(1)}, f32[1024,1024]{1,0:T(8,128)}, u32[]{:S(2)}) copy-start(f32[1024,1024]{1,0:T(8,128)} %copy-done) | copy-start | bytes 12582916
  540.8 142.0 %copy-start.27 = (f32[1024]{0:T(1024)S(1)}, f32[1024]{0:T(1024)}, u32[]{:S(2)}) copy-start(f32[1024]{0:T(1024)} %copy-done.26) | copy-start | bytes 12292
  540.8 142.0 %copy-start.34 = (f32[1024]{0:T(1024)S(1)}, f32[1024]{0:T(1024)}, u32[]{:S(2)}) copy-start(f32[1024]{0:T(1024)} %copy-done.33) | copy-start | bytes 12292
  540.8 142.0 %copy-start.36 = (f32[1024]{0:T(1024)S(1)}, f32[1024]{0:T(1024)}, u32[]{:S(2)}) copy-start(f32[1024]{0:T(1024)} %copy-done.35) | copy-start | bytes 12292
  540.8 142.0 %copy-start.46 = (f32[1024]{0:T(1024)S(1)}, f32[1024]{0:T(1024)}, u32[]{:S(2)}) copy-start(f32[1024]{0:T(1024)} %copy-done.45) | copy-start | bytes 12292
  701.1 40.8 %slice-start.8 = ((s8[6291456]{0:T(1024)(128)(4,1)}), s8[4194304]{0:T(1024)(128)(4,1)S(1)}, s32[]{:S(2)}) async-start(s8[6291456]{0:T(1024)(128)(4,1)} %bitcast.222), calls=%async_computation.8 | async-start | bytes 8388608
  704.8 37.2 %slice-start.9 = ((s8[6291456]{0:T(1024)(128)(4,1)}), s8[2097152]{0:T(1024)(128)(4,1)S(1)}, s32[]{:S(2)}) async-start(s8[6291456]{0:T(1024)(128)(4,1)} %bitcast.222), calls=%async_computation.9 | async-start | bytes 4194304
  749.4 17.7 %collective-permute-start.12 = (bf16[1024,1024]{1,0:T(8,128)(2,1)}, bf16[1024,1024]{1,0:T(8,128)(2,1)S(1)}, u32[]{:S(2)}, u32[]{:S(2)}) collective-permute-start(bf16[1024,1024]{1,0:T(8,128)(2,1)} %get-tuple-element.225), channel_id=1, source_target_pairs={{0,1},{1,0},{2,3},{3,2},{4,5},{5,4},{6,7},{7,6},{8,9},{9,8},{10,11... | collective-permute-start | bytes 6291464 | tf_op jit(solution)/shard_map/ppermute | solution.py:422
  771.7 210.6 %collective-permute-start.13 = (f32[256,1024]{1,0:T(8,128)S(1)}, f32[256,1024]{1,0:T(8,128)S(1)}, u32[]{:S(2)}, u32[]{:S(2)}) collective-permute-start(f32[256,1024]{1,0:T(8,128)S(1)} %get-tuple-element.176), channel_id=1, source_target_pairs={{0,0},{16,1},{2,2},{18,3},{4,4},{20,5},{6,6},{22,7},{8,8},{24,9},{... | collective-permute-start | bytes 3145736 | tf_op jit(solution)/shard_map/ppermute | solution.py:1639
  772.5 209.8 %collective-permute-start.14 = (f32[256,1024]{1,0:T(8,128)S(1)}, f32[256,1024]{1,0:T(8,128)}, u32[]{:S(2)}, u32[]{:S(2)}) collective-permute-start(f32[256,1024]{1,0:T(8,128)S(1)} %get-tuple-element.177), channel_id=1, source_target_pairs={{8,0},{24,1},{10,2},{26,3},{12,4},{28,5},{14,6},{30,7},{0,8},{16,9... | collective-permute-start | bytes 3145736 | tf_op jit(solution)/shard_map/ppermute | solution.py:1639
  966.7 14.3 %copy-start.38 = (f32[2,1664]{1,0:T(2,128)S(1)}, f32[2,1664]{1,0:T(2,128)}, u32[]{:S(2)}) copy-start(f32[2,1664]{1,0:T(2,128)} %param.31) | copy-start | bytes 39940
  966.7 14.3 %copy-start.39 = (f32[2,1664]{1,0:T(2,128)S(1)}, f32[2,1664]{1,0:T(2,128)}, u32[]{:S(2)}) copy-start(f32[2,1664]{1,0:T(2,128)} %param.26) | copy-start | bytes 39940
  (48 other events, 361.2 us)

commit v4 on v3

--- a/solution.py
+++ b/solution.py
@@ -1,5 +1,6 @@
 from functools import partial
 import math
+from types import SimpleNamespace
 
 import jax
 import jax.numpy as jnp
@@ -453,73 +454,6 @@
     return jnp.where(lane // HEAD_DIM == head, item, jnp.zeros_like(item))
 
 
-def attn_fwd_kernel(qkv_ref, cos_ref, sin_ref, mixed_ref, low_ref, lse_ref, qs_ref):
-    cosine, sine = cos_ref[...], sin_ref[...]
-    queries = qkv_ref[:, 0:PAIR]
-    key_rows = qkv_ref[:, PAIR : 2 * PAIR]
-    values = qkv_ref[:, 2 * PAIR : 3 * PAIR]
-    queries = (queries * cosine + swap_halves(queries) * sine).astype(BF)
-    key_rows = (key_rows * cosine + swap_halves(key_rows) * sine).astype(BF)
-    low_ref[:, 0:PAIR] = queries
-    low_ref[:, PAIR : 2 * PAIR] = key_rows
-    low_ref[:, 2 * PAIR : 3 * PAIR] = values.astype(BF)
-    qs_ref[...] = queries * jnp.asarray(HEAD_DIM**-0.5, BF)
-    values_t = values.T.astype(BF)
-    keys_by_head = [head_mask(key_rows, head) for head in range(2)]
-    length = qs_ref.shape[0]
-
-    @pl.loop(0, length // ROWS_Q)
-    def _(step):
-        rows = pl.ds(pl.multiple_of(step * ROWS_Q, ROWS_Q), ROWS_Q)
-        block = qs_ref[rows, :]
-        outs = []
-        for head in range(2):
-            scores = lax.dot_general(keys_by_head[head], block, NT, preferred_element_type=F32)
-            top = jnp.max(scores, axis=0, keepdims=True)
-            exponent = jnp.exp(scores - top)
-            total = jnp.sum(exponent, axis=0, keepdims=True)
-            lse_ref[0, head : head + 1, rows] = top + jnp.log(total)
-            probs = (exponent * (1.0 / total)).astype(BF)
-            outs.append(
-                jnp.dot(
-                    values_t[head * HEAD_DIM : (head + 1) * HEAD_DIM],
-                    probs,
-                    preferred_element_type=F32,
-                )
-            )
-        mixed_ref[rows, :] = jnp.concatenate(outs, axis=0).T.astype(BF)
-
-
-def attend(qkv_all, cos_wide, sin_wide):
-    length, width = qkv_all.shape
-    pairs = width // (3 * PAIR)
-    table = pl.BlockSpec((length, PAIR), lambda pair: (0, 0))
-    triple = pl.BlockSpec((length, 3 * PAIR), lambda pair: (0, pair))
-    return pl.pallas_call(
-        attn_fwd_kernel,
-        grid=(pairs,),
-        in_specs=[triple, table, table],
-        out_specs=[
-            pl.BlockSpec((length, PAIR), lambda pair: (0, pair)),
-            triple,
-            pl.BlockSpec((1, 8, length), lambda pair: (pair, 0, 0)),
-        ],
-        out_shape=[
-            jax.ShapeDtypeStruct((length, pairs * PAIR), BF),
-            jax.ShapeDtypeStruct((length, width), BF),
-            jax.ShapeDtypeStruct((pairs, 8, length), F32),
-        ],
-        scratch_shapes=[pltpu.VMEM((length, PAIR), BF)],
-        compiler_params=pltpu.CompilerParams(vmem_limit_bytes=VMEM_LIMIT),
-        cost_estimate=pl.CostEstimate(
-            flops=16 * pairs * length * length * PAIR,
-            bytes_accessed=length * width * 8,
-            transcendentals=2 * pairs * length * length,
-        ),
-        name="attend",
-    )(qkv_all, cos_wide, sin_wide)
-
-
 def attn_bwd_kernel(
     low_ref, dout_ref, lse_ref, cos_ref, sin_ref, grad_ref, bias_ref, dq_ref, dk_ref, dv_ref
 ):
@@ -653,380 +587,6 @@
 
 def aligned(start, size, unit=None):
     return pl.ds(pl.multiple_of(start, unit or size), size)
-
-
-def gather_kernel(
-    qkv_in, up_in, down_in, proj_in, clip_in, coord_in, vec_in,
-    qkv_out, up_out, down_out, proj_out, clip_out, coord_out, vec_out,
-    qkv_full, up_full, down_full, proj_full,
-    qkv_away, up_away,
-    qkv_slab, up_slab, down_slab, proj_slab, clip_slab,
-    z_send, z_recv, p_send, p_recv, d_send, d_recv, c_send, c_recv, l_in, l_out,
-    m_send, m_recv, m_load,
-):
-    at = Places()
-    ring, seq, chip, core = at.ring, at.seq, at.chip, at.core
-    other, up_chip = at.other, at.up
-    over_x, over_y, near_x, near_y = at.over_x, at.over_y, at.near_x, at.near_y
-    layers = qkv_in.shape[0]
-    loads = {}
-
-    def start_load(name, layer, slot):
-        source, full = {
-            "qkv": (qkv_in, qkv_full),
-            "up": (up_in, up_full),
-            "down": (down_in, down_full),
-            "proj": (proj_in, proj_full),
-        }[name]
-        copy = pltpu.make_async_copy(source.at[layer], full.at[layer], l_in.at[slot])
-        copy.start()
-        loads[name, layer] = copy
-
-    outs = {"qkv": qkv_out, "up": up_out, "down": down_out, "proj": proj_out}
-    slabs = {"qkv": qkv_slab, "up": up_slab, "down": down_slab, "proj": proj_slab}
-    items = [(name, layer) for layer in range(layers) for name in ("qkv", "proj", "up", "down")]
-
-    def place(name, layer, chip_at, part):
-        slab = slabs[name].shape[1]
-        if part is None:
-            start, size = chip_at * slab, slab
-        else:
-            size = slab // 4
-            start = chip_at * slab + part * size
-        rows = pl.ds(pl.multiple_of(start, size), size)
-        if name == "proj":
-            return outs[name].at[layer, 0, rows, :]
-        return outs[name].at[layer, rows, :]
-
-    for idx, (name, layer) in enumerate(items):
-        start_load(name, layer, idx)
-    clip_load = pltpu.make_async_copy(clip_in.at[lax.rem(seq, 2)], clip_slab, m_load.at[0])
-    clip_load.start()
-    barrier = pltpu.get_barrier_semaphore()
-    for target in (other, up_chip, at.down):
-        pl.semaphore_signal(barrier, inc=1, device_id=target, device_id_type=pl.DeviceIdType.MESH)
-    for step in range(1, 4):
-        for half in range(2):
-            pl.semaphore_signal(
-                barrier,
-                inc=1,
-                device_id={"fsdp": 2 * chip + half, "seq": seq ^ step},
-                device_id_type=pl.DeviceIdType.MESH,
-            )
-    pl.semaphore_wait(barrier, 9)
-
-    length = clip_in.shape[1]
-    token_core = seq // 2
-    token_rows = aligned(seq * length, length)
-    stays = core == token_core
-    clip_copies = []
-    for turn in range(2):
-        target = {"seq": 2 * core + turn, "fsdp": 2 * chip + token_core}
-        slot = 2 * lax.rem(seq, 2)
-        copies = [
-            remote(
-                clip_in.at[turn], clip_out.at[token_rows, :], m_send.at[2 * turn], m_recv.at[slot], target
-            ),
-            remote(
-                coord_in.at[turn], coord_out.at[seq], m_send.at[2 * turn + 1], m_recv.at[slot + 1], target
-            ),
-        ]
-        away = jnp.logical_not(jnp.logical_and(stays, lax.rem(seq, 2) == turn))
-        clip_copies.append((away, copies))
-
-        @pl.when(away)
-        def _(copies=copies):
-            for copy in copies:
-                copy.start()
-
-    clip_load.wait()
-    clip_store = pltpu.make_async_copy(clip_slab, clip_out.at[token_rows, :], m_load.at[1])
-
-    @pl.when(stays)
-    def _():
-        clip_store.start()
-        coord_out[seq] = coord_in[lax.rem(seq, 2)]
-
-    vec_out[2 * chip + core] = vec_in[...]
-    vec_swap = remote(
-        vec_in, vec_out.at[2 * chip + core], m_send.at[8], m_recv.at[8], other
-    )
-    vec_swap.start()
-
-    def clip_arrived():
-        for part in range(2):
-            came = jnp.logical_not(jnp.logical_and(stays, lax.rem(seq, 2) == part))
-
-            @pl.when(came)
-            def _(part=part):
-                rows = aligned((2 * core + part) * length, length)
-                remote(
-                    clip_in.at[0], clip_out.at[rows, :], m_send.at[0], m_recv.at[2 * part], other
-                ).wait_recv()
-                remote(
-                    coord_in.at[0],
-                    coord_out.at[2 * core + part],
-                    m_send.at[0],
-                    m_recv.at[2 * part + 1],
-                    other,
-                ).wait_recv()
-
-        @pl.when(stays)
-        def _():
-            clip_store.wait()
-
-        rows = clip_out.at[aligned(core * 2 * length, 2 * length), :]
-        swaps = [remote(rows, rows, m_send.at[4], m_recv.at[4], other)]
-        ref = coord_out.at[pl.ds(2 * core, 2)]
-        swaps.append(remote(ref, ref, m_send.at[5], m_recv.at[5], other))
-        for copy in swaps:
-            copy.start()
-        return swaps
-
-    vec_copies = []
-
-    def vec_hop(hop):
-        (vec_copies[-1] if vec_copies else vec_swap).wait_recv()
-        ref = vec_out.at[pl.ds(2 * at.back(hop), 2)]
-        copy = remote(ref, ref, m_send.at[9 + hop], m_recv.at[9 + hop], up_chip)
-        copy.start()
-        vec_copies.append(copy)
-
-    swaps, prepared = {}, []
-
-    def prepare():
-        if len(prepared) == len(items):
-            return
-        idx = len(prepared)
-        name, layer = items[idx]
-        prepared.append(name)
-        slab = slabs[name]
-        loads[name, layer].wait()
-        swaps[idx] = None
-        if name in ("down", "proj"):
-            full = down_full if name == "down" else proj_full
-            slab[layer] = full[layer].astype(BF)
-            return
-        full, away, kinds = (
-            (qkv_full, qkv_away, 3) if name == "qkv" else (up_full, up_away, 1)
-        )
-        half, columns = full.shape[1], full.shape[2]
-        width = columns // (kinds * 2 * ring)
-        rows = aligned(core * half, half)
-        for pair in range(ring):
-            for kind in range(kinds):
-                place = slice((pair * kinds + kind) * width, (pair * kinds + kind + 1) * width)
-                for ref, which in ((None, core), (away, 1 - core)):
-                    start = (kind * 2 * ring + 2 * pair + which) * width
-                    block = full[layer, :, aligned(start, width)].astype(BF)
-                    if ref is None:
-                        slab[layer, rows, place] = block
-                    else:
-                        ref[layer, :, place] = block
-        swaps[idx] = remote(
-            away.at[layer], slab.at[layer, rows, :], c_send.at[idx], c_recv.at[idx], other
-        )
-        swaps[idx].start()
-
-    hops = ring - 1
-    order = []
-    for first in range(0, len(items), 2):
-        for hop in range(hops):
-            order += [(first, hop), (first + 1, hop)]
-
-    stores = []
-    z_copies = {}
-
-    def begin(idx):
-        name, layer = items[idx]
-        if swaps[idx] is not None:
-            swaps[idx].wait_recv()
-        store = pltpu.make_async_copy(
-            slabs[name].at[layer], place(name, layer, chip, None), l_out.at[idx]
-        )
-        store.start()
-        stores.append(store)
-
-    def z_copy(idx, hop):
-        name, layer = items[idx]
-        part = None if name == "proj" else seq
-        source = place(name, layer, lax.rem(chip - hop + ring, ring), part)
-        if hop == 0:
-            if part is None:
-                from_ref = slabs[name].at[layer]
-            else:
-                size = slabs[name].shape[1] // 4
-                from_ref = slabs[name].at[layer, pl.ds(pl.multiple_of(seq * size, size), size), :]
-        else:
-            from_ref = source
-        slot = idx * hops + hop
-        copy = remote(from_ref, source, z_send.at[slot], z_recv.at[slot], up_chip)
-        copy.start()
-        z_copies[idx, hop] = copy
-
-    plane, far = {}, {}
-
-    def plane_copies(idx, hop):
-        name, layer = items[idx]
-        ref = place(name, layer, lax.rem(chip - hop - 1 + ring, ring), seq)
-        slot = 2 * (idx * hops + hop)
-        plane[idx, hop] = [
-            remote(ref, ref, p_send.at[slot], p_recv.at[slot], over_x),
-            remote(ref, ref, p_send.at[slot + 1], p_recv.at[slot + 1], over_y),
-        ]
-        for copy in plane[idx, hop]:
-            copy.start()
-
-    def far_copies(idx, hop):
-        name, layer = items[idx]
-        slot = 2 * (idx * hops + hop)
-        size = slabs[name].shape[1] // 4
-        half = size // 2
-        base = lax.rem(chip - hop - 1 + ring, ring) * 4 * size
-        for copy in plane[idx, hop]:
-            copy.wait_recv()
-        made = []
-        for turn, (origin, target) in enumerate(((near_y, over_x), (near_x, over_y))):
-            rows = pl.ds(pl.multiple_of(base + origin * size + turn * half, half), half)
-            ref = outs[name].at[layer, rows, :]
-            made.append(
-                remote(ref, ref, d_send.at[slot + turn], d_recv.at[slot + turn], target)
-            )
-        far[idx, hop] = made
-        for copy in made:
-            copy.start()
-
-    pending = []
-    proj_swaps = []
-    clip_swaps = []
-    prepare()
-    prepare()
-    begin(0)
-    z_copy(0, 0)
-    begin(1)
-    z_copy(1, 0)
-    prepare()
-    prepare()
-    for event, (idx, hop) in enumerate(order):
-        if event == 2:
-            clip_swaps = clip_arrived()
-        if 3 <= event < 3 + hops:
-            vec_hop(event - 3)
-        if event % 2 == 1:
-            prepare()
-        z_copies[idx, hop].wait_recv()
-        if hop + 1 < hops:
-            z_copy(idx, hop + 1)
-        elif idx + 2 < len(items):
-            begin(idx + 2)
-            z_copy(idx + 2, 0)
-        name, layer = items[idx]
-        if name == "proj":
-            if hop + 1 == hops:
-                stores[idx].wait()
-                slot = len(items) + layer
-                swap = remote(
-                    proj_out.at[layer, 0],
-                    proj_out.at[layer, 1],
-                    c_send.at[slot],
-                    c_recv.at[slot],
-                    other,
-                )
-                swap.start()
-                proj_swaps.append(swap)
-        else:
-            plane_copies(idx, hop)
-            pending.append((idx, hop))
-            if len(pending) > 1:
-                far_copies(*pending.pop(0))
-    while pending:
-        far_copies(*pending.pop(0))
-
-    for key, made in far.items():
-        for copy in made:
-            copy.wait()
-    for made in plane.values():
-        for copy in made:
-            copy.wait_send()
-    for copy in z_copies.values():
-        copy.wait_send()
-    for copy in swaps.values():
-        if copy is not None:
-            copy.wait_send()
-    for copy in proj_swaps + clip_swaps:
-        copy.wait()
-    vec_copies[-1].wait_recv()
-    for copy in [vec_swap] + vec_copies:
-        copy.wait_send()
-    for away, copies in clip_copies:
-
-        @pl.when(away)
-        def _(copies=copies):
-            for copy in copies:
-                copy.wait_send()
-
-    for idx, store in enumerate(stores):
-        if items[idx][0] != "proj":
-            store.wait()
-
-
-def gather_weights(qkv, up, down, proj, clips, coords, vectors):
-    layers, rows, width = proj.shape
-    parts = lax.axis_size("fsdp")
-    ring = parts // 2
-    count = 4 * layers
-    hops = ring - 1
-    anywhere = pl.BlockSpec(memory_space=pl.ANY)
-    vmem = pl.BlockSpec(memory_space=pltpu.VMEM)
-    dma = pltpu.SemaphoreType.DMA
-    down_rows = down.shape[1]
-    halves = qkv.shape[2] // 2, up.shape[2] // 2
-    shapes = [
-        ((layers, parts * rows, halves[0]), BF),
-        ((layers, parts * rows, halves[1]), BF),
-        ((layers, ring * down_rows, width), BF),
-        ((layers, 2, ring * rows, width), BF),
-        ((4 * clips.shape[1], width), F32),
-        ((4,) + coords.shape[1:], jnp.int32),
-        ((parts,) + vectors.shape, F32),
-    ]
-    return pl.pallas_call(
-        gather_kernel,
-        in_specs=[anywhere] * 5 + [vmem] * 2,
-        out_specs=[anywhere] * 5 + [vmem] * 2,
-        out_shape=[jax.ShapeDtypeStruct(*shape) for shape in shapes],
-        scratch_shapes=[
-            pltpu.VMEM(qkv.shape, F32),
-            pltpu.VMEM(up.shape, F32),
-            pltpu.VMEM(down.shape, F32),
-            pltpu.VMEM(proj.shape, F32),
-            pltpu.VMEM((layers, rows, halves[0]), BF),
-            pltpu.VMEM((layers, rows, halves[1]), BF),
-            pltpu.VMEM((layers, 2 * rows, halves[0]), BF),
-            pltpu.VMEM((layers, 2 * rows, halves[1]), BF),
-            pltpu.VMEM((layers, down_rows, width), BF),
-            pltpu.VMEM((layers, rows, width), BF),
-            pltpu.VMEM(clips.shape[1:], F32),
-            dma((count * hops,)),
-            dma((count * hops,)),
-            dma((2 * count * hops,)),
-            dma((2 * count * hops,)),
-            dma((2 * count * hops,)),
-            dma((2 * count * hops,)),
-            dma((count + layers,)),
-            dma((count + layers,)),
-            dma((count,)),
-            dma((count,)),
-            dma((9 + hops,)),
-            dma((9 + hops,)),
-            dma((2,)),
-        ],
-        compiler_params=pltpu.CompilerParams(
-            collective_id=0, has_side_effects=True, vmem_limit_bytes=VMEM_LIMIT
-        ),
-        cost_estimate=pl.CostEstimate(flops=0, bytes_accessed=600_000_000, transcendentals=0),
-        name="gather_weights",
-    )(qkv, up, down, proj, clips, coords, vectors)
 
 
 ADD_ROWS = 32
@@ -1526,11 +1086,6 @@
     return center * inverse, inverse
 
 
-def norm_forward(hidden, gain, shift):
-    scaled, _ = norm_parts(hidden)
-    return (scaled * gain + shift).astype(BF)
-
-
 def norm_backward(hidden, gain, grad):
     scaled, inverse = norm_parts(hidden)
     entry = grad * gain
@@ -1558,11 +1113,684 @@
     return lax.dot_general(left, right, (((0,), (0,)), ((), ())), preferred_element_type=F32)
 
 
-def own_bias(bias, core, fsdp_parts, kinds):
-    width = bias.shape[0] // (kinds * fsdp_parts)
-    view = bias.reshape(kinds, fsdp_parts // 2, 2, width)
-    mine = pick(view, core, 2)
-    return mine.transpose(1, 0, 2).reshape(-1)
+def rotation_tables(packed):
+    lane = lax.broadcasted_iota(jnp.int32, packed.shape, 1)
+    first = lane % HEAD_DIM < HEAD_DIM // 2
+    turned = pltpu.roll(packed, HEAD_DIM // 2, 1)
+    return jnp.where(first, packed, turned), jnp.where(first, -turned, packed)
+
+
+def each_block(count, body):
+    @pl.loop(0, count)
+    def _(step):
+        body(aligned(step * ROWS_Q, ROWS_Q))
+
+
+class Forward:
+    def __init__(self, at, refs, layers):
+        self.at, self.refs, self.layers = at, refs, layers
+        self.blocks = refs.res.shape[0] // ROWS_Q
+        self.pairs = refs.mixed.shape[1] // PAIR
+        self.saves, self.slot = [], 0
+        self.mixed_copies, self.part_copies = {}, {}
+
+    def save(self, src, dst):
+        copy = pltpu.make_async_copy(src, dst, self.refs.save_sem.at[self.slot])
+        self.slot += 1
+        copy.start()
+        self.saves.append(copy)
+        return copy
+
+    def settle(self):
+        for copy in self.saves:
+            copy.wait()
+        self.saves = []
+
+    def bring(self, pairs):
+        copies = []
+        for src, dst in pairs:
+            copies.append(pltpu.make_async_copy(src, dst, self.refs.save_sem.at[self.slot]))
+            self.slot += 1
+        for copy in copies:
+            copy.start()
+        for copy in copies:
+            copy.wait()
+
+    def vec(self, layer, row, width):
+        return self.refs.vecs[layer, row : row + 1, 0:width]
+
+    def unpack_vectors(self):
+        refs, at = self.refs, self.at
+        ring = at.ring
+        per_shard = refs.vec_rows
+        for layer in range(self.layers):
+            places = [(row, row // 8, row % 8) for row in range(48)]
+            for pair in range(ring):
+                for kind in range(3):
+                    places.append((48 + kind * 8 + 2 * pair + at.core, 6, pair * 3 + kind))
+                for part in range(4):
+                    places.append((72 + (2 * pair + at.core) * 4 + part, 7, pair * 4 + part))
+            for source, row, block in places:
+                shard, entry = source // per_shard, layer * per_shard + source % per_shard
+                if not isinstance(source, int):
+                    shard = lax.div(source, per_shard)
+                    entry = layer * per_shard + lax.rem(source, per_shard)
+                refs.vecs[layer, row : row + 1, block * 128 : (block + 1) * 128] = refs.vec_out[
+                    shard, pl.ds(entry, 1), :
+                ]
+
+    def normed(self, rows, layer, first):
+        hidden = self.refs.res[rows, :]
+        scaled, _ = norm_parts(hidden)
+        width = hidden.shape[1]
+        return (scaled * self.vec(layer, first, width) + self.vec(layer, first + 1, width)).astype(BF)
+
+    def qkv(self, layer, weight):
+        refs = self.refs
+        width = weight.shape[1]
+        self.settle()
+        self.bring([(weight, refs.w_one.at[:, pl.ds(0, width)])])
+
+        def body(rows):
+            normed = self.normed(rows, layer, 0)
+            refs.norm[rows, :] = normed
+            for pair in range(self.pairs):
+                cols = slice(pair * 3 * PAIR, (pair + 1) * 3 * PAIR)
+                block = dot(normed, refs.w_one[:, cols]) + refs.vecs[layer, 6:7, cols]
+                cosine, sine = rotation_tables(refs.tables[rows, :])
+                for kind in range(3):
+                    part = block[:, kind * PAIR : (kind + 1) * PAIR]
+                    if kind < 2:
+                        part = part * cosine + swap_halves(part) * sine
+                    start = pair * 3 * PAIR + kind * PAIR
+                    refs.low[rows, start : start + PAIR] = part.astype(BF)
+
+        each_block(self.blocks, body)
+        self.save(refs.norm, refs.normed_out[layer])
+        self.save(refs.low, refs.low_out[layer])
+
+    def attend(self, layer, pair):
+        refs = self.refs
+        base = pair * 3 * PAIR
+        key_rows = refs.low[:, base + PAIR : base + 2 * PAIR]
+        for head in range(2):
+            refs.keys[head] = head_mask(key_rows, head)
+        refs.values_t[...] = refs.low[:, base + 2 * PAIR : base + 3 * PAIR].astype(F32).T.astype(BF)
+
+        def body(rows):
+            block = refs.low[rows, base : base + PAIR] * jnp.asarray(HEAD_DIM**-0.5, BF)
+            outs = []
+            for head in range(2):
+                scores = lax.dot_general(refs.keys[head], block, NT, preferred_element_type=F32)
+                top = jnp.max(scores, axis=0, keepdims=True)
+                exponent = jnp.exp(scores - top)
+                total = jnp.sum(exponent, axis=0, keepdims=True)
+                refs.lse_out[layer, pair, head : head + 1, rows] = top + jnp.log(total)
+                probs = (exponent * (1.0 / total)).astype(BF)
+                outs.append(dot(refs.values_t[head * HEAD_DIM : (head + 1) * HEAD_DIM], probs))
+            refs.mixed[rows, pair * PAIR : (pair + 1) * PAIR] = (
+                jnp.concatenate(outs, axis=0).T.astype(BF)
+            )
+
+        each_block(self.blocks, body)
+        slot = layer * (self.pairs + 2) + pair
+        cols = pl.ds(pair * PAIR, PAIR)
+        copy = remote(
+            refs.mixed.at[:, cols],
+            refs.mixed_other.at[:, cols],
+            refs.x_send.at[slot],
+            refs.x_recv.at[slot],
+            self.at.other,
+        )
+        copy.start()
+        self.mixed_copies[layer, pair] = copy
+
+    def project(self, layer, own, other):
+        refs = self.refs
+        half = own.shape[0]
+        self.bring(
+            [
+                (own, refs.w_two.at[pl.ds(0, half), :]),
+                (other, refs.w_two.at[pl.ds(half, half), :]),
+            ]
+        )
+        self.settle()
+        for pair in range(self.pairs):
+            self.mixed_copies[layer, pair].wait()
+        width = refs.res.shape[1]
+
+        def body(rows):
+            total = dot(refs.mixed[rows, :], refs.w_two[0:half, :])
+            total = total + dot(refs.mixed_other[rows, :], refs.w_two[half : 2 * half, :])
+            refs.res[rows, :] = refs.res[rows, :] + total + self.vec(layer, 4, width)
+            refs.norm[rows, :] = self.normed(rows, layer, 2)
+
+        each_block(self.blocks, body)
+        self.save(refs.mixed, refs.mixed_out[layer])
+        self.save(refs.res, refs.after_out[layer])
+        self.save(refs.norm, refs.normed_two_out[layer])
+
+    def hidden_units(self, layer, half, up_weight, down_weight):
+        refs = self.refs
+        if half == 0:
+            self.settle()
+            self.bring([(up_weight, refs.w_one), (down_weight, refs.w_two)])
+        width = refs.res.shape[1]
+        tiles = refs.w_one.shape[1] // 512
+        blocks = self.blocks // 2
+
+        @pl.loop(half * blocks, (half + 1) * blocks)
+        def _(step):
+            rows = aligned(step * ROWS_Q, ROWS_Q)
+
+            @pl.loop(0, tiles)
+            def _(tile):
+                cols = aligned(tile * 512, 512)
+                upward = dot(refs.norm[rows, :], refs.w_one[:, cols]) + refs.vecs[layer, 7:8, cols]
+                active, slope = gelu_and_slope(upward)
+                refs.act[rows, cols] = active.astype(BF)
+                refs.slope[rows, cols] = slope.astype(BF)
+
+            part = dot(refs.act[rows, :], refs.w_two[...])
+            refs.res[rows, :] = refs.res[rows, :] + part + self.vec(layer, 5, width)
+            refs.part[rows, :] = part.astype(BF)
+
+        rows = pl.ds(half * blocks * ROWS_Q, blocks * ROWS_Q)
+        slot = layer * (self.pairs + 2) + self.pairs + half
+        copy = remote(
+            refs.part.at[rows, :],
+            refs.part_other.at[rows, :],
+            refs.x_send.at[slot],
+            refs.x_recv.at[slot],
+            self.at.other,
+        )
+        copy.start()
+        self.part_copies[layer, half] = copy
+        if half == 1:
+            self.save(refs.act, refs.active_out[layer])
+            self.save(refs.slope, refs.slope_out[layer])
+
+    def join(self, layer):
+        refs = self.refs
+        for half in range(2):
+            self.part_copies[layer, half].wait()
+
+        def body(rows):
+            refs.res[rows, :] = refs.res[rows, :] + refs.part_other[rows, :].astype(F32)
+
+        each_block(self.blocks, body)
+        self.save(refs.res, refs.result_out[layer])
+
+
+WEIGHTS = ("qkv", "proj", "up", "down")
+
+
+def forward_kernel(names, layers, vec_rows, *operands):
+    refs = SimpleNamespace(**dict(zip(names, operands)))
+    for name in (*WEIGHTS, "proj_two", "normed", "low", "mixed", "after", "normed_two", "active", "slope", "result"):
+        label = name + "_out"
+        setattr(refs, label, [getattr(refs, label + str(layer)) for layer in range(layers)])
+    refs.vec_rows = vec_rows
+    at = Places()
+    ring, seq, chip, core = at.ring, at.seq, at.chip, at.core
+    full = {name: getattr(refs, name + "_full") for name in WEIGHTS}
+    source = {name: getattr(refs, name + "_in") for name in WEIGHTS}
+    slabs = {name: getattr(refs, name + "_slab") for name in WEIGHTS}
+    outs = {name: getattr(refs, name + "_out") for name in WEIGHTS}
+    items = [(name, layer) for layer in range(layers) for name in WEIGHTS]
+    loads = {}
+
+    def start_load(name, layer):
+        copy = pltpu.make_async_copy(
+            source[name].at[layer], full[name], refs.l_in.at[items.index((name, layer))]
+        )
+        copy.start()
+        loads[name, layer] = copy
+
+    for name in WEIGHTS:
+        start_load(name, 0)
+    barrier = pltpu.get_barrier_semaphore()
+    for target in (at.other, at.up, at.down):
+        pl.semaphore_signal(barrier, inc=1, device_id=target, device_id_type=pl.DeviceIdType.MESH)
+    for step in range(1, 4):
+        for half in range(2):
+            pl.semaphore_signal(
+                barrier,
+                inc=1,
+                device_id={"fsdp": 2 * chip + half, "seq": seq ^ step},
+                device_id_type=pl.DeviceIdType.MESH,
+            )
+    pl.semaphore_wait(barrier, 9)
+
+    length = refs.clip_in.shape[1]
+    token_core = seq // 2
+    token_rows = aligned(seq * length, length)
+    stays = core == token_core
+
+    class Move:
+        def __init__(self, base, pairs):
+            self.base, self.pairs, self.copies = base, pairs, []
+
+        def start(self):
+            for turn in range(2):
+                target = {"seq": 2 * core + turn, "fsdp": 2 * chip + token_core}
+                away = jnp.logical_not(jnp.logical_and(stays, lax.rem(seq, 2) == turn))
+                copies = [
+                    remote(
+                        src.at[turn],
+                        place(seq),
+                        refs.m_send.at[self.base + 2 * turn + idx],
+                        refs.m_recv.at[self.base + 2 * lax.rem(seq, 2) + idx],
+                        target,
+                    )
+                    for idx, (src, place) in enumerate(self.pairs)
+                ]
+                self.copies.append((away, copies))
+
+                @pl.when(away)
+                def _(copies=copies):
+                    for copy in copies:
+                        copy.start()
+
+            @pl.when(stays)
+            def _():
+                for idx, (src, place) in enumerate(self.pairs):
+                    bounce = refs.clip_slab if idx == 0 else refs.table_slab
+                    sem = refs.m_load.at[self.base // 6 * 2 + idx]
+                    load = pltpu.make_async_copy(src.at[lax.rem(seq, 2)], bounce, sem)
+                    load.start()
+                    load.wait()
+                    store = pltpu.make_async_copy(bounce, place(seq), sem)
+                    store.start()
+                    store.wait()
+
+        def swap(self):
+            for part in range(2):
+                came = jnp.logical_not(jnp.logical_and(stays, lax.rem(seq, 2) == part))
+
+                @pl.when(came)
+                def _(part=part):
+                    for idx, (src, place) in enumerate(self.pairs):
+                        remote(
+                            src.at[0],
+                            place(2 * core + part),
+                            refs.m_send.at[self.base],
+                            refs.m_recv.at[self.base + 2 * part + idx],
+                            at.other,
+                        ).wait_recv()
+
+            self.swaps = []
+            for idx, (src, place) in enumerate(self.pairs):
+                for part in range(2):
+                    slot = 24 + self.base // 6 * 4 + 2 * idx + part
+                    ref = place(2 * core + part)
+                    self.swaps.append(
+                        remote(ref, ref, refs.m_send.at[slot], refs.m_recv.at[slot], at.other)
+                    )
+            for copy in self.swaps:
+                copy.start()
+
+        def arrived(self):
+            for copy in self.swaps:
+                copy.wait_recv()
+
+        def drain(self):
+            for copy in self.swaps:
+                copy.wait_send()
+            for away, copies in self.copies:
+
+                @pl.when(away)
+                def _(copies=copies):
+                    for copy in copies:
+                        copy.wait_send()
+
+    def chunk_of(ref):
+        return lambda number: ref.at[aligned(number * length, length), :]
+
+    tokens = Move(0, [(refs.clip_in, chunk_of(refs.clip_out)), (refs.table_in, chunk_of(refs.table_out))])
+    cotangents = Move(6, [(refs.cot_in, chunk_of(refs.cot_out))])
+    tokens.start()
+
+    refs.vec_out[2 * chip + core] = refs.vec_in[...]
+    vec_swap = remote(
+        refs.vec_in, refs.vec_out.at[2 * chip + core], refs.m_send.at[16], refs.m_recv.at[16], at.other
+    )
+    vec_swap.start()
+    vec_copies = [vec_swap]
+
+    def vec_hop(hop):
+        vec_copies[-1].wait_recv()
+        ref = refs.vec_out.at[pl.ds(2 * at.back(hop), 2)]
+        slot = 17 + hop
+        copy = remote(ref, ref, refs.m_send.at[slot], refs.m_recv.at[slot], at.up)
+        copy.start()
+        vec_copies.append(copy)
+
+    def place(name, layer, chip_at, part):
+        slab = slabs[name].shape[1]
+        if part is None:
+            return outs[name][layer].at[aligned(chip_at * slab, slab), :]
+        size = slab // 4
+        return outs[name][layer].at[aligned(chip_at * slab + part * size, size), :]
+
+    swaps, prepared, stores = {}, [], []
+
+    def prepare():
+        if len(prepared) == len(items):
+            return
+        idx = len(prepared)
+        name, layer = items[idx]
+        prepared.append(name)
+        slab = slabs[name]
+        loads[name, layer].wait()
+        swaps[idx] = None
+        if name in ("down", "proj"):
+            slab[layer] = full[name][...].astype(BF)
+        else:
+            away, kinds = (refs.qkv_away, 3) if name == "qkv" else (refs.up_away, 1)
+            half, columns = full[name].shape
+            width = columns // (kinds * 2 * ring)
+            rows = aligned(core * half, half)
+            for pair in range(ring):
+                for kind in range(kinds):
+                    cols = slice((pair * kinds + kind) * width, (pair * kinds + kind + 1) * width)
+                    for mine in (True, False):
+                        which = core if mine else 1 - core
+                        start = (kind * 2 * ring + 2 * pair + which) * width
+                        block = full[name][:, aligned(start, width)].astype(BF)
+                        if mine:
+                            slab[layer, rows, cols] = block
+                        else:
+                            away[layer, :, cols] = block
+            swaps[idx] = remote(
+                away.at[layer],
+                slab.at[layer, rows, :],
+                refs.c_send.at[idx],
+                refs.c_recv.at[idx],
+                at.other,
+            )
+            swaps[idx].start()
+        if layer + 1 < layers:
+            start_load(name, layer + 1)
+
+    hops = ring - 1
+    order = []
+    for first in range(0, len(items), 2):
+        for hop in range(hops):
+            order += [(first, hop), (first + 1, hop)]
+    z_copies, plane, far, proj_swaps = {}, {}, {}, {}
+
+    def begin(idx):
+        name, layer = items[idx]
+        if swaps[idx] is not None:
+            swaps[idx].wait_recv()
+        store = pltpu.make_async_copy(
+            slabs[name].at[layer], place(name, layer, chip, None), refs.l_out.at[idx]
+        )
+        store.start()
+        stores.append(store)
+
+    def z_copy(idx, hop):
+        name, layer = items[idx]
+        part = None if name == "proj" else seq
+        target = place(name, layer, at.back(hop), part)
+        from_ref = target
+        if hop == 0:
+            from_ref = slabs[name].at[layer]
+            if part is not None:
+                size = slabs[name].shape[1] // 4
+                from_ref = slabs[name].at[layer, aligned(seq * size, size), :]
+        slot = idx * hops + hop
+        copy = remote(from_ref, target, refs.z_send.at[slot], refs.z_recv.at[slot], at.up)
+        copy.start()
+        z_copies[idx, hop] = copy
+
+    def plane_copies(idx, hop):
+        name, layer = items[idx]
+        ref = place(name, layer, at.back(hop + 1), seq)
+        slot = 2 * (idx * hops + hop)
+        plane[idx, hop] = [
+            remote(ref, ref, refs.p_send.at[slot], refs.p_recv.at[slot], at.over_x),
+            remote(ref, ref, refs.p_send.at[slot + 1], refs.p_recv.at[slot + 1], at.over_y),
+        ]
+        for copy in plane[idx, hop]:
+            copy.start()
+
+    def far_copies(idx, hop):
+        name, layer = items[idx]
+        slot = 2 * (idx * hops + hop)
+        size = slabs[name].shape[1] // 4
+        half = size // 2
+        base = at.back(hop + 1) * 4 * size
+        for copy in plane[idx, hop]:
+            copy.wait_recv()
+        made = []
+        for turn, (origin, target) in enumerate(((at.near_y, at.over_x), (at.near_x, at.over_y))):
+            ref = outs[name][layer].at[aligned(base + origin * size + turn * half, half), :]
+            made.append(
+                remote(ref, ref, refs.d_send.at[slot + turn], refs.d_recv.at[slot + turn], target)
+            )
+        far[idx, hop] = made
+        for copy in made:
+            copy.start()
+
+    pending = []
+
+    def flush(keep):
+        while len(pending) > keep:
+            far_copies(*pending.pop(0))
+
+    def event(number):
+        idx, hop = order[number]
+        z_copies[idx, hop].wait_recv()
+        if hop + 1 < hops:
+            z_copy(idx, hop + 1)
+        elif idx + 2 < len(items):
+            begin(idx + 2)
+            z_copy(idx + 2, 0)
+        name, layer = items[idx]
+        if name == "proj":
+            if hop + 1 == hops:
+                stores[idx].wait()
+                slot = len(items) + layer
+                proj_swaps[layer] = remote(
+                    outs["proj"][layer],
+                    refs.proj_two_out[layer],
+                    refs.c_send.at[slot],
+                    refs.c_recv.at[slot],
+                    at.other,
+                )
+                proj_swaps[layer].start()
+        else:
+            plane_copies(idx, hop)
+            pending.append((idx, hop))
+            flush(1)
+        prepare()
+
+    def complete(name, layer):
+        idx = items.index((name, layer))
+        if name == "proj":
+            proj_swaps[layer].wait_recv()
+            return
+        stores[idx].wait()
+        flush(0)
+        for hop in range(hops):
+            for copy in far[idx, hop]:
+                copy.wait_recv()
+
+    work = Forward(at, refs, layers)
+
+    def take_tokens():
+        tokens.arrived()
+        vec_copies[-1].wait_recv()
+        work.bring([(refs.clip_out, refs.res), (refs.table_out, refs.tables)])
+        work.unpack_vectors()
+
+    def qkv(layer):
+        complete("qkv", layer)
+        work.qkv(layer, outs["qkv"][layer])
+
+    def project(layer):
+        complete("proj", layer)
+        work.project(layer, outs["proj"][layer], refs.proj_two_out[layer])
+
+    def hidden_units(layer, half):
+        if half == 0:
+            complete("up", layer)
+            complete("down", layer)
+        work.hidden_units(layer, half, outs["up"][layer], outs["down"][layer])
+
+    prepare()
+    prepare()
+    begin(0)
+    z_copy(0, 0)
+    begin(1)
+    z_copy(1, 0)
+    prepare()
+    prepare()
+    per_layer = 4 * hops
+    chunks = []
+    for layer in range(layers):
+        first = layer * per_layer + 2 * hops
+        if layer == 0:
+            chunks.append((first, take_tokens))
+        chunks.append((first + 1, partial(qkv, layer)))
+        for pair in range(work.pairs):
+            chunks.append((first + 1 + pair, partial(work.attend, layer, pair)))
+        chunks.append((first + 5, partial(project, layer)))
+        chunks.append((first + 7, partial(hidden_units, layer, 0)))
+        chunks.append((first + 8, partial(hidden_units, layer, 1)))
+        chunks.append((first + 9, partial(work.join, layer)))
+    for number in range(len(order)):
+        while chunks and chunks[0][0] <= number:
+            chunks.pop(0)[1]()
+        if number == 2:
+            tokens.swap()
+        if 3 <= number < 3 + hops:
+            vec_hop(number - 3)
+        if number == per_layer:
+            cotangents.start()
+        if number == per_layer + 6:
+            cotangents.swap()
+        event(number)
+    flush(0)
+    for _, chunk in chunks:
+        chunk()
+
+    work.settle()
+    cotangents.arrived()
+    for made in plane.values():
+        for copy in made:
+            copy.wait_send()
+    for made in far.values():
+        for copy in made:
+            copy.wait_send()
+    for copy in z_copies.values():
+        copy.wait_send()
+    for copy in swaps.values():
+        if copy is not None:
+            copy.wait_send()
+    for copy in proj_swaps.values():
+        copy.wait_send()
+    for copy in vec_copies:
+        copy.wait_send()
+    tokens.drain()
+    cotangents.drain()
+
+
+def forward(qkv, up, down, proj, clips, cots, tables, vectors, vec_rows):
+    layers, rows, width = proj.shape
+    parts = lax.axis_size("fsdp")
+    ring = parts // 2
+    count, hops = 4 * layers, ring - 1
+    length = 4 * clips.shape[1]
+    down_rows = down.shape[1]
+    qkv_half, up_half = qkv.shape[2] // 2, up.shape[2] // 2
+    pairs = qkv_half // (3 * PAIR)
+    inputs = {
+        "qkv_in": qkv, "up_in": up, "down_in": down, "proj_in": proj, "clip_in": clips, "cot_in": cots,
+        "table_in": tables, "vec_in": vectors,
+    }
+    outputs = {}
+    for layer in range(layers):
+        for name, shape, dtype in (
+            ("qkv", (parts * rows, qkv_half), BF),
+            ("up", (parts * rows, up_half), BF),
+            ("down", (ring * down_rows, width), BF),
+            ("proj", (ring * rows, width), BF),
+            ("proj_two", (ring * rows, width), BF),
+            ("normed", (length, width), BF),
+            ("low", (length, qkv_half), BF),
+            ("mixed", (length, pairs * PAIR), BF),
+            ("after", (length, width), F32),
+            ("normed_two", (length, width), BF),
+            ("active", (length, up_half), BF),
+            ("slope", (length, up_half), BF),
+            ("result", (length, width), F32),
+        ):
+            outputs[name + "_out" + str(layer)] = (shape, dtype)
+    outputs["clip_out"] = ((length, width), F32)
+    outputs["cot_out"] = ((length, width), F32)
+    outputs["table_out"] = ((length, PAIR), F32)
+    outputs["vec_out"] = ((parts,) + vectors.shape, F32)
+    outputs["lse_out"] = ((layers, pairs, 8, length), F32)
+    in_vmem = ("vec_in", "vec_out", "lse_out")
+    anywhere = pl.BlockSpec(memory_space=pl.ANY)
+    vmem = pl.BlockSpec(memory_space=pltpu.VMEM)
+    dma = pltpu.SemaphoreType.DMA
+    scratch = {
+        "qkv_full": pltpu.VMEM(qkv.shape[1:], F32),
+        "up_full": pltpu.VMEM(up.shape[1:], F32),
+        "down_full": pltpu.VMEM(down.shape[1:], F32),
+        "proj_full": pltpu.VMEM(proj.shape[1:], F32),
+        "qkv_away": pltpu.VMEM((layers, rows, qkv_half), BF),
+        "up_away": pltpu.VMEM((layers, rows, up_half), BF),
+        "qkv_slab": pltpu.VMEM((layers, 2 * rows, qkv_half), BF),
+        "up_slab": pltpu.VMEM((layers, 2 * rows, up_half), BF),
+        "down_slab": pltpu.VMEM((layers, down_rows, width), BF),
+        "proj_slab": pltpu.VMEM((layers, rows, width), BF),
+        "clip_slab": pltpu.VMEM(clips.shape[1:], F32),
+        "table_slab": pltpu.VMEM(tables.shape[1:], F32),
+        "res": pltpu.VMEM((length, width), F32),
+        "tables": pltpu.VMEM((length, PAIR), F32),
+        "vecs": pltpu.VMEM((layers, 8, up_half), F32),
+        "norm": pltpu.VMEM((length, width), BF),
+        "low": pltpu.VMEM((length, qkv_half), BF),
+        "keys": pltpu.VMEM((2, length, PAIR), BF),
+        "values_t": pltpu.VMEM((PAIR, length), BF),
+        "mixed": pltpu.VMEM((length, pairs * PAIR), BF),
+        "mixed_other": pltpu.VMEM((length, pairs * PAIR), BF),
+        "w_one": pltpu.VMEM((width, up_half), BF),
+        "w_two": pltpu.VMEM((ring * down_rows, width), BF),
+        "act": pltpu.VMEM((length, up_half), BF),
+        "slope": pltpu.VMEM((length, up_half), BF),
+        "part": pltpu.VMEM((length, width), BF),
+        "part_other": pltpu.VMEM((length, width), BF),
+        "z_send": dma((count * hops,)), "z_recv": dma((count * hops,)),
+        "p_send": dma((2 * count * hops,)), "p_recv": dma((2 * count * hops,)),
+        "d_send": dma((2 * count * hops,)), "d_recv": dma((2 * count * hops,)),
+        "c_send": dma((count + layers,)), "c_recv": dma((count + layers,)),
+        "l_in": dma((count,)), "l_out": dma((count,)),
+        "m_send": dma((32,)), "m_recv": dma((32,)), "m_load": dma((4,)),
+        "x_send": dma((layers * (pairs + 2),)), "x_recv": dma((layers * (pairs + 2),)),
+        "save_sem": dma((16 * layers,)),
+    }
+    names = [*inputs, *outputs, *scratch]
+    results = pl.pallas_call(
+        partial(forward_kernel, names, layers, vec_rows),
+        in_specs=[vmem if name in in_vmem else anywhere for name in inputs],
+        out_specs=[vmem if name in in_vmem else anywhere for name in outputs],
+        out_shape=[jax.ShapeDtypeStruct(*shape) for shape in outputs.values()],
+        scratch_shapes=list(scratch.values()),
+        compiler_params=pltpu.CompilerParams(
+            collective_id=0, has_side_effects=True, vmem_limit_bytes=62 * 1024 * 1024
+        ),
+        cost_estimate=pl.CostEstimate(
+            flops=60_000_000_000, bytes_accessed=600_000_000, transcendentals=0
+        ),
+        name="forward",
+    )(*inputs.values())
+    return SimpleNamespace(**dict(zip(outputs, results)))
 
 
 def spread_bias(grad, core, fsdp_parts, kinds):
@@ -1607,24 +1835,6 @@
     core = lax.rem(shard, 2)
     even = lax.rem(seq, 2) == 0
 
-    def to_clips(item):
-        halves = []
-        for turn in range(2):
-            piece = jnp.where(even, item[turn], item[1 - turn])
-            pairs = []
-            for src_seq in range(seq_parts):
-                for src in range(parts):
-                    dst_seq = 2 * (src % 2) + (src_seq + turn) % 2
-                    dst = src - src % 2 + src_seq // 2
-                    pairs.append((src_seq * parts + src, dst_seq * parts + dst))
-            halves.append(lax.ppermute(piece, ("seq", "fsdp"), pairs))
-        mine = jnp.where(
-            even, jnp.stack([halves[0], halves[1]]), jnp.stack([halves[1], halves[0]])
-        )
-        other = swap_core(mine)
-        both = jnp.where(core == 0, jnp.stack([mine, other]), jnp.stack([other, mine]))
-        return both.reshape((4,) + item.shape[1:])
-
     def from_clips(item):
         mine = pick(item.reshape((2, 2, chunk_len) + item.shape[1:]), core)
         pieces = [None, None]
@@ -1641,55 +1851,43 @@
             even, jnp.stack([pieces[0], pieces[1]]), jnp.stack([pieces[1], pieces[0]])
         )
 
-    coord_rows = jnp.pad(jnp.swapaxes(patch_coords, 0, 1), ((0, 0), (0, 5), (0, 0)))
-    vector_rows = vector_params.astype(BF).astype(F32).reshape(-1)
-    vector_rows = jnp.pad(vector_rows, (0, -vector_rows.shape[0] % 1024)).reshape(8, -1)
-    qkv_all_w, up_all_w, down_all_w, proj_all_w, hidden, coords, vector_got = gather_weights(
-        qkv_weight, up_weight, down_weight, proj_weight, clip_tokens, coord_rows, vector_rows
-    )
-    layers = [
-        (qkv_all_w[idx], proj_all_w[idx, 0], proj_all_w[idx, 1], up_all_w[idx], down_all_w[idx])
-        for idx in range(layer_count)
-    ]
-    coords = jnp.swapaxes(coords[:, :3], 0, 1).reshape(3, 4 * chunk_len)
-    cosine, sine = rotary_tables(coords, HEAD_DIM // 2)
+    tables = []
+    for idx in range(batch_local):
+        cosine, sine = rotary_tables(patch_coords[:, idx], HEAD_DIM // 2)
+        tables.append(jnp.concatenate([cosine, sine, cosine, sine], axis=1))
+    share = vector_params.shape[1]
+    vector_rows = vector_params.astype(BF).astype(F32).reshape(-1, 128)
+    vector_rows = jnp.pad(vector_rows, ((0, -vector_rows.shape[0] % 8), (0, 0)))
+    kept = forward(
+        qkv_weight,
+        up_weight,
+        down_weight,
+        proj_weight,
+        clip_tokens,
+        out_cotangent,
+        jnp.stack(tables),
+        vector_rows,
+        share // 128,
+    )
+    vector_all = kept.vec_out.reshape(parts, -1)[:, : vector_params.size]
+    vector_all = vector_all.reshape(parts, layer_count, share).transpose(1, 0, 2)
+    vector_all = vector_all.reshape(layer_count, -1)
+    cosine, sine = kept.table_out[:, : HEAD_DIM // 2], kept.table_out[:, HEAD_DIM // 2 : HEAD_DIM]
     cos_wide = jnp.concatenate([cosine] * 4, axis=1)
     sin_wide = jnp.concatenate([-sine, sine, -sine, sine], axis=1)
-    vector_all = vector_got.reshape(parts, -1)[:, : vector_params.size]
-    vector_all = vector_all.reshape(parts, layer_count, -1).transpose(1, 0, 2)
-    vector_all = vector_all.reshape(layer_count, -1)
-
-    saved = []
-    for idx in range(layer_count):
-        qkv_w, proj_w, proj_other, up_w, down_w = layers[idx]
-        gain_one, shift_one, gain_two, shift_two, proj_bias, down_bias, qkv_bias, up_bias = pieces(
-            vector_all[idx]
-        )
-        qkv_bias = own_bias(qkv_bias, core, parts, 3)
-        up_bias = own_bias(up_bias, core, parts, 1)
-        normed = norm_forward(hidden, gain_one, shift_one)
-        qkv_all = dot(normed, qkv_w) + qkv_bias
-        mixed, low_all, lse = attend(qkv_all, cos_wide, sin_wide)
-        mixed_other = swap_core(mixed)
-        after_attn = hidden + (dot(mixed, proj_w) + dot(mixed_other, proj_other)) + proj_bias
-        normed_two = norm_forward(after_attn, gain_two, shift_two)
-        upward = dot(normed_two, up_w) + up_bias
-        active, slope = gelu_and_slope(upward)
-        active, slope = active.astype(BF), slope.astype(BF)
-        part = dot(active, down_w)
-        other = swap_core(part.astype(BF))
-        result = after_attn + (part + other.astype(F32)) + down_bias
-        saved.append((hidden, normed, low_all, lse, mixed, after_attn, normed_two, active, slope))
-        hidden = result
-    block_output = from_clips(hidden)
-
-    grad = to_clips(out_cotangent).reshape(4 * chunk_len, D)
+    block_output = from_clips(getattr(kept, "result_out" + str(layer_count - 1)))
+
+    grad = kept.cot_out
     sums = [None] * layer_count
     vector_sums = [None] * layer_count
     squares = jnp.zeros((8, 128), F32)
     for idx in reversed(range(layer_count)):
-        qkv_w, proj_w, proj_other, up_w, down_w = layers[idx]
-        entry, normed, low_all, lse, mixed, after_attn, normed_two, active, slope = saved[idx]
+        qkv_w, proj_w, up_w, down_w, normed, low_all, mixed, after_attn, normed_two, active, slope = [
+            getattr(kept, name + "_out" + str(idx))
+            for name in (*WEIGHTS, "normed", "low", "mixed", "after", "normed_two", "active", "slope")
+        ]
+        entry = kept.clip_out if idx == 0 else getattr(kept, "result_out" + str(idx - 1))
+        lse = kept.lse_out[idx]
         gain_one, shift_one, gain_two, shift_two, proj_bias, down_bias, qkv_bias, up_bias = pieces(
             vector_all[idx]
         )
@@ -1755,7 +1953,6 @@
     param_count = sum(master.size for master in masters) * parts
     factor = jnp.minimum(1.0, CLIP_RATIO * math.sqrt(float(param_count)) / (norm_value + 1e-06))
 
-    share = vector_params.shape[1]
     vector_total = jnp.stack([item[6].reshape(-1)[: 2 * share] for item in sums])
     vector_grad = lax.dynamic_slice_in_dim(vector_total, core * share, share, 1) / clip_count
     vector_new = adam_update(vector_params, vector_grad, first_vector, second_vector, factor)

time: 996 us -> 909 us (0.913)
  matrix products: 192 us -> 107 us
  Pallas kernels: 671 us -> 708 us
  waiting for transfers between devices: 32.4 us -> 0.02 us
    dot_general x10 -> x0, matrix products: 57.9 us -> none  [dot(): return jnp.dot(left, right, preferred_element_type=F32)]
    pallas_call x3 -> x1, Pallas kernels: 252 us -> 291 us  [forward(): pl.pallas_call(partial(forward_kernel, names, layers, vec_rows), in_specs...]
    ppermute x2 -> x0, waiting for transfers between devices: 25.4 us -> none  [to_clips(): halves.append(lax.ppermute(piece, ('seq', 'fsdp'), pairs))]
    dot_general x8, matrix products: 73.2 us -> 51.4 us  [dot_nt(): return lax.dot_general(left, right, NT, preferred_element_type=F32)]
  transfers between devices with their start and end apart: 15 -> 8, of which waited for: 2 -> 0; matrix products, arithmetic and copies ran while one was open for 11% -> 13% of each run, Pallas kernels for 38% -> 42%
where the time goes in v4:
time: 909 us; the launch traced here: 903 us
  Pallas kernels  708 us (78%)
  matrix products  107 us (12%)
  other arithmetic  60.5 us (7%)
  starting transfers between devices  12.9 us (1%)
  local copies, waits for them, and re-layouts  10.5 us (1%)
    pallas_call x2, Pallas kernels, reduce_grads(): pl.pallas_call(partial(reduce_kernel, last), in_specs=[anywhere] * 4 + [v...  294 us
    pallas_call x1, Pallas kernels, forward(): pl.pallas_call(partial(forward_kernel, names, layers, vec_rows), in_specs...  291 us
    pallas_call x2, Pallas kernels, attend_grad(): pl.pallas_call(attn_bwd_kernel, grid=(pairs,), in_specs=[triple, pl.Block...  74.4 us
    dot_general x8, matrix products, dot_tn(): lax.dot_general(left, right, (((0,), (0,)), ((), ())), preferred_element_...  56.1 us
    dot_general x8, matrix products, dot_nt(): return lax.dot_general(left, right, NT, preferred_element_type=F32)  51.4 us
    pallas_call x4, Pallas kernels, adam_matrix(): pl.pallas_call(partial(adam_kernel, kinds, ring, count), grid_spec=pltpu....  48.8 us
  transfers between devices with their start and end apart: 8, of which 0 were waited for; matrix products, arithmetic and copies ran while one was open for 13% of the time, Pallas kernels for 42%

profile of v4, /device:TPU:0, one launch (start us, length us, event | category | flops | bytes accessed | tf_op | source)
XLA Modules:
  0.0 903.5 jit_solution(10007148525752535908)
XLA Ops:
  5.6 291.0 %forward.1 = (bf16[1024,1536]{1,0:T(8,128)(2,1)}, bf16[1024,2048]{1,0:T(8,128)(2,1)}, bf16[2048,1024]{1,0:T(8,128)(2,1)}, bf16[512,1024]{1,0:T(8,128)(2,1)}, bf1...) custom-call(f32[2,128,3072]{2,1,0:T(8,128)} %refs_4_.4, ...), custom_call_target="tpu_custom_call" | custom-call | flops 60000002048 | bytes 600000000 | tf_op jit(solution)/shard_map/forward/pallas_call | solution.py:1779
  296.6 3.3 select_bitcast_fusion.3
  300.4 9.4 %collective-permute-start = (f32[256,1024]{1,0:T(8,128)}, f32[256,1024]{1,0:T(8,128)}, u32[]{:S(2)}, u32[]{:S(2)}) collective-permute-start(f32[256,1024]{1,0:T(8,128)} %get-tuple-element.200), channel_id=1, source_target_pairs={{0,0},{16,1},{2,2},{18,3},{4,4},{20,5},{6,6},{22,7},{8,8},{24,9},{... | collective-permute-start | bytes 3145736 | tf_op jit(solution)/shard_map/ppermute | solution.py:1849
  309.9 7.8 fusion
  317.7 6.4 fusion.46
  326.6 2.7 multiply_reduce_fusion.11
  332.1 2.8 multiply_reduce_fusion.9
  339.5 2.7 multiply_reduce_fusion.7
  344.8 10.2 %convolution_convert_fusion.2.down_grad = bf16[2048,1024]{1,0:T(8,128)(2,1)} fusion(bf16[1024,2048]{1,0:T(8,128)(2,1)} %get-tuple-element.128, f32[1024,1024]{1,0:T(8,128)} %get-tuple-element.98), kind=kOutput, calls=%fused_computation.32 | convolution fusion | flops 4298113024 | bytes 12582912 | tf_op jit(solution)/shard_map/dot_general | solution.py:1113
  356.9 9.0 %convolution_convert_fusion.3.up_grad = bf16[1024,2048]{1,0:T(8,128)(2,1)} fusion(bf16[1024,1024]{1,0:T(8,128)(2,1)S(1)} %copy-done.37, f32[1024,2048]{1,0:T(8,128)S(1)} %bitcast.129, bf16[1024,2048]{1,0:T(8,128)(2,1)} %get-tuple-element.101), kind=kOutput, calls=%fused_computation.33 | convolution fusion | flops 4303355904 | bytes 18874368 | tf_op jit(solution)/shard_map/dot_general | solution.py:1113
  366.0 3.0 multiply_reduce_fusion
  375.5 37.2 %attend_grad.2 = (bf16[1024,1536]{1,0:T(8,128)(2,1)}, f32[8,1536]{1,0:T(8,128)}) custom-call(bf16[1024,1536]{1,0:T(8,128)(2,1)} %get-tuple-element.105.low_ref, bf16[1024,512]{1,0:T(8,128)(2,1)} %convolution_convert_fusion.9.dout_ref, f32[4,8,1024]{2,1,0:T(8,128)} %get-tuple-element.206.lse_ref, f32[1024,128]{1,0:T(8,128)} %pad_maximum_fusion.cos_ref, ...), custom_call_target="tpu_custom_call" | custom-call | flops 21474836480 | bytes 9437184 | tf_op jit(solution)/shard_map/attend_grad/pallas_call | solution.py:520
  412.6 7.2 fusion.47
  420.4 4.2 maximum_select_fusion
  425.5 4.9 convolution_convert_fusion.6.proj_grad
  430.4 5.0 convolution_convert_fusion.qkv_grad
  435.5 2.6 multiply_reduce_fusion.1
  442.1 4.6 fusion.2
  446.8 11.7 %fusion.48 = (bf16[1024,1024]{1,0:T(8,128)(2,1)}, f32[1024,1024]{1,0:T(8,128)}) fusion(bf16[1024,2048]{1,0:T(8,128)(2,1)} %get-tuple-element.114, f32[1024,2048]{1,0:T(8,128)S(1)} %get-tuple-element.240, bf16[1024,2048]{1,0:T(8,128)(2,1)S(1)} %copy-done.29), kind=kOutput, calls=%fused_computation.157 | convolution fusion | flops 4302307328 | bytes 23068672 | tf_op jit(solution)/shard_map/dot_general | solution.py:1109
  459.9 141.7 %reduce_grads.2 = (bf16[256,1536]{1,0:T(8,128)(2,1)}, bf16[128,1536]{1,0:T(8,128)(2,1)}, bf16[128,1024]{1,0:T(8,128)(2,1)}, bf16[256,2048]{1,0:T(8,128)(2,1)}, b...) custom-call(bf16[1024,1536]{1,0:T(8,128)(2,1)} %convolution_convert_fusion.qkv_grad, ...), custom_call_target="tpu_custom_call" | custom-call | bytes 300000000 | tf_op jit(solution)/shard_map/reduce_grads/pallas_call | solution.py:967
  602.4 10.8 %convolution_convert_fusion.5.up_grad = bf16[1024,2048]{1,0:T(8,128)(2,1)} fusion(bf16[1024,1024]{1,0:T(8,128)(2,1)} %get-tuple-element.122, f32[1024,2048]{1,0:T(8,128)} %copy-done.27, bf16[1024,2048]{1,0:T(8,128)(2,1)S(1)} %copy-done.30), kind=kOutput, calls=%fused_computation.35 | convolution fusion | flops 4303355904 | bytes 18874368 | tf_op jit(solution)/shard_map/dot_general | solution.py:1113
  622.1 37.3 %attend_grad.3 = (bf16[1024,1536]{1,0:T(8,128)(2,1)}, f32[8,1536]{1,0:T(8,128)}) custom-call(bf16[1024,1536]{1,0:T(8,128)(2,1)} %get-tuple-element.116.low_ref, bf16[1024,512]{1,0:T(8,128)(2,1)} %convolution_convert_fusion.8.dout_ref, f32[4,8,1024]{2,1,0:T(8,128)} %get-tuple-element.205.lse_ref, f32[1024,128]{1,0:T(8,128)} %pad_maximum_fusion.cos_ref, ...), custom_call_target="tpu_custom_call" | custom-call | flops 21474836480 | bytes 9437184 | tf_op jit(solution)/shard_map/attend_grad/pallas_call | solution.py:520
  659.4 9.1 %fusion.49 = (bf16[1024,1024]{1,0:T(8,128)(2,1)}, f32[1024,1024]{1,0:T(8,128)}) fusion(bf16[1024,1536]{1,0:T(8,128)(2,1)} %get-tuple-element.118, bf16[1024,1536]{1,0:T(8,128)(2,1)} %get-tuple-element.119), kind=kOutput, calls=%fused_computation.158 | convolution fusion | flops 3222274048 | bytes 12582912 | tf_op jit(solution)/shard_map/dot_general | solution.py:1109
  668.9 6.3 convolution_convert_fusion.4.down_grad
  676.1 4.9 convolution_convert_fusion.7.proj_grad
  681.0 5.0 convolution_convert_fusion.1.qkv_grad
  693.6 152.1 %reduce_grads.3 = (bf16[256,1536]{1,0:T(8,128)(2,1)}, bf16[128,1536]{1,0:T(8,128)(2,1)}, bf16[128,1024]{1,0:T(8,128)(2,1)}, bf16[256,2048]{1,0:T(8,128)(2,1)}, b...) custom-call(bf16[1024,1536]{1,0:T(8,128)(2,1)} %convolution_convert_fusion.1.qkv_grad, ...), custom_call_target="tpu_custom_call" | custom-call | bytes 300000000 | tf_op jit(solution)/shard_map/reduce_grads/pallas_call | solution.py:967
  848.5 5.0 update.5
  853.4 11.9 %update.4 = (f32[2,128,3072]{2,1,0:T(8,128)}, f32[2,128,3072]{2,1,0:T(8,128)}, f32[2,128,3072]{2,1,0:T(8,128)}, f32[2,128,3072]{2,1,0:T(8,128)}, bf16[2,128,3072]{2,1,0:T(8,128)(2,1)}) custom-call(s32[1]{0:T(128)} %bitcast.37.core_ref, f32[1]{0:T(128)} %bitcast.38.factor_ref, bf16[256,1536]{1,0:T(8,128)(2,1)} %get-tuple-element.134.refs_0_, ...), custom_call_target="tpu_custom_call" | custom-call | flops 15728640 | bytes 25165824 | tf_op jit(solution)/shard_map/update/pallas_call | solution.py:1063
  865.4 17.6 %update.7 = (f32[2,512,1024]{2,1,0:T(8,128)}, f32[2,512,1024]{2,1,0:T(8,128)}, f32[2,512,1024]{2,1,0:T(8,128)}, f32[2,512,1024]{2,1,0:T(8,128)}, bf16[2,512,1024]{2,1,0:T(8,128)(2,1)}) custom-call(s32[1]{0:T(128)} %bitcast.37.core_ref, f32[1]{0:T(128)} %bitcast.38.factor_ref, bf16[512,1024]{1,0:T(8,128)(2,1)} %get-tuple-element.147.refs_0_, ...), custom_call_target="tpu_custom_call" | custom-call | flops 20971520 | bytes 33554432 | tf_op jit(solution)/shard_map/update/pallas_call | solution.py:1063
  883.0 14.2 %update.6 = (f32[2,128,4096]{2,1,0:T(8,128)}, f32[2,128,4096]{2,1,0:T(8,128)}, f32[2,128,4096]{2,1,0:T(8,128)}, f32[2,128,4096]{2,1,0:T(8,128)}, bf16[2,128,4096]{2,1,0:T(8,128)(2,1)}) custom-call(s32[1]{0:T(128)} %bitcast.37.core_ref, f32[1]{0:T(128)} %bitcast.38.factor_ref, bf16[256,2048]{1,0:T(8,128)(2,1)} %get-tuple-element.142.refs_0_, ...), custom_call_target="tpu_custom_call" | custom-call | flops 20971520 | bytes 33554432 | tf_op jit(solution)/shard_map/update/pallas_call | solution.py:1063
  898.6 3.2 maximum_select_fusion.1
  (200 shorter events, 54.5 us)
Async XLA Ops:
  296.6 13.2 %copy-start.15 = (f32[1024,1024]{1,0:T(8,128)S(1)}, f32[1024,1024]{1,0:T(8,128)}, u32[]{:S(2)}) copy-start(f32[1024,1024]{1,0:T(8,128)} %get-tuple-element.98) | copy-start | bytes 12582916
  300.0 120.5 %collective-permute-start.1 = (f32[256,1024]{1,0:T(8,128)}, f32[256,1024]{1,0:T(8,128)}, u32[]{:S(2)}, u32[]{:S(2)}) collective-permute-start(f32[256,1024]{1,0:T(8,128)} %get-tuple-element.201), channel_id=1, source_target_pairs={{8,0},{24,1},{10,2},{26,3},{12,4},{28,5},{14,6},{30,7},{0,8},{16,9... | collective-permute-start | bytes 3145736 | tf_op jit(solution)/shard_map/ppermute | solution.py:1849
  300.4 120.0 %collective-permute-start = (f32[256,1024]{1,0:T(8,128)}, f32[256,1024]{1,0:T(8,128)}, u32[]{:S(2)}, u32[]{:S(2)}) collective-permute-start(f32[256,1024]{1,0:T(8,128)} %get-tuple-element.200), channel_id=1, source_target_pairs={{0,0},{16,1},{2,2},{18,3},{4,4},{20,5},{6,6},{22,7},{8,8},{24,9},{... | collective-permute-start | bytes 3145736 | tf_op jit(solution)/shard_map/ppermute | solution.py:1849
  309.8 7.8 copy-start.31
  309.8 7.8 copy-start.36
  317.6 6.5 copy-start.28
  324.1 41.9 %collective-permute-start.2 = (bf16[1024,1024]{1,0:T(8,128)(2,1)}, bf16[1024,1024]{1,0:T(8,128)(2,1)S(1)}, u32[]{:S(2)}, u32[]{:S(2)}) collective-permute-start(bf16[1024,1024]{1,0:T(8,128)(2,1)} %get-tuple-element.231), channel_id=1, source_target_pairs={{0,1},{1,0},{2,3},{3,2},{4,5},{5,4},{6,7},{7,6},{8,9},{9,8},{10,11... | collective-permute-start | bytes 6291464 | tf_op jit(solution)/shard_map/ppermute | solution.py:423
  324.1 5.3 copy-start.19
  329.5 5.3 copy-start.18
  344.8 11.5 %copy-start.20 = (f32[1024]{0:T(1024)}, f32[1024]{0:T(1024)S(1)}, u32[]{:S(2)}) copy-start(f32[1024]{0:T(1024)S(1)} %broadcast_multiply_fusion.3) | copy-start | bytes 12292
  344.8 12.1 %slice-start = ((s8[8388608]{0:T(1024)(128)(4,1)}), s8[4194304]{0:T(1024)(128)(4,1)S(1)}, s32[]{:S(2)}) async-start(s8[8388608]{0:T(1024)(128)(4,1)} %bitcast.128), calls=%async_computation | async-start | bytes 8388608
  344.8 11.5 %copy-start.2 = (f32[1024,1024]{1,0:T(8,128)S(1)}, f32[1024,1024]{1,0:T(8,128)}, u32[]{:S(2)}) copy-start(f32[1024,1024]{1,0:T(8,128)} %get-tuple-element.115) | copy-start | bytes 12582916
  344.8 12.1 %slice-start.1 = ((s8[8388608]{0:T(1024)(128)(4,1)}), s8[4194304]{0:T(1024)(128)(4,1)S(1)}, s32[]{:S(2)}) async-start(s8[8388608]{0:T(1024)(128)(4,1)} %bitcast.128), calls=%async_computation.1 | async-start | bytes 8388608
  356.9 9.1 %copy-start.4 = (f32[1024,1024]{1,0:T(8,128)S(1)}, f32[1024,1024]{1,0:T(8,128)}, u32[]{:S(2)}) copy-start(f32[1024,1024]{1,0:T(8,128)} %get-tuple-element.99) | copy-start | bytes 12582916
  356.9 9.1 %copy-start.13 = (f32[1024,1024]{1,0:T(8,128)S(1)}, f32[1024,1024]{1,0:T(8,128)}, u32[]{:S(2)}) copy-start(f32[1024,1024]{1,0:T(8,128)} %get-tuple-element.232) | copy-start | bytes 12582916
  375.5 37.2 %copy-start.33 = (bf16[1024,1536]{1,0:T(8,128)(2,1)S(1)}, bf16[1024,1536]{1,0:T(8,128)(2,1)}, u32[]{:S(2)}) copy-start(bf16[1024,1536]{1,0:T(8,128)(2,1)} %get-tuple-element.110) | copy-start | bytes 9437188
  419.9 15.6 %collective-permute-start.3 = (bf16[1024,1024]{1,0:T(8,128)(2,1)}, bf16[1024,1024]{1,0:T(8,128)(2,1)S(1)}, u32[]{:S(2)}, u32[]{:S(2)}) collective-permute-start(bf16[1024,1024]{1,0:T(8,128)(2,1)} %get-tuple-element.233), channel_id=1, source_target_pairs={{0,1},{1,0},{2,3},{3,2},{4,5},{5,4},{6,7},{7,6},{8,9},{9,8},{10,11... | collective-permute-start | bytes 6291464 | tf_op jit(solution)/shard_map/ppermute | solution.py:423
  440.2 6.5 copy-start.5
  446.8 11.8 %copy-start.27 = (f32[1024,2048]{1,0:T(8,128)}, f32[1024,2048]{1,0:T(8,128)S(1)}, u32[]{:S(2)}) copy-start(f32[1024,2048]{1,0:T(8,128)S(1)} %get-tuple-element.240) | copy-start | bytes 25165828
  458.5 154.7 %collective-permute-start.4 = (bf16[1024,1024]{1,0:T(8,128)(2,1)}, bf16[1024,1024]{1,0:T(8,128)(2,1)S(1)}, u32[]{:S(2)}, u32[]{:S(2)}) collective-permute-start(bf16[1024,1024]{1,0:T(8,128)(2,1)} %get-tuple-element.235), channel_id=1, source_target_pairs={{0,1},{1,0},{2,3},{3,2},{4,5},{5,4},{6,7},{7,6},{8,9},{9,8},{10,11... | collective-permute-start | bytes 6291464 | tf_op jit(solution)/shard_map/ppermute | solution.py:423
  459.9 142.5 %copy-start.30 = (bf16[1024,2048]{1,0:T(8,128)(2,1)S(1)}, bf16[1024,2048]{1,0:T(8,128)(2,1)}, u32[]{:S(2)}) copy-start(bf16[1024,2048]{1,0:T(8,128)(2,1)} %get-tuple-element.113) | copy-start | bytes 12582916
  602.4 10.8 %copy-start = (f32[1024,1024]{1,0:T(8,128)S(1)}, f32[1024,1024]{1,0:T(8,128)}, u32[]{:S(2)}) copy-start(f32[1024,1024]{1,0:T(8,128)} %get-tuple-element.111) | copy-start | bytes 12582916
  602.4 10.8 %copy-start.7 = (f32[1024,1024]{1,0:T(8,128)S(1)}, f32[1024,1024]{1,0:T(8,128)}, u32[]{:S(2)}) copy-start(f32[1024,1024]{1,0:T(8,128)} %get-tuple-element.236) | copy-start | bytes 12582916
  659.4 9.5 %copy-start.38 = (bf16[1024,2048]{1,0:T(8,128)(2,1)S(1)}, bf16[1024,2048]{1,0:T(8,128)(2,1)}, u32[]{:S(2)}) copy-start(bf16[1024,2048]{1,0:T(8,128)(2,1)} %get-tuple-element.123) | copy-start | bytes 12582916
  668.5 17.5 %collective-permute-start.5 = (bf16[1024,1024]{1,0:T(8,128)(2,1)}, bf16[1024,1024]{1,0:T(8,128)(2,1)S(1)}, u32[]{:S(2)}, u32[]{:S(2)}) collective-permute-start(bf16[1024,1024]{1,0:T(8,128)(2,1)} %get-tuple-element.237), channel_id=1, source_target_pairs={{0,1},{1,0},{2,3},{3,2},{4,5},{5,4},{6,7},{7,6},{8,9},{9,8},{10,11... | collective-permute-start | bytes 6291464 | tf_op jit(solution)/shard_map/ppermute | solution.py:423
  681.0 5.0 copy-start.3
  681.0 5.0 copy-start.14
  690.7 208.0 %collective-permute-start.7 = (f32[256,1024]{1,0:T(8,128)S(1)}, f32[256,1024]{1,0:T(8,128)S(1)}, u32[]{:S(2)}, u32[]{:S(2)}) collective-permute-start(f32[256,1024]{1,0:T(8,128)S(1)} %get-tuple-element.199), channel_id=1, source_target_pairs={{8,0},{24,1},{10,2},{26,3},{12,4},{28,5},{14,6},{30,7},{0,8},{16,9... | collective-permute-start | bytes 3145736 | tf_op jit(solution)/shard_map/ppermute | solution.py:1849
  691.2 207.5 %collective-permute-start.6 = (f32[256,1024]{1,0:T(8,128)S(1)}, f32[256,1024]{1,0:T(8,128)}, u32[]{:S(2)}, u32[]{:S(2)}) collective-permute-start(f32[256,1024]{1,0:T(8,128)S(1)} %get-tuple-element.198), channel_id=1, source_target_pairs={{0,0},{16,1},{2,2},{18,3},{4,4},{20,5},{6,6},{22,7},{8,8},{24,9},{... | collective-permute-start | bytes 3145736 | tf_op jit(solution)/shard_map/ppermute | solution.py:1849
  883.0 14.2 %copy-start.22 = (f32[2,1664]{1,0:T(2,128)S(1)}, f32[2,1664]{1,0:T(2,128)}, u32[]{:S(2)}) copy-start(f32[2,1664]{1,0:T(2,128)} %param.21) | copy-start | bytes 39940
  883.0 14.3 %copy-start.23 = (f32[2,1664]{1,0:T(2,128)S(1)}, f32[2,1664]{1,0:T(2,128)}, u32[]{:S(2)}) copy-start(f32[2,1664]{1,0:T(2,128)} %param.31) | copy-start | bytes 39940
  883.0 14.3 %copy-start.24 = (f32[2,1664]{1,0:T(2,128)S(1)}, f32[2,1664]{1,0:T(2,128)}, u32[]{:S(2)}) copy-start(f32[2,1664]{1,0:T(2,128)} %param.26) | copy-start | bytes 39940
  (19 other events, 69.4 us)

commit v5 on v4

--- a/solution.py
+++ b/solution.py
@@ -408,6 +408,7 @@
 
 
 ROWS_Q = 256
+ADD_ROWS = 32
 PAIR = 2 * HEAD_DIM
 BF = jnp.bfloat16
 F32 = jnp.float32
@@ -452,99 +453,6 @@
 def head_mask(item, head):
     lane = lax.broadcasted_iota(jnp.int32, item.shape, 1)
     return jnp.where(lane // HEAD_DIM == head, item, jnp.zeros_like(item))
-
-
-def attn_bwd_kernel(
-    low_ref, dout_ref, lse_ref, cos_ref, sin_ref, grad_ref, bias_ref, dq_ref, dk_ref, dv_ref
-):
-    length = low_ref.shape[0]
-    key_rows = low_ref[:, PAIR : 2 * PAIR]
-    values = low_ref[:, 2 * PAIR : 3 * PAIR]
-    keys_t = key_rows.astype(F32).T.astype(BF)
-    keys_by_head = [head_mask(key_rows, head) for head in range(2)]
-    values_by_head = [head_mask(values, head) for head in range(2)]
-    scale = HEAD_DIM**-0.5
-    dk_ref[...] = jnp.zeros_like(dk_ref)
-    dv_ref[...] = jnp.zeros_like(dv_ref)
-
-    @pl.loop(0, length // ROWS_Q)
-    def _(step):
-        rows = pl.ds(pl.multiple_of(step * ROWS_Q, ROWS_Q), ROWS_Q)
-        block = low_ref[rows, 0:PAIR]
-        scaled = block * jnp.asarray(scale, BF)
-        dout = dout_ref[rows, :]
-        outs = []
-        for head in range(2):
-            scores = lax.dot_general(keys_by_head[head], scaled, NT, preferred_element_type=F32)
-            probs = jnp.exp(scores - lse_ref[0, head : head + 1, rows])
-            prob_grad = lax.dot_general(values_by_head[head], dout, NT, preferred_element_type=F32)
-            delta = jnp.sum(probs * prob_grad, axis=0, keepdims=True)
-            score_low = (probs * (prob_grad - delta) * scale).astype(BF)
-            dv_ref[head] += jnp.dot(probs.astype(BF), dout, preferred_element_type=F32)
-            dk_ref[head] += jnp.dot(score_low, block, preferred_element_type=F32)
-            outs.append(
-                jnp.dot(
-                    keys_t[head * HEAD_DIM : (head + 1) * HEAD_DIM],
-                    score_low,
-                    preferred_element_type=F32,
-                )
-            )
-        dq_ref[rows, :] = jnp.concatenate(outs, axis=0).T
-
-    lane = lax.broadcasted_iota(jnp.int32, (length, PAIR), 1)
-    first = lane // HEAD_DIM == 0
-    cosine, sine = cos_ref[...], sin_ref[...]
-
-    def rounded(item):
-        return item.astype(BF).astype(F32)
-
-    def back(item):
-        return item * cosine - swap_halves(item) * sine
-
-    parts = [
-        back(rounded(dq_ref[...])),
-        back(rounded(jnp.where(first, dk_ref[0], dk_ref[1]))),
-        rounded(jnp.where(first, dv_ref[0], dv_ref[1])),
-    ]
-    for idx, part in enumerate(parts):
-        cols = slice(idx * PAIR, (idx + 1) * PAIR)
-        grad_ref[:, cols] = part.astype(BF)
-        bias_ref[:, cols] = jnp.broadcast_to(jnp.sum(part, axis=0, keepdims=True), (8, PAIR))
-
-
-def attend_grad(low_all, mixed_grad, lse, cos_wide, sin_wide):
-    length, width = low_all.shape
-    pairs = width // (3 * PAIR)
-    table = pl.BlockSpec((length, PAIR), lambda pair: (0, 0))
-    triple = pl.BlockSpec((length, 3 * PAIR), lambda pair: (0, pair))
-    return pl.pallas_call(
-        attn_bwd_kernel,
-        grid=(pairs,),
-        in_specs=[
-            triple,
-            pl.BlockSpec((length, PAIR), lambda pair: (0, pair)),
-            pl.BlockSpec((1, 8, length), lambda pair: (pair, 0, 0)),
-            table,
-            table,
-        ],
-        out_specs=[triple, pl.BlockSpec((8, 3 * PAIR), lambda pair: (0, pair))],
-        out_shape=[
-            jax.ShapeDtypeStruct((length, width), BF),
-            jax.ShapeDtypeStruct((8, width), F32),
-        ],
-        scratch_shapes=[
-            pltpu.VMEM((length, PAIR), F32),
-            pltpu.VMEM((2, length, PAIR), F32),
-            pltpu.VMEM((2, length, PAIR), F32),
-        ],
-        compiler_params=pltpu.CompilerParams(vmem_limit_bytes=VMEM_LIMIT),
-        cost_estimate=pl.CostEstimate(
-            flops=40 * pairs * length * length * PAIR,
-            bytes_accessed=length * width * 6,
-            transcendentals=2 * pairs * length * length,
-        ),
-        name="attend_grad",
-    )(low_all, mixed_grad, lse, cos_wide, sin_wide)
 
 
 class Places:
@@ -587,414 +495,6 @@
 
 def aligned(start, size, unit=None):
     return pl.ds(pl.multiple_of(start, unit or size), size)
-
-
-ADD_ROWS = 32
-
-
-def add_into(target, term):
-    rows = target.shape[0]
-
-    @pl.loop(0, rows // ADD_ROWS)
-    def _(step):
-        at = aligned(step * ADD_ROWS, ADD_ROWS)
-        total = target[at, :].astype(F32) + term[at, :].astype(F32)
-        target[at, :] = total.astype(BF)
-
-
-class Sems:
-    def __init__(self, ref):
-        self.ref, self.used = ref, 0
-
-    def take(self):
-        self.used += 1
-        return self.ref.at[self.used - 1]
-
-
-class Sum:
-    def __init__(self, at, sems, grad, own, one, two, three, z_first, x_first, stage, layer):
-        self.at, self.sems = at, sems
-        self.grad, self.own, self.one, self.two, self.three = grad, own, one, two, three
-        self.z_first, self.x_first = z_first, x_first
-        self.stage, self.layer = stage, layer
-        self.rows = grad.shape[0] // (4 * at.ring)
-        self.sends, self.loads = [], {}
-        self.first, self.second, self.hop = {}, {}, {}
-
-    def make(self, src, dst, target):
-        copy = remote(src, dst, self.sems[0].take(), self.sems[1].take(), target)
-        copy.start()
-        self.sends.append(copy)
-        return copy
-
-    def load(self, src, dst):
-        copy = pltpu.make_async_copy(src, dst, self.sems[2].take())
-        copy.start()
-        return copy
-
-    def kept(self):
-        at = self.at
-        if self.x_first:
-            return [(at.at_x, 1), (2 + at.at_x, 1)]
-        return [(2 * at.at_y, 2)]
-
-    def given(self):
-        at = self.at
-        if self.x_first:
-            return [(1 - at.at_x, 1), (3 - at.at_x, 1)]
-        return [(2 * (1 - at.at_y), 2)]
-
-    def fetch_own(self, tile):
-        base = self.at.back(tile + 1) * 4 * self.rows
-        copies = []
-        if self.z_first:
-            copies.append(
-                self.load(self.grad.at[aligned(base, 4 * self.rows), :], self.own.at[tile])
-            )
-        else:
-            place = 0
-            for first, count in self.kept():
-                size = count * self.rows
-                copies.append(
-                    self.load(
-                        self.grad.at[aligned(base + first * self.rows, size, self.rows), :],
-                        self.own.at[tile, pl.ds(place, size), :],
-                    )
-                )
-                place += size
-        self.loads[tile] = copies
-
-    def own_ready(self, tile):
-        for copy in self.loads[tile]:
-            copy.wait()
-
-    def plane_one(self, tile, source, base):
-        target = self.at.over_x if self.x_first else self.at.over_y
-        place, made = 0, []
-        for first, count in self.given():
-            size = count * self.rows
-            made.append(
-                self.make(
-                    source.at[aligned(base + first * self.rows, size, self.rows), :],
-                    self.one.at[tile, pl.ds(place, size), :],
-                    target,
-                )
-            )
-            place += size
-        self.first[tile] = made
-
-    def plane_two(self, tile, kept_ref):
-        for copy in self.first[tile]:
-            copy.wait_recv()
-        place = 0
-        for ref in kept_ref:
-            size = ref.shape[0]
-            add_into(self.one.at[tile, pl.ds(place, size), :], ref)
-            place += size
-        at = self.at
-        target = at.over_y if self.x_first else at.over_x
-        keep = at.at_y if self.x_first else at.at_x
-        self.keep_ref = lambda: self.one.at[tile, aligned(keep * self.rows, self.rows), :]
-        self.second[tile] = self.make(
-            self.one.at[tile, aligned((1 - keep) * self.rows, self.rows), :],
-            self.two.at[tile],
-            target,
-        )
-
-    def plane_three(self, tile):
-        at = self.at
-        keep = at.at_y if self.x_first else at.at_x
-        self.second[tile].wait_recv()
-        add_into(self.two.at[tile], self.one.at[tile, aligned(keep * self.rows, self.rows), :])
-
-    def start(self, tile):
-        base = self.at.back(tile + 1) * 4 * self.rows
-        if self.z_first:
-            self.own_ready(tile)
-            self.hop[0] = self.make(self.own.at[0], self.three.at[0], self.at.up)
-        else:
-            self.plane_one(tile, self.grad, base)
-
-    def middle(self, tile):
-        self.own_ready(tile)
-        self.plane_two(tile, [self.own.at[tile]])
-
-    def finish(self, tile):
-        self.plane_three(tile)
-        if tile > 0:
-            self.hop[tile - 1].wait_recv()
-            add_into(self.two.at[tile], self.three.at[tile - 1])
-        if tile < self.at.ring - 1:
-            self.hop[tile] = self.make(self.two.at[tile], self.three.at[tile], self.at.up)
-
-    def ring_step(self, tile):
-        last = tile == self.at.ring - 1
-        self.hop[tile - 1].wait_recv()
-        self.own_ready(tile)
-        total = self.three.at[tile - 1]
-        add_into(total, self.own.at[tile])
-        if last:
-            self.plane_one(0, total, 0)
-        else:
-            self.hop[tile] = self.make(total, self.three.at[tile], self.at.up)
-
-    def slab_middle(self):
-        total = self.three.at[self.at.ring - 2]
-        refs = [
-            total.at[aligned(first * self.rows, count * self.rows, self.rows), :]
-            for first, count in self.kept()
-        ]
-        self.plane_two(0, refs)
-
-    def slab_finish(self):
-        self.plane_three(0)
-
-    def total(self):
-        return self.two.at[0 if self.z_first else self.at.ring - 1]
-
-    def place(self, quarter, turn=0, size=None):
-        size = size or self.rows
-        return self.stage.at[aligned(quarter * self.rows + turn * size, size), :]
-
-    def gather(self):
-        at = self.at
-        self.kept_store = self.load(self.total(), self.place(at.seq))
-        self.near = [
-            self.make(self.total(), self.place(at.seq), at.over_x),
-            self.make(self.total(), self.place(at.seq), at.over_y),
-        ]
-
-    def gather_far(self):
-        at = self.at
-        for copy in self.near:
-            copy.wait_recv()
-        half = self.rows // 2
-        self.far = []
-        for turn, (origin, target) in enumerate(((at.near_y, at.over_x), (at.near_x, at.over_y))):
-            ref = self.place(origin, turn, half)
-            self.far.append(self.make(ref, ref, target))
-
-    def gather_end(self, arrive):
-        at = self.at
-        self.kept_store.wait()
-        for copy in self.far:
-            copy.wait_recv()
-        self.swap = None
-        if arrive is not None:
-            half = 2 * self.rows
-            self.swap = self.make(
-                self.stage.at[aligned((1 - at.core) * half, half), :], arrive, at.other
-            )
-
-    def drain(self):
-        if self.swap is not None:
-            self.swap.wait_recv()
-        for copy in self.sends:
-            copy.wait_send()
-
-
-def reduce_kernel(
-    last,
-    qkv_grad, proj_grad, up_grad, down_grad, vec_in, square_in,
-    qkv_stage, qkv_arrive, proj_stage, up_stage, up_arrive, down_stage, vec_out, square_out,
-    qkv_own, qkv_one, qkv_two, qkv_three,
-    proj_own, proj_one, proj_two, proj_three,
-    up_own, up_one, up_two, up_three,
-    down_own, down_one, down_two, down_three,
-    vec_got, vec_hop, vec_sum, square_got, square_sum,
-    send_sem, recv_sem, load_sem,
-):
-    at = Places()
-    ring = at.ring
-    sems = (Sems(send_sem), Sems(recv_sem), Sems(load_sem))
-    greet((at.other, at.over_x, at.over_y, at.down), 4)
-    qkv = Sum(at, sems, qkv_grad, qkv_own, qkv_one, qkv_two, qkv_three, True, True, qkv_stage, 0)
-    proj = Sum(
-        at, sems, proj_grad, proj_own, proj_one, proj_two, proj_three, True, False, proj_stage, 0
-    )
-    up = Sum(at, sems, up_grad, up_own, up_one, up_two, up_three, False, True, up_stage, 0)
-    down = Sum(
-        at, sems, down_grad, down_own, down_one, down_two, down_three, False, False, down_stage, 0
-    )
-    wide, slabs = (up, down), (qkv, proj)
-
-    vec_copies = []
-
-    def vec_copy(src, dst, target):
-        copy = remote(src, dst, sems[0].take(), sems[1].take(), target)
-        copy.start()
-        vec_copies.append(copy)
-        return copy
-
-    partners = (at.other, at.over_x, at.over_y)
-    vec_sum[0] = vec_in[...]
-
-    for item in slabs:
-        item.fetch_own(0)
-    for item in wide:
-        item.start(0)
-    for item in slabs:
-        item.start(0)
-    for item in wide:
-        item.start(1)
-    for tile in range(ring):
-        for item in wide:
-            item.fetch_own(tile)
-        if tile > 0:
-            for item in slabs:
-                item.fetch_own(tile)
-    vec_state = {"copy": vec_copy(vec_sum.at[0], vec_got.at[0], partners[0])}
-
-    def vec_step(idx):
-        vec_state["copy"].wait_recv()
-        if idx <= 3:
-            vec_sum[idx] = vec_sum[idx - 1] + vec_got[idx - 1]
-            if idx < 3:
-                vec_state["copy"] = vec_copy(vec_sum.at[idx], vec_got.at[idx], partners[idx])
-            else:
-                vec_state["copy"] = vec_copy(
-                    vec_sum.at[3, at.back(1)], vec_hop.at[0], at.up
-                )
-        else:
-            hop = idx - 3
-            vec_hop[hop - 1] = vec_hop[hop - 1] + vec_sum[3, at.back(hop + 1)]
-            if hop < ring - 1:
-                vec_state["copy"] = vec_copy(vec_hop.at[hop - 1], vec_hop.at[hop], at.up)
-
-    for tile in range(ring):
-        for item in wide:
-            item.middle(tile)
-        if tile + 2 < ring:
-            for item in wide:
-                item.start(tile + 2)
-        if tile > 0:
-            for item in wide:
-                item.finish(tile - 1)
-        if tile + 1 < ring:
-            for item in slabs:
-                item.ring_step(tile + 1)
-        vec_step(tile + 1)
-    for item in slabs:
-        item.slab_middle()
-    vec_step(5)
-    for item in wide:
-        item.finish(ring - 1)
-        item.gather()
-    vec_step(6)
-    vec_total = vec_hop[ring - 2]
-    vec_out[...] = vec_total
-    for item in slabs:
-        item.slab_finish()
-        item.gather()
-
-    def squares(ref):
-        rows, columns = ref.shape
-        total = jnp.zeros((8, 128), F32)
-
-        def body(step, total):
-            part = ref[aligned(step * 16, 16), :].astype(F32)
-            part = part * part
-            part = part[0:8] + part[8:16]
-            for column in range(0, columns, 128):
-                total = total + part[:, column : column + 128]
-            return total
-
-        return lax.fori_loop(0, rows // 16, body, total)
-
-    total = square_in[...]
-    for item in (*wide, *slabs):
-        total = total + squares(item.total())
-    vec_square = vec_total * vec_total * 0.125
-    for column in range(0, vec_square.shape[1], 128):
-        total = total + vec_square[:, column : column + 128]
-    square_sum[0] = total
-    if last:
-        for idx, target in enumerate(partners):
-            copy = vec_copy(square_sum.at[idx], square_got.at[idx], target)
-            if idx == 0:
-                for item in wide:
-                    item.gather_far()
-            if idx == 1:
-                for item in slabs:
-                    item.gather_far()
-            copy.wait_recv()
-            square_sum[idx + 1] = square_sum[idx] + square_got[idx]
-        total = square_sum[3]
-        for hop in range(ring - 1):
-            source = square_sum.at[3] if hop == 0 else square_got.at[2 + hop]
-            copy = vec_copy(source, square_got.at[3 + hop], at.up)
-            if hop == 0:
-                for item in wide:
-                    item.gather_end(up_arrive if item is up else None)
-            copy.wait_recv()
-            total = total + square_got[3 + hop]
-        square_out[...] = total
-    else:
-        square_out[...] = total
-        for item in (*wide, *slabs):
-            item.gather_far()
-        for item in wide:
-            item.gather_end(up_arrive if item is up else None)
-    for item in slabs:
-        item.gather_end(qkv_arrive if item is qkv else None)
-    for item in (*wide, *slabs):
-        item.drain()
-    for copy in vec_copies:
-        copy.wait_send()
-
-
-def reduce_grads(grads, vec, squares, last, call_id):
-    ring = lax.axis_size("fsdp") // 2
-    anywhere = pl.BlockSpec(memory_space=pl.ANY)
-    vmem = pl.BlockSpec(memory_space=pltpu.VMEM)
-    dma = pltpu.SemaphoreType.DMA
-    scratch, slab_shapes = [], []
-    for idx, grad in enumerate(grads):
-        slab, width = grad.shape[0] // ring, grad.shape[1]
-        quarter = slab // 4
-        slab_shapes.append(jax.ShapeDtypeStruct((slab, width), BF))
-        z_first = idx < 2
-        tiles = 1 if z_first else ring
-        scratch += [
-            pltpu.VMEM((ring, slab if z_first else 2 * quarter, width), BF),
-            pltpu.VMEM((tiles, 2 * quarter, width), BF),
-            pltpu.VMEM((tiles, quarter, width), BF),
-            pltpu.VMEM((ring - 1, slab if z_first else quarter, width), BF),
-        ]
-    half = [
-        jax.ShapeDtypeStruct((shape.shape[0] // 2, shape.shape[1]), BF) for shape in slab_shapes
-    ]
-    return pl.pallas_call(
-        partial(reduce_kernel, last),
-        in_specs=[anywhere] * 4 + [vmem] * 2,
-        out_specs=[anywhere] * 6 + [vmem] * 2,
-        out_shape=[
-            slab_shapes[0],
-            half[0],
-            slab_shapes[1],
-            slab_shapes[2],
-            half[2],
-            slab_shapes[3],
-            jax.ShapeDtypeStruct(vec.shape[1:], F32),
-            jax.ShapeDtypeStruct((8, 128), F32),
-        ],
-        scratch_shapes=[
-            *scratch,
-            pltpu.VMEM((3,) + vec.shape, F32),
-            pltpu.VMEM((ring - 1,) + vec.shape[1:], F32),
-            pltpu.VMEM((4,) + vec.shape, F32),
-            pltpu.VMEM((3 + ring - 1, 8, 128), F32),
-            pltpu.VMEM((4, 8, 128), F32),
-            dma((120,)),
-            dma((120,)),
-            dma((120,)),
-        ],
-        compiler_params=pltpu.CompilerParams(
-            collective_id=call_id, has_side_effects=True, vmem_limit_bytes=VMEM_LIMIT
-        ),
-        cost_estimate=pl.CostEstimate(flops=0, bytes_accessed=300_000_000, transcendentals=0),
-        name="reduce_grads",
-    )(*grads, vec, squares)
 
 
 def adam_kernel(
@@ -1084,15 +584,6 @@
     spread = jnp.mean(center * center, axis=-1, keepdims=True)
     inverse = lax.rsqrt(spread + 1e-06)
     return center * inverse, inverse
-
-
-def norm_backward(hidden, gain, grad):
-    scaled, inverse = norm_parts(hidden)
-    entry = grad * gain
-    mean_one = jnp.mean(entry, axis=-1, keepdims=True)
-    mean_two = jnp.mean(entry * scaled, axis=-1, keepdims=True)
-    result = inverse * (entry - mean_one - scaled * mean_two)
-    return result, jnp.sum(grad * scaled, axis=0), jnp.sum(grad, axis=0)
 
 
 def gelu_and_slope(upward):
@@ -1733,8 +1224,9 @@
     outputs["cot_out"] = ((length, width), F32)
     outputs["table_out"] = ((length, PAIR), F32)
     outputs["vec_out"] = ((parts,) + vectors.shape, F32)
+    outputs["vecs"] = ((layers, 8, up_half), F32)
     outputs["lse_out"] = ((layers, pairs, 8, length), F32)
-    in_vmem = ("vec_in", "vec_out", "lse_out")
+    in_vmem = ("vec_in", "vec_out", "vecs", "lse_out")
     anywhere = pl.BlockSpec(memory_space=pl.ANY)
     vmem = pl.BlockSpec(memory_space=pltpu.VMEM)
     dma = pltpu.SemaphoreType.DMA
@@ -1753,7 +1245,6 @@
         "table_slab": pltpu.VMEM(tables.shape[1:], F32),
         "res": pltpu.VMEM((length, width), F32),
         "tables": pltpu.VMEM((length, PAIR), F32),
-        "vecs": pltpu.VMEM((layers, 8, up_half), F32),
         "norm": pltpu.VMEM((length, width), BF),
         "low": pltpu.VMEM((length, qkv_half), BF),
         "keys": pltpu.VMEM((2, length, PAIR), BF),
@@ -1793,13 +1284,736 @@
     return SimpleNamespace(**dict(zip(outputs, results)))
 
 
-def spread_bias(grad, core, fsdp_parts, kinds):
-    width = grad.shape[0] // (kinds * (fsdp_parts // 2))
-    view = grad.reshape(fsdp_parts // 2, kinds, width).transpose(1, 0, 2)
-    zero = jnp.zeros_like(view)
-    first = jnp.where(core == 0, view, zero)
-    second = jnp.where(core == 0, zero, view)
-    return jnp.stack([first, second], axis=2).reshape(-1)
+def add_into(target, term):
+    @pl.loop(0, target.shape[0] // ADD_ROWS)
+    def _(step):
+        at = aligned(step * ADD_ROWS, ADD_ROWS)
+        target[at, :] = (target[at, :].astype(F32) + term[at, :].astype(F32)).astype(BF)
+
+
+class Sems:
+    def __init__(self, ref):
+        self.ref, self.used = ref, 0
+
+    def take(self):
+        self.used += 1
+        return self.ref.at[self.used - 1]
+
+
+class Sum:
+    def __init__(self, at, sems, refs, name, layer, z_first, x_first, compute):
+        self.at, self.sems = at, sems
+        self.own, self.one, self.two, self.three = [
+            getattr(refs, name + part) for part in ("_own", "_one", "_two", "_three")
+        ]
+        self.stage = getattr(refs, name + "_stage" + str(layer))
+        self.arrive = getattr(refs, name + "_arrive" + str(layer), None)
+        self.z_first, self.x_first, self.compute = z_first, x_first, compute
+        self.rows = self.two.shape[1]
+        self.sends, self.slot_sends = [], [[], []]
+        self.first, self.second, self.hop = {}, {}, {}
+        self.swap = None
+
+    def make(self, src, dst, target, slot=None):
+        copy = remote(src, dst, self.sems[0].take(), self.sems[1].take(), target)
+        copy.start()
+        (self.sends if slot is None else self.slot_sends[slot]).append(copy)
+        return copy
+
+    def pieces(self, mine):
+        at = self.at
+        if self.x_first:
+            side = at.at_x if mine else 1 - at.at_x
+            return [(side, 1), (2 + side, 1)]
+        return [(2 * (at.at_y if mine else 1 - at.at_y), 2)]
+
+    def tile(self, tile):
+        slot = tile % 2
+        for copy in self.slot_sends[slot]:
+            copy.wait_send()
+        self.slot_sends[slot] = []
+        self.compute(tile, self.own.at[slot])
+
+    def start(self, tile):
+        self.tile(tile)
+        slot = tile % 2
+        if self.z_first:
+            self.hop[0] = self.make(self.own.at[slot], self.three.at[0], self.at.up, slot)
+        else:
+            self.plane_one(tile, self.own.at[slot], slot)
+
+    def plane_one(self, tile, source, slot=None):
+        target = self.at.over_x if self.x_first else self.at.over_y
+        place, made = 0, []
+        for first, count in self.pieces(False):
+            size = count * self.rows
+            made.append(
+                self.make(
+                    source.at[aligned(first * self.rows, size, self.rows), :],
+                    self.one.at[tile, pl.ds(place, size), :],
+                    target,
+                    slot,
+                )
+            )
+            place += size
+        self.first[tile] = made
+
+    def plane_two(self, tile, source):
+        for copy in self.first[tile]:
+            copy.wait_recv()
+        place = 0
+        for first, count in self.pieces(True):
+            size = count * self.rows
+            add_into(
+                self.one.at[tile, pl.ds(place, size), :],
+                source.at[aligned(first * self.rows, size, self.rows), :],
+            )
+            place += size
+        at = self.at
+        target, keep = (at.over_y, at.at_y) if self.x_first else (at.over_x, at.at_x)
+        self.second[tile] = self.make(
+            self.one.at[tile, aligned((1 - keep) * self.rows, self.rows), :],
+            self.two.at[tile],
+            target,
+        )
+
+    def plane_three(self, tile):
+        keep = self.at.at_y if self.x_first else self.at.at_x
+        self.second[tile].wait_recv()
+        add_into(self.two.at[tile], self.one.at[tile, aligned(keep * self.rows, self.rows), :])
+
+    def middle(self, tile):
+        self.plane_two(tile, self.own.at[tile % 2])
+
+    def finish(self, tile):
+        self.plane_three(tile)
+        if tile > 0:
+            self.hop[tile - 1].wait_recv()
+            add_into(self.two.at[tile], self.three.at[tile - 1])
+        if tile < self.at.ring - 1:
+            self.hop[tile] = self.make(self.two.at[tile], self.three.at[tile], self.at.up)
+        else:
+            self.gather()
+
+    def ring_step(self, tile):
+        self.tile(tile)
+        self.hop[tile - 1].wait_recv()
+        total = self.three.at[tile - 1]
+        add_into(total, self.own.at[tile % 2])
+        if tile == self.at.ring - 1:
+            self.plane_one(0, total)
+        else:
+            self.hop[tile] = self.make(total, self.three.at[tile], self.at.up)
+
+    def slab_middle(self):
+        self.plane_two(0, self.three.at[self.at.ring - 2])
+
+    def slab_finish(self):
+        self.plane_three(0)
+        self.gather()
+
+    def total(self):
+        return self.two.at[0 if self.z_first else self.at.ring - 1]
+
+    def place(self, quarter, turn=0, size=None):
+        size = size or self.rows
+        return self.stage.at[aligned(quarter * self.rows + turn * size, size), :]
+
+    def gather(self):
+        at = self.at
+        self.store = pltpu.make_async_copy(self.total(), self.place(at.seq), self.sems[2].take())
+        self.store.start()
+        self.near = [
+            self.make(self.total(), self.place(at.seq), at.over_x),
+            self.make(self.total(), self.place(at.seq), at.over_y),
+        ]
+
+    def gather_far(self):
+        at = self.at
+        for copy in self.near:
+            copy.wait_recv()
+        half = self.rows // 2
+        self.far = []
+        for turn, (origin, target) in enumerate(((at.near_y, at.over_x), (at.near_x, at.over_y))):
+            ref = self.place(origin, turn, half)
+            self.far.append(self.make(ref, ref, target))
+
+    def gather_end(self):
+        at = self.at
+        self.store.wait()
+        for copy in self.far:
+            copy.wait_recv()
+        if self.arrive is not None:
+            half = 2 * self.rows
+            self.swap = self.make(
+                self.stage.at[aligned((1 - at.core) * half, half), :], self.arrive, at.other
+            )
+
+    def drain(self):
+        if self.swap is not None:
+            self.swap.wait_recv()
+        for copy in self.sends + self.slot_sends[0] + self.slot_sends[1]:
+            copy.wait_send()
+        self.sends, self.slot_sends = [], [[], []]
+
+
+class VectorSum:
+    def __init__(self, at, sems, source, got, hop, total):
+        self.at, self.sems = at, sems
+        self.got, self.hop, self.total = got, hop, total
+        self.copies, self.step = [], 0
+        self.partners = (at.other, at.over_x, at.over_y)
+
+    def send(self, src, dst, target):
+        copy = remote(src, dst, self.sems[0].take(), self.sems[1].take(), target)
+        copy.start()
+        self.copies.append(copy)
+
+    def advance(self):
+        idx, at = self.step, self.at
+        self.step += 1
+        if idx == 0:
+            self.send(self.total.at[0], self.got.at[0], self.partners[0])
+            return
+        self.copies[-1].wait_recv()
+        if idx <= 3:
+            self.total[idx] = self.total[idx - 1] + self.got[idx - 1]
+            if idx < 3:
+                self.send(self.total.at[idx], self.got.at[idx], self.partners[idx])
+            else:
+                self.send(self.total.at[3, at.back(1)], self.hop.at[0], at.up)
+            return
+        hop = idx - 3
+        self.hop[hop - 1] = self.hop[hop - 1] + self.total[3, at.back(hop + 1)]
+        if hop < at.ring - 1:
+            self.send(self.hop.at[hop - 1], self.hop.at[hop], at.up)
+
+
+class Backward:
+    def __init__(self, at, refs, layers):
+        self.at, self.refs, self.layers = at, refs, layers
+        self.blocks = refs.grad.shape[0] // ROWS_Q
+        self.pairs = refs.low.shape[1] // (3 * PAIR)
+        self.slot = 0
+        self.part_copies = {}
+
+    def bring(self, pairs):
+        copies = []
+        for src, dst in pairs:
+            copies.append(pltpu.make_async_copy(src, dst, self.refs.load_sem.at[self.slot]))
+            self.slot += 1
+        for copy in copies:
+            copy.start()
+        return copies
+
+    def bring_now(self, pairs):
+        for copy in self.bring(pairs):
+            copy.wait()
+
+    def saved(self, name, layer):
+        return getattr(self.refs, name + "_in" + str(layer))
+
+    def add_vec(self, row, value):
+        total = jnp.sum(value, axis=0, keepdims=True)
+        width = value.shape[1]
+        self.refs.vgrad[row : row + 1, 0:width] = self.refs.vgrad[row : row + 1, 0:width] + total
+
+    def send_part(self, key, landing):
+        refs = self.refs
+        slot = len(self.part_copies)
+        copy = remote(
+            refs.part, landing, refs.x_send.at[slot], refs.x_recv.at[slot], self.at.other
+        )
+        copy.start()
+        self.part_copies[key] = copy
+
+    def units(self, layer):
+        refs = self.refs
+        if layer == self.layers - 1:
+            self.bring_now([(refs.cot_in, refs.grad)])
+        self.bring_now(
+            [
+                (self.saved("down", layer), refs.w_one),
+                (self.saved("up", layer), refs.w_two),
+                (self.saved("slope", layer), refs.ups),
+            ]
+        )
+        refs.vgrad[...] = jnp.zeros_like(refs.vgrad)
+        tiles = refs.w_one.shape[0] // 512
+
+        def body(rows):
+            grad = refs.grad[rows, :]
+            self.add_vec(5, grad)
+            refs.grad_low[rows, :] = grad.astype(BF)
+
+            @pl.loop(0, tiles)
+            def _(tile):
+                cols = aligned(tile * 512, 512)
+                value = dot_nt(refs.grad_low[rows, :], refs.w_one[cols, :])
+                value = value * refs.ups[rows, cols].astype(F32)
+                total = jnp.sum(value, axis=0, keepdims=True)
+                refs.vgrad[7:8, cols] = refs.vgrad[7:8, cols] + total
+                refs.ups[rows, cols] = value.astype(BF)
+
+            part = dot_nt(refs.ups[rows, :], refs.w_two[...])
+            refs.part_f[rows, :] = part
+            refs.part[rows, :] = part.astype(BF)
+
+        each_block(self.blocks, body)
+        self.send_part((layer, 0), refs.got_one)
+
+    def vec(self, layer, row, width):
+        return self.refs.vecs[layer, row : row + 1, 0:width]
+
+    def norm_blocks(self, layer, first, landing, source, use):
+        refs = self.refs
+
+        def copy_of(step):
+            slot = lax.rem(step, 2)
+            rows = aligned(step * ROWS_Q, ROWS_Q)
+            return pltpu.make_async_copy(
+                source.at[rows, :], refs.aux.at[slot], refs.aux_sem.at[slot]
+            )
+
+        copy_of(0).start()
+
+        @pl.loop(0, self.blocks)
+        def _(step):
+            @pl.when(step + 1 < self.blocks)
+            def _():
+                copy_of(step + 1).start()
+
+            copy_of(step).wait()
+            rows = aligned(step * ROWS_Q, ROWS_Q)
+            use(rows, self.norm_back(rows, layer, first, landing, refs.aux[lax.rem(step, 2)]))
+
+    def norm_back(self, rows, layer, first, landing, hidden):
+        refs = self.refs
+        width = refs.grad.shape[1]
+        part = refs.part_f[rows, :] + landing[rows, :].astype(F32)
+        scaled, inverse = norm_parts(hidden)
+        entry = part * self.vec(layer, first, width)
+        mean_one = jnp.mean(entry, axis=-1, keepdims=True)
+        mean_two = jnp.mean(entry * scaled, axis=-1, keepdims=True)
+        self.add_vec(first, part * scaled)
+        self.add_vec(first + 1, part)
+        grad = refs.grad[rows, :] + inverse * (entry - mean_one - scaled * mean_two)
+        refs.grad[rows, :] = grad
+        return grad
+
+    def after(self, layer):
+        refs = self.refs
+        half = refs.mixed_grad.shape[1]
+        weight = refs.w_one.at[pl.ds(0, half), :]
+        self.bring_now([(self.saved("proj", layer), weight)])
+        self.part_copies[layer, 0].wait()
+
+        def body(rows, grad):
+            self.add_vec(4, grad)
+            low = grad.astype(BF)
+            refs.after_low[rows, :] = low
+            refs.mixed_grad[rows, :] = dot_nt(low, refs.w_one[0:half, :]).astype(BF)
+
+        self.norm_blocks(layer, 2, refs.got_one, self.saved("after", layer), body)
+        self.entry_load = self.bring(
+            [(self.saved("qkv", layer), refs.w_two.at[:, pl.ds(0, refs.low.shape[1])])]
+        )
+
+    def attend(self, layer, pair):
+        refs = self.refs
+        if pair == 0:
+            self.bring_now([(self.saved("low", layer), refs.low)])
+        base = pair * 3 * PAIR
+        query_cols, key_cols, value_cols = [
+            slice(base + kind * PAIR, base + (kind + 1) * PAIR) for kind in range(3)
+        ]
+        refs.keys_t[...] = refs.low[:, key_cols].astype(F32).T.astype(BF)
+        scale = HEAD_DIM**-0.5
+        refs.dk[...] = jnp.zeros_like(refs.dk)
+        refs.dv[...] = jnp.zeros_like(refs.dv)
+
+        def body(rows):
+            block = refs.low[rows, query_cols]
+            dout = refs.mixed_grad[rows, pair * PAIR : (pair + 1) * PAIR]
+            outs = []
+            for head in range(2):
+                mine, dmine = head_mask(block, head), head_mask(dout, head)
+                scores = dot_nt(refs.low[:, key_cols], mine * jnp.asarray(scale, BF))
+                probs = jnp.exp(scores - refs.lse_in[layer, pair, head : head + 1, rows])
+                prob_grad = dot_nt(refs.low[:, value_cols], dmine)
+                delta = jnp.sum(probs * prob_grad, axis=0, keepdims=True)
+                score_low = (probs * (prob_grad - delta) * scale).astype(BF)
+                refs.dv[...] += dot(probs.astype(BF), dmine)
+                refs.dk[...] += dot(score_low, mine)
+                outs.append(dot(refs.keys_t[head * HEAD_DIM : (head + 1) * HEAD_DIM], score_low))
+            refs.dq[rows, :] = jnp.concatenate(outs, axis=0).T
+
+        each_block(self.blocks, body)
+
+        def last(rows):
+            cosine, sine = rotation_tables(refs.tables[rows, :])
+
+            def back(item):
+                item = item.astype(BF).astype(F32)
+                return item * cosine - swap_halves(item) * sine
+
+            parts = (
+                back(refs.dq[rows, :]),
+                back(refs.dk[rows, :]),
+                refs.dv[rows, :].astype(BF).astype(F32),
+            )
+            for kind, part in enumerate(parts):
+                cols = slice(base + kind * PAIR, base + (kind + 1) * PAIR)
+                refs.vgrad[6:7, cols] = refs.vgrad[6:7, cols] + jnp.sum(part, axis=0, keepdims=True)
+                refs.low[rows, cols] = part.astype(BF)
+
+        each_block(self.blocks, last)
+
+    def heads(self, layer):
+        refs = self.refs
+        width = refs.low.shape[1]
+        for copy in self.entry_load:
+            copy.wait()
+
+        def body(rows):
+            part = dot_nt(refs.low[rows, :], refs.w_two[:, 0:width])
+            refs.part_f[rows, :] = part
+            refs.part[rows, :] = part.astype(BF)
+
+        each_block(self.blocks, body)
+        self.send_part((layer, 1), refs.got_two)
+
+    def entry(self, layer):
+        refs = self.refs
+        self.part_copies[layer, 1].wait()
+        source = self.saved("entry", layer)
+        self.norm_blocks(layer, 0, refs.got_two, source, lambda rows, grad: None)
+
+    def weight_tile(self, name, layer):
+        refs = self.refs
+        source, right = {
+            "down": ("active", refs.grad_low),
+            "up": ("normed_two", refs.ups),
+            "proj": ("mixed", refs.after_low),
+            "qkv": ("normed", refs.low),
+        }[name]
+        saved = self.saved(source, layer)
+
+        def compute(tile, out):
+            rows, columns = out.shape
+            held = refs.stream.at[:, pl.ds(0, rows)]
+            self.bring_now([(saved.at[:, aligned(self.at.back(tile + 1) * rows, rows)], held)])
+            high, wide = min(rows, 256), min(columns, 512)
+
+            @pl.loop(0, rows // high)
+            def _(row):
+                at_rows = aligned(row * high, high)
+
+                @pl.loop(0, columns // wide)
+                def _(column):
+                    cols = aligned(column * wide, wide)
+                    out[at_rows, cols] = dot_tn(refs.stream[:, at_rows], right[:, cols]).astype(BF)
+
+        return compute
+
+    def vector_rows(self, target):
+        refs, at = self.refs, self.at
+        target[...] = jnp.zeros_like(target)
+        per_chip = refs.vec_rows * 2
+        keep = (at.core == 0).astype(F32)
+        for row in range(48):
+            source = refs.vgrad[row // 8 : row // 8 + 1, row % 8 * 128 : (row % 8 + 1) * 128]
+            place = row % per_chip
+            target[row // per_chip, place : place + 1, :] = source * keep
+        places = []
+        for pair in range(at.ring):
+            for kind in range(3):
+                places.append((48 + kind * 8 + 2 * pair + at.core, 6, pair * 3 + kind))
+            for part in range(4):
+                places.append((72 + (2 * pair + at.core) * 4 + part, 7, pair * 4 + part))
+        for place, row, block in places:
+            target[lax.div(place, per_chip), pl.ds(lax.rem(place, per_chip), 1), :] = refs.vgrad[
+                row : row + 1, block * 128 : (block + 1) * 128
+            ]
+
+
+def squares_of(ref):
+    rows, columns = ref.shape
+
+    def body(step, total):
+        part = ref[aligned(step * 16, 16), :].astype(F32)
+        part = part * part
+        part = part[0:8] + part[8:16]
+        for column in range(0, columns, 128):
+            total = total + part[:, column : column + 128]
+        return total
+
+    return lax.fori_loop(0, rows // 16, body, jnp.zeros((8, 128), F32))
+
+
+def backward_kernel(names, layers, vec_rows, *operands):
+    refs = SimpleNamespace(**dict(zip(names, operands)))
+    refs.vec_rows = vec_rows
+    at = Places()
+    ring = at.ring
+    sems = (Sems(refs.send_sem), Sems(refs.recv_sem), Sems(refs.store_sem))
+    greet((at.other, at.over_x, at.over_y, at.down), 4)
+    work = Backward(at, refs, layers)
+    sums = {}
+    for layer in range(layers):
+        for name, z_first, x_first in (
+            ("qkv", True, True),
+            ("proj", True, False),
+            ("up", False, True),
+            ("down", False, False),
+        ):
+            sums[name, layer] = Sum(
+                at, sems, refs, name, layer, z_first, x_first, work.weight_tile(name, layer)
+            )
+    vectors = [
+        VectorSum(at, sems, None, refs.vec_got.at[layer], refs.vec_hop.at[layer], refs.vec_sum.at[layer])
+        for layer in range(layers)
+    ]
+    refs.square_sum[0] = jnp.zeros((8, 128), F32)
+    steps = []
+
+    def free(sem):
+        for target in (at.over_x, at.over_y, at.down):
+            pl.semaphore_signal(sem, inc=1, device_id=target, device_id_type=pl.DeviceIdType.MESH)
+
+    def wide_steps(layer):
+        items = [sums["down", layer], sums["up", layer]]
+
+        def turn(tile):
+            for item in items:
+                item.middle(tile)
+            if tile + 2 < ring:
+                for item in items:
+                    item.start(tile + 2)
+            if tile > 0:
+                for item in items:
+                    item.finish(tile - 1)
+
+        def begin(tile):
+            if tile == 0 and layer + 1 < layers:
+                pl.semaphore_wait(refs.free_wide, 3)
+            for item in items:
+                item.start(tile)
+
+        def end():
+            for item in items:
+                item.finish(ring - 1)
+
+        def far():
+            for item in items:
+                item.gather_far()
+
+        def close():
+            for item in items:
+                item.gather_end()
+                refs.square_sum[0] = refs.square_sum[0] + squares_of(item.total())
+            if layer > 0:
+                for item in items:
+                    item.drain()
+                free(refs.free_wide)
+
+        turns = [partial(begin, 0), partial(begin, 1)]
+        turns += [partial(turn, tile) for tile in range(ring)]
+        return turns + [end, far, close]
+
+    def slab_steps(name, layer):
+        item = sums[name, layer]
+
+        def begin():
+            item.start(0)
+
+        def close():
+            item.gather_end()
+            refs.square_sum[0] = refs.square_sum[0] + squares_of(item.total())
+            if layer > 0:
+                item.drain()
+
+        turns = [begin] + [partial(item.ring_step, tile) for tile in range(1, ring)]
+        return turns + [item.slab_middle, item.slab_finish, item.gather_far, close]
+
+    def run(steps, count=1):
+        for _ in range(count):
+            if steps:
+                steps.pop(0)()
+
+    late = []
+    for layer in reversed(range(layers)):
+        last = layer == 0
+        wide, proj, qkv = wide_steps(layer), slab_steps("proj", layer), slab_steps("qkv", layer)
+        work.units(layer)
+        run(late, 3)
+        run(wide, 2)
+        run(late, 2)
+        work.after(layer)
+        run(late, 2)
+        if layer + 1 == layers:
+            run(proj)
+        for pair in range(work.pairs):
+            work.attend(layer, pair)
+            run(wide)
+            run(late, 3)
+            if layer + 1 == layers and pair > 0:
+                run(proj)
+        while late:
+            run(late)
+        if layer + 1 < layers:
+            free(refs.free_slab)
+            pl.semaphore_wait(refs.free_slab, 3)
+            run(proj)
+        work.heads(layer)
+        run(wide)
+        run(proj)
+        run(qkv)
+        work.entry(layer)
+        if last:
+            save = pltpu.make_async_copy(refs.grad, refs.input_grad, sems[2].take())
+            save.start()
+        work.vector_rows(refs.vec_sum.at[layer, 0])
+        run(qkv)
+        run(wide)
+        run(proj)
+        vector = [vectors[layer].advance] * 7
+        while proj or qkv or vector:
+            late += wide[:1] + qkv[:1] + proj[:1] + vector[:1]
+            qkv, proj, vector, wide = qkv[1:], proj[1:], vector[1:], wide[1:]
+        late = late + wide
+        wide = []
+    while late:
+        run(late)
+    save.wait()
+    total = refs.square_sum[0]
+    for layer in range(layers):
+        vec_total = refs.vec_hop[layer, ring - 2]
+        refs.vec_out[layer] = vec_total
+        part = vec_total * vec_total * 0.125
+        for row in range(0, part.shape[0], 8):
+            total = total + part[row : row + 8]
+    refs.square_sum[0] = total
+    copies = []
+
+    def square_copy(src, dst, target):
+        copy = remote(src, dst, sems[0].take(), sems[1].take(), target)
+        copy.start()
+        copies.append(copy)
+        copy.wait_recv()
+
+    for idx, target in enumerate((at.other, at.over_x, at.over_y)):
+        square_copy(refs.square_sum.at[idx], refs.square_got.at[idx], target)
+        refs.square_sum[idx + 1] = refs.square_sum[idx] + refs.square_got[idx]
+    total = refs.square_sum[3]
+    for hop in range(ring - 1):
+        source = refs.square_sum.at[3] if hop == 0 else refs.square_got.at[2 + hop]
+        square_copy(source, refs.square_got.at[3 + hop], at.up)
+        total = total + refs.square_got[3 + hop]
+    refs.square_out[...] = total
+    for name in WEIGHTS:
+        sums[name, 0].drain()
+    for vector in vectors:
+        for copy in vector.copies:
+            copy.wait_send()
+    for copy in copies:
+        copy.wait_send()
+
+
+def backward(kept, layers, vec_rows):
+    ring = lax.axis_size("fsdp") // 2
+    length, width = kept.cot_out.shape
+    qkv_half, up_half = kept.low_out0.shape[1], kept.slope_out0.shape[1]
+    half = kept.mixed_out0.shape[1]
+    inputs = {
+        "cot_in": kept.cot_out,
+        "tables": kept.table_out,
+        "vecs": kept.vecs,
+        "lse_in": kept.lse_out,
+    }
+    for layer in range(layers):
+        for name in (*WEIGHTS, "normed", "low", "mixed", "after", "normed_two", "active", "slope"):
+            inputs[name + "_in" + str(layer)] = getattr(kept, name + "_out" + str(layer))
+        entry = kept.clip_out if layer == 0 else getattr(kept, "result_out" + str(layer - 1))
+        inputs["entry_in" + str(layer)] = entry
+    slabs = {
+        "qkv": (width // ring, qkv_half),
+        "proj": (half // ring, width),
+        "up": (width // ring, up_half),
+        "down": (up_half // ring, width),
+    }
+    outputs, scratch = {}, {}
+    dma, regular = pltpu.SemaphoreType.DMA, pltpu.SemaphoreType.REGULAR
+    for name, (rows, columns) in slabs.items():
+        for layer in range(layers):
+            outputs[name + "_stage" + str(layer)] = ((rows, columns), BF)
+            if name in ("qkv", "up"):
+                outputs[name + "_arrive" + str(layer)] = ((rows // 2, columns), BF)
+        z_first = name in ("qkv", "proj")
+        tiles, quarter = 1 if z_first else ring, rows // 4
+        scratch[name + "_own"] = pltpu.VMEM((2, rows, columns), BF)
+        scratch[name + "_one"] = pltpu.VMEM((tiles, 2 * quarter, columns), BF)
+        scratch[name + "_two"] = pltpu.VMEM((tiles, quarter, columns), BF)
+        scratch[name + "_three"] = pltpu.VMEM(
+            (ring - 1, rows if z_first else quarter, columns), BF
+        )
+    outputs["input_grad"] = ((length, width), F32)
+    outputs["vec_out"] = ((layers, 32, 128), F32)
+    outputs["square_out"] = ((8, 128), F32)
+    scratch |= {
+        "grad": pltpu.VMEM((length, width), F32),
+        "aux": pltpu.VMEM((2, ROWS_Q, width), F32),
+        "aux_sem": dma((2,)),
+        "part_f": pltpu.VMEM((length, width), F32),
+        "grad_low": pltpu.VMEM((length, width), BF),
+        "after_low": pltpu.VMEM((length, width), BF),
+        "part": pltpu.VMEM((length, width), BF),
+        "got_one": pltpu.VMEM((length, width), BF),
+        "got_two": pltpu.VMEM((length, width), BF),
+        "ups": pltpu.VMEM((length, up_half), BF),
+        "w_one": pltpu.VMEM((up_half, width), BF),
+        "w_two": pltpu.VMEM((width, up_half), BF),
+        "low": pltpu.VMEM((length, qkv_half), BF),
+        "mixed_grad": pltpu.VMEM((length, half), BF),
+        "stream": pltpu.VMEM((length, up_half // ring), BF),
+        "keys_t": pltpu.VMEM((PAIR, length), BF),
+        "dq": pltpu.VMEM((length, PAIR), F32),
+        "dk": pltpu.VMEM((length, PAIR), F32),
+        "dv": pltpu.VMEM((length, PAIR), F32),
+        "vgrad": pltpu.VMEM((8, up_half), F32),
+        "vec_got": pltpu.VMEM((layers, 3, ring, 32, 128), F32),
+        "vec_hop": pltpu.VMEM((layers, ring - 1, 32, 128), F32),
+        "vec_sum": pltpu.VMEM((layers, 4, ring, 32, 128), F32),
+        "square_got": pltpu.VMEM((3 + ring - 1, 8, 128), F32),
+        "square_sum": pltpu.VMEM((4, 8, 128), F32),
+        "send_sem": dma((120 * layers,)),
+        "recv_sem": dma((120 * layers,)),
+        "store_sem": dma((8 * layers,)),
+        "load_sem": dma((32 * layers,)),
+        "x_send": dma((2 * layers,)),
+        "x_recv": dma((2 * layers,)),
+        "free_wide": regular,
+        "free_slab": regular,
+    }
+    in_vmem = ("tables", "vecs", "lse_in", "vec_out", "square_out")
+    anywhere = pl.BlockSpec(memory_space=pl.ANY)
+    vmem = pl.BlockSpec(memory_space=pltpu.VMEM)
+    names = [*inputs, *outputs, *scratch]
+    results = pl.pallas_call(
+        partial(backward_kernel, names, layers, vec_rows),
+        in_specs=[vmem if name in in_vmem else anywhere for name in inputs],
+        out_specs=[vmem if name in in_vmem else anywhere for name in outputs],
+        out_shape=[jax.ShapeDtypeStruct(*shape) for shape in outputs.values()],
+        scratch_shapes=list(scratch.values()),
+        compiler_params=pltpu.CompilerParams(
+            collective_id=1, has_side_effects=True, vmem_limit_bytes=63 * 1024 * 1024
+        ),
+        cost_estimate=pl.CostEstimate(
+            flops=100_000_000_000, bytes_accessed=600_000_000, transcendentals=0
+        ),
+        name="backward",
+    )(*inputs.values())
+    return SimpleNamespace(**dict(zip(outputs, results)))
 
 
 def fast_device(
@@ -1869,98 +2083,29 @@
         vector_rows,
         share // 128,
     )
-    vector_all = kept.vec_out.reshape(parts, -1)[:, : vector_params.size]
-    vector_all = vector_all.reshape(parts, layer_count, share).transpose(1, 0, 2)
-    vector_all = vector_all.reshape(layer_count, -1)
-    cosine, sine = kept.table_out[:, : HEAD_DIM // 2], kept.table_out[:, HEAD_DIM // 2 : HEAD_DIM]
-    cos_wide = jnp.concatenate([cosine] * 4, axis=1)
-    sin_wide = jnp.concatenate([-sine, sine, -sine, sine], axis=1)
     block_output = from_clips(getattr(kept, "result_out" + str(layer_count - 1)))
 
-    grad = kept.cot_out
-    sums = [None] * layer_count
-    vector_sums = [None] * layer_count
-    squares = jnp.zeros((8, 128), F32)
-    for idx in reversed(range(layer_count)):
-        qkv_w, proj_w, up_w, down_w, normed, low_all, mixed, after_attn, normed_two, active, slope = [
-            getattr(kept, name + "_out" + str(idx))
-            for name in (*WEIGHTS, "normed", "low", "mixed", "after", "normed_two", "active", "slope")
-        ]
-        entry = kept.clip_out if idx == 0 else getattr(kept, "result_out" + str(idx - 1))
-        lse = kept.lse_out[idx]
-        gain_one, shift_one, gain_two, shift_two, proj_bias, down_bias, qkv_bias, up_bias = pieces(
-            vector_all[idx]
-        )
-        down_bias_grad = jnp.sum(grad, axis=0)
-        grad_low = grad.astype(BF)
-        upward_grad = dot_nt(grad_low, down_w) * slope.astype(F32)
-        up_bias_grad = jnp.sum(upward_grad, axis=0)
-        upward_low = upward_grad.astype(BF)
-        part = dot_nt(upward_low, up_w)
-        other = swap_core(part.astype(BF))
-        down_grad = dot_tn(active, grad_low).astype(BF)
-        up_grad = dot_tn(normed_two, upward_low).astype(BF)
-        attn_in, gain_two_grad, shift_two_grad = norm_backward(
-            after_attn, gain_two, part + other.astype(F32)
-        )
-        after_grad = grad + attn_in
-        proj_bias_grad = jnp.sum(after_grad, axis=0)
-        after_low = after_grad.astype(BF)
-        mixed_grad = dot_nt(after_low, proj_w).astype(BF)
-        proj_grad = dot_tn(mixed, after_low).astype(BF)
-        qkv_low, bias_rows = attend_grad(low_all, mixed_grad, lse, cos_wide, sin_wide)
-        part = dot_nt(qkv_low, qkv_w)
-        other = swap_core(part.astype(BF))
-        qkv_grad = dot_tn(normed, qkv_low).astype(BF)
-        attn_in, gain_one_grad, shift_one_grad = norm_backward(
-            entry, gain_one, part + other.astype(F32)
-        )
-        grad = after_grad + attn_in
-
-        shared = jnp.concatenate(
-            [
-                gain_one_grad,
-                shift_one_grad,
-                gain_two_grad,
-                shift_two_grad,
-                proj_bias_grad,
-                down_bias_grad,
-            ]
-        )
-        vector_sums[idx] = jnp.concatenate(
-            [
-                jnp.where(core == 0, shared, jnp.zeros_like(shared)),
-                spread_bias(bias_rows[0], core, parts, 3),
-                spread_bias(up_bias_grad, core, parts, 1),
-            ]
-        )
-
-        total_vec = vector_sums[idx].reshape(ring, -1)
-        pad = -total_vec.shape[1] % 1024
-        total_vec = jnp.pad(total_vec, ((0, 0), (0, pad))).reshape(ring, 8, -1)
-        sums[idx] = reduce_grads(
-            (qkv_grad, proj_grad, up_grad, down_grad),
-            total_vec,
-            squares,
-            idx == 0,
-            1 + idx,
-        )
-        squares = sums[idx][7]
-    input_grad = from_clips(grad)
+    back = backward(kept, layer_count, share // 128)
+    input_grad = from_clips(back.input_grad)
 
     clip_count = batch_local * parts
-    norm_value = jnp.sqrt(jnp.sum(squares)) / clip_count
+    norm_value = jnp.sqrt(jnp.sum(back.square_out)) / clip_count
     param_count = sum(master.size for master in masters) * parts
     factor = jnp.minimum(1.0, CLIP_RATIO * math.sqrt(float(param_count)) / (norm_value + 1e-06))
 
-    vector_total = jnp.stack([item[6].reshape(-1)[: 2 * share] for item in sums])
+    vector_total = back.vec_out.reshape(layer_count, -1)[:, : 2 * share]
     vector_grad = lax.dynamic_slice_in_dim(vector_total, core * share, share, 1) / clip_count
     vector_new = adam_update(vector_params, vector_grad, first_vector, second_vector, factor)
     updates = [(vector_grad, *vector_new, vector_new[2].astype(BF))]
-    for kind, keys in enumerate(((0, 1), (2,), (3, 4), (5,))):
+    for kind, name in enumerate(WEIGHTS):
+        parts_of = ("_stage", "_arrive") if name in ("qkv", "up") else ("_stage",)
         updates.append(
             adam_matrix(
-                [item[key] for item in sums for key in keys],
+                [
+                    getattr(back, name + part + str(layer))
+                    for layer in range(layer_count)
+                    for part in parts_of
+                ],
                 masters[kind + 1],
                 firsts[kind + 1],
                 seconds[kind + 1],

time: 909 us -> 798 us (0.88)
  matrix products: 107 us -> 0 us
  Pallas kernels: 708 us -> 756 us
  other arithmetic: 60.5 us -> 18.5 us
  local copies, waits for them, and re-layouts: 10.5 us -> 0.08 us
    dot_general x16 -> x0, matrix products: 107 us -> none  [the longest x8 56.1 us: dot_tn(): lax.dot_general(left, right, (((0,), (0,)), ((), ())), preferred_element_...]
    pallas_call x4 -> x1, Pallas kernels: 368 us -> 416 us  [backward(): pl.pallas_call(partial(backward_kernel, names, layers, vec_rows), in_spec...]
    reduce_sum x16 -> x1, other arithmetic: 36.9 us -> 0.6 us  [fast_device(): norm_value = jnp.sqrt(jnp.sum(back.square_out)) / clip_count]
  transfers between devices with their start and end apart: 8 -> 4, of which waited for: 0 -> 0; matrix products, arithmetic and copies ran while one was open for 13% -> 1% of each run, Pallas kernels for 42% -> 59%
where the time goes in v5:
time: 798 us; the launch traced here: 791 us
  Pallas kernels  756 us (95%)
  other arithmetic  18.5 us (2%)
  starting transfers between devices  13.6 us (2%)
    pallas_call x1, Pallas kernels, backward(): pl.pallas_call(partial(backward_kernel, names, layers, vec_rows), in_spec...  416 us
    pallas_call x1, Pallas kernels, forward(): pl.pallas_call(partial(forward_kernel, names, layers, vec_rows), in_specs...  291 us
    pallas_call x4, Pallas kernels, adam_matrix(): pl.pallas_call(partial(adam_kernel, kinds, ring, count), grid_spec=pltpu....  48.8 us
  transfers between devices with their start and end apart: 4, of which 0 were waited for; matrix products, arithmetic and copies ran while one was open for 1% of the time, Pallas kernels for 59%

profile of v5, /device:TPU:0, one launch (start us, length us, event | category | flops | bytes accessed | tf_op | source)
XLA Modules:
  0.0 790.9 jit_solution(14610875075336196600)
XLA Ops:
  0.7 0.8 slice_convert_fusion.1
  1.5 0.7 convert_element_type.41
  2.2 0.6 pad_convert_fusion.operands_7_
  2.8 1.7 fusion.3
  4.6 0.2 maximum_bitcast_fusion.1
  4.7 0.2 maximum_bitcast_fusion
  4.9 0.7 pad_maximum_fusion.operands_6_
  5.6 291.1 %forward.1 = (bf16[1024,1536]{1,0:T(8,128)(2,1)}, bf16[1024,2048]{1,0:T(8,128)(2,1)}, bf16[2048,1024]{1,0:T(8,128)(2,1)}, bf16[512,1024]{1,0:T(8,128)(2,1)}, bf1...) custom-call(f32[2,128,3072]{2,1,0:T(8,128)} %refs_4_.4, ...), custom_call_target="tpu_custom_call" | custom-call | flops 60000002048 | bytes 600000000 | tf_op jit(solution)/shard_map/forward/pallas_call | solution.py:1270
  296.7 3.2 select_bitcast_fusion.3
  299.9 0.4 collective-permute-start.1
  300.3 9.4 %collective-permute-start = (f32[256,1024]{1,0:T(8,128)}, f32[256,1024]{1,0:T(8,128)}, u32[]{:S(2)}, u32[]{:S(2)}) collective-permute-start(f32[256,1024]{1,0:T(8,128)} %get-tuple-element.162), channel_id=1, source_target_pairs={{0,0},{16,1},{2,2},{18,3},{4,4},{20,5},{6,6},{22,7},{8,8},{24,9},{... | collective-permute-start | bytes 3145736 | tf_op jit(solution)/shard_map/ppermute | solution.py:2063
  309.7 416.0 %backward.1 = (bf16[256,1536]{1,0:T(8,128)(2,1)}, bf16[128,1536]{1,0:T(8,128)(2,1)}, bf16[256,1536]{1,0:T(8,128)(2,1)}, bf16[128,1536]{1,0:T(8,128)(2,1)}, bf16[...) custom-call(f32[1024,1024]{1,0:T(8,128)} %get-tuple-element.93.opera, ...), custom_call_target="tpu_custom_call" | custom-call | flops 99999997952 | bytes 600000000 | tf_op jit(solution)/shard_map/backward/pallas_call | solution.py:2002
  725.8 0.0 copy-start.4
  725.8 0.0 copy-start.1
  725.8 1.7 select_bitcast_fusion.1
  727.5 2.1 collective-permute-start.3
  729.6 1.6 collective-permute-start.2
  731.2 0.0 copy-done.4
  731.2 0.6 reduce_sum.9
  732.6 0.0 copy-done.1
  732.6 5.0 update.5
  737.6 11.9 %update.4 = (f32[2,128,3072]{2,1,0:T(8,128)}, f32[2,128,3072]{2,1,0:T(8,128)}, f32[2,128,3072]{2,1,0:T(8,128)}, f32[2,128,3072]{2,1,0:T(8,128)}, bf16[2,128,3072]{2,1,0:T(8,128)(2,1)}) custom-call(s32[1]{0:T(128)} %bitcast.18.core_ref, f32[1]{0:T(128)} %bitcast.19.factor_ref, bf16[256,1536]{1,0:T(8,128)(2,1)} %get-tuple-element.124.refs_0_, ...), custom_call_target="tpu_custom_call" | custom-call | flops 15728640 | bytes 25165824 | tf_op jit(solution)/shard_map/update/pallas_call | solution.py:563
  749.5 17.6 %update.7 = (f32[2,512,1024]{2,1,0:T(8,128)}, f32[2,512,1024]{2,1,0:T(8,128)}, f32[2,512,1024]{2,1,0:T(8,128)}, f32[2,512,1024]{2,1,0:T(8,128)}, bf16[2,512,1024]{2,1,0:T(8,128)(2,1)}) custom-call(s32[1]{0:T(128)} %bitcast.18.core_ref, f32[1]{0:T(128)} %bitcast.19.factor_ref, bf16[512,1024]{1,0:T(8,128)(2,1)} %get-tuple-element.137.refs_0_, ...), custom_call_target="tpu_custom_call" | custom-call | flops 20971520 | bytes 33554432 | tf_op jit(solution)/shard_map/update/pallas_call | solution.py:563
  767.2 0.0 copy-start.3
  767.2 14.2 %update.6 = (f32[2,128,4096]{2,1,0:T(8,128)}, f32[2,128,4096]{2,1,0:T(8,128)}, f32[2,128,4096]{2,1,0:T(8,128)}, f32[2,128,4096]{2,1,0:T(8,128)}, bf16[2,128,4096]{2,1,0:T(8,128)(2,1)}) custom-call(s32[1]{0:T(128)} %bitcast.18.core_ref, f32[1]{0:T(128)} %bitcast.19.factor_ref, bf16[256,2048]{1,0:T(8,128)(2,1)} %get-tuple-element.132.refs_0_, ...), custom_call_target="tpu_custom_call" | custom-call | flops 20971520 | bytes 33554432 | tf_op jit(solution)/shard_map/update/pallas_call | solution.py:563
  781.5 0.7 fusion.6
  782.1 0.0 collective-permute-done.1
  782.1 0.0 collective-permute-done
  782.1 4.2 maximum_select_fusion
  786.4 0.0 collective-permute-done.3
  786.4 0.0 collective-permute-done.2
  786.4 3.2 maximum_select_fusion.1
  (11 shorter events, 0.1 us)
Async XLA Ops:
  299.9 482.2 %collective-permute-start.1 = (f32[256,1024]{1,0:T(8,128)}, f32[256,1024]{1,0:T(8,128)}, u32[]{:S(2)}, u32[]{:S(2)}) collective-permute-start(f32[256,1024]{1,0:T(8,128)} %get-tuple-element.163), channel_id=1, source_target_pairs={{8,0},{24,1},{10,2},{26,3},{12,4},{28,5},{14,6},{30,7},{0,8},{16,9... | collective-permute-start | bytes 3145736 | tf_op jit(solution)/shard_map/ppermute | solution.py:2063
  300.3 481.8 %collective-permute-start = (f32[256,1024]{1,0:T(8,128)}, f32[256,1024]{1,0:T(8,128)}, u32[]{:S(2)}, u32[]{:S(2)}) collective-permute-start(f32[256,1024]{1,0:T(8,128)} %get-tuple-element.162), channel_id=1, source_target_pairs={{0,0},{16,1},{2,2},{18,3},{4,4},{20,5},{6,6},{22,7},{8,8},{24,9},{... | collective-permute-start | bytes 3145736 | tf_op jit(solution)/shard_map/ppermute | solution.py:2063
  725.8 5.5 copy-start.4
  725.8 6.8 copy-start.1
  727.5 58.9 %collective-permute-start.3 = (f32[256,1024]{1,0:T(8,128)S(1)}, f32[256,1024]{1,0:T(8,128)S(1)}, u32[]{:S(2)}, u32[]{:S(2)}) collective-permute-start(f32[256,1024]{1,0:T(8,128)S(1)} %get-tuple-element.161), channel_id=1, source_target_pairs={{8,0},{24,1},{10,2},{26,3},{12,4},{28,5},{14,6},{30,7},{0,8},{16,9... | collective-permute-start | bytes 3145736 | tf_op jit(solution)/shard_map/ppermute | solution.py:2063
  729.6 56.8 %collective-permute-start.2 = (f32[256,1024]{1,0:T(8,128)S(1)}, f32[256,1024]{1,0:T(8,128)}, u32[]{:S(2)}, u32[]{:S(2)}) collective-permute-start(f32[256,1024]{1,0:T(8,128)S(1)} %get-tuple-element.160), channel_id=1, source_target_pairs={{0,0},{16,1},{2,2},{18,3},{4,4},{20,5},{6,6},{22,7},{8,8},{24,9},{... | collective-permute-start | bytes 3145736 | tf_op jit(solution)/shard_map/ppermute | solution.py:2063
  767.2 14.2 %copy-start = (f32[2,1664]{1,0:T(2,128)S(1)}, f32[2,1664]{1,0:T(2,128)}, u32[]{:S(2)}) copy-start(f32[2,1664]{1,0:T(2,128)} %param.21) | copy-start | bytes 39940
  767.2 14.3 %copy-start.2 = (f32[2,1664]{1,0:T(2,128)S(1)}, f32[2,1664]{1,0:T(2,128)}, u32[]{:S(2)}) copy-start(f32[2,1664]{1,0:T(2,128)} %param.31) | copy-start | bytes 39940
  767.2 14.3 %copy-start.3 = (f32[2,1664]{1,0:T(2,128)S(1)}, f32[2,1664]{1,0:T(2,128)}, u32[]{:S(2)}) copy-start(f32[2,1664]{1,0:T(2,128)} %param.26) | copy-start | bytes 39940

commit v6 on v5

--- a/solution.py
+++ b/solution.py
@@ -622,7 +622,7 @@
         self.at, self.refs, self.layers = at, refs, layers
         self.blocks = refs.res.shape[0] // ROWS_Q
         self.pairs = refs.mixed.shape[1] // PAIR
-        self.saves, self.slot = [], 0
+        self.saves, self.loads, self.slot = [], [], 0
         self.mixed_copies, self.part_copies = {}, {}
 
     def save(self, src, dst):
@@ -638,14 +638,16 @@
         self.saves = []
 
     def bring(self, pairs):
-        copies = []
         for src, dst in pairs:
-            copies.append(pltpu.make_async_copy(src, dst, self.refs.save_sem.at[self.slot]))
+            copy = pltpu.make_async_copy(src, dst, self.refs.save_sem.at[self.slot])
             self.slot += 1
-        for copy in copies:
             copy.start()
-        for copy in copies:
+            self.loads.append(copy)
+
+    def arrive(self):
+        for copy in self.loads:
             copy.wait()
+        self.loads = []
 
     def vec(self, layer, row, width):
         return self.refs.vecs[layer, row : row + 1, 0:width]
@@ -676,11 +678,20 @@
         width = hidden.shape[1]
         return (scaled * self.vec(layer, first, width) + self.vec(layer, first + 1, width)).astype(BF)
 
-    def qkv(self, layer, weight):
+    def load_qkv(self, weight):
+        self.bring([(weight, self.refs.w_one.at[:, pl.ds(0, weight.shape[1])])])
+
+    def load_proj(self, own, other):
+        half, target = own.shape[0], self.refs.w_two
+        self.bring([(own, target.at[pl.ds(0, half), :]), (other, target.at[pl.ds(half, half), :])])
+
+    def load_units(self, up_weight, down_weight):
+        self.bring([(up_weight, self.refs.w_one), (down_weight, self.refs.w_two)])
+
+    def qkv(self, layer):
         refs = self.refs
-        width = weight.shape[1]
         self.settle()
-        self.bring([(weight, refs.w_one.at[:, pl.ds(0, width)])])
+        self.arrive()
 
         def body(rows):
             normed = self.normed(rows, layer, 0)
@@ -703,25 +714,26 @@
     def attend(self, layer, pair):
         refs = self.refs
         base = pair * 3 * PAIR
-        key_rows = refs.low[:, base + PAIR : base + 2 * PAIR]
-        for head in range(2):
-            refs.keys[head] = head_mask(key_rows, head)
-        refs.values_t[...] = refs.low[:, base + 2 * PAIR : base + 3 * PAIR].astype(F32).T.astype(BF)
+        key_cols, value_cols = [
+            slice(base + kind * PAIR, base + (kind + 1) * PAIR) for kind in (1, 2)
+        ]
 
         def body(rows):
             block = refs.low[rows, base : base + PAIR] * jnp.asarray(HEAD_DIM**-0.5, BF)
             outs = []
             for head in range(2):
-                scores = lax.dot_general(refs.keys[head], block, NT, preferred_element_type=F32)
-                top = jnp.max(scores, axis=0, keepdims=True)
+                scores = dot_nt(head_mask(block, head), refs.low[:, key_cols])
+                top = jnp.max(scores, axis=1, keepdims=True)
                 exponent = jnp.exp(scores - top)
-                total = jnp.sum(exponent, axis=0, keepdims=True)
-                refs.lse_out[layer, pair, head : head + 1, rows] = top + jnp.log(total)
+                total = jnp.sum(exponent, axis=1, keepdims=True)
+                sums = jnp.broadcast_to(top + jnp.log(total), (ROWS_Q, PAIR)).T
+                refs.lse_out[layer, pair, head : head + 1, rows] = sums[0:1]
                 probs = (exponent * (1.0 / total)).astype(BF)
-                outs.append(dot(refs.values_t[head * HEAD_DIM : (head + 1) * HEAD_DIM], probs))
-            refs.mixed[rows, pair * PAIR : (pair + 1) * PAIR] = (
-                jnp.concatenate(outs, axis=0).T.astype(BF)
-            )
+                outs.append(dot(probs, refs.low[:, value_cols]))
+            lane = lax.broadcasted_iota(jnp.int32, outs[0].shape, 1)
+            refs.mixed[rows, pair * PAIR : (pair + 1) * PAIR] = jnp.where(
+                lane < HEAD_DIM, outs[0], outs[1]
+            ).astype(BF)
 
         each_block(self.blocks, body)
         slot = layer * (self.pairs + 2) + pair
@@ -736,15 +748,10 @@
         copy.start()
         self.mixed_copies[layer, pair] = copy
 
-    def project(self, layer, own, other):
+    def project(self, layer):
         refs = self.refs
-        half = own.shape[0]
-        self.bring(
-            [
-                (own, refs.w_two.at[pl.ds(0, half), :]),
-                (other, refs.w_two.at[pl.ds(half, half), :]),
-            ]
-        )
+        half = refs.mixed.shape[1]
+        self.arrive()
         self.settle()
         for pair in range(self.pairs):
             self.mixed_copies[layer, pair].wait()
@@ -761,11 +768,11 @@
         self.save(refs.res, refs.after_out[layer])
         self.save(refs.norm, refs.normed_two_out[layer])
 
-    def hidden_units(self, layer, half, up_weight, down_weight):
+    def hidden_units(self, layer, half):
         refs = self.refs
         if half == 0:
             self.settle()
-            self.bring([(up_weight, refs.w_one), (down_weight, refs.w_two)])
+            self.arrive()
         width = refs.res.shape[1]
         tiles = refs.w_one.shape[1] // 512
         blocks = self.blocks // 2
@@ -1081,6 +1088,7 @@
             z_copy(idx + 2, 0)
         name, layer = items[idx]
         if name == "proj":
+            flush(0)
             if hop + 1 == hops:
                 stores[idx].wait()
                 slot = len(items) + layer
@@ -1117,19 +1125,18 @@
         work.bring([(refs.clip_out, refs.res), (refs.table_out, refs.tables)])
         work.unpack_vectors()
 
-    def qkv(layer):
+    def load_qkv(layer):
         complete("qkv", layer)
-        work.qkv(layer, outs["qkv"][layer])
-
-    def project(layer):
+        work.load_qkv(outs["qkv"][layer])
+
+    def load_proj(layer):
         complete("proj", layer)
-        work.project(layer, outs["proj"][layer], refs.proj_two_out[layer])
-
-    def hidden_units(layer, half):
-        if half == 0:
-            complete("up", layer)
-            complete("down", layer)
-        work.hidden_units(layer, half, outs["up"][layer], outs["down"][layer])
+        work.load_proj(outs["proj"][layer], refs.proj_two_out[layer])
+
+    def load_units(layer):
+        complete("up", layer)
+        complete("down", layer)
+        work.load_units(outs["up"][layer], outs["down"][layer])
 
     prepare()
     prepare()
@@ -1145,13 +1152,16 @@
         first = layer * per_layer + 2 * hops
         if layer == 0:
             chunks.append((first, take_tokens))
-        chunks.append((first + 1, partial(qkv, layer)))
+        chunks.append((first + 1, partial(load_qkv, layer)))
+        chunks.append((first + 2, partial(work.qkv, layer)))
+        chunks.append((first + 2, partial(load_proj, layer)))
         for pair in range(work.pairs):
-            chunks.append((first + 1 + pair, partial(work.attend, layer, pair)))
-        chunks.append((first + 5, partial(project, layer)))
-        chunks.append((first + 7, partial(hidden_units, layer, 0)))
-        chunks.append((first + 8, partial(hidden_units, layer, 1)))
-        chunks.append((first + 9, partial(work.join, layer)))
+            chunks.append((first + 2 + pair, partial(work.attend, layer, pair)))
+        chunks.append((first + 7, partial(work.project, layer)))
+        chunks.append((first + 7, partial(load_units, layer)))
+        chunks.append((first + 8, partial(work.hidden_units, layer, 0)))
+        chunks.append((first + 9, partial(work.hidden_units, layer, 1)))
+        chunks.append((first + 10, partial(work.join, layer)))
     for number in range(len(order)):
         while chunks and chunks[0][0] <= number:
             chunks.pop(0)[1]()
@@ -1247,8 +1257,6 @@
         "tables": pltpu.VMEM((length, PAIR), F32),
         "norm": pltpu.VMEM((length, width), BF),
         "low": pltpu.VMEM((length, qkv_half), BF),
-        "keys": pltpu.VMEM((2, length, PAIR), BF),
-        "values_t": pltpu.VMEM((PAIR, length), BF),
         "mixed": pltpu.VMEM((length, pairs * PAIR), BF),
         "mixed_other": pltpu.VMEM((length, pairs * PAIR), BF),
         "w_one": pltpu.VMEM((width, up_half), BF),
@@ -1495,7 +1503,20 @@
         self.blocks = refs.grad.shape[0] // ROWS_Q
         self.pairs = refs.low.shape[1] // (3 * PAIR)
         self.slot = 0
-        self.part_copies = {}
+        self.part_copies, self.loads = {}, {}
+
+    def prefetch(self, key, pairs):
+        self.loads[key] = self.bring(pairs)
+
+    def arrive(self, key):
+        for copy in self.loads.pop(key):
+            copy.wait()
+
+    def prefetch_units(self, layer, which):
+        refs = self.refs
+        targets = {"down": refs.w_one, "up": refs.w_two, "slope": refs.ups}
+        for name in which:
+            self.prefetch((name, layer), [(self.saved(name, layer), targets[name])])
 
     def bring(self, pairs):
         copies = []
@@ -1506,10 +1527,6 @@
             copy.start()
         return copies
 
-    def bring_now(self, pairs):
-        for copy in self.bring(pairs):
-            copy.wait()
-
     def saved(self, name, layer):
         return getattr(self.refs, name + "_in" + str(layer))
 
@@ -1530,14 +1547,9 @@
     def units(self, layer):
         refs = self.refs
         if layer == self.layers - 1:
-            self.bring_now([(refs.cot_in, refs.grad)])
-        self.bring_now(
-            [
-                (self.saved("down", layer), refs.w_one),
-                (self.saved("up", layer), refs.w_two),
-                (self.saved("slope", layer), refs.ups),
-            ]
-        )
+            self.arrive(("cot", 0))
+        for name in ("down", "slope", "up"):
+            self.arrive((name, layer))
         refs.vgrad[...] = jnp.zeros_like(refs.vgrad)
         tiles = refs.w_one.shape[0] // 512
 
@@ -1561,6 +1573,8 @@
 
         each_block(self.blocks, body)
         self.send_part((layer, 0), refs.got_one)
+        weight = refs.w_one.at[pl.ds(0, refs.mixed_grad.shape[1]), :]
+        self.prefetch(("proj", layer), [(self.saved("proj", layer), weight)])
 
     def vec(self, layer, row, width):
         return self.refs.vecs[layer, row : row + 1, 0:width]
@@ -1604,8 +1618,8 @@
     def after(self, layer):
         refs = self.refs
         half = refs.mixed_grad.shape[1]
-        weight = refs.w_one.at[pl.ds(0, half), :]
-        self.bring_now([(self.saved("proj", layer), weight)])
+        self.prefetch(("low", layer), [(self.saved("low", layer), refs.low)])
+        self.arrive(("proj", layer))
         self.part_copies[layer, 0].wait()
 
         def body(rows, grad):
@@ -1615,14 +1629,15 @@
             refs.mixed_grad[rows, :] = dot_nt(low, refs.w_one[0:half, :]).astype(BF)
 
         self.norm_blocks(layer, 2, refs.got_one, self.saved("after", layer), body)
-        self.entry_load = self.bring(
-            [(self.saved("qkv", layer), refs.w_two.at[:, pl.ds(0, refs.low.shape[1])])]
-        )
+        weight = refs.w_two.at[:, pl.ds(0, refs.low.shape[1])]
+        self.prefetch(("qkv", layer), [(self.saved("qkv", layer), weight)])
+        if layer > 0:
+            self.prefetch_units(layer - 1, ("down",))
 
     def attend(self, layer, pair):
         refs = self.refs
         if pair == 0:
-            self.bring_now([(self.saved("low", layer), refs.low)])
+            self.arrive(("low", layer))
         base = pair * 3 * PAIR
         query_cols, key_cols, value_cols = [
             slice(base + kind * PAIR, base + (kind + 1) * PAIR) for kind in range(3)
@@ -1672,8 +1687,7 @@
     def heads(self, layer):
         refs = self.refs
         width = refs.low.shape[1]
-        for copy in self.entry_load:
-            copy.wait()
+        self.arrive(("qkv", layer))
 
         def body(rows):
             part = dot_nt(refs.low[rows, :], refs.w_two[:, 0:width])
@@ -1682,6 +1696,8 @@
 
         each_block(self.blocks, body)
         self.send_part((layer, 1), refs.got_two)
+        if layer > 0:
+            self.prefetch_units(layer - 1, ("up", "slope"))
 
     def entry(self, layer):
         refs = self.refs
@@ -1691,18 +1707,23 @@
 
     def weight_tile(self, name, layer):
         refs = self.refs
+        stream = getattr(refs, name + "_stream")
         source, right = {
             "down": ("active", refs.grad_low),
             "up": ("normed_two", refs.ups),
             "proj": ("mixed", refs.after_low),
             "qkv": ("normed", refs.low),
         }[name]
-        saved = self.saved(source, layer)
+        def fetch(tile, layer):
+            rows = stream.shape[1]
+            cols = aligned(self.at.back(tile + 1) * rows, rows)
+            self.prefetch((name, "tile"), [(self.saved(source, layer).at[:, cols], stream)])
 
         def compute(tile, out):
             rows, columns = out.shape
-            held = refs.stream.at[:, pl.ds(0, rows)]
-            self.bring_now([(saved.at[:, aligned(self.at.back(tile + 1) * rows, rows)], held)])
+            if (name, "tile") not in self.loads:
+                fetch(tile, layer)
+            self.arrive((name, "tile"))
             high, wide = min(rows, 256), min(columns, 512)
 
             @pl.loop(0, rows // high)
@@ -1712,7 +1733,12 @@
                 @pl.loop(0, columns // wide)
                 def _(column):
                     cols = aligned(column * wide, wide)
-                    out[at_rows, cols] = dot_tn(refs.stream[:, at_rows], right[:, cols]).astype(BF)
+                    out[at_rows, cols] = dot_tn(stream[:, at_rows], right[:, cols]).astype(BF)
+
+            if tile + 1 < self.at.ring:
+                fetch(tile + 1, layer)
+            elif layer > 0:
+                fetch(0, layer - 1)
 
         return compute
 
@@ -1759,6 +1785,8 @@
     sems = (Sems(refs.send_sem), Sems(refs.recv_sem), Sems(refs.store_sem))
     greet((at.other, at.over_x, at.over_y, at.down), 4)
     work = Backward(at, refs, layers)
+    work.prefetch(("cot", 0), [(refs.cot_in, refs.grad)])
+    work.prefetch_units(layers - 1, ("down", "slope", "up"))
     sums = {}
     for layer in range(layers):
         for name, z_first, x_first in (
@@ -1951,6 +1979,7 @@
                 outputs[name + "_arrive" + str(layer)] = ((rows // 2, columns), BF)
         z_first = name in ("qkv", "proj")
         tiles, quarter = 1 if z_first else ring, rows // 4
+        scratch[name + "_stream"] = pltpu.VMEM((length, rows), BF)
         scratch[name + "_own"] = pltpu.VMEM((2, rows, columns), BF)
         scratch[name + "_one"] = pltpu.VMEM((tiles, 2 * quarter, columns), BF)
         scratch[name + "_two"] = pltpu.VMEM((tiles, quarter, columns), BF)
@@ -1975,7 +2004,6 @@
         "w_two": pltpu.VMEM((width, up_half), BF),
         "low": pltpu.VMEM((length, qkv_half), BF),
         "mixed_grad": pltpu.VMEM((length, half), BF),
-        "stream": pltpu.VMEM((length, up_half // ring), BF),
         "keys_t": pltpu.VMEM((PAIR, length), BF),
         "dq": pltpu.VMEM((length, PAIR), F32),
         "dk": pltpu.VMEM((length, PAIR), F32),

time: 798 us -> 754 us (0.945)
  Pallas kernels: 756 us -> 715 us
    pallas_call x1, Pallas kernels: 291 us -> 267 us  [forward(): pl.pallas_call(partial(forward_kernel, names, layers, vec_rows), in_specs...]
    pallas_call x1, Pallas kernels: 416 us -> 399 us  [backward(): pl.pallas_call(partial(backward_kernel, names, layers, vec_rows), in_spec...]
  transfers between devices with their start and end apart: 4 -> 4, of which waited for: 0 -> 0; matrix products, arithmetic and copies ran while one was open for 1% -> 1% of each run, Pallas kernels for 59% -> 60%
where the time goes in v6:
time: 754 us; the launch traced here: 748 us
  Pallas kernels  715 us (95%)
  other arithmetic  18.5 us (2%)
  starting transfers between devices  12.1 us (2%)
    pallas_call x1, Pallas kernels, backward(): pl.pallas_call(partial(backward_kernel, names, layers, vec_rows), in_spec...  399 us
    pallas_call x1, Pallas kernels, forward(): pl.pallas_call(partial(forward_kernel, names, layers, vec_rows), in_specs...  267 us
    pallas_call x4, Pallas kernels, adam_matrix(): pl.pallas_call(partial(adam_kernel, kinds, ring, count), grid_spec=pltpu....  48.8 us
  transfers between devices with their start and end apart: 4, of which 0 were waited for; matrix products, arithmetic and copies ran while one was open for 1% of the time, Pallas kernels for 60%

profile of v6, /device:TPU:0, one launch (start us, length us, event | category | flops | bytes accessed | tf_op | source)
XLA Modules:
  0.0 748.4 jit_solution(8092576242440826342)
XLA Ops:
  0.7 0.8 slice_convert_fusion.1
  1.5 0.7 convert_element_type.41
  2.2 0.6 pad_convert_fusion.operands_7_
  2.8 1.7 fusion.3
  4.6 0.2 maximum_bitcast_fusion.1
  4.7 0.2 maximum_bitcast_fusion
  4.9 0.7 pad_maximum_fusion.operands_6_
  5.6 267.5 %forward.1 = (bf16[1024,1536]{1,0:T(8,128)(2,1)}, bf16[1024,2048]{1,0:T(8,128)(2,1)}, bf16[2048,1024]{1,0:T(8,128)(2,1)}, bf16[512,1024]{1,0:T(8,128)(2,1)}, bf1...) custom-call(f32[2,128,3072]{2,1,0:T(8,128)} %refs_4_.4, ...), custom_call_target="tpu_custom_call" | custom-call | flops 60000002048 | bytes 600000000 | tf_op jit(solution)/shard_map/forward/pallas_call | solution.py:1278
  273.1 3.2 select_bitcast_fusion.3
  276.3 0.0 collective-permute-start.1
  276.3 9.4 %collective-permute-start = (f32[256,1024]{1,0:T(8,128)}, f32[256,1024]{1,0:T(8,128)}, u32[]{:S(2)}, u32[]{:S(2)}) collective-permute-start(f32[256,1024]{1,0:T(8,128)} %get-tuple-element.162), channel_id=1, source_target_pairs={{0,0},{16,1},{2,2},{18,3},{4,4},{20,5},{6,6},{22,7},{8,8},{24,9},{... | collective-permute-start | bytes 3145736 | tf_op jit(solution)/shard_map/ppermute | solution.py:2091
  285.7 398.6 %backward.1 = (bf16[256,1536]{1,0:T(8,128)(2,1)}, bf16[128,1536]{1,0:T(8,128)(2,1)}, bf16[256,1536]{1,0:T(8,128)(2,1)}, bf16[128,1536]{1,0:T(8,128)(2,1)}, bf16[...) custom-call(f32[1024,1024]{1,0:T(8,128)} %get-tuple-element.93.opera, ...), custom_call_target="tpu_custom_call" | custom-call | flops 99999997952 | bytes 600000000 | tf_op jit(solution)/shard_map/backward/pallas_call | solution.py:2030
  684.3 0.0 copy-start.4
  684.4 0.0 copy-start.1
  684.4 1.7 select_bitcast_fusion.1
  686.1 1.0 collective-permute-start.3
  687.1 1.6 collective-permute-start.2
  688.7 0.0 copy-done.4
  688.8 0.6 reduce_sum.9
  690.1 0.0 copy-done.1
  690.2 5.0 update.5
  695.1 11.9 %update.4 = (f32[2,128,3072]{2,1,0:T(8,128)}, f32[2,128,3072]{2,1,0:T(8,128)}, f32[2,128,3072]{2,1,0:T(8,128)}, f32[2,128,3072]{2,1,0:T(8,128)}, bf16[2,128,3072]{2,1,0:T(8,128)(2,1)}) custom-call(s32[1]{0:T(128)} %bitcast.18.core_ref, f32[1]{0:T(128)} %bitcast.19.factor_ref, bf16[256,1536]{1,0:T(8,128)(2,1)} %get-tuple-element.124.refs_0_, ...), custom_call_target="tpu_custom_call" | custom-call | flops 15728640 | bytes 25165824 | tf_op jit(solution)/shard_map/update/pallas_call | solution.py:563
  707.1 17.6 %update.7 = (f32[2,512,1024]{2,1,0:T(8,128)}, f32[2,512,1024]{2,1,0:T(8,128)}, f32[2,512,1024]{2,1,0:T(8,128)}, f32[2,512,1024]{2,1,0:T(8,128)}, bf16[2,512,1024]{2,1,0:T(8,128)(2,1)}) custom-call(s32[1]{0:T(128)} %bitcast.18.core_ref, f32[1]{0:T(128)} %bitcast.19.factor_ref, bf16[512,1024]{1,0:T(8,128)(2,1)} %get-tuple-element.137.refs_0_, ...), custom_call_target="tpu_custom_call" | custom-call | flops 20971520 | bytes 33554432 | tf_op jit(solution)/shard_map/update/pallas_call | solution.py:563
  724.7 0.0 copy-start.3
  724.7 14.2 %update.6 = (f32[2,128,4096]{2,1,0:T(8,128)}, f32[2,128,4096]{2,1,0:T(8,128)}, f32[2,128,4096]{2,1,0:T(8,128)}, f32[2,128,4096]{2,1,0:T(8,128)}, bf16[2,128,4096]{2,1,0:T(8,128)(2,1)}) custom-call(s32[1]{0:T(128)} %bitcast.18.core_ref, f32[1]{0:T(128)} %bitcast.19.factor_ref, bf16[256,2048]{1,0:T(8,128)(2,1)} %get-tuple-element.132.refs_0_, ...), custom_call_target="tpu_custom_call" | custom-call | flops 20971520 | bytes 33554432 | tf_op jit(solution)/shard_map/update/pallas_call | solution.py:563
  739.0 0.7 fusion.6
  739.6 0.0 collective-permute-done.1
  739.6 0.0 collective-permute-done
  739.6 4.2 maximum_select_fusion
  743.9 0.0 collective-permute-done.3
  743.9 0.0 collective-permute-done.2
  743.9 3.2 maximum_select_fusion.1
  (11 shorter events, 0.1 us)
Async XLA Ops:
  276.3 463.3 %collective-permute-start.1 = (f32[256,1024]{1,0:T(8,128)}, f32[256,1024]{1,0:T(8,128)}, u32[]{:S(2)}, u32[]{:S(2)}) collective-permute-start(f32[256,1024]{1,0:T(8,128)} %get-tuple-element.163), channel_id=1, source_target_pairs={{8,0},{24,1},{10,2},{26,3},{12,4},{28,5},{14,6},{30,7},{0,8},{16,9... | collective-permute-start | bytes 3145736 | tf_op jit(solution)/shard_map/ppermute | solution.py:2091
  276.3 463.3 %collective-permute-start = (f32[256,1024]{1,0:T(8,128)}, f32[256,1024]{1,0:T(8,128)}, u32[]{:S(2)}, u32[]{:S(2)}) collective-permute-start(f32[256,1024]{1,0:T(8,128)} %get-tuple-element.162), channel_id=1, source_target_pairs={{0,0},{16,1},{2,2},{18,3},{4,4},{20,5},{6,6},{22,7},{8,8},{24,9},{... | collective-permute-start | bytes 3145736 | tf_op jit(solution)/shard_map/ppermute | solution.py:2091
  684.3 4.4 copy-start.4
  684.4 5.7 copy-start.1
  686.1 57.8 %collective-permute-start.3 = (f32[256,1024]{1,0:T(8,128)S(1)}, f32[256,1024]{1,0:T(8,128)S(1)}, u32[]{:S(2)}, u32[]{:S(2)}) collective-permute-start(f32[256,1024]{1,0:T(8,128)S(1)} %get-tuple-element.161), channel_id=1, source_target_pairs={{8,0},{24,1},{10,2},{26,3},{12,4},{28,5},{14,6},{30,7},{0,8},{16,9... | collective-permute-start | bytes 3145736 | tf_op jit(solution)/shard_map/ppermute | solution.py:2091
  687.1 56.8 %collective-permute-start.2 = (f32[256,1024]{1,0:T(8,128)S(1)}, f32[256,1024]{1,0:T(8,128)}, u32[]{:S(2)}, u32[]{:S(2)}) collective-permute-start(f32[256,1024]{1,0:T(8,128)S(1)} %get-tuple-element.160), channel_id=1, source_target_pairs={{0,0},{16,1},{2,2},{18,3},{4,4},{20,5},{6,6},{22,7},{8,8},{24,9},{... | collective-permute-start | bytes 3145736 | tf_op jit(solution)/shard_map/ppermute | solution.py:2091
  724.7 14.2 %copy-start = (f32[2,1664]{1,0:T(2,128)S(1)}, f32[2,1664]{1,0:T(2,128)}, u32[]{:S(2)}) copy-start(f32[2,1664]{1,0:T(2,128)} %param.21) | copy-start | bytes 39940
  724.7 14.3 %copy-start.2 = (f32[2,1664]{1,0:T(2,128)S(1)}, f32[2,1664]{1,0:T(2,128)}, u32[]{:S(2)}) copy-start(f32[2,1664]{1,0:T(2,128)} %param.31) | copy-start | bytes 39940
  724.7 14.3 %copy-start.3 = (f32[2,1664]{1,0:T(2,128)S(1)}, f32[2,1664]{1,0:T(2,128)}, u32[]{:S(2)}) copy-start(f32[2,1664]{1,0:T(2,128)} %param.26) | copy-start | bytes 39940

commit v7 on v6

--- a/solution.py
+++ b/solution.py
@@ -9,6 +9,8 @@
 from jax.experimental.pallas import tpu as pltpu
 from jax.sharding import PartitionSpec as P
 
+FSDP = "fsdp"
+SEQ = "seq"
 D = 1024
 HEADS = 16
 HEAD_DIM = 64
@@ -168,12 +170,12 @@
         axis=1,
     ).astype(jnp.bfloat16)
     packed = stacked.reshape(row_count, 3, seq_parts, local_heads * HEAD_DIM)
-    by_heads = lax.all_to_all(packed, "seq", split_axis=2, concat_axis=0, tiled=True)
+    by_heads = lax.all_to_all(packed, SEQ, split_axis=2, concat_axis=0, tiled=True)
     full_len = by_heads.shape[0]
     by_heads = by_heads.reshape(full_len, 3, local_heads, HEAD_DIM)
     mixed_rows, log_sums = attend_forward(by_heads[:, 0], by_heads[:, 1], by_heads[:, 2])
     mixed_low = mixed_rows.astype(jnp.bfloat16).reshape(full_len, 1, local_heads * HEAD_DIM)
-    by_tokens = lax.all_to_all(mixed_low, "seq", split_axis=0, concat_axis=1, tiled=True).reshape(
+    by_tokens = lax.all_to_all(mixed_low, SEQ, split_axis=0, concat_axis=1, tiled=True).reshape(
         row_count, D
     )
     after_attn = hidden + jnp.dot(by_tokens, proj_w, preferred_element_type=jnp.float32) + proj_bias
@@ -226,7 +228,7 @@
     )
     head_grad = lax.all_to_all(
         mixed_grad.reshape(row_count, seq_parts, local_heads * HEAD_DIM),
-        "seq",
+        SEQ,
         split_axis=1,
         concat_axis=0,
         tiled=True,
@@ -242,7 +244,7 @@
         .reshape(full_len, 3, 1, local_heads * HEAD_DIM)
     )
     token_grad = (
-        lax.all_to_all(stacked_grad, "seq", split_axis=0, concat_axis=2, tiled=True)
+        lax.all_to_all(stacked_grad, SEQ, split_axis=0, concat_axis=2, tiled=True)
         .reshape(row_count, 3, HEADS, HEAD_DIM)
         .astype(jnp.float32)
     )
@@ -310,8 +312,8 @@
     lowered = tuple((master.astype(jnp.bfloat16) for master in masters))
     layer_count = vector_params.shape[0]
     batch_local = clip_tokens.shape[0]
-    seq_parts = lax.axis_size("seq")
-    fsdp_parts = lax.axis_size("fsdp")
+    seq_parts = lax.axis_size(SEQ)
+    fsdp_parts = lax.axis_size(FSDP)
     grad_accum = tuple(
         (
             jnp.zeros((layer_count, master.shape[1] * fsdp_parts) + master.shape[2:], jnp.float32)
@@ -326,11 +328,11 @@
         saved_layers = []
         for layer_idx in range(layer_count):
             weights = (
-                lax.all_gather(lowered[0][layer_idx], "fsdp", axis=0, tiled=True),
-                lax.all_gather(lowered[1][layer_idx], "fsdp", axis=0, tiled=True),
-                lax.all_gather(lowered[2][layer_idx], "fsdp", axis=0, tiled=True),
-                lax.all_gather(lowered[3][layer_idx], "fsdp", axis=0, tiled=True),
-                lax.all_gather(lowered[4][layer_idx], "fsdp", axis=0, tiled=True),
+                lax.all_gather(lowered[0][layer_idx], FSDP, axis=0, tiled=True),
+                lax.all_gather(lowered[1][layer_idx], FSDP, axis=0, tiled=True),
+                lax.all_gather(lowered[2][layer_idx], FSDP, axis=0, tiled=True),
+                lax.all_gather(lowered[3][layer_idx], FSDP, axis=0, tiled=True),
+                lax.all_gather(lowered[4][layer_idx], FSDP, axis=0, tiled=True),
             )
             hidden, saved_state = layer_forward(hidden, cosine, sine_table, weights, seq_parts)
             saved_layers.append(saved_state)
@@ -338,11 +340,11 @@
         grad_rows = out_cotangent[batch_idx]
         for layer_idx in reversed(range(layer_count)):
             weights = (
-                lax.all_gather(lowered[0][layer_idx], "fsdp", axis=0, tiled=True),
-                lax.all_gather(lowered[1][layer_idx], "fsdp", axis=0, tiled=True),
-                lax.all_gather(lowered[2][layer_idx], "fsdp", axis=0, tiled=True),
-                lax.all_gather(lowered[3][layer_idx], "fsdp", axis=0, tiled=True),
-                lax.all_gather(lowered[4][layer_idx], "fsdp", axis=0, tiled=True),
+                lax.all_gather(lowered[0][layer_idx], FSDP, axis=0, tiled=True),
+                lax.all_gather(lowered[1][layer_idx], FSDP, axis=0, tiled=True),
+                lax.all_gather(lowered[2][layer_idx], FSDP, axis=0, tiled=True),
+                lax.all_gather(lowered[3][layer_idx], FSDP, axis=0, tiled=True),
+                lax.all_gather(lowered[4][layer_idx], FSDP, axis=0, tiled=True),
             )
             grad_rows, layer_grads = layer_backward(
                 grad_rows, saved_layers[layer_idx], weights, cosine, sine_table, seq_parts
@@ -355,19 +357,19 @@
             )
         input_rows.append(grad_rows)
     shard_sums = (
-        lax.psum_scatter(grad_accum[0], "fsdp", scatter_dimension=1, tiled=True),
-        lax.psum_scatter(grad_accum[1], "fsdp", scatter_dimension=1, tiled=True),
-        lax.psum_scatter(grad_accum[2], "fsdp", scatter_dimension=1, tiled=True),
-        lax.psum_scatter(grad_accum[3], "fsdp", scatter_dimension=1, tiled=True),
-        lax.psum_scatter(grad_accum[4], "fsdp", scatter_dimension=1, tiled=True),
+        lax.psum_scatter(grad_accum[0], FSDP, scatter_dimension=1, tiled=True),
+        lax.psum_scatter(grad_accum[1], FSDP, scatter_dimension=1, tiled=True),
+        lax.psum_scatter(grad_accum[2], FSDP, scatter_dimension=1, tiled=True),
+        lax.psum_scatter(grad_accum[3], FSDP, scatter_dimension=1, tiled=True),
+        lax.psum_scatter(grad_accum[4], FSDP, scatter_dimension=1, tiled=True),
     )
     seq_sums = lax.psum(
-        (shard_sums[0], shard_sums[1], shard_sums[2], shard_sums[3], shard_sums[4]), "seq"
+        (shard_sums[0], shard_sums[1], shard_sums[2], shard_sums[3], shard_sums[4]), SEQ
     )
     clip_count = batch_local * fsdp_parts
     grad_shards = tuple((sum_item / clip_count for sum_item in seq_sums))
     local_squares = sum((jnp.sum(grad_item * grad_item) for grad_item in grad_shards))
-    squares_total = lax.psum(local_squares, "fsdp")
+    squares_total = lax.psum(local_squares, FSDP)
     norm_value = jnp.sqrt(squares_total)
     param_count = sum((master.size for master in masters)) * fsdp_parts
     factor = jnp.minimum(1.0, CLIP_RATIO * math.sqrt(float(param_count)) / (norm_value + 1e-06))
@@ -420,18 +422,18 @@
 
 
 def swap_core(item):
-    parts = lax.axis_size("fsdp")
-    return lax.ppermute(item, "fsdp", [(idx, idx ^ 1) for idx in range(parts)])
+    parts = lax.axis_size(FSDP)
+    return lax.ppermute(item, FSDP, [(idx, idx ^ 1) for idx in range(parts)])
 
 
 def send_up(item):
-    parts = lax.axis_size("fsdp")
-    return lax.ppermute(item, "fsdp", [(idx, (idx + 2) % parts) for idx in range(parts)])
+    parts = lax.axis_size(FSDP)
+    return lax.ppermute(item, FSDP, [(idx, (idx + 2) % parts) for idx in range(parts)])
 
 
 def swap_seq(item, mask):
-    parts = lax.axis_size("seq")
-    return lax.ppermute(item, "seq", [(idx, idx ^ mask) for idx in range(parts)])
+    parts = lax.axis_size(SEQ)
+    return lax.ppermute(item, SEQ, [(idx, idx ^ mask) for idx in range(parts)])
 
 
 def pick(item, index, axis=0):
@@ -457,19 +459,19 @@
 
 class Places:
     def __init__(self):
-        shard, seq = lax.axis_index("fsdp"), lax.axis_index("seq")
-        parts = lax.axis_size("fsdp")
+        shard, seq = lax.axis_index(FSDP), lax.axis_index(SEQ)
+        parts = lax.axis_size(FSDP)
         self.ring = parts // 2
         self.seq = seq
         self.chip, self.core = shard // 2, lax.rem(shard, 2)
         self.at_x, self.at_y = lax.rem(seq, 2), seq // 2
         self.near_x = 2 * self.at_y + 1 - self.at_x
         self.near_y = 2 * (1 - self.at_y) + self.at_x
-        self.other = {"fsdp": shard + 1 - 2 * self.core}
-        self.up = {"fsdp": lax.rem(shard + 2, parts)}
-        self.down = {"fsdp": lax.rem(shard + parts - 2, parts)}
-        self.over_x = {"seq": self.near_x}
-        self.over_y = {"seq": self.near_y}
+        self.other = {FSDP: shard + 1 - 2 * self.core}
+        self.up = {FSDP: lax.rem(shard + 2, parts)}
+        self.down = {FSDP: lax.rem(shard + parts - 2, parts)}
+        self.over_x = {SEQ: self.near_x}
+        self.over_y = {SEQ: self.near_y}
 
     def back(self, hops):
         return lax.rem(self.chip - hops + self.ring, self.ring)
@@ -542,8 +544,8 @@
 
 def adam_matrix(grads, master, first, second, factor, core, kinds, count):
     layers, rows, columns = master.shape
-    ring = lax.axis_size("fsdp") // 2
-    block = 32 if columns > 1024 else 64
+    ring = lax.axis_size(FSDP) // 2
+    block = 16 if columns > 1024 else 64
     steps = rows // block
     per_layer = len(grads) // layers
 
@@ -855,7 +857,7 @@
             pl.semaphore_signal(
                 barrier,
                 inc=1,
-                device_id={"fsdp": 2 * chip + half, "seq": seq ^ step},
+                device_id={FSDP: 2 * chip + half, SEQ: seq ^ step},
                 device_id_type=pl.DeviceIdType.MESH,
             )
     pl.semaphore_wait(barrier, 9)
@@ -871,7 +873,7 @@
 
         def start(self):
             for turn in range(2):
-                target = {"seq": 2 * core + turn, "fsdp": 2 * chip + token_core}
+                target = {SEQ: 2 * core + turn, FSDP: 2 * chip + token_core}
                 away = jnp.logical_not(jnp.logical_and(stays, lax.rem(seq, 2) == turn))
                 copies = [
                     remote(
@@ -1201,17 +1203,17 @@
 
 def forward(qkv, up, down, proj, clips, cots, tables, vectors, vec_rows):
     layers, rows, width = proj.shape
-    parts = lax.axis_size("fsdp")
+    parts = lax.axis_size(FSDP)
     ring = parts // 2
     count, hops = 4 * layers, ring - 1
     length = 4 * clips.shape[1]
     down_rows = down.shape[1]
     qkv_half, up_half = qkv.shape[2] // 2, up.shape[2] // 2
     pairs = qkv_half // (3 * PAIR)
-    inputs = {
-        "qkv_in": qkv, "up_in": up, "down_in": down, "proj_in": proj, "clip_in": clips, "cot_in": cots,
-        "table_in": tables, "vec_in": vectors,
-    }
+    inputs = dict(
+        qkv_in=qkv, up_in=up, down_in=down, proj_in=proj, clip_in=clips, cot_in=cots,
+        table_in=tables, vec_in=vectors,
+    )
     outputs = {}
     for layer in range(layers):
         for name, shape, dtype in (
@@ -1240,40 +1242,40 @@
     anywhere = pl.BlockSpec(memory_space=pl.ANY)
     vmem = pl.BlockSpec(memory_space=pltpu.VMEM)
     dma = pltpu.SemaphoreType.DMA
-    scratch = {
-        "qkv_full": pltpu.VMEM(qkv.shape[1:], F32),
-        "up_full": pltpu.VMEM(up.shape[1:], F32),
-        "down_full": pltpu.VMEM(down.shape[1:], F32),
-        "proj_full": pltpu.VMEM(proj.shape[1:], F32),
-        "qkv_away": pltpu.VMEM((layers, rows, qkv_half), BF),
-        "up_away": pltpu.VMEM((layers, rows, up_half), BF),
-        "qkv_slab": pltpu.VMEM((layers, 2 * rows, qkv_half), BF),
-        "up_slab": pltpu.VMEM((layers, 2 * rows, up_half), BF),
-        "down_slab": pltpu.VMEM((layers, down_rows, width), BF),
-        "proj_slab": pltpu.VMEM((layers, rows, width), BF),
-        "clip_slab": pltpu.VMEM(clips.shape[1:], F32),
-        "table_slab": pltpu.VMEM(tables.shape[1:], F32),
-        "res": pltpu.VMEM((length, width), F32),
-        "tables": pltpu.VMEM((length, PAIR), F32),
-        "norm": pltpu.VMEM((length, width), BF),
-        "low": pltpu.VMEM((length, qkv_half), BF),
-        "mixed": pltpu.VMEM((length, pairs * PAIR), BF),
-        "mixed_other": pltpu.VMEM((length, pairs * PAIR), BF),
-        "w_one": pltpu.VMEM((width, up_half), BF),
-        "w_two": pltpu.VMEM((ring * down_rows, width), BF),
-        "act": pltpu.VMEM((length, up_half), BF),
-        "slope": pltpu.VMEM((length, up_half), BF),
-        "part": pltpu.VMEM((length, width), BF),
-        "part_other": pltpu.VMEM((length, width), BF),
-        "z_send": dma((count * hops,)), "z_recv": dma((count * hops,)),
-        "p_send": dma((2 * count * hops,)), "p_recv": dma((2 * count * hops,)),
-        "d_send": dma((2 * count * hops,)), "d_recv": dma((2 * count * hops,)),
-        "c_send": dma((count + layers,)), "c_recv": dma((count + layers,)),
-        "l_in": dma((count,)), "l_out": dma((count,)),
-        "m_send": dma((32,)), "m_recv": dma((32,)), "m_load": dma((4,)),
-        "x_send": dma((layers * (pairs + 2),)), "x_recv": dma((layers * (pairs + 2),)),
-        "save_sem": dma((16 * layers,)),
-    }
+    scratch = dict(
+        qkv_full=pltpu.VMEM(qkv.shape[1:], F32),
+        up_full=pltpu.VMEM(up.shape[1:], F32),
+        down_full=pltpu.VMEM(down.shape[1:], F32),
+        proj_full=pltpu.VMEM(proj.shape[1:], F32),
+        qkv_away=pltpu.VMEM((layers, rows, qkv_half), BF),
+        up_away=pltpu.VMEM((layers, rows, up_half), BF),
+        qkv_slab=pltpu.VMEM((layers, 2 * rows, qkv_half), BF),
+        up_slab=pltpu.VMEM((layers, 2 * rows, up_half), BF),
+        down_slab=pltpu.VMEM((layers, down_rows, width), BF),
+        proj_slab=pltpu.VMEM((layers, rows, width), BF),
+        clip_slab=pltpu.VMEM(clips.shape[1:], F32),
+        table_slab=pltpu.VMEM(tables.shape[1:], F32),
+        res=pltpu.VMEM((length, width), F32),
+        tables=pltpu.VMEM((length, PAIR), F32),
+        norm=pltpu.VMEM((length, width), BF),
+        low=pltpu.VMEM((length, qkv_half), BF),
+        mixed=pltpu.VMEM((length, pairs * PAIR), BF),
+        mixed_other=pltpu.VMEM((length, pairs * PAIR), BF),
+        w_one=pltpu.VMEM((width, up_half), BF),
+        w_two=pltpu.VMEM((ring * down_rows, width), BF),
+        act=pltpu.VMEM((length, up_half), BF),
+        slope=pltpu.VMEM((length, up_half), BF),
+        part=pltpu.VMEM((length, width), BF),
+        part_other=pltpu.VMEM((length, width), BF),
+        z_send=dma((count * hops,)), z_recv=dma((count * hops,)),
+        p_send=dma((2 * count * hops,)), p_recv=dma((2 * count * hops,)),
+        d_send=dma((2 * count * hops,)), d_recv=dma((2 * count * hops,)),
+        c_send=dma((count + layers,)), c_recv=dma((count + layers,)),
+        l_in=dma((count,)), l_out=dma((count,)),
+        m_send=dma((32,)), m_recv=dma((32,)), m_load=dma((4,)),
+        x_send=dma((layers * (pairs + 2),)), x_recv=dma((layers * (pairs + 2),)),
+        save_sem=dma((16 * layers,)),
+    )
     names = [*inputs, *outputs, *scratch]
     results = pl.pallas_call(
         partial(forward_kernel, names, layers, vec_rows),
@@ -1949,27 +1951,27 @@
 
 
 def backward(kept, layers, vec_rows):
-    ring = lax.axis_size("fsdp") // 2
+    ring = lax.axis_size(FSDP) // 2
     length, width = kept.cot_out.shape
     qkv_half, up_half = kept.low_out0.shape[1], kept.slope_out0.shape[1]
     half = kept.mixed_out0.shape[1]
-    inputs = {
-        "cot_in": kept.cot_out,
-        "tables": kept.table_out,
-        "vecs": kept.vecs,
-        "lse_in": kept.lse_out,
-    }
+    inputs = dict(
+        cot_in=kept.cot_out,
+        tables=kept.table_out,
+        vecs=kept.vecs,
+        lse_in=kept.lse_out,
+    )
     for layer in range(layers):
         for name in (*WEIGHTS, "normed", "low", "mixed", "after", "normed_two", "active", "slope"):
             inputs[name + "_in" + str(layer)] = getattr(kept, name + "_out" + str(layer))
         entry = kept.clip_out if layer == 0 else getattr(kept, "result_out" + str(layer - 1))
         inputs["entry_in" + str(layer)] = entry
-    slabs = {
-        "qkv": (width // ring, qkv_half),
-        "proj": (half // ring, width),
-        "up": (width // ring, up_half),
-        "down": (up_half // ring, width),
-    }
+    slabs = dict(
+        qkv=(width // ring, qkv_half),
+        proj=(half // ring, width),
+        up=(width // ring, up_half),
+        down=(up_half // ring, width),
+    )
     outputs, scratch = {}, {}
     dma, regular = pltpu.SemaphoreType.DMA, pltpu.SemaphoreType.REGULAR
     for name, (rows, columns) in slabs.items():
@@ -1989,40 +1991,40 @@
     outputs["input_grad"] = ((length, width), F32)
     outputs["vec_out"] = ((layers, 32, 128), F32)
     outputs["square_out"] = ((8, 128), F32)
-    scratch |= {
-        "grad": pltpu.VMEM((length, width), F32),
-        "aux": pltpu.VMEM((2, ROWS_Q, width), F32),
-        "aux_sem": dma((2,)),
-        "part_f": pltpu.VMEM((length, width), F32),
-        "grad_low": pltpu.VMEM((length, width), BF),
-        "after_low": pltpu.VMEM((length, width), BF),
-        "part": pltpu.VMEM((length, width), BF),
-        "got_one": pltpu.VMEM((length, width), BF),
-        "got_two": pltpu.VMEM((length, width), BF),
-        "ups": pltpu.VMEM((length, up_half), BF),
-        "w_one": pltpu.VMEM((up_half, width), BF),
-        "w_two": pltpu.VMEM((width, up_half), BF),
-        "low": pltpu.VMEM((length, qkv_half), BF),
-        "mixed_grad": pltpu.VMEM((length, half), BF),
-        "keys_t": pltpu.VMEM((PAIR, length), BF),
-        "dq": pltpu.VMEM((length, PAIR), F32),
-        "dk": pltpu.VMEM((length, PAIR), F32),
-        "dv": pltpu.VMEM((length, PAIR), F32),
-        "vgrad": pltpu.VMEM((8, up_half), F32),
-        "vec_got": pltpu.VMEM((layers, 3, ring, 32, 128), F32),
-        "vec_hop": pltpu.VMEM((layers, ring - 1, 32, 128), F32),
-        "vec_sum": pltpu.VMEM((layers, 4, ring, 32, 128), F32),
-        "square_got": pltpu.VMEM((3 + ring - 1, 8, 128), F32),
-        "square_sum": pltpu.VMEM((4, 8, 128), F32),
-        "send_sem": dma((120 * layers,)),
-        "recv_sem": dma((120 * layers,)),
-        "store_sem": dma((8 * layers,)),
-        "load_sem": dma((32 * layers,)),
-        "x_send": dma((2 * layers,)),
-        "x_recv": dma((2 * layers,)),
-        "free_wide": regular,
-        "free_slab": regular,
-    }
+    scratch |= dict(
+        grad=pltpu.VMEM((length, width), F32),
+        aux=pltpu.VMEM((2, ROWS_Q, width), F32),
+        aux_sem=dma((2,)),
+        part_f=pltpu.VMEM((length, width), F32),
+        grad_low=pltpu.VMEM((length, width), BF),
+        after_low=pltpu.VMEM((length, width), BF),
+        part=pltpu.VMEM((length, width), BF),
+        got_one=pltpu.VMEM((length, width), BF),
+        got_two=pltpu.VMEM((length, width), BF),
+        ups=pltpu.VMEM((length, up_half), BF),
+        w_one=pltpu.VMEM((up_half, width), BF),
+        w_two=pltpu.VMEM((width, up_half), BF),
+        low=pltpu.VMEM((length, qkv_half), BF),
+        mixed_grad=pltpu.VMEM((length, half), BF),
+        keys_t=pltpu.VMEM((PAIR, length), BF),
+        dq=pltpu.VMEM((length, PAIR), F32),
+        dk=pltpu.VMEM((length, PAIR), F32),
+        dv=pltpu.VMEM((length, PAIR), F32),
+        vgrad=pltpu.VMEM((8, up_half), F32),
+        vec_got=pltpu.VMEM((layers, 3, ring, 32, 128), F32),
+        vec_hop=pltpu.VMEM((layers, ring - 1, 32, 128), F32),
+        vec_sum=pltpu.VMEM((layers, 4, ring, 32, 128), F32),
+        square_got=pltpu.VMEM((3 + ring - 1, 8, 128), F32),
+        square_sum=pltpu.VMEM((4, 8, 128), F32),
+        send_sem=dma((120 * layers,)),
+        recv_sem=dma((120 * layers,)),
+        store_sem=dma((8 * layers,)),
+        load_sem=dma((32 * layers,)),
+        x_send=dma((2 * layers,)),
+        x_recv=dma((2 * layers,)),
+        free_wide=regular,
+        free_slab=regular,
+    )
     in_vmem = ("tables", "vecs", "lse_in", "vec_out", "square_out")
     anywhere = pl.BlockSpec(memory_space=pl.ANY)
     vmem = pl.BlockSpec(memory_space=pltpu.VMEM)
@@ -2069,11 +2071,11 @@
     seconds = (second_vector, second_qkv, second_proj, second_up, second_down)
     layer_count = vector_params.shape[0]
     batch_local, chunk_len = clip_tokens.shape[:2]
-    seq_parts = lax.axis_size("seq")
-    parts = lax.axis_size("fsdp")
+    seq_parts = lax.axis_size(SEQ)
+    parts = lax.axis_size(FSDP)
     ring = parts // 2
-    seq = lax.axis_index("seq")
-    shard = lax.axis_index("fsdp")
+    seq = lax.axis_index(SEQ)
+    shard = lax.axis_index(FSDP)
     core = lax.rem(shard, 2)
     even = lax.rem(seq, 2) == 0
 
@@ -2088,7 +2090,7 @@
                     dst_seq = 2 * (src % 2) + (src_seq + turn) % 2
                     dst = src - src % 2 + src_seq // 2
                     pairs.append((dst_seq * parts + dst, src_seq * parts + src))
-            pieces[turn] = lax.ppermute(piece, ("seq", "fsdp"), pairs)
+            pieces[turn] = lax.ppermute(piece, (SEQ, FSDP), pairs)
         return jnp.where(
             even, jnp.stack([pieces[0], pieces[1]]), jnp.stack([pieces[1], pieces[0]])
         )
@@ -2157,54 +2159,54 @@
 
 def solution(mesh):
     in_specs = (
-        P("fsdp", "seq", None),
-        P(None, "fsdp", "seq"),
-        P("fsdp", "seq", None),
-        P(None, "fsdp"),
-        P(None, "fsdp", None),
-        P(None, "fsdp", None),
-        P(None, "fsdp", None),
-        P(None, "fsdp", None),
-        P(None, "fsdp"),
-        P(None, "fsdp", None),
-        P(None, "fsdp", None),
-        P(None, "fsdp", None),
-        P(None, "fsdp", None),
-        P(None, "fsdp"),
-        P(None, "fsdp", None),
-        P(None, "fsdp", None),
-        P(None, "fsdp", None),
-        P(None, "fsdp", None),
+        P(FSDP, SEQ, None),
+        P(None, FSDP, SEQ),
+        P(FSDP, SEQ, None),
+        P(None, FSDP),
+        P(None, FSDP, None),
+        P(None, FSDP, None),
+        P(None, FSDP, None),
+        P(None, FSDP, None),
+        P(None, FSDP),
+        P(None, FSDP, None),
+        P(None, FSDP, None),
+        P(None, FSDP, None),
+        P(None, FSDP, None),
+        P(None, FSDP),
+        P(None, FSDP, None),
+        P(None, FSDP, None),
+        P(None, FSDP, None),
+        P(None, FSDP, None),
     )
     out_specs = (
-        P("fsdp", "seq", None),
-        P("fsdp", "seq", None),
-        P(None, "fsdp"),
-        P(None, "fsdp", None),
-        P(None, "fsdp", None),
-        P(None, "fsdp", None),
-        P(None, "fsdp", None),
+        P(FSDP, SEQ, None),
+        P(FSDP, SEQ, None),
+        P(None, FSDP),
+        P(None, FSDP, None),
+        P(None, FSDP, None),
+        P(None, FSDP, None),
+        P(None, FSDP, None),
         P(),
-        P(None, "fsdp"),
-        P(None, "fsdp", None),
-        P(None, "fsdp", None),
-        P(None, "fsdp", None),
-        P(None, "fsdp", None),
-        P(None, "fsdp"),
-        P(None, "fsdp", None),
-        P(None, "fsdp", None),
-        P(None, "fsdp", None),
-        P(None, "fsdp", None),
-        P(None, "fsdp"),
-        P(None, "fsdp", None),
-        P(None, "fsdp", None),
-        P(None, "fsdp", None),
-        P(None, "fsdp", None),
-        P(None, "fsdp"),
-        P(None, "fsdp", None),
-        P(None, "fsdp", None),
-        P(None, "fsdp", None),
-        P(None, "fsdp", None),
+        P(None, FSDP),
+        P(None, FSDP, None),
+        P(None, FSDP, None),
+        P(None, FSDP, None),
+        P(None, FSDP, None),
+        P(None, FSDP),
+        P(None, FSDP, None),
+        P(None, FSDP, None),
+        P(None, FSDP, None),
+        P(None, FSDP, None),
+        P(None, FSDP),
+        P(None, FSDP, None),
+        P(None, FSDP, None),
+        P(None, FSDP, None),
+        P(None, FSDP, None),
+        P(None, FSDP),
+        P(None, FSDP, None),
+        P(None, FSDP, None),
+        P(None, FSDP, None),
+        P(None, FSDP, None),
     )
     body = fast_device if fits_fast(mesh) else general_device
     return jax.shard_map(

time: 754 us -> 763 us (1.012)
  Pallas kernels: 715 us -> 723 us
    pallas_call x4, Pallas kernels: 48.8 us -> 56.9 us  [adam_matrix(): pl.pallas_call(partial(adam_kernel, kinds, ring, count), grid_spec=pltpu....]
where the time goes in v7:
time: 763 us; the launch traced here: 757 us
  Pallas kernels  723 us (95%)
  other arithmetic  18.5 us (2%)
  starting transfers between devices  12.1 us (2%)
    pallas_call x1, Pallas kernels, backward(): pl.pallas_call(partial(backward_kernel, names, layers, vec_rows), in_spec...  399 us
    pallas_call x1, Pallas kernels, forward(): pl.pallas_call(partial(forward_kernel, names, layers, vec_rows), in_specs...  267 us
    pallas_call x4, Pallas kernels, adam_matrix(): pl.pallas_call(partial(adam_kernel, kinds, ring, count), grid_spec=pltpu....  56.9 us
  transfers between devices with their start and end apart: 4, of which 0 were waited for; matrix products, arithmetic and copies ran while one was open for 1% of the time, Pallas kernels for 60%

profile of v7, /device:TPU:0, one launch (start us, length us, event | category | flops | bytes accessed | tf_op | source)
XLA Modules:
  0.0 756.6 jit_solution(11013412495983666466)
XLA Ops:
  0.7 0.8 slice_convert_fusion.1
  1.5 0.7 convert_element_type.41
  2.2 0.6 pad_convert_fusion.operands_7_
  2.8 1.7 fusion.3
  4.6 0.2 maximum_bitcast_fusion.1
  4.7 0.2 maximum_bitcast_fusion
  4.9 0.7 pad_maximum_fusion.operands_6_
  5.6 267.5 %forward.1 = (bf16[1024,1536]{1,0:T(8,128)(2,1)}, bf16[1024,2048]{1,0:T(8,128)(2,1)}, bf16[2048,1024]{1,0:T(8,128)(2,1)}, bf16[512,1024]{1,0:T(8,128)(2,1)}, bf1...) custom-call(f32[2,128,3072]{2,1,0:T(8,128)} %refs_4_.4, ...), custom_call_target="tpu_custom_call" | custom-call | flops 60000002048 | bytes 600000000 | tf_op jit(solution)/shard_map/forward/pallas_call | solution.py:1280
  273.1 3.2 select_bitcast_fusion.3
  276.3 0.0 collective-permute-start.1
  276.3 9.4 %collective-permute-start = (f32[256,1024]{1,0:T(8,128)}, f32[256,1024]{1,0:T(8,128)}, u32[]{:S(2)}, u32[]{:S(2)}) collective-permute-start(f32[256,1024]{1,0:T(8,128)} %get-tuple-element.162), channel_id=1, source_target_pairs={{0,0},{16,1},{2,2},{18,3},{4,4},{20,5},{6,6},{22,7},{8,8},{24,9},{... | collective-permute-start | bytes 3145736 | tf_op jit(solution)/shard_map/ppermute | solution.py:2093
  285.7 398.6 %backward.1 = (bf16[256,1536]{1,0:T(8,128)(2,1)}, bf16[128,1536]{1,0:T(8,128)(2,1)}, bf16[256,1536]{1,0:T(8,128)(2,1)}, bf16[128,1536]{1,0:T(8,128)(2,1)}, bf16[...) custom-call(f32[1024,1024]{1,0:T(8,128)} %get-tuple-element.93.opera, ...), custom_call_target="tpu_custom_call" | custom-call | flops 99999997952 | bytes 600000000 | tf_op jit(solution)/shard_map/backward/pallas_call | solution.py:2032
  684.3 0.0 copy-start.4
  684.4 1.7 select_bitcast_fusion.1
  686.1 1.0 collective-permute-start.3
  687.1 1.6 collective-permute-start.2
  688.8 0.6 reduce_sum.9
  690.2 5.0 update.5
  695.1 16.5 %update.4 = (f32[2,128,3072]{2,1,0:T(8,128)}, f32[2,128,3072]{2,1,0:T(8,128)}, f32[2,128,3072]{2,1,0:T(8,128)}, f32[2,128,3072]{2,1,0:T(8,128)}, bf16[2,128,3072]{2,1,0:T(8,128)(2,1)}) custom-call(s32[1]{0:T(128)} %bitcast.18.core_ref, f32[1]{0:T(128)} %bitcast.19.factor_ref, bf16[256,1536]{1,0:T(8,128)(2,1)} %get-tuple-element.124.refs_0_, ...), custom_call_target="tpu_custom_call" | custom-call | flops 15728640 | bytes 25165824 | tf_op jit(solution)/shard_map/update/pallas_call | solution.py:565
  711.6 17.6 %update.7 = (f32[2,512,1024]{2,1,0:T(8,128)}, f32[2,512,1024]{2,1,0:T(8,128)}, f32[2,512,1024]{2,1,0:T(8,128)}, f32[2,512,1024]{2,1,0:T(8,128)}, bf16[2,512,1024]{2,1,0:T(8,128)(2,1)}) custom-call(s32[1]{0:T(128)} %bitcast.18.core_ref, f32[1]{0:T(128)} %bitcast.19.factor_ref, bf16[512,1024]{1,0:T(8,128)(2,1)} %get-tuple-element.137.refs_0_, ...), custom_call_target="tpu_custom_call" | custom-call | flops 20971520 | bytes 33554432 | tf_op jit(solution)/shard_map/update/pallas_call | solution.py:565
  729.3 0.0 copy-start.3
  729.3 17.8 %update.6 = (f32[2,128,4096]{2,1,0:T(8,128)}, f32[2,128,4096]{2,1,0:T(8,128)}, f32[2,128,4096]{2,1,0:T(8,128)}, f32[2,128,4096]{2,1,0:T(8,128)}, bf16[2,128,4096]{2,1,0:T(8,128)(2,1)}) custom-call(s32[1]{0:T(128)} %bitcast.18.core_ref, f32[1]{0:T(128)} %bitcast.19.factor_ref, bf16[256,2048]{1,0:T(8,128)(2,1)} %get-tuple-element.132.refs_0_, ...), custom_call_target="tpu_custom_call" | custom-call | flops 20971520 | bytes 33554432 | tf_op jit(solution)/shard_map/update/pallas_call | solution.py:565
  747.1 0.0 copy-done
  747.1 0.0 copy-done.2
  747.1 0.0 copy-done.3
  747.1 0.7 fusion.6
  747.8 0.0 collective-permute-done.1
  747.8 0.0 collective-permute-done
  747.8 4.2 maximum_select_fusion
  752.1 0.0 collective-permute-done.3
  752.1 0.0 collective-permute-done.2
  752.1 3.2 maximum_select_fusion.1
  (11 shorter events, 0.1 us)
Async XLA Ops:
  276.3 471.5 %collective-permute-start.1 = (f32[256,1024]{1,0:T(8,128)}, f32[256,1024]{1,0:T(8,128)}, u32[]{:S(2)}, u32[]{:S(2)}) collective-permute-start(f32[256,1024]{1,0:T(8,128)} %get-tuple-element.163), channel_id=1, source_target_pairs={{8,0},{24,1},{10,2},{26,3},{12,4},{28,5},{14,6},{30,7},{0,8},{16,9... | collective-permute-start | bytes 3145736 | tf_op jit(solution)/shard_map/ppermute | solution.py:2093
  276.3 471.5 %collective-permute-start = (f32[256,1024]{1,0:T(8,128)}, f32[256,1024]{1,0:T(8,128)}, u32[]{:S(2)}, u32[]{:S(2)}) collective-permute-start(f32[256,1024]{1,0:T(8,128)} %get-tuple-element.162), channel_id=1, source_target_pairs={{0,0},{16,1},{2,2},{18,3},{4,4},{20,5},{6,6},{22,7},{8,8},{24,9},{... | collective-permute-start | bytes 3145736 | tf_op jit(solution)/shard_map/ppermute | solution.py:2093
  684.3 4.4 copy-start.4
  684.4 5.7 copy-start.1
  686.1 66.0 %collective-permute-start.3 = (f32[256,1024]{1,0:T(8,128)S(1)}, f32[256,1024]{1,0:T(8,128)S(1)}, u32[]{:S(2)}, u32[]{:S(2)}) collective-permute-start(f32[256,1024]{1,0:T(8,128)S(1)} %get-tuple-element.161), channel_id=1, source_target_pairs={{8,0},{24,1},{10,2},{26,3},{12,4},{28,5},{14,6},{30,7},{0,8},{16,9... | collective-permute-start | bytes 3145736 | tf_op jit(solution)/shard_map/ppermute | solution.py:2093
  687.1 64.9 %collective-permute-start.2 = (f32[256,1024]{1,0:T(8,128)S(1)}, f32[256,1024]{1,0:T(8,128)}, u32[]{:S(2)}, u32[]{:S(2)}) collective-permute-start(f32[256,1024]{1,0:T(8,128)S(1)} %get-tuple-element.160), channel_id=1, source_target_pairs={{0,0},{16,1},{2,2},{18,3},{4,4},{20,5},{6,6},{22,7},{8,8},{24,9},{... | collective-permute-start | bytes 3145736 | tf_op jit(solution)/shard_map/ppermute | solution.py:2093
  729.3 17.8 %copy-start = (f32[2,1664]{1,0:T(2,128)S(1)}, f32[2,1664]{1,0:T(2,128)}, u32[]{:S(2)}) copy-start(f32[2,1664]{1,0:T(2,128)} %param.21) | copy-start | bytes 39940
  729.3 17.8 %copy-start.2 = (f32[2,1664]{1,0:T(2,128)S(1)}, f32[2,1664]{1,0:T(2,128)}, u32[]{:S(2)}) copy-start(f32[2,1664]{1,0:T(2,128)} %param.31) | copy-start | bytes 39940
  729.3 17.8 %copy-start.3 = (f32[2,1664]{1,0:T(2,128)S(1)}, f32[2,1664]{1,0:T(2,128)}, u32[]{:S(2)}) copy-start(f32[2,1664]{1,0:T(2,128)} %param.26) | copy-start | bytes 39940

commit v8 on v7

--- a/solution.py
+++ b/solution.py
@@ -545,7 +545,7 @@
 def adam_matrix(grads, master, first, second, factor, core, kinds, count):
     layers, rows, columns = master.shape
     ring = lax.axis_size(FSDP) // 2
-    block = 16 if columns > 1024 else 64
+    block = 64 if columns > 1024 else min(128, rows)
     steps = rows // block
     per_layer = len(grads) // layers
 

time: 763 us -> 746 us (0.978)
  Pallas kernels: 723 us -> 707 us
    pallas_call x4, Pallas kernels: 56.9 us -> 41.2 us  [adam_matrix(): pl.pallas_call(partial(adam_kernel, kinds, ring, count), grid_spec=pltpu....]
  transfers between devices with their start and end apart: 4 -> 4, of which waited for: 0 -> 0; matrix products, arithmetic and copies ran while one was open for 1% -> 1% of each run, Pallas kernels for 60% -> 59%
where the time goes in v8:
time: 746 us; the launch traced here: 741 us
  Pallas kernels  707 us (95%)
  other arithmetic  18.5 us (2%)
  starting transfers between devices  12.1 us (2%)
    pallas_call x1, Pallas kernels, backward(): pl.pallas_call(partial(backward_kernel, names, layers, vec_rows), in_spec...  399 us
    pallas_call x1, Pallas kernels, forward(): pl.pallas_call(partial(forward_kernel, names, layers, vec_rows), in_specs...  267 us
    pallas_call x4, Pallas kernels, adam_matrix(): pl.pallas_call(partial(adam_kernel, kinds, ring, count), grid_spec=pltpu....  41.2 us
  transfers between devices with their start and end apart: 4, of which 0 were waited for; matrix products, arithmetic and copies ran while one was open for 1% of the time, Pallas kernels for 59%

profile of v8, /device:TPU:0, one launch (start us, length us, event | category | flops | bytes accessed | tf_op | source)
XLA Modules:
  0.0 740.8 jit_solution(11410700208490413198)
XLA Ops:
  0.7 0.8 slice_convert_fusion.1
  1.5 0.7 convert_element_type.41
  2.2 0.6 pad_convert_fusion.operands_7_
  2.8 1.7 fusion.3
  4.6 0.2 maximum_bitcast_fusion.1
  4.7 0.2 maximum_bitcast_fusion
  4.9 0.7 pad_maximum_fusion.operands_6_
  5.6 267.5 %forward.1 = (bf16[1024,1536]{1,0:T(8,128)(2,1)}, bf16[1024,2048]{1,0:T(8,128)(2,1)}, bf16[2048,1024]{1,0:T(8,128)(2,1)}, bf16[512,1024]{1,0:T(8,128)(2,1)}, bf1...) custom-call(f32[2,128,3072]{2,1,0:T(8,128)} %refs_4_.4, ...), custom_call_target="tpu_custom_call" | custom-call | flops 60000002048 | bytes 600000000 | tf_op jit(solution)/shard_map/forward/pallas_call | solution.py:1280
  273.1 3.2 select_bitcast_fusion.3
  276.3 0.0 collective-permute-start.1
  276.3 9.4 %collective-permute-start = (f32[256,1024]{1,0:T(8,128)}, f32[256,1024]{1,0:T(8,128)}, u32[]{:S(2)}, u32[]{:S(2)}) collective-permute-start(f32[256,1024]{1,0:T(8,128)} %get-tuple-element.162), channel_id=1, source_target_pairs={{0,0},{16,1},{2,2},{18,3},{4,4},{20,5},{6,6},{22,7},{8,8},{24,9},{... | collective-permute-start | bytes 3145736 | tf_op jit(solution)/shard_map/ppermute | solution.py:2093
  285.7 398.6 %backward.1 = (bf16[256,1536]{1,0:T(8,128)(2,1)}, bf16[128,1536]{1,0:T(8,128)(2,1)}, bf16[256,1536]{1,0:T(8,128)(2,1)}, bf16[128,1536]{1,0:T(8,128)(2,1)}, bf16[...) custom-call(f32[1024,1024]{1,0:T(8,128)} %get-tuple-element.93.opera, ...), custom_call_target="tpu_custom_call" | custom-call | flops 99999997952 | bytes 600000000 | tf_op jit(solution)/shard_map/backward/pallas_call | solution.py:2032
  684.3 0.0 copy-start.4
  684.4 1.7 select_bitcast_fusion.1
  686.1 1.0 collective-permute-start.3
  687.1 1.6 collective-permute-start.2
  688.8 0.6 reduce_sum.9
  690.2 4.1 update.5
  694.3 10.2 %update.4 = (f32[2,128,3072]{2,1,0:T(8,128)}, f32[2,128,3072]{2,1,0:T(8,128)}, f32[2,128,3072]{2,1,0:T(8,128)}, f32[2,128,3072]{2,1,0:T(8,128)}, bf16[2,128,3072]{2,1,0:T(8,128)(2,1)}) custom-call(s32[1]{0:T(128)} %bitcast.18.core_ref, f32[1]{0:T(128)} %bitcast.19.factor_ref, bf16[256,1536]{1,0:T(8,128)(2,1)} %get-tuple-element.124.refs_0_, ...), custom_call_target="tpu_custom_call" | custom-call | flops 15728640 | bytes 25165824 | tf_op jit(solution)/shard_map/update/pallas_call | solution.py:565
  704.5 14.1 %update.7 = (f32[2,512,1024]{2,1,0:T(8,128)}, f32[2,512,1024]{2,1,0:T(8,128)}, f32[2,512,1024]{2,1,0:T(8,128)}, f32[2,512,1024]{2,1,0:T(8,128)}, bf16[2,512,1024]{2,1,0:T(8,128)(2,1)}) custom-call(s32[1]{0:T(128)} %bitcast.18.core_ref, f32[1]{0:T(128)} %bitcast.19.factor_ref, bf16[512,1024]{1,0:T(8,128)(2,1)} %get-tuple-element.137.refs_0_, ...), custom_call_target="tpu_custom_call" | custom-call | flops 20971520 | bytes 33554432 | tf_op jit(solution)/shard_map/update/pallas_call | solution.py:565
  718.6 0.0 copy-start.3
  718.6 12.8 %update.6 = (f32[2,128,4096]{2,1,0:T(8,128)}, f32[2,128,4096]{2,1,0:T(8,128)}, f32[2,128,4096]{2,1,0:T(8,128)}, f32[2,128,4096]{2,1,0:T(8,128)}, bf16[2,128,4096]{2,1,0:T(8,128)(2,1)}) custom-call(s32[1]{0:T(128)} %bitcast.18.core_ref, f32[1]{0:T(128)} %bitcast.19.factor_ref, bf16[256,2048]{1,0:T(8,128)(2,1)} %get-tuple-element.132.refs_0_, ...), custom_call_target="tpu_custom_call" | custom-call | flops 20971520 | bytes 33554432 | tf_op jit(solution)/shard_map/update/pallas_call | solution.py:565
  731.4 0.0 copy-done
  731.4 0.0 copy-done.2
  731.4 0.0 copy-done.3
  731.4 0.7 fusion.6
  732.1 0.0 collective-permute-done.1
  732.1 0.0 collective-permute-done
  732.1 4.2 maximum_select_fusion
  736.3 0.0 collective-permute-done.3
  736.3 0.0 collective-permute-done.2
  736.3 3.2 maximum_select_fusion.1
  (11 shorter events, 0.1 us)
Async XLA Ops:
  276.3 455.8 %collective-permute-start.1 = (f32[256,1024]{1,0:T(8,128)}, f32[256,1024]{1,0:T(8,128)}, u32[]{:S(2)}, u32[]{:S(2)}) collective-permute-start(f32[256,1024]{1,0:T(8,128)} %get-tuple-element.163), channel_id=1, source_target_pairs={{8,0},{24,1},{10,2},{26,3},{12,4},{28,5},{14,6},{30,7},{0,8},{16,9... | collective-permute-start | bytes 3145736 | tf_op jit(solution)/shard_map/ppermute | solution.py:2093
  276.3 455.8 %collective-permute-start = (f32[256,1024]{1,0:T(8,128)}, f32[256,1024]{1,0:T(8,128)}, u32[]{:S(2)}, u32[]{:S(2)}) collective-permute-start(f32[256,1024]{1,0:T(8,128)} %get-tuple-element.162), channel_id=1, source_target_pairs={{0,0},{16,1},{2,2},{18,3},{4,4},{20,5},{6,6},{22,7},{8,8},{24,9},{... | collective-permute-start | bytes 3145736 | tf_op jit(solution)/shard_map/ppermute | solution.py:2093
  684.3 4.4 copy-start.4
  684.4 5.7 copy-start.1
  686.1 50.2 %collective-permute-start.3 = (f32[256,1024]{1,0:T(8,128)S(1)}, f32[256,1024]{1,0:T(8,128)S(1)}, u32[]{:S(2)}, u32[]{:S(2)}) collective-permute-start(f32[256,1024]{1,0:T(8,128)S(1)} %get-tuple-element.161), channel_id=1, source_target_pairs={{8,0},{24,1},{10,2},{26,3},{12,4},{28,5},{14,6},{30,7},{0,8},{16,9... | collective-permute-start | bytes 3145736 | tf_op jit(solution)/shard_map/ppermute | solution.py:2093
  687.1 49.2 %collective-permute-start.2 = (f32[256,1024]{1,0:T(8,128)S(1)}, f32[256,1024]{1,0:T(8,128)}, u32[]{:S(2)}, u32[]{:S(2)}) collective-permute-start(f32[256,1024]{1,0:T(8,128)S(1)} %get-tuple-element.160), channel_id=1, source_target_pairs={{0,0},{16,1},{2,2},{18,3},{4,4},{20,5},{6,6},{22,7},{8,8},{24,9},{... | collective-permute-start | bytes 3145736 | tf_op jit(solution)/shard_map/ppermute | solution.py:2093
  718.5 12.8 %copy-start = (f32[2,1664]{1,0:T(2,128)S(1)}, f32[2,1664]{1,0:T(2,128)}, u32[]{:S(2)}) copy-start(f32[2,1664]{1,0:T(2,128)} %param.21) | copy-start | bytes 39940
  718.6 12.8 %copy-start.2 = (f32[2,1664]{1,0:T(2,128)S(1)}, f32[2,1664]{1,0:T(2,128)}, u32[]{:S(2)}) copy-start(f32[2,1664]{1,0:T(2,128)} %param.31) | copy-start | bytes 39940
  718.6 12.8 %copy-start.3 = (f32[2,1664]{1,0:T(2,128)S(1)}, f32[2,1664]{1,0:T(2,128)}, u32[]{:S(2)}) copy-start(f32[2,1664]{1,0:T(2,128)} %param.26) | copy-start | bytes 39940
